TPU v7x, 32 devices: a whole 2x2x4 slice. The times are simulated.
32 devices in a mesh: rep: 2 (over x), batch: 16 (over z, y, core).
Axes of the slice: x: 2, y: 2, z: 4, core: 2. Of those that a mesh axis runs over, the one named last changes fastest.
Arguments:
- tokens: bfloat16 [8192, 8192], P(('rep', 'batch')), parts along dimension 0, may hold values from -6 to 6
- key_matrix: bfloat16 [8192, 768], P('batch'), may hold values from -0.0625 to 0.0625
- adapter_down_factors: bfloat16 [8192, 16, 64], P('batch'), may hold values from -0.0625 to 0.0625
- adapter_up_factors: bfloat16 [16, 64, 768], replicated, may hold values from -0.75 to 0.75
- request_block_list: int32 [16], P('rep'), parts along dimension 0, may hold values from 1 to 16, 32 in all
- request_adapter_index: int32 [16], P('rep'), parts along dimension 0, may hold values from 0 to 15
- request_tail_tokens: int32 [16], P('rep'), parts along dimension 0, may hold values from 1 to 128
Outputs:
- keys: bfloat16 [8192, 768], P(('rep', 'batch')), parts along dimension 0
There are 2 independent parts, one for each index of `rep`. A program takes and returns all parts, laid end to end along the dimension named above; an argument that names none is the same for every part. Nothing has to cross between parts.
Inputs may be any that keep to these rules, and one draw needn't show every extreme that they name: request_block_list sum to 32, each at least 1, one exactly 16.
All inputs are finite; a program needn't handle non-finite values.
Results may differ from a plain program's by a relative error of at most 0.004.
Values may be sent and summed in bfloat16 or wider, within the bound.
No kernel may reach another device: no remote copies, remote signals or barrier semaphores. Data moves between devices by JAX's collectives and lax.ppermute only.
A program may use at most 128 MiB of HBM per device.

v0:
```python
import jax
import jax.numpy as jnp
from jax import lax
from jax.sharding import PartitionSpec as P

BLOCK = 128


def block_table(request_block_list, request_adapter_index, request_tail_tokens, count_blocks):
    block_ends = jnp.cumsum(request_block_list)
    block_index = jnp.arange(count_blocks, dtype=jnp.int32)
    owner_req = jnp.sum((block_ends[None, :] <= block_index[:, None]).astype(jnp.int32), axis=1)
    request_ids = jnp.arange(request_block_list.shape[0], dtype=jnp.int32)
    matched = owner_req[:, None] == request_ids[None, :]
    adapter_of = jnp.sum(jnp.where(matched, request_adapter_index[None, :], 0), axis=1)
    last_of = jnp.sum(jnp.where(matched, block_ends[None, :] - 1, 0), axis=1)
    tail_of = jnp.sum(jnp.where(matched, request_tail_tokens[None, :], 0), axis=1)
    limit_of = jnp.where(last_of == block_index, tail_of, BLOCK)
    return (adapter_of, limit_of)


def shards(
    tokens,
    key_matrix,
    adapter_down_factors,
    adapter_up_factors,
    request_block_list,
    request_adapter_index,
    request_tail_tokens,
):
    local_rows = tokens.shape[0]
    local_blocks = local_rows // BLOCK
    devices = lax.axis_size("batch")
    all_blocks = local_blocks * devices
    adapter_of, limit_of = block_table(
        request_block_list, request_adapter_index, request_tail_tokens, all_blocks
    )
    first_block = lax.axis_index("batch") * local_blocks
    current_adapter = lax.dynamic_slice_in_dim(adapter_of, first_block, local_blocks)
    my_limit = lax.dynamic_slice_in_dim(limit_of, first_block, local_blocks)
    out_width = key_matrix.shape[1]
    columns = tokens
    base = jnp.dot(
        columns,
        lax.all_gather(key_matrix, "batch", axis=0, tiled=True),
        preferred_element_type=jnp.float32,
    )
    request_segment = lax.all_gather(adapter_down_factors, "batch", axis=0, tiled=True)
    columns = tokens
    blocked = columns.reshape(local_blocks, BLOCK, request_segment.shape[0])
    chosen = jnp.take(request_segment, current_adapter, axis=1)
    low_sum = jnp.einsum("btp,pbr->btr", blocked, chosen, preferred_element_type=jnp.float32)
    low = low_sum.astype(jnp.bfloat16)
    up_factor_picked = jnp.take(adapter_up_factors, current_adapter, axis=0)
    delta = jnp.einsum("btr,bro->bto", low, up_factor_picked, preferred_element_type=jnp.float32)
    live = (jnp.arange(BLOCK, dtype=jnp.int32)[None, :] < my_limit[:, None]).astype(jnp.float32)
    summed = (base.reshape(local_blocks, BLOCK, out_width) + delta) * live[:, :, None]
    return summed.reshape(local_rows, out_width).astype(jnp.bfloat16)


def solution(mesh):
    placed = (
        P(("rep", "batch"), None),
        P("batch", None),
        P("batch", None, None),
        P(),
        P("rep"),
        P("rep"),
        P("rep"),
    )
    return jax.shard_map(
        shards, mesh=mesh, in_specs=placed, out_specs=P(("rep", "batch"), None), check_vma=False
    )
```

profile of v0, /device:TPU:0, one launch (start us, length us, event | category | flops | bytes accessed | tf_op | source)
XLA Modules:
  0.0 264.0 jit_solution(10430940765894854064)
XLA Ops:
  6.5 0.0 copy-start
  6.5 0.0 all-gather.3.cloned.1.call-start
  6.5 0.7 all-gather.3.cloned.1.call-update
  7.3 0.0 all-gather.5.cloned.1.call-start
  7.3 0.7 all-gather.5.cloned.1.call-update
  8.0 0.8 reduce-window.7
  8.8 0.1 convert_reduce_fusion
  8.9 0.8 select_reduce_fusion.1
  9.7 0.1 dynamic_slice.7
  9.8 0.1 compare_and_fusion
  9.9 0.0 copy-done
  9.9 0.6 gather_fusion.1
  10.4 0.1 compare_convert_fusion
  10.5 102.6 %all-gather.3.cloned.1.call-done = bf16[8192,768]{1,0:T(8,128)(2,1)} async-done(((bf16[512,768]{1,0:T(8,128)(2,1)}), bf16[8192,768]{1,0:T(8,128)(2,1)}) %all-gather.3.cloned.1.call-update) | async-done | bytes 12582928 | tf_op jit(solution)/shard_map/all_gather | solution.py:45
  113.1 8.8 %fusion.18 = f32[256,768]{1,0:T(8,128)S(1)} fusion(bf16[256,8192]{1,0:T(8,128)(2,1)} %param.7, bf16[8192,768]{1,0:T(8,128)(2,1)} %all-gather.3.cloned.1.call-done), kind=kOutput, calls=%fused_computation.27 | convolution fusion | flops 3221225472 | bytes 17563648 | tf_op jit(solution)/shard_map/dot_general | solution.py:43
  122.0 121.9 %all-gather.5.cloned.1.call-done = bf16[8192,16,64]{0,2,1:T(8,128)(2,1)} async-done(((bf16[512,16,64]{0,2,1:T(8,128)(2,1)}), bf16[8192,16,64]{0,2,1:T(8,128)(2,1)}) %all-gather.5.cloned.1.call-update) | async-done | bytes 16777232 | tf_op jit(solution)/shard_map/all_gather | solution.py:48
  243.8 7.8 %gather_fusion = bf16[2,8192,64]{1,2,0:T(8,128)(2,1)} fusion(bf16[8192,16,64]{0,2,1:T(8,128)(2,1)} %all-gather.5.cloned.1.call-done, s32[1024]{0:T(1024)S(1)} %pad_clamp_fusion), kind=kCustom, calls=%fused_computation | custom fusion | bytes 4194312 | tf_op jit(solution)/shard_map/jit(_take)/gather | solution.py:51
  251.6 5.5 %fusion.5 = bf16[2,128,768]{2,1,0:T(8,128)(2,1)} fusion(f32[2,128,768]{2,1,0:T(8,128)S(1)} %bitcast.18, bf16[2,128,8192]{2,1,0:T(8,128)(2,1)} %bitcast.16, bf16[2,8192,64]{1,2,0:T(8,128)(2,1)} %gather_fusion, pred[2]{0:T(512)(128)(4,1)S(1)} %get-tuple-element.8, f32[2,128]{1,0:T(2,128)S(1)} %compare_convert_fusion, bf16[2,64,768]{2,1,0:T(8,128)(2,1)S(1)} %gather_fusion.1), kind=kOutput, calls=%fused_computation.8 | convolution fusion | flops 295354368 | bytes 7668738 | tf_op jit(solution)/shard_map/btr,bro->bto/dot_general | solution.py:55
  (3 shorter events, 0.0 us)
Async XLA Ops:
  6.5 3.3 %copy-start = (bf16[16,64,768]{2,1,0:T(8,128)(2,1)S(1)}, bf16[16,64,768]{2,1,0:T(8,128)(2,1)}, u32[]{:S(2)}) copy-start(bf16[16,64,768]{2,1,0:T(8,128)(2,1)} %param.10) | copy-start | bytes 4718596
  6.5 106.6 %all-gather.3.cloned.1.call-start = ((), (), s32[]{:S(2)}) async-start(), calls=%async_computation | async-start | bytes 13369344 | tf_op jit(solution)/shard_map/all_gather | solution.py:45
  7.3 236.6 %all-gather.5.cloned.1.call-start = ((), (), s32[]{:S(2)}) async-start(), calls=%async_computation.1 | async-start | bytes 17825792 | tf_op jit(solution)/shard_map/all_gather | solution.py:48
Sparse Core Ops, SparseCore 0:
  9.6 103.4 all-gather.2
  115.3 128.5 all-gather.4
where the time goes:
time: 264 us
  waiting for transfers between devices  226 us (86%)
  matrix products  14.3 us (5%)
  between operations  13.4 us (5%)
  local copies, waits for them, and re-layouts  8.44 us (3%)
    all_gather x1, waiting for transfers between devices, shards(): lax.all_gather(adapter_down_factors, 'batch', axis=0, tiled=True)  122 us
    all_gather x1, waiting for transfers between devices, shards(): lax.all_gather(key_matrix, 'batch', axis=0, tiled=True)  103 us
    dot_general x1, matrix products, shards(): jnp.dot(columns, lax.all_gather(key_matrix, 'batch', axis=0, tiled=True),...  8.83 us
    gather x1, local copies, waits for them, and re-layouts, shards(): chosen = jnp.take(request_segment, current_adapter, axis=1)  7.8 us
    dot_general x1, matrix products, shards(): jnp.einsum('btr,bro->bto', low, up_factor_picked, preferred_element_type=...  5.48 us
  transfers between devices with their start and end apart: 2, of which 2 were waited for; matrix products, arithmetic and copies ran while one was open for 4% of the time, Pallas kernels for 0%

commit v1 on v0

v1 whole, which is shorter than its diff:
```python
import jax
import jax.numpy as jnp
from jax import lax
from jax.sharding import PartitionSpec as P

BLOCK = 128
LAYER_CHIPS = 4


def block_table(request_block_list, request_adapter_index, request_tail_tokens, count_blocks):
    block_ends = jnp.cumsum(request_block_list)
    block_index = jnp.arange(count_blocks, dtype=jnp.int32)
    owner_req = jnp.sum((block_ends[None, :] <= block_index[:, None]).astype(jnp.int32), axis=1)
    request_ids = jnp.arange(request_block_list.shape[0], dtype=jnp.int32)
    matched = owner_req[:, None] == request_ids[None, :]
    adapter_of = jnp.sum(jnp.where(matched, request_adapter_index[None, :], 0), axis=1)
    last_of = jnp.sum(jnp.where(matched, block_ends[None, :] - 1, 0), axis=1)
    tail_of = jnp.sum(jnp.where(matched, request_tail_tokens[None, :], 0), axis=1)
    limit_of = jnp.where(last_of == block_index, tail_of, BLOCK)
    return (owner_req, adapter_of, limit_of)


def swap(value, axis, bit):
    return lax.ppermute(value, axis, [(i, i ^ bit) for i in range(lax.axis_size(axis))])


def shards(
    tokens,
    key_matrix,
    adapter_down_factors,
    adapter_up_factors,
    request_block_list,
    request_adapter_index,
    request_tail_tokens,
):
    rows, width = tokens.shape
    depth, out_width = key_matrix.shape
    adapters, rank = adapter_down_factors.shape[1:]
    reps, devices = lax.axis_size("rep"), lax.axis_size("batch")
    group = 2 * LAYER_CHIPS // reps
    layers = devices // group
    part = depth // reps
    rep, me = lax.axis_index("rep"), lax.axis_index("batch")
    layer, spot = me // group, me % group
    local_blocks = rows // BLOCK

    owner_of, adapter_of, limit_of = block_table(
        request_block_list, request_adapter_index, request_tail_tokens, local_blocks * devices
    )

    part_starts = [(rep ^ h) * part for h in range(reps)]

    down = jnp.transpose(adapter_down_factors, (1, 2, 0))
    requests = request_adapter_index.shape[0]
    if requests < adapters:
        slots, slot_of = requests, owner_of
        picks = [request_adapter_index[q] for q in range(requests)]
    else:
        slots, slot_of = adapters, adapter_of
        picks = range(adapters)
    down = jnp.concatenate(
        [
            jnp.concatenate(
                [lax.dynamic_slice(down, (q, 0, start), (1, rank, part)) for q in picks], 0
            )
            for start in part_starts
        ],
        2,
    ).reshape(slots * rank, depth)

    key_parts = [lax.dynamic_slice_in_dim(key_matrix, start, part, 0) for start in part_starts]
    held_key = key_parts[0]
    bundles = []
    bit = layers // 2
    while bit:
        moved = [([bit], swap(held_key, "batch", bit * group), swap(down, "batch", bit * group))]
        if bundles:
            from_keys = [k for _, k, _ in bundles]
            from_downs = [d for _, _, d in bundles]
            from_keys = from_keys[0] if len(bundles) == 1 else jnp.concatenate(from_keys, 0)
            from_downs = from_downs[0] if len(bundles) == 1 else jnp.concatenate(from_downs, 0)
            order = [t ^ bit for ts, _, _ in bundles for t in ts]
            moved.append(
                (order, swap(from_keys, "batch", bit * group), swap(from_downs, "batch", bit * group))
            )
        bundles = bundles + moved
        bit //= 2
    weights, downs = {0: jnp.concatenate(key_parts, 0)}, {0: down}
    for ts, k, d in bundles:
        halves = [k] + [swap(k, "rep", h) for h in range(1, reps)]
        for i, t in enumerate(ts):
            weights[t] = jnp.concatenate([half[i * part : (i + 1) * part] for half in halves], 0)
            downs[t] = d[i * slots * rank : (i + 1) * slots * rank]

    def columns(spot_of, t):
        start = ((layer ^ t) * group + spot_of) * depth
        return [lax.dynamic_slice_in_dim(tokens, start + p, part, 1) for p in part_starts]

    pieces = []
    for s in range(group):
        piece = jnp.concatenate(sum([columns(spot ^ s, t) for t in range(layers)], []), 1)
        pieces.append(swap(piece, "batch", s) if s else piece)
    held = jnp.concatenate(pieces, 0)

    base = low = 0.0
    for t in weights:
        mine = held[:, t * depth : (t + 1) * depth]
        base = base + jnp.dot(mine, weights[t], preferred_element_type=jnp.float32)
        low = low + lax.dot_general(
            mine, downs[t], (((1,), (1,)), ((), ())), preferred_element_type=jnp.float32
        )
    base = base.reshape(group, rows, out_width)

    spots = spot ^ jnp.arange(group, dtype=jnp.int32)
    blocks_of = (layer * group + spots)[:, None] * local_blocks + jnp.arange(local_blocks)[None, :]
    slot_here = jnp.take(slot_of, blocks_of)
    chosen = slot_here[:, :, None] == jnp.arange(slots)[None, None, :]
    low = low.reshape(group, local_blocks, BLOCK, slots, rank)
    low = jnp.sum(jnp.where(chosen[:, :, None, :, None], low, 0.0), axis=3)
    low = low.reshape(group, rows, rank)

    bit = 1
    while bit < group:
        gone = swap(low[1::2], "batch", bit)
        low = low[0::2] + gone
        sent = base[1::2]
        if bit > 1:
            sent = sent.astype(jnp.bfloat16)
        base = base[0::2] + swap(sent, "batch", bit).astype(jnp.float32)
        bit *= 2
    base, low = base[0], low[0].astype(jnp.bfloat16)

    first = me * local_blocks
    my_adapter = lax.dynamic_slice_in_dim(adapter_of, first, local_blocks)
    my_limit = lax.dynamic_slice_in_dim(limit_of, first, local_blocks)
    up = jnp.take(adapter_up_factors, my_adapter, axis=0)
    delta = jnp.einsum(
        "btr,bro->bto", low.reshape(local_blocks, BLOCK, rank), up, preferred_element_type=jnp.float32
    )
    live = (jnp.arange(BLOCK, dtype=jnp.int32)[None, :] < my_limit[:, None]).astype(jnp.float32)
    summed = (base.reshape(local_blocks, BLOCK, out_width) + delta) * live[:, :, None]
    return summed.reshape(rows, out_width).astype(jnp.bfloat16)


def solution(mesh):
    placed = (
        P(("rep", "batch"), None),
        P("batch", None),
        P("batch", None, None),
        P(),
        P("rep"),
        P("rep"),
        P("rep"),
    )
    return jax.shard_map(
        shards, mesh=mesh, in_specs=placed, out_specs=P(("rep", "batch"), None), check_vma=False
    )
```

time: 264 us -> 146 us (0.55)
  waiting for transfers between devices: 226 us -> 50.4 us
  local copies, waits for them, and re-layouts: 8.44 us -> 41.9 us
  starting transfers between devices: 0.04 us -> 16.4 us
  other arithmetic: 1.84 us -> 10.8 us
  matrix products: 14.3 us -> 10.9 us
    all_gather x2 -> x0, waiting for transfers between devices: 224 us -> none  [the longest x1 122 us: shards(): lax.all_gather(adapter_down_factors, 'batch', axis=0, tiled=True)]
    ppermute x0 -> x16, waiting for transfers between devices: none -> 50.4 us  [swap(): lax.ppermute(value, axis, [(i, i ^ bit) for i in range(lax.axis_size(axis...]
    unnamed x2 -> x35, local copies, waits for them, and re-layouts: 0.01 us -> 22.3 us
    ppermute x0 -> x16, starting transfers between devices: none -> 16.4 us  [swap(): lax.ppermute(value, axis, [(i, i ^ bit) for i in range(lax.axis_size(axis...]
    gather x2 -> x3, local copies, waits for them, and re-layouts: 8.36 us -> 1.29 us  [the longest x2 0.73 us: shards(): slot_here = jnp.take(slot_of, blocks_of)]
    concatenate x0 -> x4, local copies, waits for them, and re-layouts: none -> 5.06 us  [the longest x2 3.53 us: shards(): jnp.concatenate(sum([columns(spot ^ s, t) for t in range(layers)], []), 1)]
    reshape x0 -> x2, local copies, waits for them, and re-layouts: none -> 4.24 us  [the longest x1 3.98 us: shards(): low = low.reshape(group, local_blocks, BLOCK, slots, rank)]
    slice x0 -> x6, local copies, waits for them, and re-layouts: none -> 3.96 us  [the longest x2 2.12 us: shards(): sent = base[1::2]]
  transfers between devices with their start and end apart: 2 -> 16, of which waited for: 2 -> 5; matrix products, arithmetic and copies ran while one was open for 4% -> 41% of each run, Pallas kernels for 0% -> 0%
where the time goes in v1:
time: 146 us; the launch traced here: 145 us
  waiting for transfers between devices  50.4 us (35%)
  local copies, waits for them, and re-layouts  41.9 us (29%)
  starting transfers between devices  16.4 us (11%)
  between operations  14.5 us (10%)
  matrix products  10.9 us (7%)
  other arithmetic  10.8 us (7%)
    ppermute x16, waiting for transfers between devices, swap(): lax.ppermute(value, axis, [(i, i ^ bit) for i in range(lax.axis_size(axis...  50.4 us
    unnamed x35, local copies, waits for them, and re-layouts  22.3 us
    ppermute x16, starting transfers between devices, swap(): lax.ppermute(value, axis, [(i, i ^ bit) for i in range(lax.axis_size(axis...  16.4 us
    dot_general x4, matrix products, shards(): lax.dot_general(mine, downs[t], (((1,), (1,)), ((), ())), preferred_eleme...  5.69 us
    dot_general x4, matrix products, shards(): base = base + jnp.dot(mine, weights[t], preferred_element_type=jnp.float32)  4.92 us
    reshape x1, local copies, waits for them, and re-layouts, shards(): low = low.reshape(group, local_blocks, BLOCK, slots, rank)  3.98 us
    concatenate x2, local copies, waits for them, and re-layouts, shards(): jnp.concatenate(sum([columns(spot ^ s, t) for t in range(layers)], []), 1)  3.53 us
    add x2, other arithmetic, shards(): base = base[0::2] + swap(sent, 'batch', bit).astype(jnp.float32)  3.13 us
  transfers between devices with their start and end apart: 16, of which 5 were waited for; matrix products, arithmetic and copies ran while one was open for 41% of the time, Pallas kernels for 0%

profile of v1, /device:TPU:0, one launch (start us, length us, event | category | flops | bytes accessed | tf_op | source)
XLA Modules:
  0.0 145.0 jit_solution(2516925155386671263)
XLA Ops:
  1.3 3.1 %collective-permute-start.5 = (bf16[256,768]{1,0:T(8,128)(2,1)S(1)}, bf16[256,768]{1,0:T(8,128)(2,1)S(1)}, u32[]{:S(2)}, u32[]{:S(2)}) collective-permute-start(bf16[256,768]{1,0:T(8,128)(2,1)S(1)} %get-tuple-element.53), channel_id=1, source_target_pairs={{0,4},{1,5},{2,6},{3,7},{4,0},{5,1},{6,2},{7,3},{8,12},{9,13},{10,... | collective-permute-start | bytes 1179656 | tf_op jit(solution)/shard_map/ppermute | solution.py:24
  4.4 2.6 %collective-permute-start.3 = (bf16[256,768]{1,0:T(8,128)(2,1)S(1)}, bf16[256,768]{1,0:T(8,128)(2,1)}, u32[]{:S(2)}, u32[]{:S(2)}) collective-permute-start(bf16[256,768]{1,0:T(8,128)(2,1)S(1)} %get-tuple-element.53), channel_id=1, source_target_pairs={{0,8},{1,9},{2,10},{3,11},{4,12},{5,13},{6,14},{7,15},{8,0},{9,1},... | collective-permute-start | bytes 1179656 | tf_op jit(solution)/shard_map/ppermute | solution.py:24
  7.0 1.8 %dynamic-slice_dynamic-update-slice_fusion.31 = (bf16[256,2048]{1,0:T(8,128)(2,1)}, bf16[256,2048]{1,0:T(8,128)(2,1)}, bf16[256,2048]{1,0:T(8,128)(2,1)}) fusion(bf16[256,8192]{1,0:T(8,128)(2,1)} %param.7, s32[]{:T(128)S(6)} %select_n.221, s32[]{:T(128)S(6)} %select_n.237, s32[]{:T(128)S(6)} %select_n.229), kind=kLoop, calls=%fused_computation.72 | loop fusion | bytes 786444
  8.8 1.8 %dynamic-slice_dynamic-update-slice_fusion.30 = (bf16[256,2048]{1,0:T(8,128)(2,1)}, bf16[256,2048]{1,0:T(8,128)(2,1)}, bf16[256,2048]{1,0:T(8,128)(2,1)}) fusion(bf16[256,2048]{1,0:T(8,128)(2,1)} %get-tuple-element.37, bf16[256,8192]{1,0:T(8,128)(2,1)} %param.7, s32[]{:T(128)S(6)} %select_n.222, bf16[256,2048]{1,0:T(8,128)(2,1)} %get-tuple-element.38, ...), kind=kLoop, calls=%fused_computation.71 | loop fusion | bytes 786444
  10.6 1.9 %dynamic-slice_dynamic-update-slice_fusion.29 = (bf16[256,2048]{1,0:T(8,128)(2,1)}, bf16[256,2048]{1,0:T(8,128)(2,1)}, bf16[256,2048]{1,0:T(8,128)(2,1)}, bf16[256,2048]{1,0:T(8,128)(2,1)}) fusion(bf16[256,2048]{1,0:T(8,128)(2,1)} %get-tuple-element.34, bf16[256,8192]{1,0:T(8,128)(2,1)} %param.7, s32[]{:T(128)S(6)} %select_n.223, s32[]{:T(128)S(6)} %select_n.245, ...), kind=kLoop, calls=%fused_computation.70 | loop fusion | bytes 1048592
  12.6 2.0 %dynamic-slice_dynamic-update-slice_fusion.28 = (bf16[256,2048]{1,0:T(8,128)(2,1)}, bf16[256,2048]{1,0:T(8,128)(2,1)}, bf16[256,2048]{1,0:T(8,128)(2,1)}, bf16[256,2048]{1,0:T(8,128)(2,1)}) fusion(bf16[256,2048]{1,0:T(8,128)(2,1)} %get-tuple-element.30, bf16[256,8192]{1,0:T(8,128)(2,1)} %param.7, s32[]{:T(128)S(6)} %select_n.224, ...), kind=kLoop, calls=%fused_computation.69 | loop fusion | bytes 1048592
  14.6 1.9 %dynamic-slice_dynamic-update-slice_fusion.27 = (bf16[256,2048]{1,0:T(8,128)(2,1)}, bf16[256,2048]{1,0:T(8,128)(2,1)}, bf16[256,2048]{1,0:T(8,128)(2,1)}, bf16[256,2048]{1,0:T(8,128)(2,1)}) fusion(bf16[256,2048]{1,0:T(8,128)(2,1)} %get-tuple-element.26, bf16[256,8192]{1,0:T(8,128)(2,1)} %param.7, s32[]{:T(128)S(6)} %select_n.225, ...), kind=kLoop, calls=%fused_computation.68 | loop fusion | bytes 1048592
  16.5 1.9 %dynamic-slice_dynamic-update-slice_fusion.26 = (bf16[256,2048]{1,0:T(8,128)(2,1)}, bf16[256,2048]{1,0:T(8,128)(2,1)}, bf16[256,2048]{1,0:T(8,128)(2,1)}, bf16[256,2048]{1,0:T(8,128)(2,1)}) fusion(bf16[256,2048]{1,0:T(8,128)(2,1)} %get-tuple-element.22, bf16[256,8192]{1,0:T(8,128)(2,1)} %param.7, s32[]{:T(128)S(6)} %select_n.226, ...), kind=kLoop, calls=%fused_computation.67 | loop fusion | bytes 1048592
  18.4 2.0 %dynamic-slice_dynamic-update-slice_fusion.25 = (bf16[256,2048]{1,0:T(8,128)(2,1)}, bf16[256,2048]{1,0:T(8,128)(2,1)}, bf16[256,2048]{1,0:T(8,128)(2,1)}, bf16[256,2048]{1,0:T(8,128)(2,1)}) fusion(bf16[256,2048]{1,0:T(8,128)(2,1)} %get-tuple-element.18, bf16[256,8192]{1,0:T(8,128)(2,1)} %param.7, s32[]{:T(128)S(6)} %select_n.227, ...), kind=kLoop, calls=%fused_computation.66 | loop fusion | bytes 1048592
  20.4 1.9 %dynamic-slice_dynamic-update-slice_fusion.24 = (bf16[256,2048]{1,0:T(8,128)(2,1)}, bf16[256,2048]{1,0:T(8,128)(2,1)}, bf16[256,2048]{1,0:T(8,128)(2,1)}, bf16[256,2048]{1,0:T(8,128)(2,1)}) fusion(bf16[256,2048]{1,0:T(8,128)(2,1)} %get-tuple-element.14, bf16[256,8192]{1,0:T(8,128)(2,1)} %param.7, s32[]{:T(128)S(6)} %select_n.228, ...), kind=kLoop, calls=%fused_computation.65 | loop fusion | bytes 1048592 | tf_op jit(solution)/shard_map/concatenate | solution.py:101
  23.9 1.6 %dynamic-slice_dynamic-update-slice_fusion = bf16[256,2048]{1,0:T(8,128)(2,1)} fusion(bf16[256,2048]{1,0:T(8,128)(2,1)} %dynamic-slice_dynamic-update-slice_fusion.1, bf16[256,8192]{1,0:T(8,128)(2,1)} %param.7, s32[]{:T(128)S(6)} %select_n.252), kind=kLoop, calls=%fused_computation.41 | loop fusion | bytes 262148 | tf_op jit(solution)/shard_map/concatenate | solution.py:101
  55.8 24.3 %collective-permute-done.11 = bf16[512,512]{1,0:T(8,128)(2,1)} collective-permute-done((bf16[512,512]{1,0:T(8,128)(2,1)S(1)}, bf16[512,512]{1,0:T(8,128)(2,1)}, u32[]{:S(2)}, u32[]{:S(2)}) %collective-permute-start.11) | collective-permute-done | bytes 524320 | tf_op jit(solution)/shard_map/ppermute | solution.py:24
  82.1 2.0 %collective-permute-start.13 = (bf16[512,512]{1,0:T(8,128)(2,1)}, bf16[512,512]{1,0:T(8,128)(2,1)S(1)}, u32[]{:S(2)}, u32[]{:S(2)}) collective-permute-start(bf16[512,512]{1,0:T(8,128)(2,1)} %collective-permute-done.11), channel_id=1, source_target_pairs={{0,4},{1,5},{2,6},{3,7},{4,0},{5,1},{6,2},{7,3},{8,12},{9,13},{10,... | collective-permute-start | bytes 1572872 | tf_op jit(solution)/shard_map/ppermute | solution.py:24
  85.6 2.4 %pad_maximum_fusion = bf16[1024,2048]{1,0:T(8,128)(2,1)S(1)} fusion(bf16[256,2048]{1,0:T(8,128)(2,1)} %collective-permute-done.2, bf16[256,2048]{1,0:T(8,128)(2,1)} %collective-permute-done.1, bf16[256,2048]{1,0:T(8,128)(2,1)} %collective-permute-done, bf16[256,2048]{1,0:T(8,128)(2,1)} %get-tuple-element.10), kind=kLoop, calls=%fused_computation.2 | loop fusion | flops 16777216 | bytes 8388608 | tf_op jit(solution)/shard_map/concatenate | solution.py:103
  89.0 11.6 %collective-permute-done.6 = bf16[256,768]{1,0:T(8,128)(2,1)S(1)} collective-permute-done((bf16[256,768]{1,0:T(8,128)(2,1)}, bf16[256,768]{1,0:T(8,128)(2,1)S(1)}, u32[]{:S(2)}, u32[]{:S(2)}) %collective-permute-start.6) | collective-permute-done | bytes 393248 | tf_op jit(solution)/shard_map/ppermute | solution.py:24
  102.4 2.0 %fusion.8 = f32[1024,768]{1,0:T(8,128)S(1)} fusion(bf16[1024,2048]{1,0:T(8,128)(2,1)S(1)} %pad_maximum_fusion, bf16[256,768]{1,0:T(8,128)(2,1)S(1)} %collective-permute-done.4, bf16[256,768]{1,0:T(8,128)(2,1)} %collective-permute-done.3), kind=kOutput, calls=%fused_computation.15 | convolution fusion | flops 806879232 | bytes 4980736 | tf_op jit(solution)/shard_map/dot_general | solution.py:108
  104.4 3.8 %collective-permute-done.8 = bf16[256,768]{1,0:T(8,128)(2,1)S(1)} collective-permute-done((bf16[256,768]{1,0:T(8,128)(2,1)S(1)}, bf16[256,768]{1,0:T(8,128)(2,1)S(1)}, u32[]{:S(2)}, u32[]{:S(2)}) %collective-permute-start.8) | collective-permute-done | bytes 393248 | tf_op jit(solution)/shard_map/ppermute | solution.py:24
  110.5 2.0 %fusion.6 = f32[1024,512]{1,0:T(8,128)S(1)} fusion(bf16[512,512]{1,0:T(8,128)(2,1)} %collective-permute-done.11, bf16[1024,2048]{1,0:T(8,128)(2,1)S(1)} %pad_maximum_fusion), kind=kOutput, calls=%fused_computation.13 | convolution fusion | flops 536870912 | bytes 3670016 | tf_op jit(solution)/shard_map/dot_general | solution.py:109
  113.3 2.2 %add_add_fusion.1 = f32[1024,512]{1,0:T(8,128)} fusion(f32[1024,512]{1,0:T(8,128)S(1)} %fusion.2, f32[1024,512]{1,0:T(8,128)S(1)} %fusion.10, f32[1024,512]{1,0:T(8,128)S(1)} %fusion.6, bf16[512,512]{1,0:T(8,128)(2,1)S(1)} %collective-permute-done.13, bf16[1024,2048]{1,0:T(8,128)(2,1)S(1)} %pad_maximum_fusion), kind=kOutput, calls=%fused_computation.5 | convolution fusion | flops 538443776 | bytes 9961472 | tf_op jit(solution)/shard_map/dot_general | solution.py:109
  115.5 2.9 %copy.14 = f32[1024,512]{0,1:T(8,128)} copy(f32[1024,512]{1,0:T(8,128)} %add_add_fusion.1) | data formatting | bytes 4194304 | tf_op jit(solution)/shard_map/add | solution.py:109
  118.5 4.0 %reshape.161 = f32[4,2,128,8,64]{2,1,0,4,3:T(2,128)} reshape(f32[1024,512]{0,1:T(8,128)} %copy.14) | data formatting | bytes 4194304 | tf_op jit(solution)/shard_map/reshape | solution.py:118
  122.4 2.7 %select_reduce_fusion = f32[4,2,128,64]{2,1,0,3:T(2,128)S(1)} fusion(f32[4,2,128,8,64]{2,1,0,4,3:T(2,128)} %reshape.161, pred[4,2,8]{1,0,2:T(4,128)(4,1)S(1)} %iota_compare_fusion), kind=kLoop, calls=%fused_computation.4 | loop fusion | flops 983040 | bytes 2359360 | tf_op jit(solution)/shard_map/reduce_sum | solution.py:119
  128.9 2.1 %slice_add_fusion = f32[2,256,768]{2,1,0:T(8,128)S(1)} fusion(f32[2,256,768]{2,1,0:T(8,128)} %collective-permute-done.9, f32[4,256,768]{2,1,0:T(8,128)} %bitcast.60), kind=kLoop, calls=%fused_computation.6 | loop fusion | flops 393216 | bytes 4718592 | tf_op jit(solution)/shard_map/add | solution.py:129
  132.8 10.2 %collective-permute-done.10 = bf16[1,256,768]{2,1,0:T(8,128)(2,1)} collective-permute-done((bf16[1,256,768]{2,1,0:T(8,128)(2,1)}, bf16[1,256,768]{2,1,0:T(8,128)(2,1)}, u32[]{:S(2)}, u32[]{:S(2)}) %collective-permute-start.10) | collective-permute-done | bytes 393248 | tf_op jit(solution)/shard_map/ppermute | solution.py:24
  (93 shorter events, 35.5 us)
Async XLA Ops:
  0.0 54.6 %copy-start = (bf16[16,64,768]{2,1,0:T(8,128)(2,1)S(1)}, bf16[16,64,768]{2,1,0:T(8,128)(2,1)}, u32[]{:S(2)}) copy-start(bf16[16,64,768]{2,1,0:T(8,128)(2,1)} %param.10) | copy-start | bytes 4718596
  1.3 52.5 %collective-permute-start.5 = (bf16[256,768]{1,0:T(8,128)(2,1)S(1)}, bf16[256,768]{1,0:T(8,128)(2,1)S(1)}, u32[]{:S(2)}, u32[]{:S(2)}) collective-permute-start(bf16[256,768]{1,0:T(8,128)(2,1)S(1)} %get-tuple-element.53), channel_id=1, source_target_pairs={{0,4},{1,5},{2,6},{3,7},{4,0},{5,1},{6,2},{7,3},{8,12},{9,13},{10,... | collective-permute-start | bytes 1179656 | tf_op jit(solution)/shard_map/ppermute | solution.py:24
  4.4 50.8 %collective-permute-start.3 = (bf16[256,768]{1,0:T(8,128)(2,1)S(1)}, bf16[256,768]{1,0:T(8,128)(2,1)}, u32[]{:S(2)}, u32[]{:S(2)}) collective-permute-start(bf16[256,768]{1,0:T(8,128)(2,1)S(1)} %get-tuple-element.53), channel_id=1, source_target_pairs={{0,8},{1,9},{2,10},{3,11},{4,12},{5,13},{6,14},{7,15},{8,0},{9,1},... | collective-permute-start | bytes 1179656 | tf_op jit(solution)/shard_map/ppermute | solution.py:24
  12.5 14.8 %copy-start.5 = (s32[8]{0:T(128)S(1)}, s32[8]{0:T(128)}, u32[]{:S(2)}) copy-start(s32[8]{0:T(128)} %param.12) | copy-start | bytes 100
  12.5 25.0 %copy-start.7 = (s32[8]{0:T(128)S(1)}, s32[8]{0:T(128)}, u32[]{:S(2)}) copy-start(s32[8]{0:T(128)} %param.11) | copy-start | bytes 100
  12.5 32.5 %copy-start.6 = (s32[8]{0:T(128)S(1)}, s32[8]{0:T(128)}, u32[]{:S(2)}) copy-start(s32[8]{0:T(128)} %param.13) | copy-start | bytes 100
  25.5 56.0 %collective-permute-start.2 = (bf16[256,2048]{1,0:T(8,128)(2,1)}, bf16[256,2048]{1,0:T(8,128)(2,1)}, u32[]{:S(2)}, u32[]{:S(2)}) collective-permute-start(bf16[256,2048]{1,0:T(8,128)(2,1)} %dynamic-slice_dynamic-update-slice_fusion), channel_id=1, source_target_pairs={{0,3},{1,2},{2,1},{3,0},{4,7},{5,6},{6,5},{7,4},{8,11},{9,10},{10,... | collective-permute-start | bytes 3145736 | tf_op jit(solution)/shard_map/ppermute | solution.py:24
  25.9 56.2 %collective-permute-start.1 = (bf16[256,2048]{1,0:T(8,128)(2,1)}, bf16[256,2048]{1,0:T(8,128)(2,1)}, u32[]{:S(2)}, u32[]{:S(2)}) collective-permute-start(bf16[256,2048]{1,0:T(8,128)(2,1)} %get-tuple-element.12), channel_id=1, source_target_pairs={{0,2},{1,3},{2,0},{3,1},{4,6},{5,7},{6,4},{7,5},{8,10},{9,11},{10,... | collective-permute-start | bytes 3145736 | tf_op jit(solution)/shard_map/ppermute | solution.py:24
  27.1 57.0 %collective-permute-start = (bf16[256,2048]{1,0:T(8,128)(2,1)}, bf16[256,2048]{1,0:T(8,128)(2,1)}, u32[]{:S(2)}, u32[]{:S(2)}) collective-permute-start(bf16[256,2048]{1,0:T(8,128)(2,1)} %get-tuple-element.13), channel_id=1, source_target_pairs={{0,1},{1,0},{2,3},{3,2},{4,5},{5,4},{6,7},{7,6},{8,9},{9,8},{10,11... | collective-permute-start | bytes 3145736 | tf_op jit(solution)/shard_map/ppermute | solution.py:24
  53.8 0.7 copy-start.2
  53.8 26.2 %collective-permute-start.11 = (bf16[512,512]{1,0:T(8,128)(2,1)S(1)}, bf16[512,512]{1,0:T(8,128)(2,1)}, u32[]{:S(2)}, u32[]{:S(2)}) collective-permute-start(bf16[512,512]{1,0:T(8,128)(2,1)S(1)} %bitcast.62), channel_id=1, source_target_pairs={{0,8},{1,9},{2,10},{3,11},{4,12},{5,13},{6,14},{7,15},{8,0},{9,1},... | collective-permute-start | bytes 1572872 | tf_op jit(solution)/shard_map/ppermute | solution.py:24
  55.2 24.9 %collective-permute-start.7 = (bf16[256,768]{1,0:T(8,128)(2,1)}, bf16[256,768]{1,0:T(8,128)(2,1)S(1)}, u32[]{:S(2)}, u32[]{:S(2)}) collective-permute-start(bf16[256,768]{1,0:T(8,128)(2,1)} %collective-permute-done.3), channel_id=1, source_target_pairs={{0,4},{1,5},{2,6},{3,7},{4,0},{5,1},{6,2},{7,3},{8,12},{9,13},{10,... | collective-permute-start | bytes 1179656 | tf_op jit(solution)/shard_map/ppermute | solution.py:24
  80.0 32.5 %collective-permute-start.12 = (bf16[512,512]{1,0:T(8,128)(2,1)S(1)}, bf16[512,512]{1,0:T(8,128)(2,1)S(1)}, u32[]{:S(2)}, u32[]{:S(2)}) collective-permute-start(bf16[512,512]{1,0:T(8,128)(2,1)S(1)} %bitcast.63), channel_id=1, source_target_pairs={{0,4},{1,5},{2,6},{3,7},{4,0},{5,1},{6,2},{7,3},{8,12},{9,13},{10,... | collective-permute-start | bytes 1572872 | tf_op jit(solution)/shard_map/ppermute | solution.py:24
  80.1 22.4 %collective-permute-start.4 = (bf16[256,768]{1,0:T(8,128)(2,1)}, bf16[256,768]{1,0:T(8,128)(2,1)S(1)}, u32[]{:S(2)}, u32[]{:S(2)}) collective-permute-start(bf16[256,768]{1,0:T(8,128)(2,1)} %collective-permute-done.3), channel_id=1, source_target_pairs={{0,16},{16,0},{1,17},{17,1},{2,18},{18,2},{3,19},{19,3},{4,20},{20... | collective-permute-start | bytes 1179656 | tf_op jit(solution)/shard_map/ppermute | solution.py:24
  81.5 19.1 %collective-permute-start.6 = (bf16[256,768]{1,0:T(8,128)(2,1)}, bf16[256,768]{1,0:T(8,128)(2,1)S(1)}, u32[]{:S(2)}, u32[]{:S(2)}) collective-permute-start(bf16[256,768]{1,0:T(8,128)(2,1)} %copy-done.2), channel_id=1, source_target_pairs={{0,16},{16,0},{1,17},{17,1},{2,18},{18,2},{3,19},{19,3},{4,20},{20... | collective-permute-start | bytes 1179656 | tf_op jit(solution)/shard_map/ppermute | solution.py:24
  82.1 31.2 %collective-permute-start.13 = (bf16[512,512]{1,0:T(8,128)(2,1)}, bf16[512,512]{1,0:T(8,128)(2,1)S(1)}, u32[]{:S(2)}, u32[]{:S(2)}) collective-permute-start(bf16[512,512]{1,0:T(8,128)(2,1)} %collective-permute-done.11), channel_id=1, source_target_pairs={{0,4},{1,5},{2,6},{3,7},{4,0},{5,1},{6,2},{7,3},{8,12},{9,13},{10,... | collective-permute-start | bytes 1572872 | tf_op jit(solution)/shard_map/ppermute | solution.py:24
  84.1 24.1 %collective-permute-start.8 = (bf16[256,768]{1,0:T(8,128)(2,1)S(1)}, bf16[256,768]{1,0:T(8,128)(2,1)S(1)}, u32[]{:S(2)}, u32[]{:S(2)}) collective-permute-start(bf16[256,768]{1,0:T(8,128)(2,1)S(1)} %collective-permute-done.7), channel_id=1, source_target_pairs={{0,16},{16,0},{1,17},{17,1},{2,18},{18,2},{3,19},{19,3},{4,20},{20... | collective-permute-start | bytes 1179656 | tf_op jit(solution)/shard_map/ppermute | solution.py:24
  88.0 12.6 %copy-start.3 = (bf16[256,768]{1,0:T(8,128)(2,1)S(1)}, bf16[256,768]{1,0:T(8,128)(2,1)}, u32[]{:S(2)}) copy-start(bf16[256,768]{1,0:T(8,128)(2,1)} %copy-done.2) | copy-start | bytes 1179652
  109.2 3.4 %copy-start.1 = (f32[1024,768]{1,0:T(8,128)}, f32[1024,768]{1,0:T(8,128)S(1)}, u32[]{:S(2)}) copy-start(f32[1024,768]{1,0:T(8,128)S(1)} %add_add_fusion) | copy-start | bytes 9437188
  110.5 18.4 %collective-permute-start.9 = (f32[2,256,768]{2,1,0:T(8,128)}, f32[2,256,768]{2,1,0:T(8,128)}, u32[]{:S(2)}, u32[]{:S(2)}) collective-permute-start(f32[2,256,768]{2,1,0:T(8,128)} %slice.70), channel_id=1, source_target_pairs={{0,1},{1,0},{2,3},{3,2},{4,5},{5,4},{6,7},{7,6},{8,9},{9,8},{10,11... | collective-permute-start | bytes 4718600 | tf_op jit(solution)/shard_map/ppermute | solution.py:24
  118.5 7.9 %copy-start.8 = (s32[2]{0:T(128)S(1)}, s32[2]{0:T(128)}, u32[]{:S(2)}) copy-start(s32[2]{0:T(128)} %dynamic_slice.207) | copy-start | bytes 28
  126.1 1.4 collective-permute-start.14
  127.5 5.0 %collective-permute-start.15 = (f32[1,256,64]{1,2,0:T(8,128)S(1)}, f32[1,256,64]{1,2,0:T(8,128)S(1)}, u32[]{:S(2)}, u32[]{:S(2)}) collective-permute-start(f32[1,256,64]{1,2,0:T(8,128)S(1)} %slice.96), channel_id=1, source_target_pairs={{0,2},{1,3},{2,0},{3,1},{4,6},{5,7},{6,4},{7,5},{8,10},{9,11},{10,... | collective-permute-start | bytes 196616 | tf_op jit(solution)/shard_map/ppermute | solution.py:24
  131.8 11.3 %collective-permute-start.10 = (bf16[1,256,768]{2,1,0:T(8,128)(2,1)}, bf16[1,256,768]{2,1,0:T(8,128)(2,1)}, u32[]{:S(2)}, u32[]{:S(2)}) collective-permute-start(bf16[1,256,768]{2,1,0:T(8,128)(2,1)} %slice.119), channel_id=1, source_target_pairs={{0,2},{1,3},{2,0},{3,1},{4,6},{5,7},{6,4},{7,5},{8,10},{9,11},{10,... | collective-permute-start | bytes 1179656 | tf_op jit(solution)/shard_map/ppermute | solution.py:24
  (1 other events, 0.7 us)

commit v2 on v0

v2 whole, which is shorter than its diff:
```python
import functools

import jax
import jax.numpy as jnp
from jax import lax
from jax.experimental import pallas as pl
from jax.experimental.pallas import tpu as pltpu
from jax.sharding import PartitionSpec as P

BLOCK = 128
LANES = 128
LAYER_CHIPS = 4
VMEM_BYTES = 28 * 1024 * 1024

HBM = pl.BlockSpec(memory_space=pl.ANY)
VMEM = pl.BlockSpec(memory_space=pltpu.VMEM)
SMEM = pl.BlockSpec(memory_space=pltpu.SMEM)


def call(kernel, outs, out_specs, in_specs, scratch, flops, moved):
    return pl.pallas_call(
        kernel,
        out_shape=outs,
        in_specs=in_specs,
        out_specs=out_specs,
        scratch_shapes=scratch,
        compiler_params=pltpu.CompilerParams(vmem_limit_bytes=VMEM_BYTES),
        cost_estimate=pl.CostEstimate(flops=flops, bytes_accessed=moved, transcendentals=0),
    )


def swap(value, axis, bit):
    return lax.ppermute(value, axis, [(i, i ^ bit) for i in range(lax.axis_size(axis))])


def run_copies(pairs, sems):
    copies = [pltpu.make_async_copy(a, b, sems.at[i]) for i, (a, b) in enumerate(pairs)]
    for copy in copies:
        copy.start()
    return copies


def part_start(h, part):
    return pl.multiple_of((lax.axis_index("rep") ^ h) * part, part)


def key_parts_kernel(splits, part, key, *refs):
    outs, sems = refs[:splits], refs[splits]
    pairs = [(key.at[pl.ds(part_start(h, part), part), :], outs[h]) for h in range(splits)]
    for copy in run_copies(pairs, sems):
        copy.wait()


def token_pieces_kernel(group, layers, splits, part, tokens, *refs):
    outs, sems = refs[:group], refs[group]
    depth = splits * part
    me = lax.axis_index("batch")
    layer, spot = me // group, me % group
    pairs = []
    for s in reversed(range(group)):
        for t in range(layers):
            first = ((layer ^ t) * group + (spot ^ s)) * depth
            for h in range(splits):
                start = first + part_start(h, part) if splits > 1 else first
                start = pl.multiple_of(start, part)
                pairs.append(
                    (
                        tokens.at[:, pl.ds(start, part)],
                        outs[s].at[:, pl.ds(t * depth + h * part, part)],
                    )
                )
    for copy in run_copies(pairs, sems):
        copy.wait()


def chosen_kernel(slots, rank, splits, part, picks, down, out, sems):
    pairs = []
    for q in range(slots):
        for h in range(splits):
            start = part_start(h, part) if splits > 1 else 0
            pairs.append(
                (
                    down.at[picks[q], :, pl.ds(start, part)],
                    out.at[pl.ds(q * rank, rank), pl.ds(h * part, part)],
                )
            )
    for copy in run_copies(pairs, sems):
        copy.wait()


def base_kernel(rows, depth, layers, entries, count, *refs):
    toks, arrays = refs[:2], refs[2 : 2 + count]
    outs = refs[2 + count : 4 + count]
    held = refs[4 + count]
    weights = refs[5 + count : 5 + 2 * count]
    tok_sems, sems = refs[5 + 2 * count :]
    order = []
    for t, _, _, _, _ in entries:
        if t not in order:
            order.append(t)
    token_copies = {}
    started = {}
    for t in order:
        token_copies[t] = []
        for i in range(2):
            columns = pl.ds(t * depth, depth)
            token_copies[t].append(
                pltpu.make_async_copy(
                    toks[i].at[:, columns], held.at[pl.ds(i * rows, rows), columns], tok_sems.at[i, t]
                )
            )
        for copy in token_copies[t]:
            copy.start()
        for u, a, _, _, _ in entries:
            if u == t and a not in started:
                started[a] = pltpu.make_async_copy(arrays[a], weights[a], sems.at[a])
                started[a].start()
    ready = set()
    for t in order:
        for copy in token_copies[t]:
            copy.wait()
        total = None
        for u, a, row, deep, column in entries:
            if u != t:
                continue
            if a not in ready:
                started[a].wait()
                ready.add(a)
            term = jnp.dot(
                held[:, column : column + deep],
                weights[a][row : row + deep, :],
                preferred_element_type=jnp.float32,
            )
            total = term if total is None else total + term
        for i in range(2):
            here = total[i * rows : (i + 1) * rows]
            if t == order[0]:
                outs[i][...] = here
            else:
                outs[i][...] += here


def table(lists, block):
    sizes, adapters, tails = lists
    end = jnp.int32(0)
    owner, adapter, limit = jnp.int32(0), jnp.int32(0), jnp.int32(BLOCK)
    for q in range(sizes.shape[0]):
        begin = end
        end = end + sizes[q]
        inside = (begin <= block) & (block < end)
        owner = jnp.where(inside, q, owner)
        adapter = jnp.where(inside, adapters[q], adapter)
        limit = jnp.where(inside & (block == end - 1), tails[q], limit)
    return owner, adapter, limit


def low_kernel(
    group, rows, depth, rank, entries, count, by_request, has_sum, last, *refs
):
    lists, refs = refs[:3], refs[3:]
    toks, refs = refs[:group], refs[group:]
    arrays, refs = refs[:count], refs[count:]
    if has_sum:
        before, refs = refs[0], refs[1:]
    if last:
        even, odd, refs = refs[0], refs[1], refs[2:]
    else:
        after, refs = refs[0], refs[1:]
    held, refs = refs[0], refs[1:]
    downs, refs = refs[:count], refs[count:]
    tok_sems, sems = refs
    local_blocks = rows // BLOCK
    me = lax.axis_index("batch")
    layer, spot = me // group, me % group
    first = {}
    started = {}
    for n, (t, a, _) in enumerate(entries):
        if a not in started:
            started[a] = pltpu.make_async_copy(arrays[a], downs[a], sems.at[a])
            started[a].start()
        first[t] = []
        for s in range(group):
            copy = pltpu.make_async_copy(
                toks[s].at[:, pl.ds(t * depth, depth)],
                held.at[pl.ds(s * rows, rows), pl.ds(n * depth, depth)],
                tok_sems.at[s, n],
            )
            copy.start()
            first[t].append(copy)
    slots = []
    for s in range(group):
        for j in range(local_blocks):
            block = (layer * group + (spot ^ s)) * local_blocks + j
            owner, adapter, _ = table(lists, block)
            slots.append(owner if by_request else adapter)
    ready = set()
    wide = 2 * local_blocks
    sums = [before[p] if has_sum else None for p in range(group // 2)]
    for n, (t, a, row) in enumerate(entries):
        for copy in first[t]:
            copy.wait()
        if a not in ready:
            started[a].wait()
            ready.add(a)
        for p in range(group // 2):
            chosen = jnp.concatenate(
                [
                    downs[a][pl.ds(pl.multiple_of(row + slots[p * wide + i] * rank, rank), rank), :]
                    for i in range(wide)
                ],
                0,
            )
            term = lax.dot_general(
                held[2 * p * rows : 2 * (p + 1) * rows, n * depth : (n + 1) * depth],
                chosen,
                (((1,), (1,)), ((), ())),
                preferred_element_type=jnp.float32,
            )
            sums[p] = term if sums[p] is None else sums[p] + term
    for p in range(group // 2):
        if not last:
            after[p] = sums[p]
            continue
        for out, at in ((even, 0), (odd, 1)):
            out[p] = jnp.concatenate(
                [
                    sums[p][
                        (at * local_blocks + j) * BLOCK : (at * local_blocks + j + 1) * BLOCK,
                        (at * local_blocks + j) * rank : (at * local_blocks + j + 1) * rank,
                    ]
                    for j in range(local_blocks)
                ],
                1,
            )


def final_kernel(rows, rank, bases, lows, *refs):
    lists, refs = refs[:3], refs[3:]
    base_refs, refs = refs[:bases], refs[bases:]
    low_refs, refs = refs[:lows], refs[lows:]
    ups, out, up_here, sems = refs
    local_blocks = rows // BLOCK
    me = lax.axis_index("batch")
    found = [table(lists, me * local_blocks + j) for j in range(local_blocks)]
    copies = run_copies([(ups.at[found[j][1]], up_here.at[j]) for j in range(local_blocks)], sems)
    low = low_refs[0][...]
    for ref in low_refs[1:]:
        low = low + ref[...]
    low = low.astype(jnp.bfloat16)
    for j in range(local_blocks):
        copies[j].wait()
        here = pl.ds(j * BLOCK, BLOCK)
        total = jnp.dot(
            low[:, j * rank : (j + 1) * rank], up_here[j], preferred_element_type=jnp.float32
        )
        for ref in base_refs:
            total = total + ref[here, :].astype(jnp.float32)
        live = lax.broadcasted_iota(jnp.int32, total.shape, 0) < found[j][2]
        out[here, :] = jnp.where(live, total, 0.0).astype(jnp.bfloat16)


def layer_sums(values, narrow):
    parts = [[v] for v in values]
    bit = 1
    while len(parts) > 1:
        kept = []
        for mine, theirs in zip(parts[0::2], parts[1::2]):
            sent = functools.reduce(lambda a, b: a + b.astype(a.dtype), theirs)
            if narrow and bit > 1:
                sent = sent.astype(jnp.bfloat16)
            kept.append(mine + [swap(sent, "batch", bit)])
        parts = kept
        bit *= 2
    return parts[0]


def shards(
    tokens,
    key_matrix,
    adapter_down_factors,
    adapter_up_factors,
    request_block_list,
    request_adapter_index,
    request_tail_tokens,
):
    rows, width = tokens.shape
    depth, out_width = key_matrix.shape
    adapters, rank = adapter_down_factors.shape[1:]
    reps, devices = lax.axis_size("rep"), lax.axis_size("batch")
    group = 2 * LAYER_CHIPS // reps
    layers = devices // group
    splits = reps if (depth // reps) % LANES == 0 else 1
    part = depth // splits
    local_blocks = rows // BLOCK
    held_width = layers * depth
    lists = (request_block_list, request_adapter_index, request_tail_tokens)
    f32, bf16 = jnp.float32, jnp.bfloat16

    if splits > 1:
        key_parts = call(
            functools.partial(key_parts_kernel, splits, part),
            [jax.ShapeDtypeStruct((part, out_width), bf16)] * splits,
            [HBM] * splits,
            [HBM],
            [pltpu.SemaphoreType.DMA((splits,))],
            0,
            4 * depth * out_width,
        )(key_matrix)
    else:
        key_parts = [key_matrix]

    def over_layers(own):
        bundles = []
        bit = layers // 2
        while bit:
            moved = [([bit], swap(own, "batch", bit * group))]
            if bundles:
                rest = [v for _, v in bundles]
                rest = rest[0] if len(rest) == 1 else jnp.concatenate(rest, 0)
                order = [t ^ bit for ts, _ in bundles for t in ts]
                moved.append((order, swap(rest, "batch", bit * group)))
            bundles = bundles + moved
            bit //= 2
        return bundles

    key_bundles = over_layers(key_parts[0])

    pieces = call(
        functools.partial(token_pieces_kernel, group, layers, splits, part),
        [jax.ShapeDtypeStruct((rows, held_width), bf16)] * group,
        [HBM] * group,
        [HBM],
        [pltpu.SemaphoreType.DMA((group * layers * splits,))],
        0,
        4 * rows * width,
    )(tokens)
    pieces = [pieces[0]] + [swap(pieces[s], "batch", s) for s in range(1, group)]

    down = jnp.transpose(adapter_down_factors, (1, 2, 0))
    requests = request_adapter_index.shape[0]
    by_request = requests < adapters
    slots = requests if by_request else adapters
    if by_request:
        down = call(
            functools.partial(chosen_kernel, slots, rank, splits, part),
            jax.ShapeDtypeStruct((slots * rank, depth), bf16),
            HBM,
            [SMEM, HBM],
            [pltpu.SemaphoreType.DMA((slots * splits,))],
            0,
            4 * slots * rank * depth,
        )(request_adapter_index, down)
    else:
        down = down.reshape(slots * rank, depth)
    down, _ = lax.optimization_barrier((down, key_bundles[0][1]))
    down_bundles = over_layers(down)

    arrays, entries = [], []
    for ts, value in [([0], None)] + key_bundles:
        for h in range(splits):
            if value is None:
                arrays.append(key_parts[h])
            else:
                arrays.append(swap(value, "rep", h) if h else value)
            for i, t in enumerate(ts):
                entries.append((t, len(arrays) - 1, i * part, part, t * depth + h * part))
    partial_sums = [None] * group
    for p in range(group // 2):
        partial_sums[2 * p : 2 * p + 2] = call(
            functools.partial(base_kernel, rows, depth, layers, tuple(entries), len(arrays)),
            [jax.ShapeDtypeStruct((rows, out_width), f32)] * 2,
            [VMEM] * 2,
            [HBM] * (2 + len(arrays)),
            [pltpu.VMEM((2 * rows, held_width), bf16)]
            + [pltpu.VMEM(a.shape, bf16) for a in arrays]
            + [pltpu.SemaphoreType.DMA((2, layers)), pltpu.SemaphoreType.DMA((len(arrays),))],
            4 * rows * held_width * out_width,
            2 * held_width * (2 * rows + out_width) + 8 * rows * out_width,
        )(pieces[2 * p], pieces[2 * p + 1], *arrays)
    bases = layer_sums(partial_sums, True)

    def low_call(bundles, before, last):
        taken = [value for _, value in bundles]
        at = [
            (t, a, i * slots * rank) for a, (ts, _) in enumerate(bundles) for i, t in enumerate(ts)
        ]
        pairs, tall, wide = group // 2, 2 * rows, 2 * local_blocks * rank
        if last:
            outs = [jax.ShapeDtypeStruct((pairs, BLOCK, local_blocks * rank), f32)] * 2
            out_specs = [VMEM] * 2
        else:
            outs, out_specs = jax.ShapeDtypeStruct((pairs, tall, wide), f32), VMEM
        return call(
            functools.partial(
                low_kernel, group, rows, depth, rank, tuple(at), len(taken), by_request,
                before is not None, last,
            ),
            outs,
            out_specs,
            [SMEM] * 3 + [HBM] * (group + len(taken)) + [VMEM] * (before is not None),
            [pltpu.VMEM((group * rows, len(at) * depth), bf16)]
            + [pltpu.VMEM(v.shape, bf16) for v in taken]
            + [pltpu.SemaphoreType.DMA((group, len(at))), pltpu.SemaphoreType.DMA((len(taken),))],
            2 * pairs * tall * wide * len(at) * depth,
            2 * len(at) * depth * (group * rows + slots * rank) + 4 * pairs * tall * wide,
        )(*lists, *pieces, *taken, *([before] if before is not None else []))

    early = low_call([([0], down)] + down_bundles[:-1], None, False)
    even, odd = low_call(down_bundles[-1:], early, True)
    got = swap(odd, "batch", 1)
    lows = layer_pairs(even, got)

    return call(
        functools.partial(final_kernel, rows, rank, len(bases), len(lows)),
        jax.ShapeDtypeStruct((rows, out_width), bf16),
        VMEM,
        [SMEM] * 3 + [VMEM] * (len(bases) + len(lows)) + [HBM],
        [pltpu.VMEM((local_blocks, rank, out_width), bf16), pltpu.SemaphoreType.DMA((local_blocks,))],
        2 * rows * rank * out_width,
        8 * rows * out_width,
    )(*lists, *bases, *lows, adapter_up_factors)


def layer_pairs(mine, got):
    bit = 2
    while mine.shape[0] > 1:
        total = mine + got
        mine, got = total[0::2], swap(total[1::2], "batch", bit)
        bit *= 2
    return [mine[0], got[0]]


def solution(mesh):
    placed = (
        P(("rep", "batch"), None),
        P("batch", None),
        P("batch", None, None),
        P(),
        P("rep"),
        P("rep"),
        P("rep"),
    )
    return jax.shard_map(
        shards, mesh=mesh, in_specs=placed, out_specs=P(("rep", "batch"), None), check_vma=False
    )
```

time: 264 us -> 108 us (0.41)
  waiting for transfers between devices: 226 us -> 64.7 us
  starting transfers between devices: 0.04 us -> 21.6 us
  Pallas kernels: 0 us -> 17.8 us
  matrix products: 14.3 us -> 0 us
  between operations: 13.4 us -> 0.14 us
  local copies, waits for them, and re-layouts: 8.44 us -> 3.36 us
    all_gather x2 -> x0, waiting for transfers between devices: 224 us -> none  [the longest x1 122 us: shards(): lax.all_gather(adapter_down_factors, 'batch', axis=0, tiled=True)]
    ppermute x0 -> x17, waiting for transfers between devices: none -> 64.7 us  [swap(): lax.ppermute(value, axis, [(i, i ^ bit) for i in range(lax.axis_size(axis...]
    ppermute x0 -> x17, starting transfers between devices: none -> 21.6 us  [swap(): lax.ppermute(value, axis, [(i, i ^ bit) for i in range(lax.axis_size(axis...]
    pallas_call x0 -> x8, Pallas kernels: none -> 17.8 us  [the longest x2 9.78 us: shards(): call(functools.partial(base_kernel, rows, depth, layers, tuple(entries),...]
    dot_general x2 -> x0, matrix products: 14.3 us -> none  [the longest x1 8.83 us: shards(): jnp.dot(columns, lax.all_gather(key_matrix, 'batch', axis=0, tiled=True),...]
    gather x2 -> x0, local copies, waits for them, and re-layouts: 8.36 us -> none  [the longest x1 7.8 us: shards(): chosen = jnp.take(request_segment, current_adapter, axis=1)]
    unnamed x2 -> x14, local copies, waits for them, and re-layouts: 0.01 us -> 3.35 us
  transfers between devices with their start and end apart: 2 -> 17, of which waited for: 2 -> 9; matrix products, arithmetic and copies ran while one was open for 4% -> 0% of each run, Pallas kernels for 0% -> 14%
where the time goes in v2:
time: 108 us
  waiting for transfers between devices  64.7 us (60%)
  starting transfers between devices  21.6 us (20%)
  Pallas kernels  17.8 us (16%)
  local copies, waits for them, and re-layouts  3.36 us (3%)
    ppermute x17, waiting for transfers between devices, swap(): lax.ppermute(value, axis, [(i, i ^ bit) for i in range(lax.axis_size(axis...  64.7 us
    ppermute x17, starting transfers between devices, swap(): lax.ppermute(value, axis, [(i, i ^ bit) for i in range(lax.axis_size(axis...  21.6 us
    pallas_call x2, Pallas kernels, shards(): call(functools.partial(base_kernel, rows, depth, layers, tuple(entries),...  9.78 us
    pallas_call x2, Pallas kernels, low_call(): call(functools.partial(low_kernel, group, rows, depth, rank, tuple(at), l...  3.61 us
    unnamed x14, local copies, waits for them, and re-layouts  3.35 us
  transfers between devices with their start and end apart: 17, of which 9 were waited for; matrix products, arithmetic and copies ran while one was open for 0% of the time, Pallas kernels for 14%

profile of v2, /device:TPU:0, one launch (start us, length us, event | category | flops | bytes accessed | tf_op | source)
XLA Modules:
  0.0 107.7 jit_solution(11918030817801006618)
XLA Ops:
  1.5 4.1 %collective-permute-start.1 = (bf16[256,768]{1,0:T(8,128)(2,1)S(1)}, bf16[256,768]{1,0:T(8,128)(2,1)S(1)}, u32[]{:S(2)}, u32[]{:S(2)}) collective-permute-start(bf16[256,768]{1,0:T(8,128)(2,1)S(1)} %get-tuple-element.20.refs_2_), channel_id=1, source_target_pairs={{0,8},{1,9},{2,10},{3,11},{4,12},{5,13},{6,14},{7,15},{8,0},{9,1},... | collective-permute-start | bytes 1179656 | tf_op jit(solution)/shard_map/ppermute | solution.py:33
  5.6 2.2 %copy-done = bf16[256,8192]{1,0:T(8,128)(2,1)S(1)} copy-done((bf16[256,8192]{1,0:T(8,128)(2,1)S(1)}, bf16[256,8192]{1,0:T(8,128)(2,1)}, u32[]{:S(2)}) %copy-start) | copy-done | bytes 4194328
  8.9 1.6 %collective-permute-start.8 = (bf16[256,2048]{1,0:T(8,128)(2,1)S(1)}, bf16[256,2048]{1,0:T(8,128)(2,1)S(1)}, u32[]{:S(2)}, u32[]{:S(2)}) collective-permute-start(bf16[256,2048]{1,0:T(8,128)(2,1)S(1)} %get-tuple-element.24), channel_id=1, source_target_pairs={{0,2},{1,3},{2,0},{3,1},{4,6},{5,7},{6,4},{7,5},{8,10},{9,11},{10,... | collective-permute-start | bytes 3145736 | tf_op jit(solution)/shard_map/ppermute | solution.py:33
  10.5 1.6 %collective-permute-start.3 = (bf16[256,768]{1,0:T(8,128)(2,1)S(1)}, bf16[256,768]{1,0:T(8,128)(2,1)S(1)}, u32[]{:S(2)}, u32[]{:S(2)}) collective-permute-start(bf16[256,768]{1,0:T(8,128)(2,1)S(1)} %get-tuple-element.20.refs_2_), channel_id=1, source_target_pairs={{0,4},{1,5},{2,6},{3,7},{4,0},{5,1},{6,2},{7,3},{8,12},{9,13},{10,... | collective-permute-start | bytes 1179656 | tf_op jit(solution)/shard_map/ppermute | solution.py:33
  12.0 11.2 %collective-permute-done.1.refs_4_ = bf16[256,768]{1,0:T(8,128)(2,1)S(1)} collective-permute-done((bf16[256,768]{1,0:T(8,128)(2,1)S(1)}, bf16[256,768]{1,0:T(8,128)(2,1)S(1)}, u32[]{:S(2)}, u32[]{:S(2)}) %collective-permute-start.1) | collective-permute-done | bytes 393248 | tf_op jit(solution)/shard_map/ppermute | solution.py:33
  23.9 1.5 %collective-permute-start.2 = (bf16[256,768]{1,0:T(8,128)(2,1)S(1)}, bf16[256,768]{1,0:T(8,128)(2,1)S(1)}, u32[]{:S(2)}, u32[]{:S(2)}) collective-permute-start(bf16[256,768]{1,0:T(8,128)(2,1)S(1)} %collective-permute-done.1.refs_4_), channel_id=1, source_target_pairs={{0,16},{16,0},{1,17},{17,1},{2,18},{18,2},{3,19},{19,3},{4,20},{20... | collective-permute-start | bytes 1179656 | tf_op jit(solution)/shard_map/ppermute | solution.py:33
  25.4 4.2 %collective-permute-done.3.refs_6_ = bf16[256,768]{1,0:T(8,128)(2,1)S(1)} collective-permute-done((bf16[256,768]{1,0:T(8,128)(2,1)S(1)}, bf16[256,768]{1,0:T(8,128)(2,1)S(1)}, u32[]{:S(2)}, u32[]{:S(2)}) %collective-permute-start.3) | collective-permute-done | bytes 393248 | tf_op jit(solution)/shard_map/ppermute | solution.py:33
  29.6 1.5 %collective-permute-start.4 = (bf16[256,768]{1,0:T(8,128)(2,1)S(1)}, bf16[256,768]{1,0:T(8,128)(2,1)S(1)}, u32[]{:S(2)}, u32[]{:S(2)}) collective-permute-start(bf16[256,768]{1,0:T(8,128)(2,1)S(1)} %collective-permute-done.3.refs_6_), channel_id=1, source_target_pairs={{0,16},{16,0},{1,17},{17,1},{2,18},{18,2},{3,19},{19,3},{4,20},{20... | collective-permute-start | bytes 1179656 | tf_op jit(solution)/shard_map/ppermute | solution.py:33
  31.1 6.7 %collective-permute-done.5.refs_8_ = bf16[256,768]{1,0:T(8,128)(2,1)S(1)} collective-permute-done((bf16[256,768]{1,0:T(8,128)(2,1)S(1)}, bf16[256,768]{1,0:T(8,128)(2,1)S(1)}, u32[]{:S(2)}, u32[]{:S(2)}) %collective-permute-start.5) | collective-permute-done | bytes 393248 | tf_op jit(solution)/shard_map/ppermute | solution.py:33
  37.8 1.5 %collective-permute-start.6 = (bf16[256,768]{1,0:T(8,128)(2,1)S(1)}, bf16[256,768]{1,0:T(8,128)(2,1)S(1)}, u32[]{:S(2)}, u32[]{:S(2)}) collective-permute-start(bf16[256,768]{1,0:T(8,128)(2,1)S(1)} %collective-permute-done.5.refs_8_), channel_id=1, source_target_pairs={{0,16},{16,0},{1,17},{17,1},{2,18},{18,2},{3,19},{19,3},{4,20},{20... | collective-permute-start | bytes 1179656 | tf_op jit(solution)/shard_map/ppermute | solution.py:33
  40.2 4.2 %collective-permute-done.4.refs_7_ = bf16[256,768]{1,0:T(8,128)(2,1)S(1)} collective-permute-done((bf16[256,768]{1,0:T(8,128)(2,1)S(1)}, bf16[256,768]{1,0:T(8,128)(2,1)S(1)}, u32[]{:S(2)}, u32[]{:S(2)}) %collective-permute-start.4) | collective-permute-done | bytes 393248 | tf_op jit(solution)/shard_map/ppermute | solution.py:33
  44.4 3.5 %collective-permute-start.12 = (bf16[512,512]{1,0:T(8,128)(2,1)S(1)}, bf16[512,512]{1,0:T(8,128)(2,1)S(1)}, u32[]{:S(2)}, u32[]{:S(2)}) collective-permute-start(bf16[512,512]{1,0:T(8,128)(2,1)S(1)} %shard_map.77.refs_7_), channel_id=1, source_target_pairs={{0,8},{1,9},{2,10},{3,11},{4,12},{5,13},{6,14},{7,15},{8,0},{9,1},... | collective-permute-start | bytes 1572872 | tf_op jit(solution)/shard_map/ppermute | solution.py:33
  47.8 7.2 %collective-permute-done.9.refs_1_.refs_6_ = bf16[256,2048]{1,0:T(8,128)(2,1)S(1)} collective-permute-done((bf16[256,2048]{1,0:T(8,128)(2,1)S(1)}, bf16[256,2048]{1,0:T(8,128)(2,1)S(1)}, u32[]{:S(2)}, u32[]{:S(2)}) %collective-permute-start.9) | collective-permute-done | bytes 1048608 | tf_op jit(solution)/shard_map/ppermute | solution.py:33
  55.1 4.9 %shard_map.76 = (f32[256,768]{1,0:T(8,128)S(1)}, f32[256,768]{1,0:T(8,128)S(1)}) custom-call(bf16[256,2048]{1,0:T(8,128)(2,1)S(1)} %collective-permute-done.8.refs_0_.refs_5_, bf16[256,2048]{1,0:T(8,128)(2,1)S(1)} %collective-permute-done.9.refs_1_.refs_6_, bf16[256,768]{1,0:T(8,128)(2,1)S(1)} %get-tuple-element.20.refs_2_, ...), custom_call_target="tpu_custom_call" | custom-call | flops 1610612736 | bytes 6815744 | tf_op jit(solution)/shard_map/pallas_call | solution.py:369
  60.8 1.9 %collective-permute-start.14 = (bf16[512,512]{1,0:T(8,128)(2,1)S(1)}, bf16[512,512]{1,0:T(8,128)(2,1)S(1)}, u32[]{:S(2)}, u32[]{:S(2)}) collective-permute-start(bf16[512,512]{1,0:T(8,128)(2,1)S(1)} %shard_map.77.refs_7_), channel_id=1, source_target_pairs={{0,4},{1,5},{2,6},{3,7},{4,0},{5,1},{6,2},{7,3},{8,12},{9,13},{10,... | collective-permute-start | bytes 1572872 | tf_op jit(solution)/shard_map/ppermute | solution.py:33
  62.7 6.0 %collective-permute-done.12.refs_8_ = bf16[512,512]{1,0:T(8,128)(2,1)S(1)} collective-permute-done((bf16[512,512]{1,0:T(8,128)(2,1)S(1)}, bf16[512,512]{1,0:T(8,128)(2,1)S(1)}, u32[]{:S(2)}, u32[]{:S(2)}) %collective-permute-start.12) | collective-permute-done | bytes 524320 | tf_op jit(solution)/shard_map/ppermute | solution.py:33
  68.7 4.9 %shard_map.75 = (f32[256,768]{1,0:T(8,128)S(1)}, f32[256,768]{1,0:T(8,128)S(1)}) custom-call(bf16[256,2048]{1,0:T(8,128)(2,1)S(1)} %get-tuple-element.18.refs_0_.refs_3_, bf16[256,2048]{1,0:T(8,128)(2,1)S(1)} %collective-permute-done.refs_1_.refs_4_, bf16[256,768]{1,0:T(8,128)(2,1)S(1)} %get-tuple-element.20.refs_2_, ...), custom_call_target="tpu_custom_call" | custom-call | flops 1610612736 | bytes 6815744 | tf_op jit(solution)/shard_map/pallas_call | solution.py:369
  73.7 6.2 %collective-permute-done.14.refs_9_ = bf16[512,512]{1,0:T(8,128)(2,1)S(1)} collective-permute-done((bf16[512,512]{1,0:T(8,128)(2,1)S(1)}, bf16[512,512]{1,0:T(8,128)(2,1)S(1)}, u32[]{:S(2)}, u32[]{:S(2)}) %collective-permute-start.14) | collective-permute-done | bytes 524320 | tf_op jit(solution)/shard_map/ppermute | solution.py:33
  79.9 2.3 %shard_map.78.refs_8_ = f32[2,512,256]{2,1,0:T(8,128)S(1)} custom-call(s32[8]{0:T(128)S(1)} %copy-done.5, s32[8]{0:T(128)S(1)} %copy-done.4, s32[8]{0:T(128)S(1)} %copy-done.6, bf16[256,2048]{1,0:T(8,128)(2,1)S(1)} %get-tuple-element.18.refs_0_.refs_3_, bf16[256,2048]{1,0:T(8,128)(2,1)S(1)} %collective-permute-done.refs_1_.refs_4_, ...), custom_call_target="tpu_custom_call" | custom-call | flops 805306368 | bytes 5767168 | tf_op jit(solution)/shard_map/pallas_call | solution.py:393
  82.3 8.8 %collective-permute-done.13.refs_7_ = bf16[512,512]{1,0:T(8,128)(2,1)S(1)} collective-permute-done((bf16[512,512]{1,0:T(8,128)(2,1)S(1)}, bf16[512,512]{1,0:T(8,128)(2,1)S(1)}, u32[]{:S(2)}, u32[]{:S(2)}) %collective-permute-start.13) | collective-permute-done | bytes 524320 | tf_op jit(solution)/shard_map/ppermute | solution.py:33
  91.1 1.3 %shard_map.79 = (f32[2,128,128]{2,1,0:T(8,128)S(1)}, f32[2,128,128]{2,1,0:T(8,128)S(1)}) custom-call(s32[8]{0:T(128)S(1)} %copy-done.5, s32[8]{0:T(128)S(1)} %copy-done.4, s32[8]{0:T(128)S(1)} %copy-done.6, bf16[256,2048]{1,0:T(8,128)(2,1)S(1)} %get-tuple-element.18.refs_0_.refs_3_, bf16[256,2048]{1,0:T(8,128)(2,1)S(1)} %collective-permute-done.refs_1_.refs_4_, ...), custom_call_target="tpu_custom_call" | custom-call | flops 268435456 | bytes 2621440 | tf_op jit(solution)/shard_map/pallas_call | solution.py:393
  92.6 1.6 %collective-permute-start.11 = (bf16[256,768]{1,0:T(8,128)(2,1)S(1)}, bf16[256,768]{1,0:T(8,128)(2,1)S(1)}, u32[]{:S(2)}, u32[]{:S(2)}) collective-permute-start(bf16[256,768]{1,0:T(8,128)(2,1)S(1)} %add_convert_fusion), channel_id=1, source_target_pairs={{0,2},{1,3},{2,0},{3,1},{4,6},{5,7},{6,4},{7,5},{8,10},{9,11},{10,... | collective-permute-start | bytes 1179656 | tf_op jit(solution)/shard_map/ppermute | solution.py:33
  95.4 10.1 %collective-permute-done.16 = f32[1,128,128]{2,1,0:T(8,128)S(1)} collective-permute-done((f32[1,128,128]{2,1,0:T(8,128)S(1)}, f32[1,128,128]{2,1,0:T(8,128)S(1)}, u32[]{:S(2)}, u32[]{:S(2)}) %collective-permute-start.16) | collective-permute-done | bytes 65568 | tf_op jit(solution)/shard_map/ppermute | solution.py:33
  105.5 2.1 %shard_map.80 = bf16[256,768]{1,0:T(8,128)(2,1)} custom-call(s32[8]{0:T(128)S(1)} %copy-done.5, s32[8]{0:T(128)S(1)} %copy-done.4, s32[8]{0:T(128)S(1)} %copy-done.6, f32[256,768]{1,0:T(8,128)S(1)} %get-tuple-element.22.refs_3_, f32[256,768]{1,0:T(8,128)S(1)} %collective-permute-done.7.refs_4_, bf16[256,768]{1,0:T(8,128)(2,1)S(1)} %collective-permute-done.11.refs_5_, ...), custom_call_target="tpu_custom_call" | custom-call | flops 25165824 | bytes 1572864 | tf_op jit(solution)/shard_map/pallas_call | solution.py:413
  (35 shorter events, 6.5 us)
Async XLA Ops:
  0.0 1.1 %copy-start.3 = (bf16[512,768]{1,0:T(8,128)(2,1)S(1)}, bf16[512,768]{1,0:T(8,128)(2,1)}, u32[]{:S(2)}) copy-start(bf16[512,768]{1,0:T(8,128)(2,1)} %key.1) | copy-start | bytes 2359300
  1.1 38.2 %copy-start.4 = (s32[8]{0:T(128)S(1)}, s32[8]{0:T(128)}, u32[]{:S(2)}) copy-start(s32[8]{0:T(128)} %refs_1_.5) | copy-start | bytes 100
  1.5 21.7 %collective-permute-start.1 = (bf16[256,768]{1,0:T(8,128)(2,1)S(1)}, bf16[256,768]{1,0:T(8,128)(2,1)S(1)}, u32[]{:S(2)}, u32[]{:S(2)}) collective-permute-start(bf16[256,768]{1,0:T(8,128)(2,1)S(1)} %get-tuple-element.20.refs_2_), channel_id=1, source_target_pairs={{0,8},{1,9},{2,10},{3,11},{4,12},{5,13},{6,14},{7,15},{8,0},{9,1},... | collective-permute-start | bytes 1179656 | tf_op jit(solution)/shard_map/ppermute | solution.py:33
  5.6 2.2 %copy-start = (bf16[256,8192]{1,0:T(8,128)(2,1)S(1)}, bf16[256,8192]{1,0:T(8,128)(2,1)}, u32[]{:S(2)}) copy-start(bf16[256,8192]{1,0:T(8,128)(2,1)} %tokens.1) | copy-start | bytes 12582916
  7.8 31.5 %copy-start.2 = (bf16[512,16,64]{0,2,1:T(8,128)(2,1)S(1)}, bf16[512,16,64]{0,2,1:T(8,128)(2,1)}, u32[]{:S(2)}) copy-start(bf16[512,16,64]{0,2,1:T(8,128)(2,1)} %param.9) | copy-start | bytes 3145732
  8.9 39.0 %collective-permute-start.8 = (bf16[256,2048]{1,0:T(8,128)(2,1)S(1)}, bf16[256,2048]{1,0:T(8,128)(2,1)S(1)}, u32[]{:S(2)}, u32[]{:S(2)}) collective-permute-start(bf16[256,2048]{1,0:T(8,128)(2,1)S(1)} %get-tuple-element.24), channel_id=1, source_target_pairs={{0,2},{1,3},{2,0},{3,1},{4,6},{5,7},{6,4},{7,5},{8,10},{9,11},{10,... | collective-permute-start | bytes 3145736 | tf_op jit(solution)/shard_map/ppermute | solution.py:33
  10.5 44.6 %collective-permute-start.9 = (bf16[256,2048]{1,0:T(8,128)(2,1)S(1)}, bf16[256,2048]{1,0:T(8,128)(2,1)S(1)}, u32[]{:S(2)}, u32[]{:S(2)}) collective-permute-start(bf16[256,2048]{1,0:T(8,128)(2,1)S(1)} %get-tuple-element.25), channel_id=1, source_target_pairs={{0,3},{1,2},{2,1},{3,0},{4,7},{5,6},{6,5},{7,4},{8,11},{9,10},{10,... | collective-permute-start | bytes 3145736 | tf_op jit(solution)/shard_map/ppermute | solution.py:33
  10.5 19.2 %collective-permute-start.3 = (bf16[256,768]{1,0:T(8,128)(2,1)S(1)}, bf16[256,768]{1,0:T(8,128)(2,1)S(1)}, u32[]{:S(2)}, u32[]{:S(2)}) collective-permute-start(bf16[256,768]{1,0:T(8,128)(2,1)S(1)} %get-tuple-element.20.refs_2_), channel_id=1, source_target_pairs={{0,4},{1,5},{2,6},{3,7},{4,0},{5,1},{6,2},{7,3},{8,12},{9,13},{10,... | collective-permute-start | bytes 1179656 | tf_op jit(solution)/shard_map/ppermute | solution.py:33
  23.3 14.5 %collective-permute-start.5 = (bf16[256,768]{1,0:T(8,128)(2,1)S(1)}, bf16[256,768]{1,0:T(8,128)(2,1)S(1)}, u32[]{:S(2)}, u32[]{:S(2)}) collective-permute-start(bf16[256,768]{1,0:T(8,128)(2,1)S(1)} %collective-permute-done.1.refs_4_), channel_id=1, source_target_pairs={{0,4},{1,5},{2,6},{3,7},{4,0},{5,1},{6,2},{7,3},{8,12},{9,13},{10,... | collective-permute-start | bytes 1179656 | tf_op jit(solution)/shard_map/ppermute | solution.py:33
  23.9 15.4 %collective-permute-start.2 = (bf16[256,768]{1,0:T(8,128)(2,1)S(1)}, bf16[256,768]{1,0:T(8,128)(2,1)S(1)}, u32[]{:S(2)}, u32[]{:S(2)}) collective-permute-start(bf16[256,768]{1,0:T(8,128)(2,1)S(1)} %collective-permute-done.1.refs_4_), channel_id=1, source_target_pairs={{0,16},{16,0},{1,17},{17,1},{2,18},{18,2},{3,19},{19,3},{4,20},{20... | collective-permute-start | bytes 1179656 | tf_op jit(solution)/shard_map/ppermute | solution.py:33
  29.6 14.8 %collective-permute-start.4 = (bf16[256,768]{1,0:T(8,128)(2,1)S(1)}, bf16[256,768]{1,0:T(8,128)(2,1)S(1)}, u32[]{:S(2)}, u32[]{:S(2)}) collective-permute-start(bf16[256,768]{1,0:T(8,128)(2,1)S(1)} %collective-permute-done.3.refs_6_), channel_id=1, source_target_pairs={{0,16},{16,0},{1,17},{17,1},{2,18},{18,2},{3,19},{19,3},{4,20},{20... | collective-permute-start | bytes 1179656 | tf_op jit(solution)/shard_map/ppermute | solution.py:33
  37.8 17.3 %collective-permute-start.6 = (bf16[256,768]{1,0:T(8,128)(2,1)S(1)}, bf16[256,768]{1,0:T(8,128)(2,1)S(1)}, u32[]{:S(2)}, u32[]{:S(2)}) collective-permute-start(bf16[256,768]{1,0:T(8,128)(2,1)S(1)} %collective-permute-done.5.refs_8_), channel_id=1, source_target_pairs={{0,16},{16,0},{1,17},{17,1},{2,18},{18,2},{3,19},{19,3},{4,20},{20... | collective-permute-start | bytes 1179656 | tf_op jit(solution)/shard_map/ppermute | solution.py:33
  39.3 29.4 %collective-permute-start = (bf16[256,2048]{1,0:T(8,128)(2,1)S(1)}, bf16[256,2048]{1,0:T(8,128)(2,1)S(1)}, u32[]{:S(2)}, u32[]{:S(2)}) collective-permute-start(bf16[256,2048]{1,0:T(8,128)(2,1)S(1)} %get-tuple-element.19), channel_id=1, source_target_pairs={{0,1},{1,0},{2,3},{3,2},{4,5},{5,4},{6,7},{7,6},{8,9},{9,8},{10,11... | collective-permute-start | bytes 3145736 | tf_op jit(solution)/shard_map/ppermute | solution.py:33
  44.4 24.3 %collective-permute-start.12 = (bf16[512,512]{1,0:T(8,128)(2,1)S(1)}, bf16[512,512]{1,0:T(8,128)(2,1)S(1)}, u32[]{:S(2)}, u32[]{:S(2)}) collective-permute-start(bf16[512,512]{1,0:T(8,128)(2,1)S(1)} %shard_map.77.refs_7_), channel_id=1, source_target_pairs={{0,8},{1,9},{2,10},{3,11},{4,12},{5,13},{6,14},{7,15},{8,0},{9,1},... | collective-permute-start | bytes 1572872 | tf_op jit(solution)/shard_map/ppermute | solution.py:33
  60.0 19.9 %copy-start.5 = (s32[8]{0:T(128)S(1)}, s32[8]{0:T(128)}, u32[]{:S(2)}) copy-start(s32[8]{0:T(128)} %refs_0_.5) | copy-start | bytes 100
  60.0 19.9 %copy-start.6 = (s32[8]{0:T(128)S(1)}, s32[8]{0:T(128)}, u32[]{:S(2)}) copy-start(s32[8]{0:T(128)} %refs_2_.5) | copy-start | bytes 100
  60.0 32.5 %collective-permute-start.10 = (f32[256,768]{1,0:T(8,128)S(1)}, f32[256,768]{1,0:T(8,128)S(1)}, u32[]{:S(2)}, u32[]{:S(2)}) collective-permute-start(f32[256,768]{1,0:T(8,128)S(1)} %get-tuple-element.27), channel_id=1, source_target_pairs={{0,1},{1,0},{2,3},{3,2},{4,5},{5,4},{6,7},{7,6},{8,9},{9,8},{10,11... | collective-permute-start | bytes 2359304 | tf_op jit(solution)/shard_map/ppermute | solution.py:33
  60.8 19.1 %collective-permute-start.14 = (bf16[512,512]{1,0:T(8,128)(2,1)S(1)}, bf16[512,512]{1,0:T(8,128)(2,1)S(1)}, u32[]{:S(2)}, u32[]{:S(2)}) collective-permute-start(bf16[512,512]{1,0:T(8,128)(2,1)S(1)} %shard_map.77.refs_7_), channel_id=1, source_target_pairs={{0,4},{1,5},{2,6},{3,7},{4,0},{5,1},{6,2},{7,3},{8,12},{9,13},{10,... | collective-permute-start | bytes 1572872 | tf_op jit(solution)/shard_map/ppermute | solution.py:33
  68.7 22.4 %collective-permute-start.13 = (bf16[512,512]{1,0:T(8,128)(2,1)S(1)}, bf16[512,512]{1,0:T(8,128)(2,1)S(1)}, u32[]{:S(2)}, u32[]{:S(2)}) collective-permute-start(bf16[512,512]{1,0:T(8,128)(2,1)S(1)} %collective-permute-done.12.refs_8_), channel_id=1, source_target_pairs={{0,4},{1,5},{2,6},{3,7},{4,0},{5,1},{6,2},{7,3},{8,12},{9,13},{10,... | collective-permute-start | bytes 1572872 | tf_op jit(solution)/shard_map/ppermute | solution.py:33
  73.6 31.9 %collective-permute-start.7 = (f32[256,768]{1,0:T(8,128)S(1)}, f32[256,768]{1,0:T(8,128)S(1)}, u32[]{:S(2)}, u32[]{:S(2)}) collective-permute-start(f32[256,768]{1,0:T(8,128)S(1)} %get-tuple-element.23), channel_id=1, source_target_pairs={{0,1},{1,0},{2,3},{3,2},{4,5},{5,4},{6,7},{7,6},{8,9},{9,8},{10,11... | collective-permute-start | bytes 2359304 | tf_op jit(solution)/shard_map/ppermute | solution.py:33
  82.3 23.3 %copy-start.1 = (bf16[16,64,768]{2,1,0:T(8,128)(2,1)S(1)}, bf16[16,64,768]{2,1,0:T(8,128)(2,1)}, u32[]{:S(2)}) copy-start(bf16[16,64,768]{2,1,0:T(8,128)(2,1)} %refs_8_.1) | copy-start | bytes 4718596
  92.4 1.8 %collective-permute-start.15 = (f32[2,128,128]{2,1,0:T(8,128)S(1)}, f32[2,128,128]{2,1,0:T(8,128)S(1)}, u32[]{:S(2)}, u32[]{:S(2)}) collective-permute-start(f32[2,128,128]{2,1,0:T(8,128)S(1)} %get-tuple-element.30), channel_id=1, source_target_pairs={{0,1},{1,0},{2,3},{3,2},{4,5},{5,4},{6,7},{7,6},{8,9},{9,8},{10,11... | collective-permute-start | bytes 393224 | tf_op jit(solution)/shard_map/ppermute | solution.py:33
  92.6 13.0 %collective-permute-start.11 = (bf16[256,768]{1,0:T(8,128)(2,1)S(1)}, bf16[256,768]{1,0:T(8,128)(2,1)S(1)}, u32[]{:S(2)}, u32[]{:S(2)}) collective-permute-start(bf16[256,768]{1,0:T(8,128)(2,1)S(1)} %add_convert_fusion), channel_id=1, source_target_pairs={{0,2},{1,3},{2,0},{3,1},{4,6},{5,7},{6,4},{7,5},{8,10},{9,11},{10,... | collective-permute-start | bytes 1179656 | tf_op jit(solution)/shard_map/ppermute | solution.py:33
  94.2 11.3 %collective-permute-start.16 = (f32[1,128,128]{2,1,0:T(8,128)S(1)}, f32[1,128,128]{2,1,0:T(8,128)S(1)}, u32[]{:S(2)}, u32[]{:S(2)}) collective-permute-start(f32[1,128,128]{2,1,0:T(8,128)S(1)} %get-tuple-element.31), channel_id=1, source_target_pairs={{0,2},{1,3},{2,0},{3,1},{4,6},{5,7},{6,4},{7,5},{8,10},{9,11},{10,... | collective-permute-start | bytes 196616 | tf_op jit(solution)/shard_map/ppermute | solution.py:33

commit v3 on v2

--- a/solution.py
+++ b/solution.py
@@ -9,22 +9,24 @@
 
 BLOCK = 128
 LANES = 128
+MOST = 16
 LAYER_CHIPS = 4
 VMEM_BYTES = 28 * 1024 * 1024
+FIRST_VMEM_BYTES = 56 * 1024 * 1024
 
 HBM = pl.BlockSpec(memory_space=pl.ANY)
 VMEM = pl.BlockSpec(memory_space=pltpu.VMEM)
 SMEM = pl.BlockSpec(memory_space=pltpu.SMEM)
 
 
-def call(kernel, outs, out_specs, in_specs, scratch, flops, moved):
+def call(kernel, outs, out_specs, in_specs, scratch, flops, moved, vmem=VMEM_BYTES):
     return pl.pallas_call(
         kernel,
         out_shape=outs,
         in_specs=in_specs,
         out_specs=out_specs,
         scratch_shapes=scratch,
-        compiler_params=pltpu.CompilerParams(vmem_limit_bytes=VMEM_BYTES),
+        compiler_params=pltpu.CompilerParams(vmem_limit_bytes=vmem),
         cost_estimate=pl.CostEstimate(flops=flops, bytes_accessed=moved, transcendentals=0),
     )
 
@@ -44,19 +46,13 @@
     return pl.multiple_of((lax.axis_index("rep") ^ h) * part, part)
 
 
-def key_parts_kernel(splits, part, key, *refs):
-    outs, sems = refs[:splits], refs[splits]
-    pairs = [(key.at[pl.ds(part_start(h, part), part), :], outs[h]) for h in range(splits)]
-    for copy in run_copies(pairs, sems):
-        copy.wait()
-
-
-def token_pieces_kernel(group, layers, splits, part, tokens, *refs):
+def first_kernel(group, layers, splits, part, key, tokens, *refs):
+    keys, refs = refs[:splits], refs[splits:]
     outs, sems = refs[:group], refs[group]
     depth = splits * part
     me = lax.axis_index("batch")
     layer, spot = me // group, me % group
-    pairs = []
+    pairs = [(key.at[pl.ds(part_start(h, part), part), :], keys[h]) for h in range(splits)]
     for s in reversed(range(group)):
         for t in range(layers):
             first = ((layer ^ t) * group + (spot ^ s)) * depth
@@ -73,71 +69,56 @@
         copy.wait()
 
 
-def chosen_kernel(slots, rank, splits, part, picks, down, out, sems):
+def gate_kernel(value, *refs):
+    pass
+
+
+def gate(value, *ready):
+    return pl.pallas_call(
+        gate_kernel,
+        out_shape=jax.ShapeDtypeStruct(value.shape, value.dtype),
+        in_specs=[HBM] * (1 + len(ready)),
+        out_specs=HBM,
+        input_output_aliases={0: 0},
+    )(value, *ready)
+
+
+def chosen_kernel(slots, rank, splits, part, group, layers, shift, picks, down, *refs):
+    outs, sems = refs[:-1], refs[-1]
+    layer = lax.axis_index("batch") // group
+    half = (layer * 2) // layers
     pairs = []
-    for q in range(slots):
-        for h in range(splits):
-            start = part_start(h, part) if splits > 1 else 0
-            pairs.append(
-                (
-                    down.at[picks[q], :, pl.ds(start, part)],
-                    out.at[pl.ds(q * rank, rank), pl.ds(h * part, part)],
+    for n, out in enumerate(outs):
+        first = (half ^ 1 ^ n) * shift
+        for q in range(slots):
+            for h in range(splits):
+                start = part_start(h, part) if splits > 1 else 0
+                pairs.append(
+                    (
+                        down.at[picks[first + q], :, pl.ds(start, part)],
+                        out.at[pl.ds(q * rank, rank), pl.ds(h * part, part)],
+                    )
                 )
-            )
     for copy in run_copies(pairs, sems):
         copy.wait()
 
 
-def base_kernel(rows, depth, layers, entries, count, *refs):
-    toks, arrays = refs[:2], refs[2 : 2 + count]
-    outs = refs[2 + count : 4 + count]
-    held = refs[4 + count]
-    weights = refs[5 + count : 5 + 2 * count]
-    tok_sems, sems = refs[5 + 2 * count :]
-    order = []
-    for t, _, _, _, _ in entries:
-        if t not in order:
-            order.append(t)
-    token_copies = {}
-    started = {}
-    for t in order:
-        token_copies[t] = []
-        for i in range(2):
-            columns = pl.ds(t * depth, depth)
-            token_copies[t].append(
-                pltpu.make_async_copy(
-                    toks[i].at[:, columns], held.at[pl.ds(i * rows, rows), columns], tok_sems.at[i, t]
-                )
-            )
-        for copy in token_copies[t]:
-            copy.start()
-        for u, a, _, _, _ in entries:
-            if u == t and a not in started:
-                started[a] = pltpu.make_async_copy(arrays[a], weights[a], sems.at[a])
-                started[a].start()
-    ready = set()
-    for t in order:
-        for copy in token_copies[t]:
-            copy.wait()
-        total = None
-        for u, a, row, deep, column in entries:
-            if u != t:
-                continue
-            if a not in ready:
-                started[a].wait()
-                ready.add(a)
-            term = jnp.dot(
-                held[:, column : column + deep],
-                weights[a][row : row + deep, :],
-                preferred_element_type=jnp.float32,
-            )
-            total = term if total is None else total + term
-        for i in range(2):
-            here = total[i * rows : (i + 1) * rows]
-            if t == order[0]:
-                outs[i][...] = here
-            else:
-                outs[i][...] += here
+def base_kernel(rows, tokens_of, moves, count, *refs):
+    toks, arrays = refs[:tokens_of], refs[tokens_of : tokens_of + count]
+    outs = refs[tokens_of + count : 2 * tokens_of + count]
+    held, weights, sems = refs[2 * tokens_of + count :]
+    pairs = [(tok, held.at[pl.ds(i * rows, rows), :]) for i, tok in enumerate(toks)]
+    for a, row, deep, to in moves:
+        pairs.append((arrays[a].at[pl.ds(row, deep), :], weights.at[pl.ds(to, deep), :]))
+    for copy in run_copies(pairs, sems):
+        copy.wait()
+    width = weights.shape[1]
+    step = 2 * LANES if width % (2 * LANES) == 0 else width
+    for column in range(0, width, step):
+        here = pl.ds(column, step)
+        total = jnp.dot(held[...], weights[:, here], preferred_element_type=jnp.float32)
+        for i in range(tokens_of):
+            outs[i][:, here] = total[i * rows : (i + 1) * rows]
 
 
 def table(lists, block):
@@ -155,7 +136,7 @@
 
 
 def low_kernel(
-    group, rows, depth, rank, entries, count, by_request, has_sum, last, *refs
+    group, layers, rows, depth, rank, entries, count, by_request, shift, has_sum, last, *refs
 ):
     lists, refs = refs[:3], refs[3:]
     toks, refs = refs[:group], refs[group:]
@@ -192,7 +173,7 @@
         for j in range(local_blocks):
             block = (layer * group + (spot ^ s)) * local_blocks + j
             owner, adapter, _ = table(lists, block)
-            slots.append(owner if by_request else adapter)
+            slots.append(owner - (layer * 2) // layers * shift if by_request else adapter)
     ready = set()
     wide = 2 * local_blocks
     sums = [before[p] if has_sum else None for p in range(group // 2)]
@@ -296,23 +277,24 @@
     lists = (request_block_list, request_adapter_index, request_tail_tokens)
     f32, bf16 = jnp.float32, jnp.bfloat16
 
-    if splits > 1:
-        key_parts = call(
-            functools.partial(key_parts_kernel, splits, part),
-            [jax.ShapeDtypeStruct((part, out_width), bf16)] * splits,
-            [HBM] * splits,
-            [HBM],
-            [pltpu.SemaphoreType.DMA((splits,))],
-            0,
-            4 * depth * out_width,
-        )(key_matrix)
-    else:
-        key_parts = [key_matrix]
-
-    def over_layers(own):
+    first = call(
+        functools.partial(first_kernel, group, layers, splits, part),
+        [jax.ShapeDtypeStruct((part, out_width), bf16)] * splits
+        + [jax.ShapeDtypeStruct((rows, held_width), bf16)] * group,
+        [HBM] * (splits + group),
+        [HBM] * 2,
+        [pltpu.SemaphoreType.DMA((splits + group * layers * splits,))],
+        0,
+        4 * (rows * width + depth * out_width),
+        FIRST_VMEM_BYTES,
+    )(key_matrix, tokens)
+    key_parts, pieces = first[:splits], list(first[splits:])
+
+    def over_layers(across, near):
         bundles = []
         bit = layers // 2
         while bit:
+            own = near(bundles) if bundles else across
             moved = [([bit], swap(own, "batch", bit * group))]
             if bundles:
                 rest = [v for _, v in bundles]
@@ -323,60 +305,73 @@
             bit //= 2
         return bundles
 
-    key_bundles = over_layers(key_parts[0])
-
-    pieces = call(
-        functools.partial(token_pieces_kernel, group, layers, splits, part),
-        [jax.ShapeDtypeStruct((rows, held_width), bf16)] * group,
-        [HBM] * group,
-        [HBM],
-        [pltpu.SemaphoreType.DMA((group * layers * splits,))],
-        0,
-        4 * rows * width,
-    )(tokens)
-    pieces = [pieces[0]] + [swap(pieces[s], "batch", s) for s in range(1, group)]
+    key_bundles = over_layers(key_parts[0], lambda _: key_parts[0])
+
+    for s in reversed(range(1, group)):
+        if 1 < s < group - 1:
+            pieces[s] = gate(pieces[s], pieces[s + 1])
+        pieces[s] = swap(pieces[s], "batch", s)
 
     down = jnp.transpose(adapter_down_factors, (1, 2, 0))
     requests = request_adapter_index.shape[0]
     by_request = requests < adapters
-    slots = requests if by_request else adapters
+    shift = 1 if by_request and local_blocks * devices == 2 * MOST and layers > 1 else 0
+    slots = requests - shift if by_request else adapters
     if by_request:
-        down = call(
-            functools.partial(chosen_kernel, slots, rank, splits, part),
-            jax.ShapeDtypeStruct((slots * rank, depth), bf16),
-            HBM,
+        across, down = call(
+            functools.partial(chosen_kernel, slots, rank, splits, part, group, layers, shift),
+            [jax.ShapeDtypeStruct((slots * rank, depth), bf16)] * 2,
+            [HBM] * 2,
             [SMEM, HBM],
-            [pltpu.SemaphoreType.DMA((slots * splits,))],
+            [pltpu.SemaphoreType.DMA((2 * slots * splits,))],
             0,
-            4 * slots * rank * depth,
+            8 * slots * rank * depth,
+            FIRST_VMEM_BYTES,
         )(request_adapter_index, down)
     else:
         down = down.reshape(slots * rank, depth)
-    down, _ = lax.optimization_barrier((down, key_bundles[0][1]))
-    down_bundles = over_layers(down)
-
-    arrays, entries = [], []
+        across = down
+    across = gate(across, key_bundles[0][1])
+    down = gate(down, key_bundles[-1][1])
+    down_bundles = over_layers(across, lambda _: down)
+
+    arrays, moves = [], []
     for ts, value in [([0], None)] + key_bundles:
-        for h in range(splits):
-            if value is None:
-                arrays.append(key_parts[h])
-            else:
-                arrays.append(swap(value, "rep", h) if h else value)
-            for i, t in enumerate(ts):
-                entries.append((t, len(arrays) - 1, i * part, part, t * depth + h * part))
+        if value is None:
+            arrays.extend(key_parts)
+        else:
+            arrays.append(value)
+        for i, t in enumerate(ts):
+            moves.append((len(arrays) - (splits if value is None else 1), i * part, part, t * depth))
+    for h in range(1, splits):
+        moves.append((h, 0, part, h * part))
+        for taken in (key_bundles[:1], key_bundles[1:]):
+            if taken:
+                values = [v for _, v in taken]
+                values = values[0] if len(values) == 1 else jnp.concatenate(values, 0)
+                arrays.append(swap(values, "rep", h))
+                for i, t in enumerate([t for ts, _ in taken for t in ts]):
+                    moves.append((len(arrays) - 1, i * part, part, t * depth + h * part))
     partial_sums = [None] * group
-    for p in range(group // 2):
-        partial_sums[2 * p : 2 * p + 2] = call(
-            functools.partial(base_kernel, rows, depth, layers, tuple(entries), len(arrays)),
-            [jax.ShapeDtypeStruct((rows, out_width), f32)] * 2,
-            [VMEM] * 2,
-            [HBM] * (2 + len(arrays)),
-            [pltpu.VMEM((2 * rows, held_width), bf16)]
-            + [pltpu.VMEM(a.shape, bf16) for a in arrays]
-            + [pltpu.SemaphoreType.DMA((2, layers)), pltpu.SemaphoreType.DMA((len(arrays),))],
-            4 * rows * held_width * out_width,
-            2 * held_width * (2 * rows + out_width) + 8 * rows * out_width,
-        )(pieces[2 * p], pieces[2 * p + 1], *arrays)
+    late = [2] if group > 2 else []
+    for which in ([s for s in range(group) if s not in late], late):
+        if not which:
+            continue
+        results = call(
+            functools.partial(base_kernel, rows, len(which), tuple(moves), len(arrays)),
+            [jax.ShapeDtypeStruct((rows, out_width), f32)] * len(which),
+            [VMEM] * len(which),
+            [HBM] * (len(which) + len(arrays)),
+            [
+                pltpu.VMEM((len(which) * rows, held_width), bf16),
+                pltpu.VMEM((held_width, out_width), bf16),
+                pltpu.SemaphoreType.DMA((len(which) + len(moves),)),
+            ],
+            2 * len(which) * rows * held_width * out_width,
+            2 * held_width * (len(which) * rows + out_width) + 4 * len(which) * rows * out_width,
+        )(*[pieces[s] for s in which], *arrays)
+        for s, value in zip(which, results):
+            partial_sums[s] = value
     bases = layer_sums(partial_sums, True)
 
     def low_call(bundles, before, last):
@@ -392,8 +387,8 @@
             outs, out_specs = jax.ShapeDtypeStruct((pairs, tall, wide), f32), VMEM
         return call(
             functools.partial(
-                low_kernel, group, rows, depth, rank, tuple(at), len(taken), by_request,
-                before is not None, last,
+                low_kernel, group, layers, rows, depth, rank, tuple(at), len(taken), by_request,
+                shift, before is not None, last,
             ),
             outs,
             out_specs,

time: 108 us -> 299 us (2.77)
  Pallas kernels: 17.8 us -> 199 us
  waiting for transfers between devices: 64.7 us -> 72.9 us
  starting transfers between devices: 21.6 us -> 17.2 us
  local copies, waits for them, and re-layouts: 3.36 us -> 6.87 us
    pallas_call x7 -> x9, Pallas kernels: 15.7 us -> 197 us  [the longest x1 152 us: shards(): call(functools.partial(first_kernel, group, layers, splits, part), [jax.S...]
    ppermute x17 -> x16, waiting for transfers between devices: 64.7 us -> 72.9 us  [swap(): lax.ppermute(value, axis, [(i, i ^ bit) for i in range(lax.axis_size(axis...]
    ppermute x17 -> x16, starting transfers between devices: 21.6 us -> 17.2 us  [swap(): lax.ppermute(value, axis, [(i, i ^ bit) for i in range(lax.axis_size(axis...]
    unnamed x14 -> x40, local copies, waits for them, and re-layouts: 3.35 us -> 6.85 us
  transfers between devices with their start and end apart: 17 -> 16, of which waited for: 9 -> 7; matrix products, arithmetic and copies ran while one was open for 0% -> 1% of each run, Pallas kernels for 14% -> 15%
where the time goes in v3:
time: 299 us; the launch traced here: 298 us
  Pallas kernels  199 us (67%)
  waiting for transfers between devices  72.9 us (24%)
  starting transfers between devices  17.2 us (6%)
  local copies, waits for them, and re-layouts  6.87 us (2%)
    pallas_call x1, Pallas kernels, shards(): call(functools.partial(first_kernel, group, layers, splits, part), [jax.S...  152 us
    ppermute x16, waiting for transfers between devices, swap(): lax.ppermute(value, axis, [(i, i ^ bit) for i in range(lax.axis_size(axis...  72.9 us
    pallas_call x1, Pallas kernels, shards(): call(functools.partial(chosen_kernel, slots, rank, splits, part, group, l...  29.8 us
    ppermute x16, starting transfers between devices, swap(): lax.ppermute(value, axis, [(i, i ^ bit) for i in range(lax.axis_size(axis...  17.2 us
    pallas_call x2, Pallas kernels, shards(): call(functools.partial(base_kernel, rows, len(which), tuple(moves), len(a...  8.94 us
    unnamed x40, local copies, waits for them, and re-layouts  6.85 us
  transfers between devices with their start and end apart: 16, of which 7 were waited for; matrix products, arithmetic and copies ran while one was open for 1% of the time, Pallas kernels for 15%

profile of v3, /device:TPU:0, one launch (start us, length us, event | category | flops | bytes accessed | tf_op | source)
XLA Modules:
  0.0 298.4 jit_solution(18206290632755365753)
XLA Ops:
  0.0 152.3 %shard_map.73 = (bf16[256,768]{1,0:T(8,128)(2,1)}, bf16[256,768]{1,0:T(8,128)(2,1)}, bf16[256,2048]{1,0:T(8,128)(2,1)}, bf16[256,2048]{1,0:T(8,128)(2,1)}, bf16[...) custom-call(bf16[512,768]{1,0:T(8,128)(2,1)} %key.1, bf16[256,8192]{1,0:T(8,128)(2,1)} %tokens.1), custom_call_target="tpu_custom_call" | custom-call | bytes 9961472 | tf_op jit(solution)/shard_map/pallas_call | solution.py:280
  152.3 4.1 %collective-permute-start.2 = (bf16[256,768]{1,0:T(8,128)(2,1)}, bf16[256,768]{1,0:T(8,128)(2,1)}, u32[]{:S(2)}, u32[]{:S(2)}) collective-permute-start(bf16[256,768]{1,0:T(8,128)(2,1)} %get-tuple-element.21.refs_3_.refs_1_), channel_id=1, source_target_pairs={{0,8},{1,9},{2,10},{3,11},{4,12},{5,13},{6,14},{7,15},{8,0},{9,1},... | collective-permute-start | bytes 1179656 | tf_op jit(solution)/shard_map/ppermute | solution.py:35
  156.4 1.6 collective-permute-start.3
  158.0 16.4 %collective-permute-done.2.refs_5_.refs_3_.refs_0_ = bf16[256,768]{1,0:T(8,128)(2,1)} collective-permute-done((bf16[256,768]{1,0:T(8,128)(2,1)}, bf16[256,768]{1,0:T(8,128)(2,1)}, u32[]{:S(2)}, u32[]{:S(2)}) %collective-permute-start.2) | collective-permute-done | bytes 393248 | tf_op jit(solution)/shard_map/ppermute | solution.py:35
  176.6 8.2 %collective-permute-done.4.refs_7_.refs_5_.refs_0_ = bf16[256,768]{1,0:T(8,128)(2,1)S(1)} collective-permute-done((bf16[256,768]{1,0:T(8,128)(2,1)}, bf16[256,768]{1,0:T(8,128)(2,1)S(1)}, u32[]{:S(2)}, u32[]{:S(2)}) %collective-permute-start.4) | collective-permute-done | bytes 393248 | tf_op jit(solution)/shard_map/ppermute | solution.py:35
  184.8 1.0 pad_maximum_fusion
  185.8 1.2 collective-permute-start.6
  187.9 12.7 %collective-permute-done.1.refs_2_.refs_0_.refs_6_ = bf16[256,2048]{1,0:T(8,128)(2,1)S(1)} collective-permute-done((bf16[256,2048]{1,0:T(8,128)(2,1)}, bf16[256,2048]{1,0:T(8,128)(2,1)S(1)}, u32[]{:S(2)}, u32[]{:S(2)}) %collective-permute-start.1) | collective-permute-done | bytes 1048608 | tf_op jit(solution)/shard_map/ppermute | solution.py:35
  200.6 1.0 copy-done
  201.6 1.5 collective-permute-start.8
  203.1 29.8 %shard_map.77 = (bf16[448,512]{1,0:T(8,128)(2,1)}, bf16[448,512]{1,0:T(8,128)(2,1)}) custom-call(s32[8]{0:T(128)} %refs_1_.5, bf16[16,64,512]{2,1,0:T(8,128)(2,1)} %bitcast.5), custom_call_target="tpu_custom_call" | custom-call | bytes 1835008 | tf_op jit(solution)/shard_map/pallas_call | solution.py:321
  233.0 3.4 %collective-permute-start.11 = (bf16[448,512]{1,0:T(8,128)(2,1)}, bf16[448,512]{1,0:T(8,128)(2,1)}, u32[]{:S(2)}, u32[]{:S(2)}) collective-permute-start(bf16[448,512]{1,0:T(8,128)(2,1)} %shard_map.78), channel_id=1, source_target_pairs={{0,8},{1,9},{2,10},{3,11},{4,12},{5,13},{6,14},{7,15},{8,0},{9,1},... | collective-permute-start | bytes 1376264 | tf_op jit(solution)/shard_map/ppermute | solution.py:35
  239.4 5.8 %shard_map.74 = (f32[256,768]{1,0:T(8,128)S(1)}, f32[256,768]{1,0:T(8,128)S(1)}, f32[256,768]{1,0:T(8,128)}) custom-call(bf16[256,2048]{1,0:T(8,128)(2,1)S(1)} %copy-done.2, bf16[256,2048]{1,0:T(8,128)(2,1)} %collective-permute-done.refs_1_.refs_4_, bf16[256,2048]{1,0:T(8,128)(2,1)S(1)} %copy-done.1, bf16[256,768]{1,0:T(8,128)(2,1)S(1)} %copy-done.12, ...), custom_call_target="tpu_custom_call" | custom-call | flops 2415919104 | bytes 8650752 | tf_op jit(solution)/shard_map/pallas_call | solution.py:360
  247.1 9.8 %collective-permute-done.11.refs_8_ = bf16[448,512]{1,0:T(8,128)(2,1)} collective-permute-done((bf16[448,512]{1,0:T(8,128)(2,1)}, bf16[448,512]{1,0:T(8,128)(2,1)}, u32[]{:S(2)}, u32[]{:S(2)}) %collective-permute-start.11) | collective-permute-done | bytes 458784 | tf_op jit(solution)/shard_map/ppermute | solution.py:35
  256.8 9.7 %collective-permute-done.13.refs_9_ = bf16[448,512]{1,0:T(8,128)(2,1)S(1)} collective-permute-done((bf16[448,512]{1,0:T(8,128)(2,1)}, bf16[448,512]{1,0:T(8,128)(2,1)S(1)}, u32[]{:S(2)}, u32[]{:S(2)}) %collective-permute-start.13) | collective-permute-done | bytes 458784 | tf_op jit(solution)/shard_map/ppermute | solution.py:35
  266.5 1.0 copy-done.5
  267.5 3.3 %shard_map.80.refs_8_ = f32[2,512,256]{2,1,0:T(8,128)S(1)} custom-call(s32[8]{0:T(128)S(1)} %copy-done.17, s32[8]{0:T(128)S(1)} %copy-done.16, s32[8]{0:T(128)S(1)} %copy-done.18, bf16[256,2048]{1,0:T(8,128)(2,1)S(1)} %copy-done.2, bf16[256,2048]{1,0:T(8,128)(2,1)} %collective-permute-done.refs_1_.refs_4_, ...), custom_call_target="tpu_custom_call" | custom-call | flops 805306368 | bytes 5570560 | tf_op jit(solution)/shard_map/pallas_call | solution.py:388
  270.8 5.4 %collective-permute-done.12.refs_7_ = bf16[448,512]{1,0:T(8,128)(2,1)S(1)} collective-permute-done((bf16[448,512]{1,0:T(8,128)(2,1)}, bf16[448,512]{1,0:T(8,128)(2,1)S(1)}, u32[]{:S(2)}, u32[]{:S(2)}) %collective-permute-start.12) | collective-permute-done | bytes 458784 | tf_op jit(solution)/shard_map/ppermute | solution.py:35
  276.3 2.3 shard_map.81
  278.7 3.1 %shard_map.76 = f32[256,768]{1,0:T(8,128)S(1)} custom-call(bf16[256,2048]{1,0:T(8,128)(2,1)S(1)} %collective-permute-done.8.refs_0_.refs_5_, bf16[256,768]{1,0:T(8,128)(2,1)S(1)} %copy-done.13, bf16[256,768]{1,0:T(8,128)(2,1)S(1)} %copy-done.15, bf16[256,768]{1,0:T(8,128)(2,1)} %collective-permute-done.2.refs_5_.refs_3_.refs_0_, ...), custom_call_target="tpu_custom_call" | custom-call | flops 805306368 | bytes 4980736 | tf_op jit(solution)/shard_map/pallas_call | solution.py:360
  281.9 1.4 add_convert_fusion
  283.3 1.2 collective-permute-start.10
  285.5 10.7 %collective-permute-done.15 = f32[1,128,128]{2,1,0:T(8,128)S(1)} collective-permute-done((f32[1,128,128]{2,1,0:T(8,128)S(1)}, f32[1,128,128]{2,1,0:T(8,128)S(1)}, u32[]{:S(2)}, u32[]{:S(2)}) %collective-permute-start.15) | collective-permute-done | bytes 65568 | tf_op jit(solution)/shard_map/ppermute | solution.py:35
  296.2 2.1 shard_map.82
  (62 shorter events, 9.0 us)
Async XLA Ops:
  152.3 22.1 %collective-permute-start.2 = (bf16[256,768]{1,0:T(8,128)(2,1)}, bf16[256,768]{1,0:T(8,128)(2,1)}, u32[]{:S(2)}, u32[]{:S(2)}) collective-permute-start(bf16[256,768]{1,0:T(8,128)(2,1)} %get-tuple-element.21.refs_3_.refs_1_), channel_id=1, source_target_pairs={{0,8},{1,9},{2,10},{3,11},{4,12},{5,13},{6,14},{7,15},{8,0},{9,1},... | collective-permute-start | bytes 1179656 | tf_op jit(solution)/shard_map/ppermute | solution.py:35
  156.4 20.2 %collective-permute-start.3 = (bf16[256,768]{1,0:T(8,128)(2,1)}, bf16[256,768]{1,0:T(8,128)(2,1)S(1)}, u32[]{:S(2)}, u32[]{:S(2)}) collective-permute-start(bf16[256,768]{1,0:T(8,128)(2,1)} %get-tuple-element.21.refs_3_.refs_1_), channel_id=1, source_target_pairs={{0,4},{1,5},{2,6},{3,7},{4,0},{5,1},{6,2},{7,3},{8,12},{9,13},{10,... | collective-permute-start | bytes 1179656 | tf_op jit(solution)/shard_map/ppermute | solution.py:35
  174.4 10.5 %collective-permute-start.4 = (bf16[256,768]{1,0:T(8,128)(2,1)}, bf16[256,768]{1,0:T(8,128)(2,1)S(1)}, u32[]{:S(2)}, u32[]{:S(2)}) collective-permute-start(bf16[256,768]{1,0:T(8,128)(2,1)} %collective-permute-done.2.refs_5_.refs_3_.refs_0_), channel_id=1, source_target_pairs={{0,4},{1,5},{2,6},{3,7},{4,0},{5,1},{6,2},{7,3},{8,12},{9,13},{10,... | collective-permute-start | bytes 1179656 | tf_op jit(solution)/shard_map/ppermute | solution.py:35
  175.0 25.6 %collective-permute-start.1 = (bf16[256,2048]{1,0:T(8,128)(2,1)}, bf16[256,2048]{1,0:T(8,128)(2,1)S(1)}, u32[]{:S(2)}, u32[]{:S(2)}) collective-permute-start(bf16[256,2048]{1,0:T(8,128)(2,1)} %get-tuple-element.20), channel_id=1, source_target_pairs={{0,3},{1,2},{2,1},{3,0},{4,7},{5,6},{6,5},{7,4},{8,11},{9,10},{10,... | collective-permute-start | bytes 3145736 | tf_op jit(solution)/shard_map/ppermute | solution.py:35
  175.8 60.6 %collective-permute-start = (bf16[256,2048]{1,0:T(8,128)(2,1)}, bf16[256,2048]{1,0:T(8,128)(2,1)}, u32[]{:S(2)}, u32[]{:S(2)}) collective-permute-start(bf16[256,2048]{1,0:T(8,128)(2,1)} %get-tuple-element.19), channel_id=1, source_target_pairs={{0,1},{1,0},{2,3},{3,2},{4,5},{5,4},{6,7},{7,6},{8,9},{9,8},{10,11... | collective-permute-start | bytes 3145736 | tf_op jit(solution)/shard_map/ppermute | solution.py:35
  176.6 24.0 %copy-start.7 = (bf16[256,768]{1,0:T(8,128)(2,1)}, bf16[256,768]{1,0:T(8,128)(2,1)S(1)}, u32[]{:S(2)}) copy-start(bf16[256,768]{1,0:T(8,128)(2,1)S(1)} %collective-permute-done.3.refs_6_.refs_4_) | copy-start | bytes 1179652
  184.8 51.6 %copy-start.3 = (bf16[256,768]{1,0:T(8,128)(2,1)}, bf16[256,768]{1,0:T(8,128)(2,1)S(1)}, u32[]{:S(2)}) copy-start(bf16[256,768]{1,0:T(8,128)(2,1)S(1)} %collective-permute-done.4.refs_7_.refs_5_.refs_0_) | copy-start | bytes 1179652
  185.8 50.6 %collective-permute-start.6 = (bf16[512,768]{1,0:T(8,128)(2,1)}, bf16[512,768]{1,0:T(8,128)(2,1)}, u32[]{:S(2)}, u32[]{:S(2)}) collective-permute-start(bf16[512,768]{1,0:T(8,128)(2,1)} %pad_maximum_fusion), channel_id=1, source_target_pairs={{0,16},{16,0},{1,17},{17,1},{2,18},{18,2},{3,19},{19,3},{4,20},{20... | collective-permute-start | bytes 2359304 | tf_op jit(solution)/shard_map/ppermute | solution.py:35
  187.1 49.3 %collective-permute-start.5 = (bf16[256,768]{1,0:T(8,128)(2,1)}, bf16[256,768]{1,0:T(8,128)(2,1)}, u32[]{:S(2)}, u32[]{:S(2)}) collective-permute-start(bf16[256,768]{1,0:T(8,128)(2,1)} %collective-permute-done.2.refs_5_.refs_3_.refs_0_), channel_id=1, source_target_pairs={{0,16},{16,0},{1,17},{17,1},{2,18},{18,2},{3,19},{19,3},{4,20},{20... | collective-permute-start | bytes 1179656 | tf_op jit(solution)/shard_map/ppermute | solution.py:35
  201.6 34.8 %copy-start.1 = (bf16[256,2048]{1,0:T(8,128)(2,1)S(1)}, bf16[256,2048]{1,0:T(8,128)(2,1)}, u32[]{:S(2)}) copy-start(bf16[256,2048]{1,0:T(8,128)(2,1)} %copy-done) | copy-start | bytes 3145732
  201.6 34.8 %copy-start.2 = (bf16[256,2048]{1,0:T(8,128)(2,1)S(1)}, bf16[256,2048]{1,0:T(8,128)(2,1)}, u32[]{:S(2)}) copy-start(bf16[256,2048]{1,0:T(8,128)(2,1)} %get-tuple-element.18.refs_0_.refs_3_) | copy-start | bytes 3145732
  201.6 64.9 %collective-permute-start.8 = (bf16[256,2048]{1,0:T(8,128)(2,1)}, bf16[256,2048]{1,0:T(8,128)(2,1)S(1)}, u32[]{:S(2)}, u32[]{:S(2)}) collective-permute-start(bf16[256,2048]{1,0:T(8,128)(2,1)} %shard_map.75), channel_id=1, source_target_pairs={{0,2},{1,3},{2,0},{3,1},{4,6},{5,7},{6,4},{7,5},{8,10},{9,11},{10,... | collective-permute-start | bytes 3145736 | tf_op jit(solution)/shard_map/ppermute | solution.py:35
  233.0 23.9 %collective-permute-start.11 = (bf16[448,512]{1,0:T(8,128)(2,1)}, bf16[448,512]{1,0:T(8,128)(2,1)}, u32[]{:S(2)}, u32[]{:S(2)}) collective-permute-start(bf16[448,512]{1,0:T(8,128)(2,1)} %shard_map.78), channel_id=1, source_target_pairs={{0,8},{1,9},{2,10},{3,11},{4,12},{5,13},{6,14},{7,15},{8,0},{9,1},... | collective-permute-start | bytes 1376264 | tf_op jit(solution)/shard_map/ppermute | solution.py:35
  239.4 27.0 %copy-start.16 = (s32[8]{0:T(128)S(1)}, s32[8]{0:T(128)}, u32[]{:S(2)}) copy-start(s32[8]{0:T(128)} %refs_1_.5) | copy-start | bytes 100
  239.4 27.0 %copy-start.17 = (s32[8]{0:T(128)S(1)}, s32[8]{0:T(128)}, u32[]{:S(2)}) copy-start(s32[8]{0:T(128)} %refs_0_.5) | copy-start | bytes 100
  239.4 27.1 %copy-start.18 = (s32[8]{0:T(128)S(1)}, s32[8]{0:T(128)}, u32[]{:S(2)}) copy-start(s32[8]{0:T(128)} %refs_2_.5) | copy-start | bytes 100
  247.1 34.9 %collective-permute-start.9 = (f32[256,768]{1,0:T(8,128)}, f32[256,768]{1,0:T(8,128)}, u32[]{:S(2)}, u32[]{:S(2)}) collective-permute-start(f32[256,768]{1,0:T(8,128)} %get-tuple-element.26), channel_id=1, source_target_pairs={{0,1},{1,0},{2,3},{3,2},{4,5},{5,4},{6,7},{7,6},{8,9},{9,8},{10,11... | collective-permute-start | bytes 2359304 | tf_op jit(solution)/shard_map/ppermute | solution.py:35
  247.1 19.4 %collective-permute-start.13 = (bf16[448,512]{1,0:T(8,128)(2,1)}, bf16[448,512]{1,0:T(8,128)(2,1)S(1)}, u32[]{:S(2)}, u32[]{:S(2)}) collective-permute-start(bf16[448,512]{1,0:T(8,128)(2,1)} %shard_map.79.refs_7_), channel_id=1, source_target_pairs={{0,4},{1,5},{2,6},{3,7},{4,0},{5,1},{6,2},{7,3},{8,12},{9,13},{10,... | collective-permute-start | bytes 1376264 | tf_op jit(solution)/shard_map/ppermute | solution.py:35
  256.8 19.5 %collective-permute-start.12 = (bf16[448,512]{1,0:T(8,128)(2,1)}, bf16[448,512]{1,0:T(8,128)(2,1)S(1)}, u32[]{:S(2)}, u32[]{:S(2)}) collective-permute-start(bf16[448,512]{1,0:T(8,128)(2,1)} %collective-permute-done.11.refs_8_), channel_id=1, source_target_pairs={{0,4},{1,5},{2,6},{3,7},{4,0},{5,1},{6,2},{7,3},{8,12},{9,13},{10,... | collective-permute-start | bytes 1376264 | tf_op jit(solution)/shard_map/ppermute | solution.py:35
  256.8 39.4 %collective-permute-start.7 = (f32[256,768]{1,0:T(8,128)}, f32[256,768]{1,0:T(8,128)S(1)}, u32[]{:S(2)}, u32[]{:S(2)}) collective-permute-start(f32[256,768]{1,0:T(8,128)} %copy-done.19), channel_id=1, source_target_pairs={{0,1},{1,0},{2,3},{3,2},{4,5},{5,4},{6,7},{7,6},{8,9},{9,8},{10,11... | collective-permute-start | bytes 2359304 | tf_op jit(solution)/shard_map/ppermute | solution.py:35
  278.6 5.9 %collective-permute-start.14 = (f32[2,128,128]{2,1,0:T(8,128)S(1)}, f32[2,128,128]{2,1,0:T(8,128)S(1)}, u32[]{:S(2)}, u32[]{:S(2)}) collective-permute-start(f32[2,128,128]{2,1,0:T(8,128)S(1)} %get-tuple-element.30), channel_id=1, source_target_pairs={{0,1},{1,0},{2,3},{3,2},{4,5},{5,4},{6,7},{7,6},{8,9},{9,8},{10,11... | collective-permute-start | bytes 393224 | tf_op jit(solution)/shard_map/ppermute | solution.py:35
  281.9 14.3 %copy-start.6 = (bf16[16,64,768]{2,1,0:T(8,128)(2,1)S(1)}, bf16[16,64,768]{2,1,0:T(8,128)(2,1)}, u32[]{:S(2)}) copy-start(bf16[16,64,768]{2,1,0:T(8,128)(2,1)} %refs_8_.1) | copy-start | bytes 4718596
  283.3 12.9 %collective-permute-start.10 = (bf16[256,768]{1,0:T(8,128)(2,1)S(1)}, bf16[256,768]{1,0:T(8,128)(2,1)S(1)}, u32[]{:S(2)}, u32[]{:S(2)}) collective-permute-start(bf16[256,768]{1,0:T(8,128)(2,1)S(1)} %add_convert_fusion), channel_id=1, source_target_pairs={{0,2},{1,3},{2,0},{3,1},{4,6},{5,7},{6,4},{7,5},{8,10},{9,11},{10,... | collective-permute-start | bytes 1179656 | tf_op jit(solution)/shard_map/ppermute | solution.py:35
  284.6 11.7 %collective-permute-start.15 = (f32[1,128,128]{2,1,0:T(8,128)S(1)}, f32[1,128,128]{2,1,0:T(8,128)S(1)}, u32[]{:S(2)}, u32[]{:S(2)}) collective-permute-start(f32[1,128,128]{2,1,0:T(8,128)S(1)} %get-tuple-element.31), channel_id=1, source_target_pairs={{0,2},{1,3},{2,0},{3,1},{4,6},{5,7},{6,4},{7,5},{8,10},{9,11},{10,... | collective-permute-start | bytes 196616 | tf_op jit(solution)/shard_map/ppermute | solution.py:35
  (12 other events, 52.9 us)

commit v4 on v3

--- a/solution.py
+++ b/solution.py
@@ -12,21 +12,21 @@
 MOST = 16
 LAYER_CHIPS = 4
 VMEM_BYTES = 28 * 1024 * 1024
-FIRST_VMEM_BYTES = 56 * 1024 * 1024
+CORE_FLOPS_PER_US = 1_153_500_000
 
 HBM = pl.BlockSpec(memory_space=pl.ANY)
 VMEM = pl.BlockSpec(memory_space=pltpu.VMEM)
 SMEM = pl.BlockSpec(memory_space=pltpu.SMEM)
 
 
-def call(kernel, outs, out_specs, in_specs, scratch, flops, moved, vmem=VMEM_BYTES):
+def call(kernel, outs, out_specs, in_specs, scratch, flops, moved):
     return pl.pallas_call(
         kernel,
         out_shape=outs,
         in_specs=in_specs,
         out_specs=out_specs,
         scratch_shapes=scratch,
-        compiler_params=pltpu.CompilerParams(vmem_limit_bytes=vmem),
+        compiler_params=pltpu.CompilerParams(vmem_limit_bytes=VMEM_BYTES),
         cost_estimate=pl.CostEstimate(flops=flops, bytes_accessed=moved, transcendentals=0),
     )
 
@@ -48,7 +48,8 @@
 
 def first_kernel(group, layers, splits, part, key, tokens, *refs):
     keys, refs = refs[:splits], refs[splits:]
-    outs, sems = refs[:group], refs[group]
+    outs, sems = refs[:-1], refs[-1]
+    rows = tokens.shape[0]
     depth = splits * part
     me = lax.axis_index("batch")
     layer, spot = me // group, me % group
@@ -59,12 +60,12 @@
             for h in range(splits):
                 start = first + part_start(h, part) if splits > 1 else first
                 start = pl.multiple_of(start, part)
-                pairs.append(
-                    (
-                        tokens.at[:, pl.ds(start, part)],
-                        outs[s].at[:, pl.ds(t * depth + h * part, part)],
-                    )
-                )
+                to = pl.ds(t * depth + h * part, part)
+                if s < 2:
+                    there = outs[s].at[:, to]
+                else:
+                    there = outs[2].at[pl.ds((s - 2) * rows, rows), to]
+                pairs.append((tokens.at[:, pl.ds(start, part)], there))
     for copy in run_copies(pairs, sems):
         copy.wait()
 
@@ -73,13 +74,16 @@
     pass
 
 
-def gate(value, *ready):
+def gate(value, *ready, us=0):
     return pl.pallas_call(
         gate_kernel,
         out_shape=jax.ShapeDtypeStruct(value.shape, value.dtype),
         in_specs=[HBM] * (1 + len(ready)),
         out_specs=HBM,
         input_output_aliases={0: 0},
+        cost_estimate=pl.CostEstimate(
+            flops=us * CORE_FLOPS_PER_US, bytes_accessed=0, transcendentals=0
+        ),
     )(value, *ready)
 
 
@@ -107,18 +111,34 @@
     toks, arrays = refs[:tokens_of], refs[tokens_of : tokens_of + count]
     outs = refs[tokens_of + count : 2 * tokens_of + count]
     held, weights, sems = refs[2 * tokens_of + count :]
-    pairs = [(tok, held.at[pl.ds(i * rows, rows), :]) for i, tok in enumerate(toks)]
-    for a, row, deep, to in moves:
-        pairs.append((arrays[a].at[pl.ds(row, deep), :], weights.at[pl.ds(to, deep), :]))
-    for copy in run_copies(pairs, sems):
-        copy.wait()
-    width = weights.shape[1]
+    deep, width = weights.shape
+    halves = [(0, deep // 2), (deep // 2, deep)]
+    waits = []
+    for begin, end in halves:
+        pairs = [
+            (tok.at[:, pl.ds(begin, end - begin)], held.at[pl.ds(i * rows, rows), pl.ds(begin, end - begin)])
+            for i, tok in enumerate(toks)
+        ]
+        for a, row, rows_of, to in moves:
+            if begin <= to < end:
+                pairs.append((arrays[a].at[pl.ds(row, rows_of), :], weights.at[pl.ds(to, rows_of), :]))
+        first = sum(len(w) for w in waits)
+        waits.append(run_copies(pairs, sems.at[pl.ds(first, len(pairs))]))
     step = 2 * LANES if width % (2 * LANES) == 0 else width
-    for column in range(0, width, step):
-        here = pl.ds(column, step)
-        total = jnp.dot(held[...], weights[:, here], preferred_element_type=jnp.float32)
-        for i in range(tokens_of):
-            outs[i][:, here] = total[i * rows : (i + 1) * rows]
+    for copies, (begin, end) in zip(waits, halves):
+        for copy in copies:
+            copy.wait()
+        for column in range(0, width, step):
+            here = pl.ds(column, step)
+            total = jnp.dot(
+                held[:, begin:end], weights[begin:end, here], preferred_element_type=jnp.float32
+            )
+            for i in range(tokens_of):
+                mine = total[i * rows : (i + 1) * rows]
+                if begin == 0:
+                    outs[i][:, here] = mine
+                else:
+                    outs[i][:, here] += mine
 
 
 def table(lists, block):
@@ -280,17 +300,20 @@
     first = call(
         functools.partial(first_kernel, group, layers, splits, part),
         [jax.ShapeDtypeStruct((part, out_width), bf16)] * splits
-        + [jax.ShapeDtypeStruct((rows, held_width), bf16)] * group,
-        [HBM] * (splits + group),
+        + [jax.ShapeDtypeStruct((rows, held_width), bf16)] * 2
+        + [jax.ShapeDtypeStruct(((group - 2) * rows, held_width), bf16)] * (group > 2),
+        [HBM] * (splits + 2 + (group > 2)),
         [HBM] * 2,
         [pltpu.SemaphoreType.DMA((splits + group * layers * splits,))],
         0,
         4 * (rows * width + depth * out_width),
-        FIRST_VMEM_BYTES,
     )(key_matrix, tokens)
-    key_parts, pieces = first[:splits], list(first[splits:])
-
-    def over_layers(across, near):
+    key_parts = first[:splits]
+    if group > 2:
+        far = swap(first[splits + 2], "batch", 2)
+    pieces = [first[splits], swap(first[splits + 1], "batch", 1)]
+
+    def over_layers(across, near, after):
         bundles = []
         bit = layers // 2
         while bit:
@@ -301,16 +324,25 @@
                 rest = rest[0] if len(rest) == 1 else jnp.concatenate(rest, 0)
                 order = [t ^ bit for ts, _ in bundles for t in ts]
                 moved.append((order, swap(rest, "batch", bit * group)))
+            else:
+                moved = [([bit], after(moved[0][1]))]
             bundles = bundles + moved
             bit //= 2
         return bundles
 
-    key_bundles = over_layers(key_parts[0], lambda _: key_parts[0])
-
-    for s in reversed(range(1, group)):
-        if 1 < s < group - 1:
-            pieces[s] = gate(pieces[s], pieces[s + 1])
-        pieces[s] = swap(pieces[s], "batch", s)
+    key_bundles = over_layers(
+        key_parts[0], lambda _: key_parts[0], lambda v: gate(v, pieces[1], us=2)
+    )
+    key_swaps, last_keys = [], key_bundles[-1][1]
+    for h in range(1, splits):
+        for taken in (key_bundles[:1], key_bundles[1:]):
+            if taken:
+                values = [v for _, v in taken]
+                values = values[0] if len(values) == 1 else jnp.concatenate(values, 0)
+                if key_swaps:
+                    values = gate(values, key_swaps[-1][2], us=2)
+                    last_keys = values
+                key_swaps.append((h, [t for ts, _ in taken for t in ts], swap(values, "rep", h)))
 
     down = jnp.transpose(adapter_down_factors, (1, 2, 0))
     requests = request_adapter_index.shape[0]
@@ -326,14 +358,16 @@
             [pltpu.SemaphoreType.DMA((2 * slots * splits,))],
             0,
             8 * slots * rank * depth,
-            FIRST_VMEM_BYTES,
         )(request_adapter_index, down)
     else:
         down = down.reshape(slots * rank, depth)
         across = down
     across = gate(across, key_bundles[0][1])
-    down = gate(down, key_bundles[-1][1])
-    down_bundles = over_layers(across, lambda _: down)
+    down = gate(down, last_keys)
+    down_bundles = over_layers(across, lambda _: down, lambda v: gate(v, us=10))
+    if group > 2:
+        far = gate(far, *[v for _, v in down_bundles[:2]], *[v for _, _, v in key_swaps], us=2)
+        pieces += [far[:rows], swap(far[rows:], "batch", 1)]
 
     arrays, moves = [], []
     for ts, value in [([0], None)] + key_bundles:
@@ -345,18 +379,12 @@
             moves.append((len(arrays) - (splits if value is None else 1), i * part, part, t * depth))
     for h in range(1, splits):
         moves.append((h, 0, part, h * part))
-        for taken in (key_bundles[:1], key_bundles[1:]):
-            if taken:
-                values = [v for _, v in taken]
-                values = values[0] if len(values) == 1 else jnp.concatenate(values, 0)
-                arrays.append(swap(values, "rep", h))
-                for i, t in enumerate([t for ts, _ in taken for t in ts]):
-                    moves.append((len(arrays) - 1, i * part, part, t * depth + h * part))
+    for h, ts, value in key_swaps:
+        arrays.append(value)
+        for i, t in enumerate(ts):
+            moves.append((len(arrays) - 1, i * part, part, t * depth + h * part))
     partial_sums = [None] * group
-    late = [2] if group > 2 else []
-    for which in ([s for s in range(group) if s not in late], late):
-        if not which:
-            continue
+    for which in [[s, s + 1] for s in reversed(range(0, group, 2))]:
         results = call(
             functools.partial(base_kernel, rows, len(which), tuple(moves), len(arrays)),
             [jax.ShapeDtypeStruct((rows, out_width), f32)] * len(which),
@@ -365,7 +393,7 @@
             [
                 pltpu.VMEM((len(which) * rows, held_width), bf16),
                 pltpu.VMEM((held_width, out_width), bf16),
-                pltpu.SemaphoreType.DMA((len(which) + len(moves),)),
+                pltpu.SemaphoreType.DMA((2 * len(which) + len(moves),)),
             ],
             2 * len(which) * rows * held_width * out_width,
             2 * held_width * (len(which) * rows + out_width) + 4 * len(which) * rows * out_width,
@@ -400,6 +428,7 @@
             2 * len(at) * depth * (group * rows + slots * rank) + 4 * pairs * tall * wide,
         )(*lists, *pieces, *taken, *([before] if before is not None else []))
 
+    down_bundles[-1] = (down_bundles[-1][0], gate(down_bundles[-1][1], us=30))
     early = low_call([([0], down)] + down_bundles[:-1], None, False)
     even, odd = low_call(down_bundles[-1:], early, True)
     got = swap(odd, "batch", 1)

time: 299 us -> 109 us (0.36)
  Pallas kernels: 199 us -> 20 us
  waiting for transfers between devices: 72.9 us -> 50.4 us
  local copies, waits for them, and re-layouts: 6.87 us -> 17.3 us
    pallas_call x1, Pallas kernels: 152 us -> 1.85 us  [shards(): call(functools.partial(first_kernel, group, layers, splits, part), [jax.S...]
    pallas_call x1, Pallas kernels: 29.8 us -> 1.06 us  [shards(): call(functools.partial(chosen_kernel, slots, rank, splits, part, group, l...]
    ppermute x16, waiting for transfers between devices: 72.9 us -> 50.4 us  [swap(): lax.ppermute(value, axis, [(i, i ^ bit) for i in range(lax.axis_size(axis...]
    unnamed x40 -> x58, local copies, waits for them, and re-layouts: 6.85 us -> 15.4 us
  transfers between devices with their start and end apart: 16 -> 16, of which waited for: 7 -> 7; matrix products, arithmetic and copies ran while one was open for 1% -> 2% of each run, Pallas kernels for 15% -> 14%
where the time goes in v4:
time: 109 us; the launch traced here: 108 us
  waiting for transfers between devices  50.4 us (46%)
  Pallas kernels  20 us (18%)
  starting transfers between devices  17.9 us (16%)
  local copies, waits for them, and re-layouts  17.3 us (16%)
  other arithmetic  2.49 us (2%)
    ppermute x16, waiting for transfers between devices, swap(): lax.ppermute(value, axis, [(i, i ^ bit) for i in range(lax.axis_size(axis...  50.4 us
    ppermute x16, starting transfers between devices, swap(): lax.ppermute(value, axis, [(i, i ^ bit) for i in range(lax.axis_size(axis...  17.9 us
    unnamed x58, local copies, waits for them, and re-layouts  15.4 us
    pallas_call x2, Pallas kernels, shards(): call(functools.partial(base_kernel, rows, len(which), tuple(moves), len(a...  9.25 us
    pallas_call x2, Pallas kernels, low_call(): call(functools.partial(low_kernel, group, layers, rows, depth, rank, tupl...  5.13 us
    pallas_call x1, Pallas kernels, shards(): call(functools.partial(final_kernel, rows, rank, len(bases), len(lows)),...  2.72 us
  transfers between devices with their start and end apart: 16, of which 7 were waited for; matrix products, arithmetic and copies ran while one was open for 2% of the time, Pallas kernels for 14%

profile of v4, /device:TPU:0, one launch (start us, length us, event | category | flops | bytes accessed | tf_op | source)
XLA Modules:
  0.0 108.4 jit_solution(4700365917634557486)
XLA Ops:
  0.0 2.2 %copy-done = bf16[256,8192]{1,0:T(8,128)(2,1)S(1)} copy-done((bf16[256,8192]{1,0:T(8,128)(2,1)S(1)}, bf16[256,8192]{1,0:T(8,128)(2,1)}, u32[]{:S(2)}) %copy-start) | copy-done | bytes 4194328
  2.2 1.1 %copy-done.9 = bf16[512,768]{1,0:T(8,128)(2,1)S(1)} copy-done((bf16[512,768]{1,0:T(8,128)(2,1)S(1)}, bf16[512,768]{1,0:T(8,128)(2,1)}, u32[]{:S(2)}) %copy-start.9) | copy-done | bytes 786456
  3.3 1.9 %shard_map.73 = (bf16[256,768]{1,0:T(8,128)(2,1)}, bf16[256,768]{1,0:T(8,128)(2,1)S(1)}, bf16[256,2048]{1,0:T(8,128)(2,1)S(1)}, bf16[256,2048]{1,0:T(8,128)(2,1)S(1)}, bf16[512,2048]{1,0:T(8,128)(2,1)}) custom-call(bf16[512,768]{1,0:T(8,128)(2,1)S(1)} %copy-done.9, bf16[256,8192]{1,0:T(8,128)(2,1)S(1)} %copy-done), custom_call_target="tpu_custom_call" | custom-call | bytes 9961472 | tf_op jit(solution)/shard_map/pallas_call | solution.py:300
  6.4 3.6 %collective-permute-start.1 = (bf16[256,768]{1,0:T(8,128)(2,1)}, bf16[256,768]{1,0:T(8,128)(2,1)}, u32[]{:S(2)}, u32[]{:S(2)}) collective-permute-start(bf16[256,768]{1,0:T(8,128)(2,1)} %get-tuple-element.20.refs_2_), channel_id=1, source_target_pairs={{0,8},{1,9},{2,10},{3,11},{4,12},{5,13},{6,14},{7,15},{8,0},{9,1},... | collective-permute-start | bytes 1179656 | tf_op jit(solution)/shard_map/ppermute | solution.py:35
  10.0 1.5 %collective-permute-start.7 = (bf16[512,2048]{1,0:T(8,128)(2,1)}, bf16[512,2048]{1,0:T(8,128)(2,1)}, u32[]{:S(2)}, u32[]{:S(2)}) collective-permute-start(bf16[512,2048]{1,0:T(8,128)(2,1)} %get-tuple-element.24), channel_id=1, source_target_pairs={{0,2},{1,3},{2,0},{3,1},{4,6},{5,7},{6,4},{7,5},{8,10},{9,11},{10,... | collective-permute-start | bytes 6291464 | tf_op jit(solution)/shard_map/ppermute | solution.py:35
  11.5 1.6 %collective-permute-start.2 = (bf16[256,768]{1,0:T(8,128)(2,1)}, bf16[256,768]{1,0:T(8,128)(2,1)S(1)}, u32[]{:S(2)}, u32[]{:S(2)}) collective-permute-start(bf16[256,768]{1,0:T(8,128)(2,1)} %get-tuple-element.20.refs_2_), channel_id=1, source_target_pairs={{0,4},{1,5},{2,6},{3,7},{4,0},{5,1},{6,2},{7,3},{8,12},{9,13},{10,... | collective-permute-start | bytes 1179656 | tf_op jit(solution)/shard_map/ppermute | solution.py:35
  13.1 15.5 %collective-permute-done.1.value = bf16[256,768]{1,0:T(8,128)(2,1)} collective-permute-done((bf16[256,768]{1,0:T(8,128)(2,1)}, bf16[256,768]{1,0:T(8,128)(2,1)}, u32[]{:S(2)}, u32[]{:S(2)}) %collective-permute-start.1) | collective-permute-done | bytes 393248 | tf_op jit(solution)/shard_map/ppermute | solution.py:35
  30.2 1.5 %collective-permute-start.4 = (bf16[256,768]{1,0:T(8,128)(2,1)}, bf16[256,768]{1,0:T(8,128)(2,1)}, u32[]{:S(2)}, u32[]{:S(2)}) collective-permute-start(bf16[256,768]{1,0:T(8,128)(2,1)} %shard_map.74.refs_4_.refs_0_), channel_id=1, source_target_pairs={{0,16},{16,0},{1,17},{17,1},{2,18},{18,2},{3,19},{19,3},{4,20},{20... | collective-permute-start | bytes 1179656 | tf_op jit(solution)/shard_map/ppermute | solution.py:35
  34.4 3.4 %collective-permute-start.8 = (bf16[448,512]{1,0:T(8,128)(2,1)}, bf16[448,512]{1,0:T(8,128)(2,1)S(1)}, u32[]{:S(2)}, u32[]{:S(2)}) collective-permute-start(bf16[448,512]{1,0:T(8,128)(2,1)} %shard_map.78), channel_id=1, source_target_pairs={{0,8},{1,9},{2,10},{3,11},{4,12},{5,13},{6,14},{7,15},{8,0},{9,1},... | collective-permute-start | bytes 1376264 | tf_op jit(solution)/shard_map/ppermute | solution.py:35
  37.8 7.3 %collective-permute-done.3.refs_6_ = bf16[256,768]{1,0:T(8,128)(2,1)S(1)} collective-permute-done((bf16[256,768]{1,0:T(8,128)(2,1)}, bf16[256,768]{1,0:T(8,128)(2,1)S(1)}, u32[]{:S(2)}, u32[]{:S(2)}) %collective-permute-start.3) | collective-permute-done | bytes 393248 | tf_op jit(solution)/shard_map/ppermute | solution.py:35
  45.1 1.1 pad_maximum_fusion.value
  46.2 2.3 %collective-permute-start.5 = (bf16[512,768]{1,0:T(8,128)(2,1)}, bf16[512,768]{1,0:T(8,128)(2,1)S(1)}, u32[]{:S(2)}, u32[]{:S(2)}) collective-permute-start(bf16[512,768]{1,0:T(8,128)(2,1)} %shard_map.75.refs_0_), channel_id=1, source_target_pairs={{0,16},{16,0},{1,17},{17,1},{2,18},{18,2},{3,19},{19,3},{4,20},{20... | collective-permute-start | bytes 2359304 | tf_op jit(solution)/shard_map/ppermute | solution.py:35
  48.5 9.7 %collective-permute-done.8.value = bf16[448,512]{1,0:T(8,128)(2,1)S(1)} collective-permute-done((bf16[448,512]{1,0:T(8,128)(2,1)}, bf16[448,512]{1,0:T(8,128)(2,1)S(1)}, u32[]{:S(2)}, u32[]{:S(2)}) %collective-permute-start.8) | collective-permute-done | bytes 458784 | tf_op jit(solution)/shard_map/ppermute | solution.py:35
  58.9 6.3 %collective-permute-done.9.refs_1_.refs_9_ = bf16[448,512]{1,0:T(8,128)(2,1)S(1)} collective-permute-done((bf16[448,512]{1,0:T(8,128)(2,1)}, bf16[448,512]{1,0:T(8,128)(2,1)S(1)}, u32[]{:S(2)}, u32[]{:S(2)}) %collective-permute-start.9) | collective-permute-done | bytes 458784 | tf_op jit(solution)/shard_map/ppermute | solution.py:35
  66.9 1.9 %fusion = (bf16[256,2048]{1,0:T(8,128)(2,1)S(1)}, bf16[256,2048]{1,0:T(8,128)(2,1)S(1)}) fusion(bf16[512,2048]{1,0:T(8,128)(2,1)} %shard_map.81), kind=kLoop, calls=%fused_computation.3 | loop fusion | bytes 4194304 | tf_op jit(solution)/shard_map/slice | solution.py:370
  69.3 4.5 %shard_map.76 = (f32[256,768]{1,0:T(8,128)S(1)}, f32[256,768]{1,0:T(8,128)}) custom-call(bf16[256,2048]{1,0:T(8,128)(2,1)S(1)} %get-tuple-element.18.refs_0_.refs_3_, bf16[256,2048]{1,0:T(8,128)(2,1)S(1)} %copy-done.2, bf16[256,768]{1,0:T(8,128)(2,1)} %get-tuple-element.20.refs_2_, bf16[256,768]{1,0:T(8,128)(2,1)S(1)} %copy-done.28, ...), custom_call_target="tpu_custom_call" | custom-call | flops 1610612736 | bytes 6815744 | tf_op jit(solution)/shard_map/pallas_call | solution.py:388
  74.8 4.8 %shard_map.82 = (f32[256,768]{1,0:T(8,128)S(1)}, f32[256,768]{1,0:T(8,128)}) custom-call(bf16[256,2048]{1,0:T(8,128)(2,1)S(1)} %get-tuple-element.32.refs_0_.refs_5_, bf16[256,2048]{1,0:T(8,128)(2,1)S(1)} %collective-permute-done.10.refs_1_.refs_6_, bf16[256,768]{1,0:T(8,128)(2,1)} %get-tuple-element.20.refs_2_, bf16[256,768]{1,0:T(8,128)(2,1)S(1)} %copy-done.28, ...), custom_call_target="tpu_custom_call" | custom-call | flops 1610612736 | bytes 6815744 | tf_op jit(solution)/shard_map/pallas_call | solution.py:388
  81.9 1.2 %copy-done.4 = bf16[256,2048]{1,0:T(8,128)(2,1)S(1)} copy-done((bf16[256,2048]{1,0:T(8,128)(2,1)S(1)}, bf16[256,2048]{1,0:T(8,128)(2,1)}, u32[]{:S(2)}) %copy-start.4) | copy-done | bytes 1048600
  86.2 3.0 %shard_map.84.refs_8_ = f32[2,512,256]{2,1,0:T(8,128)S(1)} custom-call(s32[8]{0:T(128)S(1)} %copy-done.23, s32[8]{0:T(128)S(1)} %copy-done.22, s32[8]{0:T(128)S(1)} %copy-done.24, bf16[256,2048]{1,0:T(8,128)(2,1)S(1)} %get-tuple-element.18.refs_0_.refs_3_, bf16[256,2048]{1,0:T(8,128)(2,1)S(1)} %copy-done.2, ...), custom_call_target="tpu_custom_call" | custom-call | flops 805306368 | bytes 5570560 | tf_op jit(solution)/shard_map/pallas_call | solution.py:416
  89.2 2.1 %shard_map.85 = (f32[2,128,128]{2,1,0:T(8,128)S(1)}, f32[2,128,128]{2,1,0:T(8,128)S(1)}) custom-call(s32[8]{0:T(128)S(1)} %copy-done.23, s32[8]{0:T(128)S(1)} %copy-done.22, s32[8]{0:T(128)S(1)} %copy-done.24, bf16[256,2048]{1,0:T(8,128)(2,1)S(1)} %get-tuple-element.18.refs_0_.refs_3_, bf16[256,2048]{1,0:T(8,128)(2,1)S(1)} %copy-done.2, ...), custom_call_target="tpu_custom_call" | custom-call | flops 268435456 | bytes 2555904 | tf_op jit(solution)/shard_map/pallas_call | solution.py:416
  91.4 1.4 %add_convert_fusion = bf16[256,768]{1,0:T(8,128)(2,1)S(1)} fusion(f32[256,768]{1,0:T(8,128)S(1)} %copy-done.13, f32[256,768]{1,0:T(8,128)} %collective-permute-done.11), kind=kLoop, calls=%fused_computation.1 | loop fusion | flops 393216 | bytes 1966080 | tf_op jit(solution)/shard_map/convert_element_type | solution.py:271
  92.9 1.6 %collective-permute-start.12 = (bf16[256,768]{1,0:T(8,128)(2,1)S(1)}, bf16[256,768]{1,0:T(8,128)(2,1)S(1)}, u32[]{:S(2)}, u32[]{:S(2)}) collective-permute-start(bf16[256,768]{1,0:T(8,128)(2,1)S(1)} %add_convert_fusion), channel_id=1, source_target_pairs={{0,2},{1,3},{2,0},{3,1},{4,6},{5,7},{6,4},{7,5},{8,10},{9,11},{10,... | collective-permute-start | bytes 1179656 | tf_op jit(solution)/shard_map/ppermute | solution.py:35
  95.1 10.6 %collective-permute-done.15 = f32[1,128,128]{2,1,0:T(8,128)S(1)} collective-permute-done((f32[1,128,128]{2,1,0:T(8,128)S(1)}, f32[1,128,128]{2,1,0:T(8,128)S(1)}, u32[]{:S(2)}, u32[]{:S(2)}) %collective-permute-start.15) | collective-permute-done | bytes 65568 | tf_op jit(solution)/shard_map/ppermute | solution.py:35
  105.7 2.7 %shard_map.86 = bf16[256,768]{1,0:T(8,128)(2,1)} custom-call(s32[8]{0:T(128)S(1)} %copy-done.23, s32[8]{0:T(128)S(1)} %copy-done.22, s32[8]{0:T(128)S(1)} %copy-done.24, f32[256,768]{1,0:T(8,128)S(1)} %copy-done.11, f32[256,768]{1,0:T(8,128)} %collective-permute-done.6.refs_4_, bf16[256,768]{1,0:T(8,128)(2,1)S(1)} %collective-permute-done.12.refs_5_, ...), custom_call_target="tpu_custom_call" | custom-call | flops 25165824 | bytes 1572864 | tf_op jit(solution)/shard_map/pallas_call | solution.py:437
  (85 shorter events, 15.5 us)
Async XLA Ops:
  5.9 22.7 %collective-permute-start = (bf16[256,2048]{1,0:T(8,128)(2,1)S(1)}, bf16[256,2048]{1,0:T(8,128)(2,1)S(1)}, u32[]{:S(2)}, u32[]{:S(2)}) collective-permute-start(bf16[256,2048]{1,0:T(8,128)(2,1)S(1)} %get-tuple-element.19), channel_id=1, source_target_pairs={{0,1},{1,0},{2,3},{3,2},{4,5},{5,4},{6,7},{7,6},{8,9},{9,8},{10,11... | collective-permute-start | bytes 3145736 | tf_op jit(solution)/shard_map/ppermute | solution.py:35
  6.4 22.2 %collective-permute-start.1 = (bf16[256,768]{1,0:T(8,128)(2,1)}, bf16[256,768]{1,0:T(8,128)(2,1)}, u32[]{:S(2)}, u32[]{:S(2)}) collective-permute-start(bf16[256,768]{1,0:T(8,128)(2,1)} %get-tuple-element.20.refs_2_), channel_id=1, source_target_pairs={{0,8},{1,9},{2,10},{3,11},{4,12},{5,13},{6,14},{7,15},{8,0},{9,1},... | collective-permute-start | bytes 1179656 | tf_op jit(solution)/shard_map/ppermute | solution.py:35
  10.0 21.8 %copy-start.8 = (bf16[512,16,64]{0,2,1:T(8,128)(2,1)S(1)}, bf16[512,16,64]{0,2,1:T(8,128)(2,1)}, u32[]{:S(2)}) copy-start(bf16[512,16,64]{0,2,1:T(8,128)(2,1)} %param.9) | copy-start | bytes 3145732
  10.0 21.8 %copy-start.22 = (s32[8]{0:T(128)S(1)}, s32[8]{0:T(128)}, u32[]{:S(2)}) copy-start(s32[8]{0:T(128)} %refs_1_.5) | copy-start | bytes 100
  10.0 55.2 %collective-permute-start.7 = (bf16[512,2048]{1,0:T(8,128)(2,1)}, bf16[512,2048]{1,0:T(8,128)(2,1)}, u32[]{:S(2)}, u32[]{:S(2)}) collective-permute-start(bf16[512,2048]{1,0:T(8,128)(2,1)} %get-tuple-element.24), channel_id=1, source_target_pairs={{0,2},{1,3},{2,0},{3,1},{4,6},{5,7},{6,4},{7,5},{8,10},{9,11},{10,... | collective-permute-start | bytes 6291464 | tf_op jit(solution)/shard_map/ppermute | solution.py:35
  11.5 26.3 %collective-permute-start.2 = (bf16[256,768]{1,0:T(8,128)(2,1)}, bf16[256,768]{1,0:T(8,128)(2,1)S(1)}, u32[]{:S(2)}, u32[]{:S(2)}) collective-permute-start(bf16[256,768]{1,0:T(8,128)(2,1)} %get-tuple-element.20.refs_2_), channel_id=1, source_target_pairs={{0,4},{1,5},{2,6},{3,7},{4,0},{5,1},{6,2},{7,3},{8,12},{9,13},{10,... | collective-permute-start | bytes 1179656 | tf_op jit(solution)/shard_map/ppermute | solution.py:35
  29.6 15.5 %collective-permute-start.3 = (bf16[256,768]{1,0:T(8,128)(2,1)}, bf16[256,768]{1,0:T(8,128)(2,1)S(1)}, u32[]{:S(2)}, u32[]{:S(2)}) collective-permute-start(bf16[256,768]{1,0:T(8,128)(2,1)} %shard_map.74.refs_4_.refs_0_), channel_id=1, source_target_pairs={{0,4},{1,5},{2,6},{3,7},{4,0},{5,1},{6,2},{7,3},{8,12},{9,13},{10,... | collective-permute-start | bytes 1179656 | tf_op jit(solution)/shard_map/ppermute | solution.py:35
  30.2 15.9 %collective-permute-start.4 = (bf16[256,768]{1,0:T(8,128)(2,1)}, bf16[256,768]{1,0:T(8,128)(2,1)}, u32[]{:S(2)}, u32[]{:S(2)}) collective-permute-start(bf16[256,768]{1,0:T(8,128)(2,1)} %shard_map.74.refs_4_.refs_0_), channel_id=1, source_target_pairs={{0,16},{16,0},{1,17},{17,1},{2,18},{18,2},{3,19},{19,3},{4,20},{20... | collective-permute-start | bytes 1179656 | tf_op jit(solution)/shard_map/ppermute | solution.py:35
  34.4 23.8 %collective-permute-start.8 = (bf16[448,512]{1,0:T(8,128)(2,1)}, bf16[448,512]{1,0:T(8,128)(2,1)S(1)}, u32[]{:S(2)}, u32[]{:S(2)}) collective-permute-start(bf16[448,512]{1,0:T(8,128)(2,1)} %shard_map.78), channel_id=1, source_target_pairs={{0,8},{1,9},{2,10},{3,11},{4,12},{5,13},{6,14},{7,15},{8,0},{9,1},... | collective-permute-start | bytes 1376264 | tf_op jit(solution)/shard_map/ppermute | solution.py:35
  46.2 19.1 %collective-permute-start.5 = (bf16[512,768]{1,0:T(8,128)(2,1)}, bf16[512,768]{1,0:T(8,128)(2,1)S(1)}, u32[]{:S(2)}, u32[]{:S(2)}) collective-permute-start(bf16[512,768]{1,0:T(8,128)(2,1)} %shard_map.75.refs_0_), channel_id=1, source_target_pairs={{0,16},{16,0},{1,17},{17,1},{2,18},{18,2},{3,19},{19,3},{4,20},{20... | collective-permute-start | bytes 2359304 | tf_op jit(solution)/shard_map/ppermute | solution.py:35
  48.5 16.7 %collective-permute-start.9 = (bf16[448,512]{1,0:T(8,128)(2,1)}, bf16[448,512]{1,0:T(8,128)(2,1)S(1)}, u32[]{:S(2)}, u32[]{:S(2)}) collective-permute-start(bf16[448,512]{1,0:T(8,128)(2,1)} %shard_map.80.refs_7_), channel_id=1, source_target_pairs={{0,4},{1,5},{2,6},{3,7},{4,0},{5,1},{6,2},{7,3},{8,12},{9,13},{10,... | collective-permute-start | bytes 1376264 | tf_op jit(solution)/shard_map/ppermute | solution.py:35
  66.8 2.3 %copy-start.26 = (bf16[512,768]{1,0:T(8,128)(2,1)S(1)}, bf16[512,768]{1,0:T(8,128)(2,1)}, u32[]{:S(2)}) copy-start(bf16[512,768]{1,0:T(8,128)(2,1)} %copy-done.25) | copy-start | bytes 2359300
  66.9 2.4 %copy-start.28 = (bf16[256,768]{1,0:T(8,128)(2,1)S(1)}, bf16[256,768]{1,0:T(8,128)(2,1)}, u32[]{:S(2)}) copy-start(bf16[256,768]{1,0:T(8,128)(2,1)} %copy-done.27) | copy-start | bytes 1179652
  68.7 6.0 %collective-permute-start.10 = (bf16[256,2048]{1,0:T(8,128)(2,1)S(1)}, bf16[256,2048]{1,0:T(8,128)(2,1)S(1)}, u32[]{:S(2)}, u32[]{:S(2)}) collective-permute-start(bf16[256,2048]{1,0:T(8,128)(2,1)S(1)} %get-tuple-element.31), channel_id=1, source_target_pairs={{0,1},{1,0},{2,3},{3,2},{4,5},{5,4},{6,7},{7,6},{8,9},{9,8},{10,11... | collective-permute-start | bytes 3145736 | tf_op jit(solution)/shard_map/ppermute | solution.py:35
  68.8 13.0 %collective-permute-start.13 = (bf16[448,512]{1,0:T(8,128)(2,1)S(1)}, bf16[448,512]{1,0:T(8,128)(2,1)}, u32[]{:S(2)}, u32[]{:S(2)}) collective-permute-start(bf16[448,512]{1,0:T(8,128)(2,1)S(1)} %copy-done.17), channel_id=1, source_target_pairs={{0,4},{1,5},{2,6},{3,7},{4,0},{5,1},{6,2},{7,3},{8,12},{9,13},{10,... | collective-permute-start | bytes 1376264 | tf_op jit(solution)/shard_map/ppermute | solution.py:35
  74.7 20.4 %collective-permute-start.6 = (f32[256,768]{1,0:T(8,128)}, f32[256,768]{1,0:T(8,128)}, u32[]{:S(2)}, u32[]{:S(2)}) collective-permute-start(f32[256,768]{1,0:T(8,128)} %get-tuple-element.23), channel_id=1, source_target_pairs={{0,1},{1,0},{2,3},{3,2},{4,5},{5,4},{6,7},{7,6},{8,9},{9,8},{10,11... | collective-permute-start | bytes 2359304 | tf_op jit(solution)/shard_map/ppermute | solution.py:35
  74.8 4.8 %copy-start.3 = (bf16[256,2048]{1,0:T(8,128)(2,1)}, bf16[256,2048]{1,0:T(8,128)(2,1)S(1)}, u32[]{:S(2)}) copy-start(bf16[256,2048]{1,0:T(8,128)(2,1)S(1)} %collective-permute-done.10.refs_1_.refs_6_) | copy-start | bytes 3145732
  80.5 10.9 %collective-permute-start.11 = (f32[256,768]{1,0:T(8,128)}, f32[256,768]{1,0:T(8,128)}, u32[]{:S(2)}, u32[]{:S(2)}) collective-permute-start(f32[256,768]{1,0:T(8,128)} %get-tuple-element.28), channel_id=1, source_target_pairs={{0,1},{1,0},{2,3},{3,2},{4,5},{5,4},{6,7},{7,6},{8,9},{9,8},{10,11... | collective-permute-start | bytes 2359304 | tf_op jit(solution)/shard_map/ppermute | solution.py:35
  89.2 2.2 %copy-start.13 = (f32[256,768]{1,0:T(8,128)S(1)}, f32[256,768]{1,0:T(8,128)}, u32[]{:S(2)}) copy-start(f32[256,768]{1,0:T(8,128)} %copy-done.12) | copy-start | bytes 2359300
  91.3 14.4 %copy-start.7 = (bf16[16,64,768]{2,1,0:T(8,128)(2,1)S(1)}, bf16[16,64,768]{2,1,0:T(8,128)(2,1)}, u32[]{:S(2)}) copy-start(bf16[16,64,768]{2,1,0:T(8,128)(2,1)} %refs_8_.1) | copy-start | bytes 4718596
  91.3 14.4 %copy-start.11 = (f32[256,768]{1,0:T(8,128)S(1)}, f32[256,768]{1,0:T(8,128)}, u32[]{:S(2)}) copy-start(f32[256,768]{1,0:T(8,128)} %copy-done.10) | copy-start | bytes 2359300
  91.3 3.1 %collective-permute-start.14 = (f32[2,128,128]{2,1,0:T(8,128)S(1)}, f32[2,128,128]{2,1,0:T(8,128)S(1)}, u32[]{:S(2)}, u32[]{:S(2)}) collective-permute-start(f32[2,128,128]{2,1,0:T(8,128)S(1)} %get-tuple-element.30), channel_id=1, source_target_pairs={{0,1},{1,0},{2,3},{3,2},{4,5},{5,4},{6,7},{7,6},{8,9},{9,8},{10,11... | collective-permute-start | bytes 393224 | tf_op jit(solution)/shard_map/ppermute | solution.py:35
  92.9 12.8 %collective-permute-start.12 = (bf16[256,768]{1,0:T(8,128)(2,1)S(1)}, bf16[256,768]{1,0:T(8,128)(2,1)S(1)}, u32[]{:S(2)}, u32[]{:S(2)}) collective-permute-start(bf16[256,768]{1,0:T(8,128)(2,1)S(1)} %add_convert_fusion), channel_id=1, source_target_pairs={{0,2},{1,3},{2,0},{3,1},{4,6},{5,7},{6,4},{7,5},{8,10},{9,11},{10,... | collective-permute-start | bytes 1179656 | tf_op jit(solution)/shard_map/ppermute | solution.py:35
  94.5 11.2 %collective-permute-start.15 = (f32[1,128,128]{2,1,0:T(8,128)S(1)}, f32[1,128,128]{2,1,0:T(8,128)S(1)}, u32[]{:S(2)}, u32[]{:S(2)}) collective-permute-start(f32[1,128,128]{2,1,0:T(8,128)S(1)} %get-tuple-element.33), channel_id=1, source_target_pairs={{0,2},{1,3},{2,0},{3,1},{4,6},{5,7},{6,4},{7,5},{8,10},{9,11},{10,... | collective-permute-start | bytes 196616 | tf_op jit(solution)/shard_map/ppermute | solution.py:35
  (21 other events, 25.2 us)

commit v5 on v3

v5 whole, which is shorter than its diff:
```python
import functools

import jax
import jax.numpy as jnp
from jax import lax
from jax.experimental import pallas as pl
from jax.experimental.pallas import tpu as pltpu
from jax.sharding import PartitionSpec as P

BLOCK = 128
LANES = 128
MOST = 16
LAYER_CHIPS = 4
VMEM_BYTES = 28 * 1024 * 1024
CORE_FLOPS_PER_US = 1_153_500_000
WAITS = {"far": 12, "keys": 0, "all": 5, "across": 0, "near": 0, "low": (5, 15)}

HBM = pl.BlockSpec(memory_space=pl.ANY)
VMEM = pl.BlockSpec(memory_space=pltpu.VMEM)
SMEM = pl.BlockSpec(memory_space=pltpu.SMEM)


def call(kernel, outs, out_specs, in_specs, scratch, flops, moved):
    return pl.pallas_call(
        kernel,
        out_shape=outs,
        in_specs=in_specs,
        out_specs=out_specs,
        scratch_shapes=scratch,
        compiler_params=pltpu.CompilerParams(vmem_limit_bytes=VMEM_BYTES),
        cost_estimate=pl.CostEstimate(flops=flops, bytes_accessed=moved, transcendentals=0),
    )


def swap(value, axis, bit):
    return lax.ppermute(value, axis, [(i, i ^ bit) for i in range(lax.axis_size(axis))])


def run_copies(pairs, sems):
    copies = [pltpu.make_async_copy(a, b, sems.at[i]) for i, (a, b) in enumerate(pairs)]
    for copy in copies:
        copy.start()
    return copies


def part_start(h, part):
    return pl.multiple_of((lax.axis_index("rep") ^ h) * part, part)


def first_kernel(group, layers, splits, part, key, tokens, *refs):
    keys, refs = refs[:splits], refs[splits:]
    outs, sems = refs[:-1], refs[-1]
    blocks = tokens.shape[0] // BLOCK
    depth = splits * part
    me = lax.axis_index("batch")
    layer, spot = me // group, me % group
    pairs = [(key.at[pl.ds(part_start(h, part), part), :], keys[h]) for h in range(splits)]
    for s in reversed(range(group)):
        for t in range(layers):
            first = ((layer ^ t) * group + (spot ^ s)) * depth
            for h in range(splits):
                start = first + part_start(h, part) if splits > 1 else first
                start = pl.multiple_of(start, part)
                to = pl.ds(t * depth + h * part, part)
                if s < 2:
                    pairs.append((tokens.at[:, pl.ds(start, part)], outs[s].at[:, to]))
                    continue
                for j in range(blocks):
                    pairs.append(
                        (
                            tokens.at[pl.ds(j * BLOCK, BLOCK), pl.ds(start, part)],
                            outs[2 + (s - 2) * blocks + j].at[:, to],
                        )
                    )
    for copy in run_copies(pairs, sems):
        copy.wait()


def stack_kernel(moves, taken, count, *refs):
    values, outs, sems = refs[:taken], refs[count:-1], refs[-1]
    pairs = []
    for o, to, a, row, rows in moves:
        pairs.append((values[a].at[pl.ds(row, rows), :], outs[o].at[pl.ds(to, rows), :]))
    for copy in run_copies(pairs, sems):
        copy.wait()


def stack(lists, *ready, us=0):
    values, moves, outs = [], [], []
    for o, rows_of in enumerate(lists):
        to = 0
        for value, row, rows in rows_of:
            moves.append((o, to, len(values), row, rows))
            values.append(value)
            to += rows
        outs.append(jax.ShapeDtypeStruct((to, value.shape[1]), value.dtype))
    count = len(values) + len(ready)
    return call(
        functools.partial(stack_kernel, tuple(moves), len(values), count),
        outs,
        [VMEM] * len(outs),
        [HBM] * count,
        [pltpu.SemaphoreType.DMA((len(moves),))],
        us * CORE_FLOPS_PER_US,
        0,
    )(*values, *ready)


def gate(value, *ready, us=0):
    return stack([[(value, 0, value.shape[0])]], *ready, us=us)[0]


def chosen_kernel(slots, rank, splits, part, group, layers, shift, picks, down, *refs):
    outs, sems = refs[:-1], refs[-1]
    layer = lax.axis_index("batch") // group
    half = (layer * 2) // layers
    pairs = []
    for n, out in enumerate(outs):
        first = (half ^ 1 ^ n) * shift
        for q in range(slots):
            for h in range(splits):
                start = part_start(h, part) if splits > 1 else 0
                pairs.append(
                    (
                        down.at[picks[first + q], :, pl.ds(start, part)],
                        out.at[pl.ds(q * rank, rank), pl.ds(h * part, part)],
                    )
                )
    for copy in run_copies(pairs, sems):
        copy.wait()


def table(lists, block):
    sizes, adapters, tails = lists
    end = jnp.int32(0)
    owner, adapter, limit = jnp.int32(0), jnp.int32(0), jnp.int32(BLOCK)
    for q in range(sizes.shape[0]):
        begin = end
        end = end + sizes[q]
        inside = (begin <= block) & (block < end)
        owner = jnp.where(inside, q, owner)
        adapter = jnp.where(inside, adapters[q], adapter)
        limit = jnp.where(inside & (block == end - 1), tails[q], limit)
    return owner, adapter, limit


def token_places(group, rows):
    near = [(s * rows, rows) for s in range(min(group, 2))]
    far = [(row, BLOCK) for row in range(2 * rows, group * rows, BLOCK)]
    return near + far


def low_kernel(
    group, layers, rows, depth, rank, entries, count, by_request, shift, has_sum, last, *refs
):
    lists, refs = refs[:3], refs[3:]
    places = token_places(group, rows)
    toks, refs = refs[: len(places)], refs[len(places) :]
    arrays, refs = refs[:count], refs[count:]
    if has_sum:
        before, refs = refs[0], refs[1:]
    if last:
        even, odd, refs = refs[0], refs[1], refs[2:]
    else:
        after, refs = refs[0], refs[1:]
    held, refs = refs[0], refs[1:]
    downs, refs = refs[:count], refs[count:]
    tok_sems, sems = refs
    local_blocks = rows // BLOCK
    me = lax.axis_index("batch")
    layer, spot = me // group, me % group
    first = {}
    started = {}
    for n, (t, a, _) in enumerate(entries):
        if a not in started:
            started[a] = pltpu.make_async_copy(arrays[a], downs[a], sems.at[a])
            started[a].start()
        first[t] = []
        for i, (to, deep) in enumerate(places):
            copy = pltpu.make_async_copy(
                toks[i].at[:, pl.ds(t * depth, depth)],
                held.at[pl.ds(to, deep), pl.ds(n * depth, depth)],
                tok_sems.at[i, n],
            )
            copy.start()
            first[t].append(copy)
    slots = []
    for s in range(group):
        for j in range(local_blocks):
            block = (layer * group + (spot ^ s)) * local_blocks + j
            owner, adapter, _ = table(lists, block)
            slots.append(owner - (layer * 2) // layers * shift if by_request else adapter)
    ready = set()
    wide = 2 * local_blocks
    sums = [before[p] if has_sum else None for p in range(group // 2)]
    for n, (t, a, row) in enumerate(entries):
        for copy in first[t]:
            copy.wait()
        if a not in ready:
            started[a].wait()
            ready.add(a)
        for p in range(group // 2):
            chosen = jnp.concatenate(
                [
                    downs[a][pl.ds(pl.multiple_of(row + slots[p * wide + i] * rank, rank), rank), :]
                    for i in range(wide)
                ],
                0,
            )
            term = lax.dot_general(
                held[2 * p * rows : 2 * (p + 1) * rows, n * depth : (n + 1) * depth],
                chosen,
                (((1,), (1,)), ((), ())),
                preferred_element_type=jnp.float32,
            )
            sums[p] = term if sums[p] is None else sums[p] + term
    for p in range(group // 2):
        if not last:
            after[p] = sums[p]
            continue
        for out, at in ((even, 0), (odd, 1)):
            out[p] = jnp.concatenate(
                [
                    sums[p][
                        (at * local_blocks + j) * BLOCK : (at * local_blocks + j + 1) * BLOCK,
                        (at * local_blocks + j) * rank : (at * local_blocks + j + 1) * rank,
                    ]
                    for j in range(local_blocks)
                ],
                1,
            )


def final_kernel(rows, rank, bases, fars, lows, *refs):
    lists, refs = refs[:3], refs[3:]
    far_refs, refs = refs[:fars], refs[fars:]
    base_refs, refs = refs[:bases], refs[bases:]
    low_refs, refs = refs[:lows], refs[lows:]
    ups, out, up_here, sems = refs
    local_blocks = rows // BLOCK
    me = lax.axis_index("batch")
    found = [table(lists, me * local_blocks + j) for j in range(local_blocks)]
    copies = run_copies([(ups.at[found[j][1]], up_here.at[j]) for j in range(local_blocks)], sems)
    low = low_refs[0][...]
    for ref in low_refs[1:]:
        low = low + ref[...]
    low = low.astype(jnp.bfloat16)
    for j in range(local_blocks):
        copies[j].wait()
        here = pl.ds(j * BLOCK, BLOCK)
        total = jnp.dot(
            low[:, j * rank : (j + 1) * rank], up_here[j], preferred_element_type=jnp.float32
        )
        for ref in base_refs:
            total = total + ref[here, :]
        if far_refs:
            total = total + far_refs[j][...].astype(jnp.float32)
        live = lax.broadcasted_iota(jnp.int32, total.shape, 0) < found[j][2]
        out[here, :] = jnp.where(live, total, 0.0).astype(jnp.bfloat16)


def shards(
    tokens,
    key_matrix,
    adapter_down_factors,
    adapter_up_factors,
    request_block_list,
    request_adapter_index,
    request_tail_tokens,
):
    rows, width = tokens.shape
    depth, out_width = key_matrix.shape
    adapters, rank = adapter_down_factors.shape[1:]
    reps, devices = lax.axis_size("rep"), lax.axis_size("batch")
    group = 2 * LAYER_CHIPS // reps
    layers = devices // group
    splits = reps if (depth // reps) % LANES == 0 else 1
    part = depth // splits
    local_blocks = rows // BLOCK
    held_width = layers * depth
    lists = (request_block_list, request_adapter_index, request_tail_tokens)
    f32, bf16 = jnp.float32, jnp.bfloat16

    far_count = (group - 2) * local_blocks
    first = call(
        functools.partial(first_kernel, group, layers, splits, part),
        [jax.ShapeDtypeStruct((part, out_width), bf16)] * splits
        + [jax.ShapeDtypeStruct((rows, held_width), bf16)] * 2
        + [jax.ShapeDtypeStruct((BLOCK, held_width), bf16)] * far_count,
        [HBM] * (splits + 2 + far_count),
        [HBM] * 2,
        [
            pltpu.SemaphoreType.DMA(
                (splits + (2 + far_count) * layers * splits,)
            )
        ],
        0,
        4 * (rows * width + depth * out_width),
    )(key_matrix, tokens)
    key_parts, first = first[:splits], first[splits:]

    far = [list(first[2 + s * local_blocks :][:local_blocks]) for s in range(group - 2)]
    sent = []
    for j in range(local_blocks if far else 0):
        if j:
            sent = stack([[(f[j], 0, BLOCK)] for f in far], *[f[j - 1] for f in far], us=WAITS["far"])
        else:
            sent = [f[j] for f in far]
        for s, f in enumerate(far):
            f[j] = swap(sent[s], "batch", 2 + s)

    down = jnp.transpose(adapter_down_factors, (1, 2, 0))
    requests = request_adapter_index.shape[0]
    by_request = requests < adapters
    shift = 1 if by_request and local_blocks * devices == 2 * MOST and layers > 1 else 0
    slots = requests - shift if by_request else adapters
    if by_request:
        across, down = call(
            functools.partial(chosen_kernel, slots, rank, splits, part, group, layers, shift),
            [jax.ShapeDtypeStruct((slots * rank, depth), bf16)] * 2,
            [VMEM] * 2,
            [SMEM, HBM],
            [pltpu.SemaphoreType.DMA((2 * slots * splits,))],
            0,
            8 * slots * rank * depth,
        )(request_adapter_index, down)
    else:
        down = down.reshape(slots * rank, depth)
        across = down

    def over_layers(across, near):
        bundles = []
        bit = layers // 2
        while bit:
            moved = [([bit], swap(near if bundles else across, "batch", bit * group))]
            if bundles:
                rest = [v for _, v in bundles]
                rest = rest[0] if len(rest) == 1 else jnp.concatenate(rest, 0)
                order = [t ^ bit for ts, _ in bundles for t in ts]
                moved.append((order, swap(rest, "batch", bit * group)))
            bundles = bundles + moved
            bit //= 2
        return bundles

    key_bundles = over_layers(key_parts[0], key_parts[0])
    rows_of_key = {}
    for h in range(splits):
        rows_of_key[0, h] = (key_parts[h], 0, part)
    for ts, value in key_bundles:
        for i, t in enumerate(ts):
            rows_of_key[t, 0] = (value, i * part, part)
    last_keys = [key_bundles[-1][1]]
    for h in range(1, splits):
        for bundles in (key_bundles[:1], key_bundles[1:]):
            if not bundles:
                continue
            values = bundles[0][1]
            if bundles is not key_bundles[:1] and len(bundles) > 1:
                values = stack([[(v, 0, v.shape[0]) for _, v in bundles]], *last_keys, us=WAITS["keys"])[0]
            last_keys = [values]
            swapped = swap(values, "rep", h)
            if len(bundles) == 1:
                last_keys = [swapped]
            for i, t in enumerate([t for ts, _ in bundles for t in ts]):
                rows_of_key[t, h] = (swapped, i * part, part)
    keys = stack(
        [[rows_of_key[t, h] for t in range(layers) for h in range(splits)]], us=WAITS["all"]
    )[0]

    across_sent = gate(across, *[v for _, v in key_bundles[:2]], us=WAITS["across"])
    down_sent = gate(down, *last_keys, us=WAITS["near"])
    down_bundles = over_layers(across_sent, down_sent)

    near = [first[0], swap(gate(first[1], *[v for _, v in down_bundles[:2]]), "batch", 1)]

    def base_of(value):
        return jnp.dot(value, keys, preferred_element_type=f32)

    fars = []
    if far:
        for j in range(local_blocks):
            theirs = swap(base_of(far[1][j]), "batch", 1)
            fars.append(swap((base_of(far[0][j]) + theirs).astype(bf16), "batch", 2))
    bases = [base_of(near[0]), swap(base_of(near[1]), "batch", 1)]
    tokens_here = near + [value for f in far for value in f]

    def low_call(bundles, before, last):
        taken = [value for _, value in bundles]
        at = [
            (t, a, i * slots * rank) for a, (ts, _) in enumerate(bundles) for i, t in enumerate(ts)
        ]
        pairs, tall, wide = group // 2, 2 * rows, 2 * local_blocks * rank
        if last:
            outs = [jax.ShapeDtypeStruct((pairs, BLOCK, local_blocks * rank), f32)] * 2
            out_specs = [VMEM] * 2
        else:
            outs, out_specs = jax.ShapeDtypeStruct((pairs, tall, wide), f32), VMEM
        return call(
            functools.partial(
                low_kernel, group, layers, rows, depth, rank, tuple(at), len(taken), by_request,
                shift, before is not None, last,
            ),
            outs,
            out_specs,
            [SMEM] * 3 + [HBM] * (len(tokens_here) + len(taken)) + [VMEM] * (before is not None),
            [pltpu.VMEM((group * rows, len(at) * depth), bf16)]
            + [pltpu.VMEM(v.shape, bf16) for v in taken]
            + [pltpu.SemaphoreType.DMA((len(tokens_here), len(at))), pltpu.SemaphoreType.DMA((len(taken),))],
            WAITS["low"][last] * CORE_FLOPS_PER_US,
            0,
        )(*lists, *tokens_here, *taken, *([before] if before is not None else []))

    early = low_call([([0], down)] + down_bundles[:-1], None, False)
    even, odd = low_call(down_bundles[-1:], early, True)
    got = swap(odd, "batch", 1)
    lows = layer_pairs(even, got)

    return call(
        functools.partial(final_kernel, rows, rank, len(bases), len(fars), len(lows)),
        jax.ShapeDtypeStruct((rows, out_width), bf16),
        VMEM,
        [SMEM] * 3 + [VMEM] * (len(fars) + len(bases) + len(lows)) + [HBM],
        [pltpu.VMEM((local_blocks, rank, out_width), bf16), pltpu.SemaphoreType.DMA((local_blocks,))],
        2 * rows * rank * out_width,
        8 * rows * out_width,
    )(*lists, *fars, *bases, *lows, adapter_up_factors)


def layer_pairs(mine, got):
    bit = 2
    while mine.shape[0] > 1:
        total = mine + got
        mine, got = total[0::2], swap(total[1::2], "batch", bit)
        bit *= 2
    return [mine[0], got[0]]


def solution(mesh):
    placed = (
        P(("rep", "batch"), None),
        P("batch", None),
        P("batch", None, None),
        P(),
        P("rep"),
        P("rep"),
        P("rep"),
    )
    return jax.shard_map(
        shards, mesh=mesh, in_specs=placed, out_specs=P(("rep", "batch"), None), check_vma=False
    )
```

time: 299 us -> 92.9 us (0.31)
  Pallas kernels: 199 us -> 12.3 us
  waiting for transfers between devices: 72.9 us -> 51.8 us
  matrix products: 0 us -> 4.38 us
  local copies, waits for them, and re-layouts: 6.87 us -> 3.36 us
  starting transfers between devices: 17.2 us -> 20.6 us
    pallas_call x1, Pallas kernels: 152 us -> 1.65 us  [shards(): call(functools.partial(first_kernel, group, layers, splits, part), [jax.S...]
    pallas_call x1, Pallas kernels: 29.8 us -> 1.06 us  [shards(): call(functools.partial(chosen_kernel, slots, rank, splits, part, group, l...]
    ppermute x16 -> x20, waiting for transfers between devices: 72.9 us -> 51.8 us  [swap(): lax.ppermute(value, axis, [(i, i ^ bit) for i in range(lax.axis_size(axis...]
    pallas_call x6 -> x7, Pallas kernels: 11.1 us -> 4.8 us  [the longest x6 2.7 us: stack(): call(functools.partial(stack_kernel, tuple(moves), len(values), count), o...]
    dot_general x0 -> x6, matrix products: none -> 4.38 us  [base_of(): return jnp.dot(value, keys, preferred_element_type=f32)]
    unnamed x40 -> x14, local copies, waits for them, and re-layouts: 6.85 us -> 3.35 us
    ppermute x16 -> x20, starting transfers between devices: 17.2 us -> 20.6 us  [swap(): lax.ppermute(value, axis, [(i, i ^ bit) for i in range(lax.axis_size(axis...]
  transfers between devices with their start and end apart: 16 -> 20, of which waited for: 7 -> 9; matrix products, arithmetic and copies ran while one was open for 1% -> 5% of each run, Pallas kernels for 15% -> 9%
where the time goes in v5:
time: 92.9 us; the launch traced here: 92.7 us
  waiting for transfers between devices  51.8 us (56%)
  starting transfers between devices  20.6 us (22%)
  Pallas kernels  12.3 us (13%)
  matrix products  4.38 us (5%)
  local copies, waits for them, and re-layouts  3.36 us (4%)
    ppermute x20, waiting for transfers between devices, swap(): lax.ppermute(value, axis, [(i, i ^ bit) for i in range(lax.axis_size(axis...  51.8 us
    ppermute x20, starting transfers between devices, swap(): lax.ppermute(value, axis, [(i, i ^ bit) for i in range(lax.axis_size(axis...  20.6 us
    pallas_call x2, Pallas kernels, low_call(): call(functools.partial(low_kernel, group, layers, rows, depth, rank, tupl...  4.77 us
    dot_general x6, matrix products, base_of(): return jnp.dot(value, keys, preferred_element_type=f32)  4.38 us
    unnamed x14, local copies, waits for them, and re-layouts  3.35 us
    pallas_call x6, Pallas kernels, stack(): call(functools.partial(stack_kernel, tuple(moves), len(values), count), o...  2.7 us
    pallas_call x1, Pallas kernels, shards(): call(functools.partial(final_kernel, rows, rank, len(bases), len(fars), l...  2.11 us
  transfers between devices with their start and end apart: 20, of which 9 were waited for; matrix products, arithmetic and copies ran while one was open for 5% of the time, Pallas kernels for 9%

profile of v5, /device:TPU:0, one launch (start us, length us, event | category | flops | bytes accessed | tf_op | source)
XLA Modules:
  0.0 92.7 jit_solution(9968966819492460484)
XLA Ops:
  0.0 2.2 %copy-done = bf16[256,8192]{1,0:T(8,128)(2,1)S(1)} copy-done((bf16[256,8192]{1,0:T(8,128)(2,1)S(1)}, bf16[256,8192]{1,0:T(8,128)(2,1)}, u32[]{:S(2)}) %copy-start) | copy-done | bytes 4194328
  2.2 1.1 %copy-done.3 = bf16[512,768]{1,0:T(8,128)(2,1)S(1)} copy-done((bf16[512,768]{1,0:T(8,128)(2,1)S(1)}, bf16[512,768]{1,0:T(8,128)(2,1)}, u32[]{:S(2)}) %copy-start.3) | copy-done | bytes 786456
  3.3 1.6 %shard_map.73 = (bf16[256,768]{1,0:T(8,128)(2,1)S(1)}, bf16[256,768]{1,0:T(8,128)(2,1)S(1)}, bf16[256,2048]{1,0:T(8,128)(2,1)S(1)}, bf16[256,2048]{1,0:T(8,128)(...) custom-call(bf16[512,768]{1,0:T(8,128)(2,1)S(1)} %copy-done.3, ...), custom_call_target="tpu_custom_call" | custom-call | bytes 9961472 | tf_op jit(solution)/shard_map/pallas_call | solution.py:285
  5.0 4.1 %collective-permute-start.2 = (bf16[256,768]{1,0:T(8,128)(2,1)S(1)}, bf16[256,768]{1,0:T(8,128)(2,1)S(1)}, u32[]{:S(2)}, u32[]{:S(2)}) collective-permute-start(bf16[256,768]{1,0:T(8,128)(2,1)S(1)} %get-tuple-element.20.refs_0_), channel_id=1, source_target_pairs={{0,8},{1,9},{2,10},{3,11},{4,12},{5,13},{6,14},{7,15},{8,0},{9,1},... | collective-permute-start | bytes 1179656 | tf_op jit(solution)/shard_map/ppermute | solution.py:36
  9.1 1.5 %collective-permute-start = (bf16[128,2048]{1,0:T(8,128)(2,1)S(1)}, bf16[128,2048]{1,0:T(8,128)(2,1)S(1)}, u32[]{:S(2)}, u32[]{:S(2)}) collective-permute-start(bf16[128,2048]{1,0:T(8,128)(2,1)S(1)} %get-tuple-element.19), channel_id=1, source_target_pairs={{0,2},{1,3},{2,0},{3,1},{4,6},{5,7},{6,4},{7,5},{8,10},{9,11},{10,... | collective-permute-start | bytes 1572872 | tf_op jit(solution)/shard_map/ppermute | solution.py:36
  10.6 1.6 %collective-permute-start.1 = (bf16[256,768]{1,0:T(8,128)(2,1)S(1)}, bf16[256,768]{1,0:T(8,128)(2,1)S(1)}, u32[]{:S(2)}, u32[]{:S(2)}) collective-permute-start(bf16[256,768]{1,0:T(8,128)(2,1)S(1)} %get-tuple-element.20.refs_0_), channel_id=1, source_target_pairs={{0,4},{1,5},{2,6},{3,7},{4,0},{5,1},{6,2},{7,3},{8,12},{9,13},{10,... | collective-permute-start | bytes 1179656 | tf_op jit(solution)/shard_map/ppermute | solution.py:36
  12.2 14.5 %collective-permute-done.2.refs_4_.refs_1_ = bf16[256,768]{1,0:T(8,128)(2,1)S(1)} collective-permute-done((bf16[256,768]{1,0:T(8,128)(2,1)S(1)}, bf16[256,768]{1,0:T(8,128)(2,1)S(1)}, u32[]{:S(2)}, u32[]{:S(2)}) %collective-permute-start.2) | collective-permute-done | bytes 393248 | tf_op jit(solution)/shard_map/ppermute | solution.py:36
  27.4 1.5 %collective-permute-start.4 = (bf16[256,768]{1,0:T(8,128)(2,1)S(1)}, bf16[256,768]{1,0:T(8,128)(2,1)S(1)}, u32[]{:S(2)}, u32[]{:S(2)}) collective-permute-start(bf16[256,768]{1,0:T(8,128)(2,1)S(1)} %collective-permute-done.2.refs_4_.refs_1_), channel_id=1, source_target_pairs={{0,16},{16,0},{1,17},{17,1},{2,18},{18,2},{3,19},{19,3},{4,20},{20... | collective-permute-start | bytes 1179656 | tf_op jit(solution)/shard_map/ppermute | solution.py:36
  28.9 1.1 %shard_map.77 = (bf16[448,512]{1,0:T(8,128)(2,1)S(1)}, bf16[448,512]{1,0:T(8,128)(2,1)S(1)}) custom-call(s32[8]{0:T(128)S(1)} %copy-done.4, bf16[16,64,512]{2,1,0:T(8,128)(2,1)S(1)} %bitcast.16), custom_call_target="tpu_custom_call" | custom-call | bytes 1835008 | tf_op jit(solution)/shard_map/pallas_call | solution.py:318
  30.3 3.5 %collective-permute-start.13 = (bf16[448,512]{1,0:T(8,128)(2,1)S(1)}, bf16[448,512]{1,0:T(8,128)(2,1)S(1)}, u32[]{:S(2)}, u32[]{:S(2)}) collective-permute-start(bf16[448,512]{1,0:T(8,128)(2,1)S(1)} %shard_map.78), channel_id=1, source_target_pairs={{0,8},{1,9},{2,10},{3,11},{4,12},{5,13},{6,14},{7,15},{8,0},{9,1},... | collective-permute-start | bytes 1376264 | tf_op jit(solution)/shard_map/ppermute | solution.py:36
  33.8 9.7 %collective-permute-done.3.refs_1_.refs_6_ = bf16[256,768]{1,0:T(8,128)(2,1)S(1)} collective-permute-done((bf16[256,768]{1,0:T(8,128)(2,1)S(1)}, bf16[256,768]{1,0:T(8,128)(2,1)S(1)}, u32[]{:S(2)}, u32[]{:S(2)}) %collective-permute-start.3) | collective-permute-done | bytes 393248 | tf_op jit(solution)/shard_map/ppermute | solution.py:36
  43.9 2.4 %collective-permute-start.5 = (bf16[512,768]{1,0:T(8,128)(2,1)S(1)}, bf16[512,768]{1,0:T(8,128)(2,1)S(1)}, u32[]{:S(2)}, u32[]{:S(2)}) collective-permute-start(bf16[512,768]{1,0:T(8,128)(2,1)S(1)} %shard_map.74.refs_1_), channel_id=1, source_target_pairs={{0,16},{16,0},{1,17},{17,1},{2,18},{18,2},{3,19},{19,3},{4,20},{20... | collective-permute-start | bytes 2359304 | tf_op jit(solution)/shard_map/ppermute | solution.py:36
  46.8 1.3 %collective-permute-start.9 = (bf16[128,2048]{1,0:T(8,128)(2,1)S(1)}, bf16[128,2048]{1,0:T(8,128)(2,1)S(1)}, u32[]{:S(2)}, u32[]{:S(2)}) collective-permute-start(bf16[128,2048]{1,0:T(8,128)(2,1)S(1)} %get-tuple-element.25), channel_id=1, source_target_pairs={{0,2},{1,3},{2,0},{3,1},{4,6},{5,7},{6,4},{7,5},{8,10},{9,11},{10,... | collective-permute-start | bytes 1572872 | tf_op jit(solution)/shard_map/ppermute | solution.py:36
  48.1 5.7 %collective-permute-done.13.refs_1_.refs_10_ = bf16[448,512]{1,0:T(8,128)(2,1)S(1)} collective-permute-done((bf16[448,512]{1,0:T(8,128)(2,1)S(1)}, bf16[448,512]{1,0:T(8,128)(2,1)S(1)}, u32[]{:S(2)}, u32[]{:S(2)}) %collective-permute-start.13) | collective-permute-done | bytes 458784 | tf_op jit(solution)/shard_map/ppermute | solution.py:36
  53.8 8.5 %collective-permute-done.14.refs_2_.refs_11_ = bf16[448,512]{1,0:T(8,128)(2,1)S(1)} collective-permute-done((bf16[448,512]{1,0:T(8,128)(2,1)S(1)}, bf16[448,512]{1,0:T(8,128)(2,1)S(1)}, u32[]{:S(2)}, u32[]{:S(2)}) %collective-permute-start.14) | collective-permute-done | bytes 458784 | tf_op jit(solution)/shard_map/ppermute | solution.py:36
  63.2 1.6 %shard_map.75 = bf16[2048,768]{1,0:T(8,128)(2,1)S(1)} custom-call(bf16[256,768]{1,0:T(8,128)(2,1)S(1)} %get-tuple-element.20.refs_0_, bf16[256,768]{1,0:T(8,128)(2,1)S(1)} %get-tuple-element.21.refs_1_, bf16[256,768]{1,0:T(8,128)(2,1)S(1)} %collective-permute-done.1.refs_0_.refs_2_, bf16[512,768]{1,0:T(8,128)(2,1)S(1)} %collective-permute-done.5.refs_3_.refs_7_, ...), custom_call_target="tpu_custom_call" | custom-call | flops 5767499776 | tf_op jit(solution)/shard_map/pallas_call | solution.py:98
  66.7 5.2 %collective-permute-done.9.refs_6_ = bf16[128,2048]{1,0:T(8,128)(2,1)S(1)} collective-permute-done((bf16[128,2048]{1,0:T(8,128)(2,1)S(1)}, bf16[128,2048]{1,0:T(8,128)(2,1)S(1)}, u32[]{:S(2)}, u32[]{:S(2)}) %collective-permute-start.9) | collective-permute-done | bytes 524320 | tf_op jit(solution)/shard_map/ppermute | solution.py:36
  72.9 3.2 %shard_map.81.refs_10_ = f32[2,512,256]{2,1,0:T(8,128)S(1)} custom-call(s32[8]{0:T(128)S(1)} %copy-done.5, s32[8]{0:T(128)S(1)} %copy-done.4, s32[8]{0:T(128)S(1)} %copy-done.6, bf16[256,2048]{1,0:T(8,128)(2,1)S(1)} %get-tuple-element.27.refs_3_, bf16[256,2048]{1,0:T(8,128)(2,1)S(1)} %collective-permute-done.15.refs_4_, ...), custom_call_target="tpu_custom_call" | custom-call | flops 5767499776 | tf_op jit(solution)/shard_map/pallas_call | solution.py:398
  76.1 2.3 %collective-permute-done.17.refs_9_ = bf16[448,512]{1,0:T(8,128)(2,1)S(1)} collective-permute-done((bf16[448,512]{1,0:T(8,128)(2,1)S(1)}, bf16[448,512]{1,0:T(8,128)(2,1)S(1)}, u32[]{:S(2)}, u32[]{:S(2)}) %collective-permute-start.17) | collective-permute-done | bytes 458784 | tf_op jit(solution)/shard_map/ppermute | solution.py:36
  78.4 1.6 %shard_map.82 = (f32[2,128,128]{2,1,0:T(8,128)S(1)}, f32[2,128,128]{2,1,0:T(8,128)S(1)}) custom-call(s32[8]{0:T(128)S(1)} %copy-done.5, s32[8]{0:T(128)S(1)} %copy-done.4, s32[8]{0:T(128)S(1)} %copy-done.6, bf16[256,2048]{1,0:T(8,128)(2,1)S(1)} %get-tuple-element.27.refs_3_, bf16[256,2048]{1,0:T(8,128)(2,1)S(1)} %collective-permute-done.15.refs_4_, ...), custom_call_target="tpu_custom_call" | custom-call | flops 17302499328 | tf_op jit(solution)/shard_map/pallas_call | solution.py:398
  82.3 1.1 %collective-permute-start.8 = (bf16[128,768]{1,0:T(8,128)(2,1)S(1)}, bf16[128,768]{1,0:T(8,128)(2,1)S(1)}, u32[]{:S(2)}, u32[]{:S(2)}) collective-permute-start(bf16[128,768]{1,0:T(8,128)(2,1)S(1)} %fusion), channel_id=1, source_target_pairs={{0,2},{1,3},{2,0},{3,1},{4,6},{5,7},{6,4},{7,5},{8,10},{9,11},{10,... | collective-permute-start | bytes 589832 | tf_op jit(solution)/shard_map/ppermute | solution.py:36
  83.4 1.1 %collective-permute-start.19 = (f32[1,128,128]{2,1,0:T(8,128)S(1)}, f32[1,128,128]{2,1,0:T(8,128)S(1)}, u32[]{:S(2)}, u32[]{:S(2)}) collective-permute-start(f32[1,128,128]{2,1,0:T(8,128)S(1)} %get-tuple-element.33), channel_id=1, source_target_pairs={{0,2},{1,3},{2,0},{3,1},{4,6},{5,7},{6,4},{7,5},{8,10},{9,11},{10,... | collective-permute-start | bytes 196616 | tf_op jit(solution)/shard_map/ppermute | solution.py:36
  85.5 4.4 %collective-permute-done.8.refs_3_ = bf16[128,768]{1,0:T(8,128)(2,1)S(1)} collective-permute-done((bf16[128,768]{1,0:T(8,128)(2,1)S(1)}, bf16[128,768]{1,0:T(8,128)(2,1)S(1)}, u32[]{:S(2)}, u32[]{:S(2)}) %collective-permute-start.8) | collective-permute-done | bytes 196640 | tf_op jit(solution)/shard_map/ppermute | solution.py:36
  90.6 2.1 %shard_map.83 = bf16[256,768]{1,0:T(8,128)(2,1)} custom-call(s32[8]{0:T(128)S(1)} %copy-done.5, s32[8]{0:T(128)S(1)} %copy-done.4, s32[8]{0:T(128)S(1)} %copy-done.6, bf16[128,768]{1,0:T(8,128)(2,1)S(1)} %collective-permute-done.8.refs_3_, bf16[128,768]{1,0:T(8,128)(2,1)S(1)} %collective-permute-done.12.refs_4_, f32[256,768]{1,0:T(8,128)S(1)} %fusion.5.refs_5_, ...), custom_call_target="tpu_custom_call" | custom-call | flops 25165824 | bytes 1572864 | tf_op jit(solution)/shard_map/pallas_call | solution.py:418
  (49 shorter events, 9.6 us)
Async XLA Ops:
  3.3 25.6 %copy-start.2 = (bf16[512,16,64]{0,2,1:T(8,128)(2,1)S(1)}, bf16[512,16,64]{0,2,1:T(8,128)(2,1)}, u32[]{:S(2)}) copy-start(bf16[512,16,64]{0,2,1:T(8,128)(2,1)} %param.9) | copy-start | bytes 3145732
  3.3 25.6 %copy-start.4 = (s32[8]{0:T(128)S(1)}, s32[8]{0:T(128)}, u32[]{:S(2)}) copy-start(s32[8]{0:T(128)} %refs_1_.5) | copy-start | bytes 100
  5.0 21.8 %collective-permute-start.2 = (bf16[256,768]{1,0:T(8,128)(2,1)S(1)}, bf16[256,768]{1,0:T(8,128)(2,1)S(1)}, u32[]{:S(2)}, u32[]{:S(2)}) collective-permute-start(bf16[256,768]{1,0:T(8,128)(2,1)S(1)} %get-tuple-element.20.refs_0_), channel_id=1, source_target_pairs={{0,8},{1,9},{2,10},{3,11},{4,12},{5,13},{6,14},{7,15},{8,0},{9,1},... | collective-permute-start | bytes 1179656 | tf_op jit(solution)/shard_map/ppermute | solution.py:36
  9.1 37.5 %collective-permute-start = (bf16[128,2048]{1,0:T(8,128)(2,1)S(1)}, bf16[128,2048]{1,0:T(8,128)(2,1)S(1)}, u32[]{:S(2)}, u32[]{:S(2)}) collective-permute-start(bf16[128,2048]{1,0:T(8,128)(2,1)S(1)} %get-tuple-element.19), channel_id=1, source_target_pairs={{0,2},{1,3},{2,0},{3,1},{4,6},{5,7},{6,4},{7,5},{8,10},{9,11},{10,... | collective-permute-start | bytes 1572872 | tf_op jit(solution)/shard_map/ppermute | solution.py:36
  10.6 36.0 %collective-permute-start.6 = (bf16[128,2048]{1,0:T(8,128)(2,1)S(1)}, bf16[128,2048]{1,0:T(8,128)(2,1)S(1)}, u32[]{:S(2)}, u32[]{:S(2)}) collective-permute-start(bf16[128,2048]{1,0:T(8,128)(2,1)S(1)} %get-tuple-element.22), channel_id=1, source_target_pairs={{0,3},{1,2},{2,1},{3,0},{4,7},{5,6},{6,5},{7,4},{8,11},{9,10},{10,... | collective-permute-start | bytes 1572872 | tf_op jit(solution)/shard_map/ppermute | solution.py:36
  10.6 19.4 %collective-permute-start.1 = (bf16[256,768]{1,0:T(8,128)(2,1)S(1)}, bf16[256,768]{1,0:T(8,128)(2,1)S(1)}, u32[]{:S(2)}, u32[]{:S(2)}) collective-permute-start(bf16[256,768]{1,0:T(8,128)(2,1)S(1)} %get-tuple-element.20.refs_0_), channel_id=1, source_target_pairs={{0,4},{1,5},{2,6},{3,7},{4,0},{5,1},{6,2},{7,3},{8,12},{9,13},{10,... | collective-permute-start | bytes 1179656 | tf_op jit(solution)/shard_map/ppermute | solution.py:36
  26.7 16.7 %collective-permute-start.3 = (bf16[256,768]{1,0:T(8,128)(2,1)S(1)}, bf16[256,768]{1,0:T(8,128)(2,1)S(1)}, u32[]{:S(2)}, u32[]{:S(2)}) collective-permute-start(bf16[256,768]{1,0:T(8,128)(2,1)S(1)} %collective-permute-done.2.refs_4_.refs_1_), channel_id=1, source_target_pairs={{0,4},{1,5},{2,6},{3,7},{4,0},{5,1},{6,2},{7,3},{8,12},{9,13},{10,... | collective-permute-start | bytes 1179656 | tf_op jit(solution)/shard_map/ppermute | solution.py:36
  27.4 16.1 %collective-permute-start.4 = (bf16[256,768]{1,0:T(8,128)(2,1)S(1)}, bf16[256,768]{1,0:T(8,128)(2,1)S(1)}, u32[]{:S(2)}, u32[]{:S(2)}) collective-permute-start(bf16[256,768]{1,0:T(8,128)(2,1)S(1)} %collective-permute-done.2.refs_4_.refs_1_), channel_id=1, source_target_pairs={{0,16},{16,0},{1,17},{17,1},{2,18},{18,2},{3,19},{19,3},{4,20},{20... | collective-permute-start | bytes 1179656 | tf_op jit(solution)/shard_map/ppermute | solution.py:36
  30.3 23.6 %collective-permute-start.13 = (bf16[448,512]{1,0:T(8,128)(2,1)S(1)}, bf16[448,512]{1,0:T(8,128)(2,1)S(1)}, u32[]{:S(2)}, u32[]{:S(2)}) collective-permute-start(bf16[448,512]{1,0:T(8,128)(2,1)S(1)} %shard_map.78), channel_id=1, source_target_pairs={{0,8},{1,9},{2,10},{3,11},{4,12},{5,13},{6,14},{7,15},{8,0},{9,1},... | collective-permute-start | bytes 1376264 | tf_op jit(solution)/shard_map/ppermute | solution.py:36
  43.9 19.3 %collective-permute-start.5 = (bf16[512,768]{1,0:T(8,128)(2,1)S(1)}, bf16[512,768]{1,0:T(8,128)(2,1)S(1)}, u32[]{:S(2)}, u32[]{:S(2)}) collective-permute-start(bf16[512,768]{1,0:T(8,128)(2,1)S(1)} %shard_map.74.refs_1_), channel_id=1, source_target_pairs={{0,16},{16,0},{1,17},{17,1},{2,18},{18,2},{3,19},{19,3},{4,20},{20... | collective-permute-start | bytes 2359304 | tf_op jit(solution)/shard_map/ppermute | solution.py:36
  46.5 15.8 %collective-permute-start.14 = (bf16[448,512]{1,0:T(8,128)(2,1)S(1)}, bf16[448,512]{1,0:T(8,128)(2,1)S(1)}, u32[]{:S(2)}, u32[]{:S(2)}) collective-permute-start(bf16[448,512]{1,0:T(8,128)(2,1)S(1)} %shard_map.79), channel_id=1, source_target_pairs={{0,4},{1,5},{2,6},{3,7},{4,0},{5,1},{6,2},{7,3},{8,12},{9,13},{10,... | collective-permute-start | bytes 1376264 | tf_op jit(solution)/shard_map/ppermute | solution.py:36
  46.7 18.1 %collective-permute-start.10 = (bf16[128,2048]{1,0:T(8,128)(2,1)S(1)}, bf16[128,2048]{1,0:T(8,128)(2,1)S(1)}, u32[]{:S(2)}, u32[]{:S(2)}) collective-permute-start(bf16[128,2048]{1,0:T(8,128)(2,1)S(1)} %get-tuple-element.26), channel_id=1, source_target_pairs={{0,3},{1,2},{2,1},{3,0},{4,7},{5,6},{6,5},{7,4},{8,11},{9,10},{10,... | collective-permute-start | bytes 1572872 | tf_op jit(solution)/shard_map/ppermute | solution.py:36
  46.8 25.1 %collective-permute-start.9 = (bf16[128,2048]{1,0:T(8,128)(2,1)S(1)}, bf16[128,2048]{1,0:T(8,128)(2,1)S(1)}, u32[]{:S(2)}, u32[]{:S(2)}) collective-permute-start(bf16[128,2048]{1,0:T(8,128)(2,1)S(1)} %get-tuple-element.25), channel_id=1, source_target_pairs={{0,2},{1,3},{2,0},{3,1},{4,6},{5,7},{6,4},{7,5},{8,10},{9,11},{10,... | collective-permute-start | bytes 1572872 | tf_op jit(solution)/shard_map/ppermute | solution.py:36
  62.4 10.5 %collective-permute-start.15 = (bf16[256,2048]{1,0:T(8,128)(2,1)S(1)}, bf16[256,2048]{1,0:T(8,128)(2,1)S(1)}, u32[]{:S(2)}, u32[]{:S(2)}) collective-permute-start(bf16[256,2048]{1,0:T(8,128)(2,1)S(1)} %shard_map.80), channel_id=1, source_target_pairs={{0,1},{1,0},{2,3},{3,2},{4,5},{5,4},{6,7},{7,6},{8,9},{9,8},{10,11... | collective-permute-start | bytes 3145736 | tf_op jit(solution)/shard_map/ppermute | solution.py:36
  65.4 6.5 %collective-permute-start.11 = (f32[128,768]{1,0:T(8,128)S(1)}, f32[128,768]{1,0:T(8,128)S(1)}, u32[]{:S(2)}, u32[]{:S(2)}) collective-permute-start(f32[128,768]{1,0:T(8,128)S(1)} %fusion.4), channel_id=1, source_target_pairs={{0,1},{1,0},{2,3},{3,2},{4,5},{5,4},{6,7},{7,6},{8,9},{9,8},{10,11... | collective-permute-start | bytes 1179656 | tf_op jit(solution)/shard_map/ppermute | solution.py:36
  65.5 12.9 %collective-permute-start.17 = (bf16[448,512]{1,0:T(8,128)(2,1)S(1)}, bf16[448,512]{1,0:T(8,128)(2,1)S(1)}, u32[]{:S(2)}, u32[]{:S(2)}) collective-permute-start(bf16[448,512]{1,0:T(8,128)(2,1)S(1)} %collective-permute-done.13.refs_1_.refs_10_), channel_id=1, source_target_pairs={{0,4},{1,5},{2,6},{3,7},{4,0},{5,1},{6,2},{7,3},{8,12},{9,13},{10,... | collective-permute-start | bytes 1376264 | tf_op jit(solution)/shard_map/ppermute | solution.py:36
  66.2 6.7 %copy-start.5 = (s32[8]{0:T(128)S(1)}, s32[8]{0:T(128)}, u32[]{:S(2)}) copy-start(s32[8]{0:T(128)} %refs_0_.5) | copy-start | bytes 100
  66.2 15.5 %collective-permute-start.7 = (f32[128,768]{1,0:T(8,128)S(1)}, f32[128,768]{1,0:T(8,128)S(1)}, u32[]{:S(2)}, u32[]{:S(2)}) collective-permute-start(f32[128,768]{1,0:T(8,128)S(1)} %fusion.3), channel_id=1, source_target_pairs={{0,1},{1,0},{2,3},{3,2},{4,5},{5,4},{6,7},{7,6},{8,9},{9,8},{10,11... | collective-permute-start | bytes 1179656 | tf_op jit(solution)/shard_map/ppermute | solution.py:36
  72.5 13.0 %collective-permute-start.12 = (bf16[128,768]{1,0:T(8,128)(2,1)S(1)}, bf16[128,768]{1,0:T(8,128)(2,1)S(1)}, u32[]{:S(2)}, u32[]{:S(2)}) collective-permute-start(bf16[128,768]{1,0:T(8,128)(2,1)S(1)} %fusion.1), channel_id=1, source_target_pairs={{0,2},{1,3},{2,0},{3,1},{4,6},{5,7},{6,4},{7,5},{8,10},{9,11},{10,... | collective-permute-start | bytes 589832 | tf_op jit(solution)/shard_map/ppermute | solution.py:36
  80.0 3.3 %collective-permute-start.18 = (f32[2,128,128]{2,1,0:T(8,128)S(1)}, f32[2,128,128]{2,1,0:T(8,128)S(1)}, u32[]{:S(2)}, u32[]{:S(2)}) collective-permute-start(f32[2,128,128]{2,1,0:T(8,128)S(1)} %get-tuple-element.32), channel_id=1, source_target_pairs={{0,1},{1,0},{2,3},{3,2},{4,5},{5,4},{6,7},{7,6},{8,9},{9,8},{10,11... | collective-permute-start | bytes 393224 | tf_op jit(solution)/shard_map/ppermute | solution.py:36
  81.1 9.5 %collective-permute-start.16 = (f32[256,768]{1,0:T(8,128)S(1)}, f32[256,768]{1,0:T(8,128)S(1)}, u32[]{:S(2)}, u32[]{:S(2)}) collective-permute-start(f32[256,768]{1,0:T(8,128)S(1)} %fusion.6), channel_id=1, source_target_pairs={{0,1},{1,0},{2,3},{3,2},{4,5},{5,4},{6,7},{7,6},{8,9},{9,8},{10,11... | collective-permute-start | bytes 2359304 | tf_op jit(solution)/shard_map/ppermute | solution.py:36
  82.2 8.3 %copy-start.1 = (bf16[16,64,768]{2,1,0:T(8,128)(2,1)S(1)}, bf16[16,64,768]{2,1,0:T(8,128)(2,1)}, u32[]{:S(2)}) copy-start(bf16[16,64,768]{2,1,0:T(8,128)(2,1)} %refs_9_.1) | copy-start | bytes 4718596
  82.3 7.6 %collective-permute-start.8 = (bf16[128,768]{1,0:T(8,128)(2,1)S(1)}, bf16[128,768]{1,0:T(8,128)(2,1)S(1)}, u32[]{:S(2)}, u32[]{:S(2)}) collective-permute-start(bf16[128,768]{1,0:T(8,128)(2,1)S(1)} %fusion), channel_id=1, source_target_pairs={{0,2},{1,3},{2,0},{3,1},{4,6},{5,7},{6,4},{7,5},{8,10},{9,11},{10,... | collective-permute-start | bytes 589832 | tf_op jit(solution)/shard_map/ppermute | solution.py:36
  83.4 7.2 %collective-permute-start.19 = (f32[1,128,128]{2,1,0:T(8,128)S(1)}, f32[1,128,128]{2,1,0:T(8,128)S(1)}, u32[]{:S(2)}, u32[]{:S(2)}) collective-permute-start(f32[1,128,128]{2,1,0:T(8,128)S(1)} %get-tuple-element.33), channel_id=1, source_target_pairs={{0,2},{1,3},{2,0},{3,1},{4,6},{5,7},{6,4},{7,5},{8,10},{9,11},{10,... | collective-permute-start | bytes 196616 | tf_op jit(solution)/shard_map/ppermute | solution.py:36
  (3 other events, 10.0 us)

commit v6 on v5

--- a/solution.py
+++ b/solution.py
@@ -13,7 +13,7 @@
 LAYER_CHIPS = 4
 VMEM_BYTES = 28 * 1024 * 1024
 CORE_FLOPS_PER_US = 1_153_500_000
-WAITS = {"far": 12, "keys": 0, "all": 5, "across": 0, "near": 0, "low": (5, 15)}
+WAITS = {"far": 20, "keys": 0, "all": 0, "across": 0, "near": 0, "low": (0, 5)}
 
 HBM = pl.BlockSpec(memory_space=pl.ANY)
 VMEM = pl.BlockSpec(memory_space=pltpu.VMEM)
@@ -47,14 +47,20 @@
     return pl.multiple_of((lax.axis_index("rep") ^ h) * part, part)
 
 
-def first_kernel(group, layers, splits, part, key, tokens, *refs):
-    keys, refs = refs[:splits], refs[splits:]
+def key_parts_kernel(splits, part, key, *refs):
+    outs, sems = refs[:splits], refs[splits]
+    pairs = [(key.at[pl.ds(part_start(h, part), part), :], outs[h]) for h in range(splits)]
+    for copy in run_copies(pairs, sems):
+        copy.wait()
+
+
+def token_pieces_kernel(group, layers, splits, part, tokens, *refs):
     outs, sems = refs[:-1], refs[-1]
     blocks = tokens.shape[0] // BLOCK
     depth = splits * part
     me = lax.axis_index("batch")
     layer, spot = me // group, me % group
-    pairs = [(key.at[pl.ds(part_start(h, part), part), :], keys[h]) for h in range(splits)]
+    pairs = []
     for s in reversed(range(group)):
         for t in range(layers):
             first = ((layer ^ t) * group + (spot ^ s)) * depth
@@ -254,7 +260,7 @@
         for ref in base_refs:
             total = total + ref[here, :]
         if far_refs:
-            total = total + far_refs[j][...].astype(jnp.float32)
+            total = total + far_refs[0][here, :].astype(jnp.float32)
         live = lax.broadcasted_iota(jnp.int32, total.shape, 0) < found[j][2]
         out[here, :] = jnp.where(live, total, 0.0).astype(jnp.bfloat16)
 
@@ -281,24 +287,31 @@
     lists = (request_block_list, request_adapter_index, request_tail_tokens)
     f32, bf16 = jnp.float32, jnp.bfloat16
 
+    if splits > 1:
+        key_parts = call(
+            functools.partial(key_parts_kernel, splits, part),
+            [jax.ShapeDtypeStruct((part, out_width), bf16)] * splits,
+            [HBM] * splits,
+            [HBM],
+            [pltpu.SemaphoreType.DMA((splits,))],
+            0,
+            4 * depth * out_width,
+        )(key_matrix)
+    else:
+        key_parts = [key_matrix]
     far_count = (group - 2) * local_blocks
     first = call(
-        functools.partial(first_kernel, group, layers, splits, part),
-        [jax.ShapeDtypeStruct((part, out_width), bf16)] * splits
-        + [jax.ShapeDtypeStruct((rows, held_width), bf16)] * 2
+        functools.partial(token_pieces_kernel, group, layers, splits, part),
+        [jax.ShapeDtypeStruct((rows, held_width), bf16)] * 2
         + [jax.ShapeDtypeStruct((BLOCK, held_width), bf16)] * far_count,
-        [HBM] * (splits + 2 + far_count),
-        [HBM] * 2,
-        [
-            pltpu.SemaphoreType.DMA(
-                (splits + (2 + far_count) * layers * splits,)
-            )
-        ],
+        [HBM] * (2 + far_count),
+        [HBM],
+        [pltpu.SemaphoreType.DMA(((2 + far_count * local_blocks) * layers * splits,))],
         0,
-        4 * (rows * width + depth * out_width),
-    )(key_matrix, tokens)
-    key_parts, first = first[:splits], first[splits:]
-
+        4 * rows * width,
+    )(tokens)
+
+    near = [first[0], swap(first[1], "batch", 1)]
     far = [list(first[2 + s * local_blocks :][:local_blocks]) for s in range(group - 2)]
     sent = []
     for j in range(local_blocks if far else 0):
@@ -312,7 +325,7 @@
     down = jnp.transpose(adapter_down_factors, (1, 2, 0))
     requests = request_adapter_index.shape[0]
     by_request = requests < adapters
-    shift = 1 if by_request and local_blocks * devices == 2 * MOST and layers > 1 else 0
+    shift = 1 if by_request and local_blocks * devices == 2 * MOST and layers == 4 else 0
     slots = requests - shift if by_request else adapters
     if by_request:
         across, down = call(
@@ -328,11 +341,11 @@
         down = down.reshape(slots * rank, depth)
         across = down
 
-    def over_layers(across, near):
+    def over_layers(own):
         bundles = []
         bit = layers // 2
         while bit:
-            moved = [([bit], swap(near if bundles else across, "batch", bit * group))]
+            moved = [([bit], swap(own, "batch", bit * group))]
             if bundles:
                 rest = [v for _, v in bundles]
                 rest = rest[0] if len(rest) == 1 else jnp.concatenate(rest, 0)
@@ -342,7 +355,7 @@
             bit //= 2
         return bundles
 
-    key_bundles = over_layers(key_parts[0], key_parts[0])
+    key_bundles = over_layers(key_parts[0])
     rows_of_key = {}
     for h in range(splits):
         rows_of_key[0, h] = (key_parts[h], 0, part)
@@ -351,36 +364,43 @@
             rows_of_key[t, 0] = (value, i * part, part)
     last_keys = [key_bundles[-1][1]]
     for h in range(1, splits):
-        for bundles in (key_bundles[:1], key_bundles[1:]):
+        for bundles in (key_bundles[:2], key_bundles[2:]):
             if not bundles:
                 continue
-            values = bundles[0][1]
-            if bundles is not key_bundles[:1] and len(bundles) > 1:
-                values = stack([[(v, 0, v.shape[0]) for _, v in bundles]], *last_keys, us=WAITS["keys"])[0]
-            last_keys = [values]
-            swapped = swap(values, "rep", h)
-            if len(bundles) == 1:
-                last_keys = [swapped]
+            if bundles[0] is key_bundles[0]:
+                values = stack([[(v, 0, v.shape[0]) for _, v in bundles]], near[1])[0]
+                swapped = swap(values, "rep", h)
+            else:
+                values = stack([[(v, 0, v.shape[0]) for _, v in bundles]], swapped, *sent, us=WAITS["keys"])[0]
+                swapped = swap(values, "rep", h)
+                last_keys = [values]
             for i, t in enumerate([t for ts, _ in bundles for t in ts]):
                 rows_of_key[t, h] = (swapped, i * part, part)
     keys = stack(
         [[rows_of_key[t, h] for t in range(layers) for h in range(splits)]], us=WAITS["all"]
     )[0]
 
-    across_sent = gate(across, *[v for _, v in key_bundles[:2]], us=WAITS["across"])
-    down_sent = gate(down, *last_keys, us=WAITS["near"])
-    down_bundles = over_layers(across_sent, down_sent)
-
-    near = [first[0], swap(gate(first[1], *[v for _, v in down_bundles[:2]]), "batch", 1)]
+    if layers == 4:
+        got = {}
+        got[2] = swap(gate(across, *[v for _, v in key_bundles[:2]], us=WAITS["across"]), "batch", 2 * group)
+        sent_last = gate(across, *last_keys, us=WAITS["near"])
+        got[3] = swap(sent_last, "batch", 3 * group)
+        sent_near = gate(down, got[2], sent_last)
+        got[1] = swap(sent_near, "batch", group)
+        down_bundles = [([t], got[t]) for t in (2, 1, 3)]
+    else:
+        down_bundles = over_layers(down)
 
     def base_of(value):
         return jnp.dot(value, keys, preferred_element_type=f32)
 
     fars = []
     if far:
+        sums = []
         for j in range(local_blocks):
             theirs = swap(base_of(far[1][j]), "batch", 1)
-            fars.append(swap((base_of(far[0][j]) + theirs).astype(bf16), "batch", 2))
+            sums.append((base_of(far[0][j]) + theirs).astype(bf16))
+        fars = [swap(jnp.concatenate(sums, 0), "batch", 2)]
     bases = [base_of(near[0]), swap(base_of(near[1]), "batch", 1)]
     tokens_here = near + [value for f in far for value in f]
 

time: 92.9 us -> 102 us (1.098)
  waiting for transfers between devices: 51.8 us -> 61.5 us
  local copies, waits for them, and re-layouts: 3.36 us -> 2.23 us
    ppermute x20 -> x19, waiting for transfers between devices: 51.8 us -> 61.5 us  [swap(): lax.ppermute(value, axis, [(i, i ^ bit) for i in range(lax.axis_size(axis...]
    unnamed x14, local copies, waits for them, and re-layouts: 3.35 us -> 2.22 us
    pallas_call x6 -> x7, Pallas kernels: 2.7 us -> 3.07 us  [stack(): call(functools.partial(stack_kernel, tuple(moves), len(values), count), o...]
    ppermute x20 -> x19, starting transfers between devices: 20.6 us -> 20.4 us  [swap(): lax.ppermute(value, axis, [(i, i ^ bit) for i in range(lax.axis_size(axis...]
  transfers between devices with their start and end apart: 20 -> 19, of which waited for: 9 -> 8; matrix products, arithmetic and copies ran while one was open for 5% -> 4% of each run, Pallas kernels for 9% -> 9%
where the time goes in v6:
time: 102 us
  waiting for transfers between devices  61.5 us (60%)
  starting transfers between devices  20.4 us (20%)
  Pallas kernels  12.9 us (13%)
  matrix products  4.31 us (4%)
  local copies, waits for them, and re-layouts  2.23 us (2%)
    ppermute x19, waiting for transfers between devices, swap(): lax.ppermute(value, axis, [(i, i ^ bit) for i in range(lax.axis_size(axis...  61.5 us
    ppermute x19, starting transfers between devices, swap(): lax.ppermute(value, axis, [(i, i ^ bit) for i in range(lax.axis_size(axis...  20.4 us
    pallas_call x2, Pallas kernels, low_call(): call(functools.partial(low_kernel, group, layers, rows, depth, rank, tupl...  4.78 us
    dot_general x6, matrix products, base_of(): return jnp.dot(value, keys, preferred_element_type=f32)  4.31 us
    pallas_call x7, Pallas kernels, stack(): call(functools.partial(stack_kernel, tuple(moves), len(values), count), o...  3.07 us
    unnamed x14, local copies, waits for them, and re-layouts  2.22 us
    pallas_call x1, Pallas kernels, shards(): call(functools.partial(final_kernel, rows, rank, len(bases), len(fars), l...  2.11 us
  transfers between devices with their start and end apart: 19, of which 8 were waited for; matrix products, arithmetic and copies ran while one was open for 4% of the time, Pallas kernels for 9%

profile of v6, /device:TPU:0, one launch (start us, length us, event | category | flops | bytes accessed | tf_op | source)
XLA Modules:
  0.0 101.7 jit_solution(10360987733570897906)
XLA Ops:
  0.0 2.2 %copy-done = bf16[256,8192]{1,0:T(8,128)(2,1)S(1)} copy-done((bf16[256,8192]{1,0:T(8,128)(2,1)S(1)}, bf16[256,8192]{1,0:T(8,128)(2,1)}, u32[]{:S(2)}) %copy-start) | copy-done | bytes 4194328
  2.2 1.5 %shard_map.74 = (bf16[256,2048]{1,0:T(8,128)(2,1)S(1)}, bf16[256,2048]{1,0:T(8,128)(2,1)S(1)}, bf16[128,2048]{1,0:T(8,128)(2,1)S(1)}, bf16[128,2048]{1,0:T(8,128...) custom-call(bf16[256,8192]{1,0:T(8,128)(2,1)S(1)} %copy-done), custom_call_target="tpu_custom_call" | custom-call | bytes 8388608 | tf_op jit(solution)/shard_map/pallas_call | solution.py:303
  4.2 2.6 %collective-permute-start.5 = (bf16[128,2048]{1,0:T(8,128)(2,1)S(1)}, bf16[128,2048]{1,0:T(8,128)(2,1)S(1)}, u32[]{:S(2)}, u32[]{:S(2)}) collective-permute-start(bf16[128,2048]{1,0:T(8,128)(2,1)S(1)} %get-tuple-element.24), channel_id=1, source_target_pairs={{0,2},{1,3},{2,0},{3,1},{4,6},{5,7},{6,4},{7,5},{8,10},{9,11},{10,... | collective-permute-start | bytes 1572872 | tf_op jit(solution)/shard_map/ppermute | solution.py:36
  7.3 2.9 %collective-permute-start.1 = (bf16[256,768]{1,0:T(8,128)(2,1)S(1)}, bf16[256,768]{1,0:T(8,128)(2,1)S(1)}, u32[]{:S(2)}, u32[]{:S(2)}) collective-permute-start(bf16[256,768]{1,0:T(8,128)(2,1)S(1)} %get-tuple-element.19.refs_0_), channel_id=1, source_target_pairs={{0,8},{1,9},{2,10},{3,11},{4,12},{5,13},{6,14},{7,15},{8,0},{9,1},... | collective-permute-start | bytes 1179656 | tf_op jit(solution)/shard_map/ppermute | solution.py:36
  10.2 1.6 %collective-permute-start = (bf16[256,768]{1,0:T(8,128)(2,1)S(1)}, bf16[256,768]{1,0:T(8,128)(2,1)S(1)}, u32[]{:S(2)}, u32[]{:S(2)}) collective-permute-start(bf16[256,768]{1,0:T(8,128)(2,1)S(1)} %get-tuple-element.19.refs_0_), channel_id=1, source_target_pairs={{0,4},{1,5},{2,6},{3,7},{4,0},{5,1},{6,2},{7,3},{8,12},{9,13},{10,... | collective-permute-start | bytes 1179656 | tf_op jit(solution)/shard_map/ppermute | solution.py:36
  11.7 1.1 %shard_map.79 = (bf16[448,512]{1,0:T(8,128)(2,1)S(1)}, bf16[448,512]{1,0:T(8,128)(2,1)S(1)}) custom-call(s32[8]{0:T(128)S(1)} %copy-done.4, bf16[16,64,512]{2,1,0:T(8,128)(2,1)S(1)} %bitcast.28), custom_call_target="tpu_custom_call" | custom-call | bytes 1835008 | tf_op jit(solution)/shard_map/pallas_call | solution.py:331
  12.8 15.5 %collective-permute-done.1.refs_0_.refs_4_.refs_1_ = bf16[256,768]{1,0:T(8,128)(2,1)S(1)} collective-permute-done((bf16[256,768]{1,0:T(8,128)(2,1)S(1)}, bf16[256,768]{1,0:T(8,128)(2,1)S(1)}, u32[]{:S(2)}, u32[]{:S(2)}) %collective-permute-start.1) | collective-permute-done | bytes 393248 | tf_op jit(solution)/shard_map/ppermute | solution.py:36
  28.8 1.4 %collective-permute-start.15 = (bf16[448,512]{1,0:T(8,128)(2,1)S(1)}, bf16[448,512]{1,0:T(8,128)(2,1)S(1)}, u32[]{:S(2)}, u32[]{:S(2)}) collective-permute-start(bf16[448,512]{1,0:T(8,128)(2,1)S(1)} %shard_map.81), channel_id=1, source_target_pairs={{0,8},{1,9},{2,10},{3,11},{4,12},{5,13},{6,14},{7,15},{8,0},{9,1},... | collective-permute-start | bytes 1376264 | tf_op jit(solution)/shard_map/ppermute | solution.py:36
  30.2 2.4 %collective-permute-start.4 = (bf16[256,768]{1,0:T(8,128)(2,1)S(1)}, bf16[256,768]{1,0:T(8,128)(2,1)S(1)}, u32[]{:S(2)}, u32[]{:S(2)}) collective-permute-start(bf16[256,768]{1,0:T(8,128)(2,1)S(1)} %collective-permute-done.1.refs_0_.refs_4_.refs_1_), channel_id=1, source_target_pairs={{0,4},{1,5},{2,6},{3,7},{4,0},{5,1},{6,2},{7,3},{8,12},{9,13},{10,... | collective-permute-start | bytes 1179656 | tf_op jit(solution)/shard_map/ppermute | solution.py:36
  33.1 1.6 %collective-permute-start.3 = (bf16[512,768]{1,0:T(8,128)(2,1)S(1)}, bf16[512,768]{1,0:T(8,128)(2,1)S(1)}, u32[]{:S(2)}, u32[]{:S(2)}) collective-permute-start(bf16[512,768]{1,0:T(8,128)(2,1)S(1)} %shard_map.75), channel_id=1, source_target_pairs={{0,16},{16,0},{1,17},{17,1},{2,18},{18,2},{3,19},{19,3},{4,20},{20... | collective-permute-start | bytes 2359304 | tf_op jit(solution)/shard_map/ppermute | solution.py:36
  34.7 13.5 %collective-permute-done.4.refs_0_.refs_6_ = bf16[256,768]{1,0:T(8,128)(2,1)S(1)} collective-permute-done((bf16[256,768]{1,0:T(8,128)(2,1)S(1)}, bf16[256,768]{1,0:T(8,128)(2,1)S(1)}, u32[]{:S(2)}, u32[]{:S(2)}) %collective-permute-start.4) | collective-permute-done | bytes 393248 | tf_op jit(solution)/shard_map/ppermute | solution.py:36
  48.2 3.9 %collective-permute-done.3.refs_1_.refs_3_.refs_5_ = bf16[512,768]{1,0:T(8,128)(2,1)S(1)} collective-permute-done((bf16[512,768]{1,0:T(8,128)(2,1)S(1)}, bf16[512,768]{1,0:T(8,128)(2,1)S(1)}, u32[]{:S(2)}, u32[]{:S(2)}) %collective-permute-start.3) | collective-permute-done | bytes 786464 | tf_op jit(solution)/shard_map/ppermute | solution.py:36
  52.3 1.6 %collective-permute-start.7 = (bf16[256,768]{1,0:T(8,128)(2,1)S(1)}, bf16[256,768]{1,0:T(8,128)(2,1)S(1)}, u32[]{:S(2)}, u32[]{:S(2)}) collective-permute-start(bf16[256,768]{1,0:T(8,128)(2,1)S(1)} %shard_map.77.refs_1_), channel_id=1, source_target_pairs={{0,16},{16,0},{1,17},{17,1},{2,18},{18,2},{3,19},{19,3},{4,20},{20... | collective-permute-start | bytes 1179656 | tf_op jit(solution)/shard_map/ppermute | solution.py:36
  53.8 1.5 %collective-permute-start.9 = (bf16[128,2048]{1,0:T(8,128)(2,1)S(1)}, bf16[128,2048]{1,0:T(8,128)(2,1)S(1)}, u32[]{:S(2)}, u32[]{:S(2)}) collective-permute-start(bf16[128,2048]{1,0:T(8,128)(2,1)S(1)} %get-tuple-element.26.refs_2_), channel_id=1, source_target_pairs={{0,2},{1,3},{2,0},{3,1},{4,6},{5,7},{6,4},{7,5},{8,10},{9,11},{10,... | collective-permute-start | bytes 1572872 | tf_op jit(solution)/shard_map/ppermute | solution.py:36
  57.0 4.9 %collective-permute-done.7.refs_7_ = bf16[256,768]{1,0:T(8,128)(2,1)S(1)} collective-permute-done((bf16[256,768]{1,0:T(8,128)(2,1)S(1)}, bf16[256,768]{1,0:T(8,128)(2,1)S(1)}, u32[]{:S(2)}, u32[]{:S(2)}) %collective-permute-start.7) | collective-permute-done | bytes 393248 | tf_op jit(solution)/shard_map/ppermute | solution.py:36
  61.9 1.6 %shard_map.78 = bf16[2048,768]{1,0:T(8,128)(2,1)S(1)} custom-call(bf16[256,768]{1,0:T(8,128)(2,1)S(1)} %get-tuple-element.19.refs_0_, bf16[256,768]{1,0:T(8,128)(2,1)S(1)} %get-tuple-element.20.refs_1_, bf16[256,768]{1,0:T(8,128)(2,1)S(1)} %collective-permute-done.refs_1_.refs_2_, bf16[512,768]{1,0:T(8,128)(2,1)S(1)} %collective-permute-done.3.refs_1_.refs_3_.refs_5_, ...), custom_call_target="tpu_custom_call" | custom-call | tf_op jit(solution)/shard_map/pallas_call | solution.py:104
  64.2 3.8 %collective-permute-done.10.refs_8_ = bf16[128,2048]{1,0:T(8,128)(2,1)S(1)} collective-permute-done((bf16[128,2048]{1,0:T(8,128)(2,1)S(1)}, bf16[128,2048]{1,0:T(8,128)(2,1)S(1)}, u32[]{:S(2)}, u32[]{:S(2)}) %collective-permute-start.10) | collective-permute-done | bytes 524320 | tf_op jit(solution)/shard_map/ppermute | solution.py:36
  68.9 10.4 %collective-permute-done.9.refs_6_ = bf16[128,2048]{1,0:T(8,128)(2,1)S(1)} collective-permute-done((bf16[128,2048]{1,0:T(8,128)(2,1)S(1)}, bf16[128,2048]{1,0:T(8,128)(2,1)S(1)}, u32[]{:S(2)}, u32[]{:S(2)}) %collective-permute-start.9) | collective-permute-done | bytes 524320 | tf_op jit(solution)/shard_map/ppermute | solution.py:36
  79.3 3.2 %shard_map.83.refs_10_ = f32[2,512,256]{2,1,0:T(8,128)S(1)} custom-call(s32[8]{0:T(128)S(1)} %copy-done.5, s32[8]{0:T(128)S(1)} %copy-done.4, s32[8]{0:T(128)S(1)} %copy-done.6, bf16[256,2048]{1,0:T(8,128)(2,1)S(1)} %get-tuple-element.28.refs_3_, bf16[256,2048]{1,0:T(8,128)(2,1)S(1)} %collective-permute-done.2.refs_2_.refs_4_, ...), custom_call_target="tpu_custom_call" | custom-call | tf_op jit(solution)/shard_map/pallas_call | solution.py:418
  82.5 1.6 %shard_map.84 = (f32[2,128,128]{2,1,0:T(8,128)S(1)}, f32[2,128,128]{2,1,0:T(8,128)S(1)}) custom-call(s32[8]{0:T(128)S(1)} %copy-done.5, s32[8]{0:T(128)S(1)} %copy-done.4, s32[8]{0:T(128)S(1)} %copy-done.6, bf16[256,2048]{1,0:T(8,128)(2,1)S(1)} %get-tuple-element.28.refs_3_, bf16[256,2048]{1,0:T(8,128)(2,1)S(1)} %collective-permute-done.2.refs_2_.refs_4_, ...), custom_call_target="tpu_custom_call" | custom-call | flops 5767499776 | tf_op jit(solution)/shard_map/pallas_call | solution.py:418
  84.2 1.0 convolution_bitcast_fusion
  87.5 1.7 %collective-permute-start.18 = (f32[1,128,128]{2,1,0:T(8,128)S(1)}, f32[1,128,128]{2,1,0:T(8,128)S(1)}, u32[]{:S(2)}, u32[]{:S(2)}) collective-permute-start(f32[1,128,128]{2,1,0:T(8,128)S(1)} %get-tuple-element.33), channel_id=1, source_target_pairs={{0,2},{1,3},{2,0},{3,1},{4,6},{5,7},{6,4},{7,5},{8,10},{9,11},{10,... | collective-permute-start | bytes 196616 | tf_op jit(solution)/shard_map/ppermute | solution.py:36
  90.2 9.4 %collective-permute-done.18 = f32[1,128,128]{2,1,0:T(8,128)S(1)} collective-permute-done((f32[1,128,128]{2,1,0:T(8,128)S(1)}, f32[1,128,128]{2,1,0:T(8,128)S(1)}, u32[]{:S(2)}, u32[]{:S(2)}) %collective-permute-start.18) | collective-permute-done | bytes 65568 | tf_op jit(solution)/shard_map/ppermute | solution.py:36
  99.6 2.1 %shard_map.85 = bf16[256,768]{1,0:T(8,128)(2,1)} custom-call(s32[8]{0:T(128)S(1)} %copy-done.5, s32[8]{0:T(128)S(1)} %copy-done.4, s32[8]{0:T(128)S(1)} %copy-done.6, bf16[256,768]{1,0:T(8,128)(2,1)S(1)} %collective-permute-done.12.refs_3_, f32[256,768]{1,0:T(8,128)S(1)} %convolution_bitcast_fusion.1.refs_4_, ...), custom_call_target="tpu_custom_call" | custom-call | flops 25165824 | bytes 1572864 | tf_op jit(solution)/shard_map/pallas_call | solution.py:438
  (50 shorter events, 8.6 us)
Async XLA Ops:
  2.2 9.6 %copy-start.2 = (bf16[512,16,64]{0,2,1:T(8,128)(2,1)S(1)}, bf16[512,16,64]{0,2,1:T(8,128)(2,1)}, u32[]{:S(2)}) copy-start(bf16[512,16,64]{0,2,1:T(8,128)(2,1)} %param.9) | copy-start | bytes 3145732
  2.2 9.6 %copy-start.4 = (s32[8]{0:T(128)S(1)}, s32[8]{0:T(128)}, u32[]{:S(2)}) copy-start(s32[8]{0:T(128)} %refs_1_.5) | copy-start | bytes 100
  3.7 29.0 %collective-permute-start.2 = (bf16[256,2048]{1,0:T(8,128)(2,1)S(1)}, bf16[256,2048]{1,0:T(8,128)(2,1)S(1)}, u32[]{:S(2)}, u32[]{:S(2)}) collective-permute-start(bf16[256,2048]{1,0:T(8,128)(2,1)S(1)} %get-tuple-element.21), channel_id=1, source_target_pairs={{0,1},{1,0},{2,3},{3,2},{4,5},{5,4},{6,7},{7,6},{8,9},{9,8},{10,11... | collective-permute-start | bytes 3145736 | tf_op jit(solution)/shard_map/ppermute | solution.py:36
  4.2 30.4 %collective-permute-start.5 = (bf16[128,2048]{1,0:T(8,128)(2,1)S(1)}, bf16[128,2048]{1,0:T(8,128)(2,1)S(1)}, u32[]{:S(2)}, u32[]{:S(2)}) collective-permute-start(bf16[128,2048]{1,0:T(8,128)(2,1)S(1)} %get-tuple-element.24), channel_id=1, source_target_pairs={{0,2},{1,3},{2,0},{3,1},{4,6},{5,7},{6,4},{7,5},{8,10},{9,11},{10,... | collective-permute-start | bytes 1572872 | tf_op jit(solution)/shard_map/ppermute | solution.py:36
  6.8 27.8 %collective-permute-start.6 = (bf16[128,2048]{1,0:T(8,128)(2,1)S(1)}, bf16[128,2048]{1,0:T(8,128)(2,1)S(1)}, u32[]{:S(2)}, u32[]{:S(2)}) collective-permute-start(bf16[128,2048]{1,0:T(8,128)(2,1)S(1)} %get-tuple-element.25), channel_id=1, source_target_pairs={{0,3},{1,2},{2,1},{3,0},{4,7},{5,6},{6,5},{7,4},{8,11},{9,10},{10,... | collective-permute-start | bytes 1572872 | tf_op jit(solution)/shard_map/ppermute | solution.py:36
  7.3 21.0 %collective-permute-start.1 = (bf16[256,768]{1,0:T(8,128)(2,1)S(1)}, bf16[256,768]{1,0:T(8,128)(2,1)S(1)}, u32[]{:S(2)}, u32[]{:S(2)}) collective-permute-start(bf16[256,768]{1,0:T(8,128)(2,1)S(1)} %get-tuple-element.19.refs_0_), channel_id=1, source_target_pairs={{0,8},{1,9},{2,10},{3,11},{4,12},{5,13},{6,14},{7,15},{8,0},{9,1},... | collective-permute-start | bytes 1179656 | tf_op jit(solution)/shard_map/ppermute | solution.py:36
  10.2 18.3 %collective-permute-start = (bf16[256,768]{1,0:T(8,128)(2,1)S(1)}, bf16[256,768]{1,0:T(8,128)(2,1)S(1)}, u32[]{:S(2)}, u32[]{:S(2)}) collective-permute-start(bf16[256,768]{1,0:T(8,128)(2,1)S(1)} %get-tuple-element.19.refs_0_), channel_id=1, source_target_pairs={{0,4},{1,5},{2,6},{3,7},{4,0},{5,1},{6,2},{7,3},{8,12},{9,13},{10,... | collective-permute-start | bytes 1179656 | tf_op jit(solution)/shard_map/ppermute | solution.py:36
  28.8 27.0 %collective-permute-start.15 = (bf16[448,512]{1,0:T(8,128)(2,1)S(1)}, bf16[448,512]{1,0:T(8,128)(2,1)S(1)}, u32[]{:S(2)}, u32[]{:S(2)}) collective-permute-start(bf16[448,512]{1,0:T(8,128)(2,1)S(1)} %shard_map.81), channel_id=1, source_target_pairs={{0,8},{1,9},{2,10},{3,11},{4,12},{5,13},{6,14},{7,15},{8,0},{9,1},... | collective-permute-start | bytes 1376264 | tf_op jit(solution)/shard_map/ppermute | solution.py:36
  30.2 18.0 %collective-permute-start.4 = (bf16[256,768]{1,0:T(8,128)(2,1)S(1)}, bf16[256,768]{1,0:T(8,128)(2,1)S(1)}, u32[]{:S(2)}, u32[]{:S(2)}) collective-permute-start(bf16[256,768]{1,0:T(8,128)(2,1)S(1)} %collective-permute-done.1.refs_0_.refs_4_.refs_1_), channel_id=1, source_target_pairs={{0,4},{1,5},{2,6},{3,7},{4,0},{5,1},{6,2},{7,3},{8,12},{9,13},{10,... | collective-permute-start | bytes 1179656 | tf_op jit(solution)/shard_map/ppermute | solution.py:36
  33.1 19.0 %collective-permute-start.3 = (bf16[512,768]{1,0:T(8,128)(2,1)S(1)}, bf16[512,768]{1,0:T(8,128)(2,1)S(1)}, u32[]{:S(2)}, u32[]{:S(2)}) collective-permute-start(bf16[512,768]{1,0:T(8,128)(2,1)S(1)} %shard_map.75), channel_id=1, source_target_pairs={{0,16},{16,0},{1,17},{17,1},{2,18},{18,2},{3,19},{19,3},{4,20},{20... | collective-permute-start | bytes 2359304 | tf_op jit(solution)/shard_map/ppermute | solution.py:36
  52.3 9.7 %collective-permute-start.7 = (bf16[256,768]{1,0:T(8,128)(2,1)S(1)}, bf16[256,768]{1,0:T(8,128)(2,1)S(1)}, u32[]{:S(2)}, u32[]{:S(2)}) collective-permute-start(bf16[256,768]{1,0:T(8,128)(2,1)S(1)} %shard_map.77.refs_1_), channel_id=1, source_target_pairs={{0,16},{16,0},{1,17},{17,1},{2,18},{18,2},{3,19},{19,3},{4,20},{20... | collective-permute-start | bytes 1179656 | tf_op jit(solution)/shard_map/ppermute | solution.py:36
  53.8 14.2 %collective-permute-start.10 = (bf16[128,2048]{1,0:T(8,128)(2,1)S(1)}, bf16[128,2048]{1,0:T(8,128)(2,1)S(1)}, u32[]{:S(2)}, u32[]{:S(2)}) collective-permute-start(bf16[128,2048]{1,0:T(8,128)(2,1)S(1)} %get-tuple-element.27.refs_3_), channel_id=1, source_target_pairs={{0,3},{1,2},{2,1},{3,0},{4,7},{5,6},{6,5},{7,4},{8,11},{9,10},{10,... | collective-permute-start | bytes 1572872 | tf_op jit(solution)/shard_map/ppermute | solution.py:36
  53.8 25.5 %collective-permute-start.9 = (bf16[128,2048]{1,0:T(8,128)(2,1)S(1)}, bf16[128,2048]{1,0:T(8,128)(2,1)S(1)}, u32[]{:S(2)}, u32[]{:S(2)}) collective-permute-start(bf16[128,2048]{1,0:T(8,128)(2,1)S(1)} %get-tuple-element.26.refs_2_), channel_id=1, source_target_pairs={{0,2},{1,3},{2,0},{3,1},{4,6},{5,7},{6,4},{7,5},{8,10},{9,11},{10,... | collective-permute-start | bytes 1572872 | tf_op jit(solution)/shard_map/ppermute | solution.py:36
  55.7 26.9 %collective-permute-start.14 = (bf16[448,512]{1,0:T(8,128)(2,1)S(1)}, bf16[448,512]{1,0:T(8,128)(2,1)S(1)}, u32[]{:S(2)}, u32[]{:S(2)}) collective-permute-start(bf16[448,512]{1,0:T(8,128)(2,1)S(1)} %shard_map.80.refs_2_), channel_id=1, source_target_pairs={{0,12},{1,13},{2,14},{3,15},{4,8},{5,9},{6,10},{7,11},{8,4},{9,5},... | collective-permute-start | bytes 1376264 | tf_op jit(solution)/shard_map/ppermute | solution.py:36
  56.1 23.2 %collective-permute-start.16 = (bf16[448,512]{1,0:T(8,128)(2,1)S(1)}, bf16[448,512]{1,0:T(8,128)(2,1)S(1)}, u32[]{:S(2)}, u32[]{:S(2)}) collective-permute-start(bf16[448,512]{1,0:T(8,128)(2,1)S(1)} %shard_map.82), channel_id=1, source_target_pairs={{0,4},{1,5},{2,6},{3,7},{4,0},{5,1},{6,2},{7,3},{8,12},{9,13},{10,... | collective-permute-start | bytes 1376264 | tf_op jit(solution)/shard_map/ppermute | solution.py:36
  63.5 15.8 %copy-start.5 = (s32[8]{0:T(128)S(1)}, s32[8]{0:T(128)}, u32[]{:S(2)}) copy-start(s32[8]{0:T(128)} %refs_0_.5) | copy-start | bytes 100
  63.5 15.8 %copy-start.6 = (s32[8]{0:T(128)S(1)}, s32[8]{0:T(128)}, u32[]{:S(2)}) copy-start(s32[8]{0:T(128)} %refs_2_.5) | copy-start | bytes 100
  64.1 21.6 %collective-permute-start.8 = (f32[128,768]{1,0:T(8,128)S(1)}, f32[128,768]{1,0:T(8,128)S(1)}, u32[]{:S(2)}, u32[]{:S(2)}) collective-permute-start(f32[128,768]{1,0:T(8,128)S(1)} %convolution_bitcast_fusion.2), channel_id=1, source_target_pairs={{0,1},{1,0},{2,3},{3,2},{4,5},{5,4},{6,7},{7,6},{8,9},{9,8},{10,11... | collective-permute-start | bytes 1179656 | tf_op jit(solution)/shard_map/ppermute | solution.py:36
  68.6 17.8 %collective-permute-start.11 = (f32[128,768]{1,0:T(8,128)S(1)}, f32[128,768]{1,0:T(8,128)S(1)}, u32[]{:S(2)}, u32[]{:S(2)}) collective-permute-start(f32[128,768]{1,0:T(8,128)S(1)} %fusion.4), channel_id=1, source_target_pairs={{0,1},{1,0},{2,3},{3,2},{4,5},{5,4},{6,7},{7,6},{8,9},{9,8},{10,11... | collective-permute-start | bytes 1179656 | tf_op jit(solution)/shard_map/ppermute | solution.py:36
  84.1 1.6 %collective-permute-start.17 = (f32[2,128,128]{2,1,0:T(8,128)S(1)}, f32[2,128,128]{2,1,0:T(8,128)S(1)}, u32[]{:S(2)}, u32[]{:S(2)}) collective-permute-start(f32[2,128,128]{2,1,0:T(8,128)S(1)} %get-tuple-element.32), channel_id=1, source_target_pairs={{0,1},{1,0},{2,3},{3,2},{4,5},{5,4},{6,7},{7,6},{8,9},{9,8},{10,11... | collective-permute-start | bytes 393224 | tf_op jit(solution)/shard_map/ppermute | solution.py:36
  85.2 14.4 %collective-permute-start.13 = (f32[256,768]{1,0:T(8,128)S(1)}, f32[256,768]{1,0:T(8,128)S(1)}, u32[]{:S(2)}, u32[]{:S(2)}) collective-permute-start(f32[256,768]{1,0:T(8,128)S(1)} %convolution_bitcast_fusion), channel_id=1, source_target_pairs={{0,1},{1,0},{2,3},{3,2},{4,5},{5,4},{6,7},{7,6},{8,9},{9,8},{10,11... | collective-permute-start | bytes 2359304 | tf_op jit(solution)/shard_map/ppermute | solution.py:36
  87.0 12.6 %copy-start.1 = (bf16[16,64,768]{2,1,0:T(8,128)(2,1)S(1)}, bf16[16,64,768]{2,1,0:T(8,128)(2,1)}, u32[]{:S(2)}) copy-start(bf16[16,64,768]{2,1,0:T(8,128)(2,1)} %refs_8_.1) | copy-start | bytes 4718596
  87.0 12.5 %collective-permute-start.12 = (bf16[256,768]{1,0:T(8,128)(2,1)S(1)}, bf16[256,768]{1,0:T(8,128)(2,1)S(1)}, u32[]{:S(2)}, u32[]{:S(2)}) collective-permute-start(bf16[256,768]{1,0:T(8,128)(2,1)S(1)} %pad_maximum_fusion), channel_id=1, source_target_pairs={{0,2},{1,3},{2,0},{3,1},{4,6},{5,7},{6,4},{7,5},{8,10},{9,11},{10,... | collective-permute-start | bytes 1179656 | tf_op jit(solution)/shard_map/ppermute | solution.py:36
  87.5 12.1 %collective-permute-start.18 = (f32[1,128,128]{2,1,0:T(8,128)S(1)}, f32[1,128,128]{2,1,0:T(8,128)S(1)}, u32[]{:S(2)}, u32[]{:S(2)}) collective-permute-start(f32[1,128,128]{2,1,0:T(8,128)S(1)} %get-tuple-element.33), channel_id=1, source_target_pairs={{0,2},{1,3},{2,0},{3,1},{4,6},{5,7},{6,4},{7,5},{8,10},{9,11},{10,... | collective-permute-start | bytes 196616 | tf_op jit(solution)/shard_map/ppermute | solution.py:36
  (2 other events, 6.9 us)

commit v7 on v6

--- a/solution.py
+++ b/solution.py
@@ -13,7 +13,7 @@
 LAYER_CHIPS = 4
 VMEM_BYTES = 28 * 1024 * 1024
 CORE_FLOPS_PER_US = 1_153_500_000
-WAITS = {"far": 20, "keys": 0, "all": 0, "across": 0, "near": 0, "low": (0, 5)}
+PHASES = (7, 6, 3)
 
 HBM = pl.BlockSpec(memory_space=pl.ANY)
 VMEM = pl.BlockSpec(memory_space=pltpu.VMEM)
@@ -54,9 +54,8 @@
         copy.wait()
 
 
-def token_pieces_kernel(group, layers, splits, part, tokens, *refs):
+def token_pieces_kernel(group, layers, splits, part, chunks, tokens, *refs):
     outs, sems = refs[:-1], refs[-1]
-    blocks = tokens.shape[0] // BLOCK
     depth = splits * part
     me = lax.axis_index("batch")
     layer, spot = me // group, me % group
@@ -71,11 +70,11 @@
                 if s < 2:
                     pairs.append((tokens.at[:, pl.ds(start, part)], outs[s].at[:, to]))
                     continue
-                for j in range(blocks):
+                for i, (row, deep) in enumerate(chunks):
                     pairs.append(
                         (
-                            tokens.at[pl.ds(j * BLOCK, BLOCK), pl.ds(start, part)],
-                            outs[2 + (s - 2) * blocks + j].at[:, to],
+                            tokens.at[pl.ds(row, deep), pl.ds(start, part)],
+                            outs[2 + (s - 2) * len(chunks) + i].at[:, to],
                         )
                     )
     for copy in run_copies(pairs, sems):
@@ -150,19 +149,12 @@
     return owner, adapter, limit
 
 
-def token_places(group, rows):
-    near = [(s * rows, rows) for s in range(min(group, 2))]
-    far = [(row, BLOCK) for row in range(2 * rows, group * rows, BLOCK)]
-    return near + far
-
-
 def low_kernel(
     group, layers, rows, depth, rank, entries, count, by_request, shift, has_sum, last, *refs
 ):
     lists, refs = refs[:3], refs[3:]
-    places = token_places(group, rows)
-    toks, refs = refs[: len(places)], refs[len(places) :]
-    arrays, refs = refs[:count], refs[count:]
+    toks, refs = refs[:group], refs[group:]
+    arrays, refs = refs[: len(count)], refs[len(count) :]
     if has_sum:
         before, refs = refs[0], refs[1:]
     if last:
@@ -170,7 +162,8 @@
     else:
         after, refs = refs[0], refs[1:]
     held, refs = refs[0], refs[1:]
-    downs, refs = refs[:count], refs[count:]
+    buffers = count[-1][0] + 1
+    downs, refs = refs[:buffers], refs[buffers:]
     tok_sems, sems = refs
     local_blocks = rows // BLOCK
     me = lax.axis_index("batch")
@@ -179,14 +172,20 @@
     started = {}
     for n, (t, a, _) in enumerate(entries):
         if a not in started:
-            started[a] = pltpu.make_async_copy(arrays[a], downs[a], sems.at[a])
-            started[a].start()
+            started[a], to = [], 0
+            for i, (buffer, tall) in enumerate(count):
+                if buffer != a:
+                    continue
+                copy = pltpu.make_async_copy(arrays[i], downs[a].at[pl.ds(to, tall), :], sems.at[i])
+                copy.start()
+                started[a].append(copy)
+                to += tall
         first[t] = []
-        for i, (to, deep) in enumerate(places):
+        for s in range(group):
             copy = pltpu.make_async_copy(
-                toks[i].at[:, pl.ds(t * depth, depth)],
-                held.at[pl.ds(to, deep), pl.ds(n * depth, depth)],
-                tok_sems.at[i, n],
+                toks[s].at[:, pl.ds(t * depth, depth)],
+                held.at[pl.ds(s * rows, rows), pl.ds(n * depth, depth)],
+                tok_sems.at[s, n],
             )
             copy.start()
             first[t].append(copy)
@@ -203,7 +202,8 @@
         for copy in first[t]:
             copy.wait()
         if a not in ready:
-            started[a].wait()
+            for copy in started[a]:
+                copy.wait()
             ready.add(a)
         for p in range(group // 2):
             chosen = jnp.concatenate(
@@ -260,7 +260,7 @@
         for ref in base_refs:
             total = total + ref[here, :]
         if far_refs:
-            total = total + far_refs[0][here, :].astype(jnp.float32)
+            total = total + far_refs[j][...].astype(jnp.float32)
         live = lax.broadcasted_iota(jnp.int32, total.shape, 0) < found[j][2]
         out[here, :] = jnp.where(live, total, 0.0).astype(jnp.bfloat16)
 
@@ -299,33 +299,34 @@
         )(key_matrix)
     else:
         key_parts = [key_matrix]
-    far_count = (group - 2) * local_blocks
-    first = call(
-        functools.partial(token_pieces_kernel, group, layers, splits, part),
+    chunks = [
+        (sum(PHASES[:i]) * rows // sum(PHASES), PHASES[i] * rows // sum(PHASES))
+        for i in range(len(PHASES) if group > 2 else 0)
+    ]
+    cut = call(
+        functools.partial(token_pieces_kernel, group, layers, splits, part, chunks),
         [jax.ShapeDtypeStruct((rows, held_width), bf16)] * 2
-        + [jax.ShapeDtypeStruct((BLOCK, held_width), bf16)] * far_count,
-        [HBM] * (2 + far_count),
+        + [jax.ShapeDtypeStruct((deep, held_width), bf16) for _, deep in chunks] * (group - 2),
+        [HBM] * (2 + (group - 2) * len(chunks)),
         [HBM],
-        [pltpu.SemaphoreType.DMA(((2 + far_count * local_blocks) * layers * splits,))],
+        [pltpu.SemaphoreType.DMA(((2 + (group - 2) * len(chunks)) * layers * splits,))],
         0,
         4 * rows * width,
     )(tokens)
-
-    near = [first[0], swap(first[1], "batch", 1)]
-    far = [list(first[2 + s * local_blocks :][:local_blocks]) for s in range(group - 2)]
-    sent = []
-    for j in range(local_blocks if far else 0):
-        if j:
-            sent = stack([[(f[j], 0, BLOCK)] for f in far], *[f[j - 1] for f in far], us=WAITS["far"])
-        else:
-            sent = [f[j] for f in far]
-        for s, f in enumerate(far):
-            f[j] = swap(sent[s], "batch", 2 + s)
+    far = [list(cut[2 + s * len(chunks) :][: len(chunks)]) for s in range(group - 2)]
+
+    def cross(i, values):
+        for s, value in enumerate(values):
+            far[s][i] = swap(value, "batch", 2 + s)
+        return [f[i] for f in far]
+
+    def whole(value):
+        return [(value, 0, value.shape[0])]
 
     down = jnp.transpose(adapter_down_factors, (1, 2, 0))
     requests = request_adapter_index.shape[0]
     by_request = requests < adapters
-    shift = 1 if by_request and local_blocks * devices == 2 * MOST and layers == 4 else 0
+    shift = 1 if by_request and local_blocks * devices == 2 * MOST and far and splits == 2 and layers == 4 else 0
     slots = requests - shift if by_request else adapters
     if by_request:
         across, down = call(
@@ -355,57 +356,83 @@
             bit //= 2
         return bundles
 
-    key_bundles = over_layers(key_parts[0])
     rows_of_key = {}
     for h in range(splits):
         rows_of_key[0, h] = (key_parts[h], 0, part)
-    for ts, value in key_bundles:
-        for i, t in enumerate(ts):
-            rows_of_key[t, 0] = (value, i * part, part)
-    last_keys = [key_bundles[-1][1]]
-    for h in range(1, splits):
-        for bundles in (key_bundles[:2], key_bundles[2:]):
-            if not bundles:
-                continue
-            if bundles[0] is key_bundles[0]:
-                values = stack([[(v, 0, v.shape[0]) for _, v in bundles]], near[1])[0]
-                swapped = swap(values, "rep", h)
-            else:
-                values = stack([[(v, 0, v.shape[0]) for _, v in bundles]], swapped, *sent, us=WAITS["keys"])[0]
-                swapped = swap(values, "rep", h)
-                last_keys = [values]
-            for i, t in enumerate([t for ts, _ in bundles for t in ts]):
-                rows_of_key[t, h] = (swapped, i * part, part)
-    keys = stack(
-        [[rows_of_key[t, h] for t in range(layers) for h in range(splits)]], us=WAITS["all"]
-    )[0]
-
-    if layers == 4:
-        got = {}
-        got[2] = swap(gate(across, *[v for _, v in key_bundles[:2]], us=WAITS["across"]), "batch", 2 * group)
-        sent_last = gate(across, *last_keys, us=WAITS["near"])
-        got[3] = swap(sent_last, "batch", 3 * group)
-        sent_near = gate(down, got[2], sent_last)
-        got[1] = swap(sent_near, "batch", group)
-        down_bundles = [([t], got[t]) for t in (2, 1, 3)]
+    other = swap(cut[1], "batch", 1)
+    if layers == 4 and splits == 2 and far:
+        keys_far = swap(key_parts[0], "batch", 2 * group)
+        keys_near = swap(key_parts[0], "batch", group)
+        tokens_here = cross(0, [f[0] for f in far])
+        opened = stack(
+            [whole(keys_far) + whole(keys_near), whole(across)] + [whole(f[1]) for f in far],
+            other,
+            *tokens_here,
+        )
+        keys_last = swap(keys_far, "batch", group)
+        halves = swap(opened[0], "rep", 1)
+        downs_far = swap(opened[1], "batch", 2 * group)
+        tokens_here = cross(1, opened[2:])
+        cut_at = (slots + 1) // 2 * rank
+        parts_of = [(0, cut_at), (cut_at, slots * rank - cut_at)]
+        opened = stack(
+            [[(v, *parts_of[0])] for v in (across, down)] + [whole(f[2]) for f in far],
+            keys_last,
+            halves,
+            downs_far,
+            *tokens_here,
+        )
+        downs_last = [swap(opened[0], "batch", 3 * group)]
+        downs_near = [swap(opened[1], "batch", group)]
+        cross(2, opened[2:])
+        halves_last = swap(keys_last, "rep", 1)
+        rows_of_key[2, 0], rows_of_key[1, 0] = whole(keys_far)[0], whole(keys_near)[0]
+        rows_of_key[3, 0], rows_of_key[3, 1] = whole(keys_last)[0], whole(halves_last)[0]
+        rows_of_key[2, 1], rows_of_key[1, 1] = (halves, 0, part), (halves, part, part)
+        opened = stack(
+            [[(v, *parts_of[1])] for v in (across, down)]
+            + [[rows_of_key[t, h] for t in range(layers) for h in range(splits)]]
+            + [sum([whole(value) for value in f], []) for f in far],
+            downs_last[0],
+            downs_near[0],
+        )
+        downs_last.append(swap(opened[0], "batch", 3 * group))
+        downs_near.append(swap(opened[1], "batch", group))
+        keys, pieces = opened[2], [cut[0], other, *opened[3:]]
+        down_bundles = [([2], [downs_far]), ([1], downs_near), ([3], downs_last)]
     else:
-        down_bundles = over_layers(down)
+        for f in range(len(chunks)):
+            cross(f, [values[f] for values in far])
+        for ts, value in over_layers(key_parts[0]):
+            for i, t in enumerate(ts):
+                rows_of_key[t, 0] = (value, i * part, part)
+            for h in range(1, splits):
+                swapped = swap(value, "rep", h)
+                for i, t in enumerate(ts):
+                    rows_of_key[t, h] = (swapped, i * part, part)
+        down_bundles = [(ts, [value]) for ts, value in over_layers(down)]
+        keys = stack([[rows_of_key[t, h] for t in range(layers) for h in range(splits)]])[0]
+        pieces = [cut[0], other]
+        if far:
+            pieces += stack([sum([whole(value) for value in f], []) for f in far])
 
     def base_of(value):
         return jnp.dot(value, keys, preferred_element_type=f32)
 
+    parts = [base_of(value) for value in pieces]
+    bases = [parts[0], swap(parts[1], "batch", 1)]
     fars = []
-    if far:
-        sums = []
+    if group > 2:
+        theirs = swap(parts[3], "batch", 1)
         for j in range(local_blocks):
-            theirs = swap(base_of(far[1][j]), "batch", 1)
-            sums.append((base_of(far[0][j]) + theirs).astype(bf16))
-        fars = [swap(jnp.concatenate(sums, 0), "batch", 2)]
-    bases = [base_of(near[0]), swap(base_of(near[1]), "batch", 1)]
-    tokens_here = near + [value for f in far for value in f]
+            here = slice(j * BLOCK, (j + 1) * BLOCK)
+            fars.append(swap((parts[2][here] + theirs[here]).astype(bf16), "batch", 2))
+        order, values = down_bundles[-1]
+        down_bundles[-1] = (order, values[:-1] + [gate(values[-1], fars[0])])
 
     def low_call(bundles, before, last):
-        taken = [value for _, value in bundles]
+        taken = [value for _, values in bundles for value in values]
+        count = tuple((a, v.shape[0]) for a, (_, values) in enumerate(bundles) for v in values)
         at = [
             (t, a, i * slots * rank) for a, (ts, _) in enumerate(bundles) for i, t in enumerate(ts)
         ]
@@ -417,20 +444,22 @@
             outs, out_specs = jax.ShapeDtypeStruct((pairs, tall, wide), f32), VMEM
         return call(
             functools.partial(
-                low_kernel, group, layers, rows, depth, rank, tuple(at), len(taken), by_request,
+                low_kernel, group, layers, rows, depth, rank, tuple(at), count, by_request,
                 shift, before is not None, last,
             ),
             outs,
             out_specs,
-            [SMEM] * 3 + [HBM] * (len(tokens_here) + len(taken)) + [VMEM] * (before is not None),
+            [SMEM] * 3 + [HBM] * (len(pieces) + len(taken)) + [VMEM] * (before is not None),
             [pltpu.VMEM((group * rows, len(at) * depth), bf16)]
-            + [pltpu.VMEM(v.shape, bf16) for v in taken]
-            + [pltpu.SemaphoreType.DMA((len(tokens_here), len(at))), pltpu.SemaphoreType.DMA((len(taken),))],
-            WAITS["low"][last] * CORE_FLOPS_PER_US,
-            0,
-        )(*lists, *tokens_here, *taken, *([before] if before is not None else []))
-
-    early = low_call([([0], down)] + down_bundles[:-1], None, False)
+            + [
+                pltpu.VMEM((sum(v.shape[0] for v in values), depth), bf16) for _, values in bundles
+            ]
+            + [pltpu.SemaphoreType.DMA((len(pieces), len(at))), pltpu.SemaphoreType.DMA((len(taken),))],
+            2 * pairs * tall * wide * len(at) * depth,
+            2 * len(at) * depth * (group * rows + slots * rank) + 4 * pairs * tall * wide,
+        )(*lists, *pieces, *taken, *([before] if before is not None else []))
+
+    early = low_call([([0], [down])] + down_bundles[:-1], None, False)
     even, odd = low_call(down_bundles[-1:], early, True)
     got = swap(odd, "batch", 1)
     lows = layer_pairs(even, got)

time: 102 us -> 104 us (1.020)
  starting transfers between devices: 20.4 us -> 25.3 us
  waiting for transfers between devices: 61.5 us -> 56.6 us
  Pallas kernels: 12.9 us -> 15.3 us
    ppermute x19 -> x23, waiting for transfers between devices: 61.5 us -> 56.6 us  [swap(): lax.ppermute(value, axis, [(i, i ^ bit) for i in range(lax.axis_size(axis...]
    ppermute x19 -> x23, starting transfers between devices: 20.4 us -> 25.3 us  [swap(): lax.ppermute(value, axis, [(i, i ^ bit) for i in range(lax.axis_size(axis...]
    pallas_call x7 -> x4, Pallas kernels: 3.07 us -> 5.74 us  [stack(): call(functools.partial(stack_kernel, tuple(moves), len(values), count), o...]
    dot_general x6 -> x4, matrix products: 4.31 us -> 3.88 us  [base_of(): return jnp.dot(value, keys, preferred_element_type=f32)]
  transfers between devices with their start and end apart: 19 -> 23, of which waited for: 8 -> 11; matrix products, arithmetic and copies ran while one was open for 4% -> 3% of each run, Pallas kernels for 9% -> 7%
where the time goes in v7:
time: 104 us
  waiting for transfers between devices  56.6 us (54%)
  starting transfers between devices  25.3 us (24%)
  Pallas kernels  15.3 us (15%)
  matrix products  3.88 us (4%)
  local copies, waits for them, and re-layouts  2.23 us (2%)
    ppermute x23, waiting for transfers between devices, swap(): lax.ppermute(value, axis, [(i, i ^ bit) for i in range(lax.axis_size(axis...  56.6 us
    ppermute x23, starting transfers between devices, swap(): lax.ppermute(value, axis, [(i, i ^ bit) for i in range(lax.axis_size(axis...  25.3 us
    pallas_call x4, Pallas kernels, stack(): call(functools.partial(stack_kernel, tuple(moves), len(values), count), o...  5.74 us
    pallas_call x2, Pallas kernels, low_call(): call(functools.partial(low_kernel, group, layers, rows, depth, rank, tupl...  4.58 us
    dot_general x4, matrix products, base_of(): return jnp.dot(value, keys, preferred_element_type=f32)  3.88 us
    unnamed x14, local copies, waits for them, and re-layouts  2.22 us
    pallas_call x1, Pallas kernels, shards(): call(functools.partial(final_kernel, rows, rank, len(bases), len(fars), l...  2.12 us
  transfers between devices with their start and end apart: 23, of which 11 were waited for; matrix products, arithmetic and copies ran while one was open for 3% of the time, Pallas kernels for 7%

profile of v7, /device:TPU:0, one launch (start us, length us, event | category | flops | bytes accessed | tf_op | source)
XLA Modules:
  0.0 103.7 jit_solution(10550793815620428487)
XLA Ops:
  0.0 2.2 %copy-done = bf16[256,8192]{1,0:T(8,128)(2,1)S(1)} copy-done((bf16[256,8192]{1,0:T(8,128)(2,1)S(1)}, bf16[256,8192]{1,0:T(8,128)(2,1)}, u32[]{:S(2)}) %copy-start) | copy-done | bytes 4194328
  4.2 2.6 %collective-permute-start.3 = (bf16[112,2048]{1,0:T(8,128)(2,1)S(1)}, bf16[112,2048]{1,0:T(8,128)(2,1)S(1)}, u32[]{:S(2)}, u32[]{:S(2)}) collective-permute-start(bf16[112,2048]{1,0:T(8,128)(2,1)S(1)} %get-tuple-element.39), channel_id=1, source_target_pairs={{0,2},{1,3},{2,0},{3,1},{4,6},{5,7},{6,4},{7,5},{8,10},{9,11},{10,... | collective-permute-start | bytes 1376264 | tf_op jit(solution)/shard_map/ppermute | solution.py:36
  7.3 2.9 %collective-permute-start.1 = (bf16[256,768]{1,0:T(8,128)(2,1)S(1)}, bf16[256,768]{1,0:T(8,128)(2,1)S(1)}, u32[]{:S(2)}, u32[]{:S(2)}) collective-permute-start(bf16[256,768]{1,0:T(8,128)(2,1)S(1)} %get-tuple-element.34.refs_2_), channel_id=1, source_target_pairs={{0,8},{1,9},{2,10},{3,11},{4,12},{5,13},{6,14},{7,15},{8,0},{9,1},... | collective-permute-start | bytes 1179656 | tf_op jit(solution)/shard_map/ppermute | solution.py:36
  10.1 1.6 %collective-permute-start = (bf16[256,768]{1,0:T(8,128)(2,1)S(1)}, bf16[256,768]{1,0:T(8,128)(2,1)S(1)}, u32[]{:S(2)}, u32[]{:S(2)}) collective-permute-start(bf16[256,768]{1,0:T(8,128)(2,1)S(1)} %get-tuple-element.34.refs_2_), channel_id=1, source_target_pairs={{0,4},{1,5},{2,6},{3,7},{4,0},{5,1},{6,2},{7,3},{8,12},{9,13},{10,... | collective-permute-start | bytes 1179656 | tf_op jit(solution)/shard_map/ppermute | solution.py:36
  12.8 15.5 %collective-permute-done.1.refs_0_.refs_6_ = bf16[256,768]{1,0:T(8,128)(2,1)S(1)} collective-permute-done((bf16[256,768]{1,0:T(8,128)(2,1)S(1)}, bf16[256,768]{1,0:T(8,128)(2,1)S(1)}, u32[]{:S(2)}, u32[]{:S(2)}) %collective-permute-start.1) | collective-permute-done | bytes 393248 | tf_op jit(solution)/shard_map/ppermute | solution.py:36
  29.6 1.6 %collective-permute-start.5 = (bf16[512,768]{1,0:T(8,128)(2,1)S(1)}, bf16[512,768]{1,0:T(8,128)(2,1)S(1)}, u32[]{:S(2)}, u32[]{:S(2)}) collective-permute-start(bf16[512,768]{1,0:T(8,128)(2,1)S(1)} %get-tuple-element.41), channel_id=1, source_target_pairs={{0,16},{16,0},{1,17},{17,1},{2,18},{18,2},{3,19},{19,3},{4,20},{20... | collective-permute-start | bytes 2359304 | tf_op jit(solution)/shard_map/ppermute | solution.py:36
  32.6 2.3 %collective-permute-start.9 = (bf16[448,512]{1,0:T(8,128)(2,1)S(1)}, bf16[448,512]{1,0:T(8,128)(2,1)S(1)}, u32[]{:S(2)}, u32[]{:S(2)}) collective-permute-start(bf16[448,512]{1,0:T(8,128)(2,1)S(1)} %get-tuple-element.45), channel_id=1, source_target_pairs={{0,8},{1,9},{2,10},{3,11},{4,12},{5,13},{6,14},{7,15},{8,0},{9,1},... | collective-permute-start | bytes 1376264 | tf_op jit(solution)/shard_map/ppermute | solution.py:36
  34.9 1.5 %collective-permute-start.8 = (bf16[96,2048]{1,0:T(8,128)(2,1)S(1)}, bf16[96,2048]{1,0:T(8,128)(2,1)S(1)}, u32[]{:S(2)}, u32[]{:S(2)}) collective-permute-start(bf16[96,2048]{1,0:T(8,128)(2,1)S(1)} %get-tuple-element.42), channel_id=1, source_target_pairs={{0,2},{1,3},{2,0},{3,1},{4,6},{5,7},{6,4},{7,5},{8,10},{9,11},{10,... | collective-permute-start | bytes 1179656 | tf_op jit(solution)/shard_map/ppermute | solution.py:36
  36.4 13.2 %collective-permute-done.6.refs_4_.refs_8_ = bf16[256,768]{1,0:T(8,128)(2,1)S(1)} collective-permute-done((bf16[256,768]{1,0:T(8,128)(2,1)S(1)}, bf16[256,768]{1,0:T(8,128)(2,1)S(1)}, u32[]{:S(2)}, u32[]{:S(2)}) %collective-permute-start.6) | collective-permute-done | bytes 393248 | tf_op jit(solution)/shard_map/ppermute | solution.py:36
  50.1 2.5 %collective-permute-done.10.refs_8_.refs_14_ = bf16[96,2048]{1,0:T(8,128)(2,1)S(1)} collective-permute-done((bf16[96,2048]{1,0:T(8,128)(2,1)S(1)}, bf16[96,2048]{1,0:T(8,128)(2,1)S(1)}, u32[]{:S(2)}, u32[]{:S(2)}) %collective-permute-start.10) | collective-permute-done | bytes 393248 | tf_op jit(solution)/shard_map/ppermute | solution.py:36
  52.6 2.4 %collective-permute-done.9.refs_6_.refs_8_ = bf16[448,512]{1,0:T(8,128)(2,1)S(1)} collective-permute-done((bf16[448,512]{1,0:T(8,128)(2,1)S(1)}, bf16[448,512]{1,0:T(8,128)(2,1)S(1)}, u32[]{:S(2)}, u32[]{:S(2)}) %collective-permute-start.9) | collective-permute-done | bytes 458784 | tf_op jit(solution)/shard_map/ppermute | solution.py:36
  55.6 2.4 %collective-permute-start.13 = (bf16[256,512]{1,0:T(8,128)(2,1)S(1)}, bf16[256,512]{1,0:T(8,128)(2,1)S(1)}, u32[]{:S(2)}, u32[]{:S(2)}) collective-permute-start(bf16[256,512]{1,0:T(8,128)(2,1)S(1)} %get-tuple-element.49), channel_id=1, source_target_pairs={{0,12},{1,13},{2,14},{3,15},{4,8},{5,9},{6,10},{7,11},{8,4},{9,5},... | collective-permute-start | bytes 786440 | tf_op jit(solution)/shard_map/ppermute | solution.py:36
  59.5 5.3 %collective-permute-done.11.refs_12_ = bf16[48,2048]{1,0:T(8,128)(2,1)S(1)} collective-permute-done((bf16[48,2048]{1,0:T(8,128)(2,1)S(1)}, bf16[48,2048]{1,0:T(8,128)(2,1)S(1)}, u32[]{:S(2)}, u32[]{:S(2)}) %collective-permute-start.11) | collective-permute-done | bytes 196640 | tf_op jit(solution)/shard_map/ppermute | solution.py:36
  64.8 2.0 %collective-permute-done.12.refs_15_ = bf16[48,2048]{1,0:T(8,128)(2,1)S(1)} collective-permute-done((bf16[48,2048]{1,0:T(8,128)(2,1)S(1)}, bf16[48,2048]{1,0:T(8,128)(2,1)S(1)}, u32[]{:S(2)}, u32[]{:S(2)}) %collective-permute-start.12) | collective-permute-done | bytes 196640 | tf_op jit(solution)/shard_map/ppermute | solution.py:36
  66.8 3.2 %collective-permute-done.14.refs_17_.refs_9_ = bf16[256,512]{1,0:T(8,128)(2,1)S(1)} collective-permute-done((bf16[256,512]{1,0:T(8,128)(2,1)S(1)}, bf16[256,512]{1,0:T(8,128)(2,1)S(1)}, u32[]{:S(2)}, u32[]{:S(2)}) %collective-permute-start.14) | collective-permute-done | bytes 262176 | tf_op jit(solution)/shard_map/ppermute | solution.py:36
  70.1 3.8 %shard_map.78 = (bf16[192,512]{1,0:T(8,128)(2,1)S(1)}, bf16[192,512]{1,0:T(8,128)(2,1)S(1)}, bf16[2048,768]{1,0:T(8,128)(2,1)S(1)}, bf16[256,2048]{1,0:T(8,128)(2,1)S(1)}, bf16[256,2048]{1,0:T(8,128)(2,1)S(1)}) custom-call(bf16[448,512]{1,0:T(8,128)(2,1)S(1)} %get-tuple-element.32.refs_2_.refs_0_, bf16[448,512]{1,0:T(8,128)(2,1)S(1)} %get-tuple-element.33.refs_1_.refs_7_, ...), custom_call_target="tpu_custom_call" | custom-call | tf_op jit(solution)/shard_map/pallas_call | solution.py:103
  75.0 1.7 %collective-permute-start.19 = (bf16[192,512]{1,0:T(8,128)(2,1)S(1)}, bf16[192,512]{1,0:T(8,128)(2,1)S(1)}, u32[]{:S(2)}, u32[]{:S(2)}) collective-permute-start(bf16[192,512]{1,0:T(8,128)(2,1)S(1)} %get-tuple-element.55), channel_id=1, source_target_pairs={{0,12},{1,13},{2,14},{3,15},{4,8},{5,9},{6,10},{7,11},{8,4},{9,5},... | collective-permute-start | bytes 589832 | tf_op jit(solution)/shard_map/ppermute | solution.py:36
  77.8 1.6 %collective-permute-start.16 = (bf16[128,768]{1,0:T(8,128)(2,1)S(1)}, bf16[128,768]{1,0:T(8,128)(2,1)S(1)}, u32[]{:S(2)}, u32[]{:S(2)}) collective-permute-start(bf16[128,768]{1,0:T(8,128)(2,1)S(1)} %get-tuple-element.60), channel_id=1, source_target_pairs={{0,2},{1,3},{2,0},{3,1},{4,6},{5,7},{6,4},{7,5},{8,10},{9,11},{10,... | collective-permute-start | bytes 589832 | tf_op jit(solution)/shard_map/ppermute | solution.py:36
  80.4 7.4 %collective-permute-done.20.refs_10_ = bf16[192,512]{1,0:T(8,128)(2,1)S(1)} collective-permute-done((bf16[192,512]{1,0:T(8,128)(2,1)S(1)}, bf16[192,512]{1,0:T(8,128)(2,1)S(1)}, u32[]{:S(2)}, u32[]{:S(2)}) %collective-permute-start.20) | collective-permute-done | bytes 196640 | tf_op jit(solution)/shard_map/ppermute | solution.py:36
  87.9 3.0 %shard_map.80.refs_9_ = f32[2,512,256]{2,1,0:T(8,128)S(1)} custom-call(s32[8]{0:T(128)S(1)} %copy-done.5, s32[8]{0:T(128)S(1)} %copy-done.4, s32[8]{0:T(128)S(1)} %copy-done.6, bf16[256,2048]{1,0:T(8,128)(2,1)S(1)} %get-tuple-element.54.refs_3_, bf16[256,2048]{1,0:T(8,128)(2,1)S(1)} %collective-permute-done.2.refs_5_.refs_4_, ...), custom_call_target="tpu_custom_call" | custom-call | flops 805306368 | bytes 5570560 | tf_op jit(solution)/shard_map/pallas_call | solution.py:445
  91.2 1.5 %shard_map.81 = (f32[2,128,128]{2,1,0:T(8,128)S(1)}, f32[2,128,128]{2,1,0:T(8,128)S(1)}) custom-call(s32[8]{0:T(128)S(1)} %copy-done.5, s32[8]{0:T(128)S(1)} %copy-done.4, s32[8]{0:T(128)S(1)} %copy-done.6, bf16[256,2048]{1,0:T(8,128)(2,1)S(1)} %get-tuple-element.54.refs_3_, bf16[256,2048]{1,0:T(8,128)(2,1)S(1)} %collective-permute-done.2.refs_5_.refs_4_, ...), custom_call_target="tpu_custom_call" | custom-call | flops 268435456 | bytes 2555904 | tf_op jit(solution)/shard_map/pallas_call | solution.py:445
  92.8 1.6 %collective-permute-start.17 = (bf16[128,768]{1,0:T(8,128)(2,1)S(1)}, bf16[128,768]{1,0:T(8,128)(2,1)S(1)}, u32[]{:S(2)}, u32[]{:S(2)}) collective-permute-start(bf16[128,768]{1,0:T(8,128)(2,1)S(1)} %get-tuple-element.59), channel_id=1, source_target_pairs={{0,2},{1,3},{2,0},{3,1},{4,6},{5,7},{6,4},{7,5},{8,10},{9,11},{10,... | collective-permute-start | bytes 589832 | tf_op jit(solution)/shard_map/ppermute | solution.py:36
  96.8 3.8 %collective-permute-done.17.refs_4_ = bf16[128,768]{1,0:T(8,128)(2,1)S(1)} collective-permute-done((bf16[128,768]{1,0:T(8,128)(2,1)S(1)}, bf16[128,768]{1,0:T(8,128)(2,1)S(1)}, u32[]{:S(2)}, u32[]{:S(2)}) %collective-permute-start.17) | collective-permute-done | bytes 196640 | tf_op jit(solution)/shard_map/ppermute | solution.py:36
  101.6 2.1 %shard_map.82 = bf16[256,768]{1,0:T(8,128)(2,1)} custom-call(s32[8]{0:T(128)S(1)} %copy-done.5, s32[8]{0:T(128)S(1)} %copy-done.4, s32[8]{0:T(128)S(1)} %copy-done.6, bf16[128,768]{1,0:T(8,128)(2,1)S(1)} %collective-permute-done.16.refs_1_.refs_3_, bf16[128,768]{1,0:T(8,128)(2,1)S(1)} %collective-permute-done.17.refs_4_, ...), custom_call_target="tpu_custom_call" | custom-call | flops 25165824 | bytes 1572864 | tf_op jit(solution)/shard_map/pallas_call | solution.py:467
  (53 shorter events, 15.6 us)
Async XLA Ops:
  3.7 24.8 %collective-permute-start.2 = (bf16[256,2048]{1,0:T(8,128)(2,1)S(1)}, bf16[256,2048]{1,0:T(8,128)(2,1)S(1)}, u32[]{:S(2)}, u32[]{:S(2)}) collective-permute-start(bf16[256,2048]{1,0:T(8,128)(2,1)S(1)} %get-tuple-element.38), channel_id=1, source_target_pairs={{0,1},{1,0},{2,3},{3,2},{4,5},{5,4},{6,7},{7,6},{8,9},{9,8},{10,11... | collective-permute-start | bytes 3145736 | tf_op jit(solution)/shard_map/ppermute | solution.py:36
  4.2 24.3 %collective-permute-start.3 = (bf16[112,2048]{1,0:T(8,128)(2,1)S(1)}, bf16[112,2048]{1,0:T(8,128)(2,1)S(1)}, u32[]{:S(2)}, u32[]{:S(2)}) collective-permute-start(bf16[112,2048]{1,0:T(8,128)(2,1)S(1)} %get-tuple-element.39), channel_id=1, source_target_pairs={{0,2},{1,3},{2,0},{3,1},{4,6},{5,7},{6,4},{7,5},{8,10},{9,11},{10,... | collective-permute-start | bytes 1376264 | tf_op jit(solution)/shard_map/ppermute | solution.py:36
  6.8 21.7 %collective-permute-start.4 = (bf16[112,2048]{1,0:T(8,128)(2,1)S(1)}, bf16[112,2048]{1,0:T(8,128)(2,1)S(1)}, u32[]{:S(2)}, u32[]{:S(2)}) collective-permute-start(bf16[112,2048]{1,0:T(8,128)(2,1)S(1)} %get-tuple-element.40), channel_id=1, source_target_pairs={{0,3},{1,2},{2,1},{3,0},{4,7},{5,6},{6,5},{7,4},{8,11},{9,10},{10,... | collective-permute-start | bytes 1376264 | tf_op jit(solution)/shard_map/ppermute | solution.py:36
  7.3 21.0 %collective-permute-start.1 = (bf16[256,768]{1,0:T(8,128)(2,1)S(1)}, bf16[256,768]{1,0:T(8,128)(2,1)S(1)}, u32[]{:S(2)}, u32[]{:S(2)}) collective-permute-start(bf16[256,768]{1,0:T(8,128)(2,1)S(1)} %get-tuple-element.34.refs_2_), channel_id=1, source_target_pairs={{0,8},{1,9},{2,10},{3,11},{4,12},{5,13},{6,14},{7,15},{8,0},{9,1},... | collective-permute-start | bytes 1179656 | tf_op jit(solution)/shard_map/ppermute | solution.py:36
  10.1 18.3 %collective-permute-start = (bf16[256,768]{1,0:T(8,128)(2,1)S(1)}, bf16[256,768]{1,0:T(8,128)(2,1)S(1)}, u32[]{:S(2)}, u32[]{:S(2)}) collective-permute-start(bf16[256,768]{1,0:T(8,128)(2,1)S(1)} %get-tuple-element.34.refs_2_), channel_id=1, source_target_pairs={{0,4},{1,5},{2,6},{3,7},{4,0},{5,1},{6,2},{7,3},{8,12},{9,13},{10,... | collective-permute-start | bytes 1179656 | tf_op jit(solution)/shard_map/ppermute | solution.py:36
  29.6 25.4 %collective-permute-start.5 = (bf16[512,768]{1,0:T(8,128)(2,1)S(1)}, bf16[512,768]{1,0:T(8,128)(2,1)S(1)}, u32[]{:S(2)}, u32[]{:S(2)}) collective-permute-start(bf16[512,768]{1,0:T(8,128)(2,1)S(1)} %get-tuple-element.41), channel_id=1, source_target_pairs={{0,16},{16,0},{1,17},{17,1},{2,18},{18,2},{3,19},{19,3},{4,20},{20... | collective-permute-start | bytes 2359304 | tf_op jit(solution)/shard_map/ppermute | solution.py:36
  31.1 18.5 %collective-permute-start.6 = (bf16[256,768]{1,0:T(8,128)(2,1)S(1)}, bf16[256,768]{1,0:T(8,128)(2,1)S(1)}, u32[]{:S(2)}, u32[]{:S(2)}) collective-permute-start(bf16[256,768]{1,0:T(8,128)(2,1)S(1)} %collective-permute-done.1.refs_0_.refs_6_), channel_id=1, source_target_pairs={{0,4},{1,5},{2,6},{3,7},{4,0},{5,1},{6,2},{7,3},{8,12},{9,13},{10,... | collective-permute-start | bytes 1179656 | tf_op jit(solution)/shard_map/ppermute | solution.py:36
  32.6 22.4 %collective-permute-start.9 = (bf16[448,512]{1,0:T(8,128)(2,1)S(1)}, bf16[448,512]{1,0:T(8,128)(2,1)S(1)}, u32[]{:S(2)}, u32[]{:S(2)}) collective-permute-start(bf16[448,512]{1,0:T(8,128)(2,1)S(1)} %get-tuple-element.45), channel_id=1, source_target_pairs={{0,8},{1,9},{2,10},{3,11},{4,12},{5,13},{6,14},{7,15},{8,0},{9,1},... | collective-permute-start | bytes 1376264 | tf_op jit(solution)/shard_map/ppermute | solution.py:36
  34.9 15.2 %collective-permute-start.8 = (bf16[96,2048]{1,0:T(8,128)(2,1)S(1)}, bf16[96,2048]{1,0:T(8,128)(2,1)S(1)}, u32[]{:S(2)}, u32[]{:S(2)}) collective-permute-start(bf16[96,2048]{1,0:T(8,128)(2,1)S(1)} %get-tuple-element.42), channel_id=1, source_target_pairs={{0,2},{1,3},{2,0},{3,1},{4,6},{5,7},{6,4},{7,5},{8,10},{9,11},{10,... | collective-permute-start | bytes 1179656 | tf_op jit(solution)/shard_map/ppermute | solution.py:36
  36.4 16.2 %collective-permute-start.10 = (bf16[96,2048]{1,0:T(8,128)(2,1)S(1)}, bf16[96,2048]{1,0:T(8,128)(2,1)S(1)}, u32[]{:S(2)}, u32[]{:S(2)}) collective-permute-start(bf16[96,2048]{1,0:T(8,128)(2,1)S(1)} %get-tuple-element.46), channel_id=1, source_target_pairs={{0,3},{1,2},{2,1},{3,0},{4,7},{5,6},{6,5},{7,4},{8,11},{9,10},{10,... | collective-permute-start | bytes 1179656 | tf_op jit(solution)/shard_map/ppermute | solution.py:36
  49.6 9.9 %collective-permute-start.7 = (bf16[256,768]{1,0:T(8,128)(2,1)S(1)}, bf16[256,768]{1,0:T(8,128)(2,1)S(1)}, u32[]{:S(2)}, u32[]{:S(2)}) collective-permute-start(bf16[256,768]{1,0:T(8,128)(2,1)S(1)} %collective-permute-done.6.refs_4_.refs_8_), channel_id=1, source_target_pairs={{0,16},{16,0},{1,17},{17,1},{2,18},{18,2},{3,19},{19,3},{4,20},{20... | collective-permute-start | bytes 1179656 | tf_op jit(solution)/shard_map/ppermute | solution.py:36
  55.6 11.3 %collective-permute-start.13 = (bf16[256,512]{1,0:T(8,128)(2,1)S(1)}, bf16[256,512]{1,0:T(8,128)(2,1)S(1)}, u32[]{:S(2)}, u32[]{:S(2)}) collective-permute-start(bf16[256,512]{1,0:T(8,128)(2,1)S(1)} %get-tuple-element.49), channel_id=1, source_target_pairs={{0,12},{1,13},{2,14},{3,15},{4,8},{5,9},{6,10},{7,11},{8,4},{9,5},... | collective-permute-start | bytes 786440 | tf_op jit(solution)/shard_map/ppermute | solution.py:36
  58.0 12.1 %collective-permute-start.14 = (bf16[256,512]{1,0:T(8,128)(2,1)S(1)}, bf16[256,512]{1,0:T(8,128)(2,1)S(1)}, u32[]{:S(2)}, u32[]{:S(2)}) collective-permute-start(bf16[256,512]{1,0:T(8,128)(2,1)S(1)} %get-tuple-element.50), channel_id=1, source_target_pairs={{0,4},{1,5},{2,6},{3,7},{4,0},{5,1},{6,2},{7,3},{8,12},{9,13},{10,... | collective-permute-start | bytes 786440 | tf_op jit(solution)/shard_map/ppermute | solution.py:36
  58.0 6.8 %collective-permute-start.11 = (bf16[48,2048]{1,0:T(8,128)(2,1)S(1)}, bf16[48,2048]{1,0:T(8,128)(2,1)S(1)}, u32[]{:S(2)}, u32[]{:S(2)}) collective-permute-start(bf16[48,2048]{1,0:T(8,128)(2,1)S(1)} %get-tuple-element.47), channel_id=1, source_target_pairs={{0,2},{1,3},{2,0},{3,1},{4,6},{5,7},{6,4},{7,5},{8,10},{9,11},{10,... | collective-permute-start | bytes 589832 | tf_op jit(solution)/shard_map/ppermute | solution.py:36
  59.5 7.3 %collective-permute-start.12 = (bf16[48,2048]{1,0:T(8,128)(2,1)S(1)}, bf16[48,2048]{1,0:T(8,128)(2,1)S(1)}, u32[]{:S(2)}, u32[]{:S(2)}) collective-permute-start(bf16[48,2048]{1,0:T(8,128)(2,1)S(1)} %get-tuple-element.48), channel_id=1, source_target_pairs={{0,3},{1,2},{2,1},{3,0},{4,7},{5,6},{6,5},{7,4},{8,11},{9,10},{10,... | collective-permute-start | bytes 589832 | tf_op jit(solution)/shard_map/ppermute | solution.py:36
  74.9 2.8 %collective-permute-start.15 = (f32[256,768]{1,0:T(8,128)S(1)}, f32[256,768]{1,0:T(8,128)S(1)}, u32[]{:S(2)}, u32[]{:S(2)}) collective-permute-start(f32[256,768]{1,0:T(8,128)S(1)} %fusion.4), channel_id=1, source_target_pairs={{0,1},{1,0},{2,3},{3,2},{4,5},{5,4},{6,7},{7,6},{8,9},{9,8},{10,11... | collective-permute-start | bytes 2359304 | tf_op jit(solution)/shard_map/ppermute | solution.py:36
  75.0 16.0 %collective-permute-start.19 = (bf16[192,512]{1,0:T(8,128)(2,1)S(1)}, bf16[192,512]{1,0:T(8,128)(2,1)S(1)}, u32[]{:S(2)}, u32[]{:S(2)}) collective-permute-start(bf16[192,512]{1,0:T(8,128)(2,1)S(1)} %get-tuple-element.55), channel_id=1, source_target_pairs={{0,12},{1,13},{2,14},{3,15},{4,8},{5,9},{6,10},{7,11},{8,4},{9,5},... | collective-permute-start | bytes 589832 | tf_op jit(solution)/shard_map/ppermute | solution.py:36
  76.7 11.2 %collective-permute-start.20 = (bf16[192,512]{1,0:T(8,128)(2,1)S(1)}, bf16[192,512]{1,0:T(8,128)(2,1)S(1)}, u32[]{:S(2)}, u32[]{:S(2)}) collective-permute-start(bf16[192,512]{1,0:T(8,128)(2,1)S(1)} %get-tuple-element.56), channel_id=1, source_target_pairs={{0,4},{1,5},{2,6},{3,7},{4,0},{5,1},{6,2},{7,3},{8,12},{9,13},{10,... | collective-permute-start | bytes 589832 | tf_op jit(solution)/shard_map/ppermute | solution.py:36
  77.8 10.1 %copy-start.5 = (s32[8]{0:T(128)S(1)}, s32[8]{0:T(128)}, u32[]{:S(2)}) copy-start(s32[8]{0:T(128)} %refs_0_.5) | copy-start | bytes 100
  77.8 13.1 %collective-permute-start.16 = (bf16[128,768]{1,0:T(8,128)(2,1)S(1)}, bf16[128,768]{1,0:T(8,128)(2,1)S(1)}, u32[]{:S(2)}, u32[]{:S(2)}) collective-permute-start(bf16[128,768]{1,0:T(8,128)(2,1)S(1)} %get-tuple-element.60), channel_id=1, source_target_pairs={{0,2},{1,3},{2,0},{3,1},{4,6},{5,7},{6,4},{7,5},{8,10},{9,11},{10,... | collective-permute-start | bytes 589832 | tf_op jit(solution)/shard_map/ppermute | solution.py:36
  80.4 16.4 %collective-permute-start.18 = (f32[256,768]{1,0:T(8,128)S(1)}, f32[256,768]{1,0:T(8,128)S(1)}, u32[]{:S(2)}, u32[]{:S(2)}) collective-permute-start(f32[256,768]{1,0:T(8,128)S(1)} %convolution_bitcast_fusion), channel_id=1, source_target_pairs={{0,1},{1,0},{2,3},{3,2},{4,5},{5,4},{6,7},{7,6},{8,9},{9,8},{10,11... | collective-permute-start | bytes 2359304 | tf_op jit(solution)/shard_map/ppermute | solution.py:36
  92.8 1.7 %collective-permute-start.21 = (f32[2,128,128]{2,1,0:T(8,128)S(1)}, f32[2,128,128]{2,1,0:T(8,128)S(1)}, u32[]{:S(2)}, u32[]{:S(2)}) collective-permute-start(f32[2,128,128]{2,1,0:T(8,128)S(1)} %get-tuple-element.58), channel_id=1, source_target_pairs={{0,1},{1,0},{2,3},{3,2},{4,5},{5,4},{6,7},{7,6},{8,9},{9,8},{10,11... | collective-permute-start | bytes 393224 | tf_op jit(solution)/shard_map/ppermute | solution.py:36
  92.8 7.8 %collective-permute-start.17 = (bf16[128,768]{1,0:T(8,128)(2,1)S(1)}, bf16[128,768]{1,0:T(8,128)(2,1)S(1)}, u32[]{:S(2)}, u32[]{:S(2)}) collective-permute-start(bf16[128,768]{1,0:T(8,128)(2,1)S(1)} %get-tuple-element.59), channel_id=1, source_target_pairs={{0,2},{1,3},{2,0},{3,1},{4,6},{5,7},{6,4},{7,5},{8,10},{9,11},{10,... | collective-permute-start | bytes 589832 | tf_op jit(solution)/shard_map/ppermute | solution.py:36
  94.5 7.1 %collective-permute-start.22 = (f32[1,128,128]{2,1,0:T(8,128)S(1)}, f32[1,128,128]{2,1,0:T(8,128)S(1)}, u32[]{:S(2)}, u32[]{:S(2)}) collective-permute-start(f32[1,128,128]{2,1,0:T(8,128)S(1)} %get-tuple-element.61), channel_id=1, source_target_pairs={{0,2},{1,3},{2,0},{3,1},{4,6},{5,7},{6,4},{7,5},{8,10},{9,11},{10,... | collective-permute-start | bytes 196616 | tf_op jit(solution)/shard_map/ppermute | solution.py:36
  (6 other events, 44.7 us)

commit v8 on v5

--- a/solution.py
+++ b/solution.py
@@ -13,7 +13,10 @@
 LAYER_CHIPS = 4
 VMEM_BYTES = 28 * 1024 * 1024
 CORE_FLOPS_PER_US = 1_153_500_000
+CFG = {'us': {}, 'z3': 2, 'c': 2, 'xcut': 2, 'ph': [11, 5]}
 WAITS = {"far": 12, "keys": 0, "all": 5, "across": 0, "near": 0, "low": (5, 15)}
+WAITS.update(CFG.get("us", {}))
+PHASES = tuple(CFG.get("ph", [8, 8]))
 
 HBM = pl.BlockSpec(memory_space=pl.ANY)
 VMEM = pl.BlockSpec(memory_space=pltpu.VMEM)
@@ -47,10 +50,9 @@
     return pl.multiple_of((lax.axis_index("rep") ^ h) * part, part)
 
 
-def first_kernel(group, layers, splits, part, key, tokens, *refs):
+def first_kernel(group, layers, splits, part, chunks, key, tokens, *refs):
     keys, refs = refs[:splits], refs[splits:]
     outs, sems = refs[:-1], refs[-1]
-    blocks = tokens.shape[0] // BLOCK
     depth = splits * part
     me = lax.axis_index("batch")
     layer, spot = me // group, me % group
@@ -65,11 +67,11 @@
                 if s < 2:
                     pairs.append((tokens.at[:, pl.ds(start, part)], outs[s].at[:, to]))
                     continue
-                for j in range(blocks):
+                for j, (row, deep) in enumerate(chunks):
                     pairs.append(
                         (
-                            tokens.at[pl.ds(j * BLOCK, BLOCK), pl.ds(start, part)],
-                            outs[2 + (s - 2) * blocks + j].at[:, to],
+                            tokens.at[pl.ds(row, deep), pl.ds(start, part)],
+                            outs[2 + (s - 2) * len(chunks) + j].at[:, to],
                         )
                     )
     for copy in run_copies(pairs, sems):
@@ -144,17 +146,17 @@
     return owner, adapter, limit
 
 
-def token_places(group, rows):
+def token_places(group, rows, chunks):
     near = [(s * rows, rows) for s in range(min(group, 2))]
-    far = [(row, BLOCK) for row in range(2 * rows, group * rows, BLOCK)]
+    far = [(s * rows + row, deep) for s in range(2, group) for row, deep in chunks]
     return near + far
 
 
 def low_kernel(
-    group, layers, rows, depth, rank, entries, count, by_request, shift, has_sum, last, *refs
+    group, layers, rows, chunks, depth, rank, entries, count, by_request, shift, has_sum, last, *refs
 ):
     lists, refs = refs[:3], refs[3:]
-    places = token_places(group, rows)
+    places = token_places(group, rows, chunks)
     toks, refs = refs[: len(places)], refs[len(places) :]
     arrays, refs = refs[:count], refs[count:]
     if has_sum:
@@ -254,7 +256,7 @@
         for ref in base_refs:
             total = total + ref[here, :]
         if far_refs:
-            total = total + far_refs[j][...].astype(jnp.float32)
+            total = total + far_refs[0][here, :].astype(jnp.float32)
         live = lax.broadcasted_iota(jnp.int32, total.shape, 0) < found[j][2]
         out[here, :] = jnp.where(live, total, 0.0).astype(jnp.bfloat16)
 
@@ -281,12 +283,16 @@
     lists = (request_block_list, request_adapter_index, request_tail_tokens)
     f32, bf16 = jnp.float32, jnp.bfloat16
 
-    far_count = (group - 2) * local_blocks
+    chunks = [
+        (sum(PHASES[:i]) * rows // sum(PHASES), PHASES[i] * rows // sum(PHASES))
+        for i in range(len(PHASES) if group > 2 else 0)
+    ]
+    far_count = (group - 2) * len(chunks)
     first = call(
-        functools.partial(first_kernel, group, layers, splits, part),
+        functools.partial(first_kernel, group, layers, splits, part, chunks),
         [jax.ShapeDtypeStruct((part, out_width), bf16)] * splits
         + [jax.ShapeDtypeStruct((rows, held_width), bf16)] * 2
-        + [jax.ShapeDtypeStruct((BLOCK, held_width), bf16)] * far_count,
+        + [jax.ShapeDtypeStruct((deep, held_width), bf16) for _, deep in chunks] * (group - 2),
         [HBM] * (splits + 2 + far_count),
         [HBM] * 2,
         [
@@ -299,11 +305,11 @@
     )(key_matrix, tokens)
     key_parts, first = first[:splits], first[splits:]
 
-    far = [list(first[2 + s * local_blocks :][:local_blocks]) for s in range(group - 2)]
+    far = [list(first[2 + s * len(chunks) :][: len(chunks)]) for s in range(group - 2)]
     sent = []
-    for j in range(local_blocks if far else 0):
+    for j, (_, deep) in enumerate(chunks):
         if j:
-            sent = stack([[(f[j], 0, BLOCK)] for f in far], *[f[j - 1] for f in far], us=WAITS["far"])
+            sent = stack([[(f[j], 0, deep)] for f in far], *[f[j - 1] for f in far], us=WAITS["far"])
         else:
             sent = [f[j] for f in far]
         for s, f in enumerate(far):
@@ -350,37 +356,56 @@
         for i, t in enumerate(ts):
             rows_of_key[t, 0] = (value, i * part, part)
     last_keys = [key_bundles[-1][1]]
+    xcut = CFG.get("xcut", 1)
     for h in range(1, splits):
-        for bundles in (key_bundles[:1], key_bundles[1:]):
+        swapped = None
+        for bundles in (key_bundles[:xcut], key_bundles[xcut:]):
             if not bundles:
                 continue
             values = bundles[0][1]
-            if bundles is not key_bundles[:1] and len(bundles) > 1:
-                values = stack([[(v, 0, v.shape[0]) for _, v in bundles]], *last_keys, us=WAITS["keys"])[0]
+            ready = [swapped] if swapped is not None and (len(bundles) > 1 or CFG.get("x3g")) else []
+            if len(bundles) > 1 or ready:
+                values = stack([[(v, 0, v.shape[0]) for _, v in bundles]], *ready, us=WAITS["keys"])[0]
             last_keys = [values]
             swapped = swap(values, "rep", h)
-            if len(bundles) == 1:
-                last_keys = [swapped]
             for i, t in enumerate([t for ts, _ in bundles for t in ts]):
                 rows_of_key[t, h] = (swapped, i * part, part)
     keys = stack(
         [[rows_of_key[t, h] for t in range(layers) for h in range(splits)]], us=WAITS["all"]
     )[0]
 
-    across_sent = gate(across, *[v for _, v in key_bundles[:2]], us=WAITS["across"])
+    across_sent = gate(across, *[v for _, v in key_bundles[:CFG.get('z3', 2)]], us=WAITS["across"])
     down_sent = gate(down, *last_keys, us=WAITS["near"])
-    down_bundles = over_layers(across_sent, down_sent)
-
-    near = [first[0], swap(gate(first[1], *[v for _, v in down_bundles[:2]]), "batch", 1)]
+    if CFG.get("zdirect") and layers == 4:
+        d = {2: swap(across_sent, "batch", 2 * group)}
+        sent3 = gate(across, *[{"k3": last_keys[0], "Z3": d[2], "gZ5": down_sent}[k] for k in CFG.get("z6", ["k3"])], us=WAITS.get("z6", 0))
+        d[1] = swap(down_sent, "batch", group)
+        d[3] = swap(sent3, "batch", 3 * group)
+        down_bundles = [([t], d[t]) for t in (2, 1, 3)]
+    else:
+        down_bundles = over_layers(across_sent, down_sent)
+
+    cm = CFG.get("c", 2)
+    near = [first[0], swap(gate(first[1], *[v for _, v in down_bundles[:cm]]) if cm else first[1], "batch", 1)]
 
     def base_of(value):
         return jnp.dot(value, keys, preferred_element_type=f32)
 
     fars = []
     if far:
-        for j in range(local_blocks):
+        sums = []
+        for j in range(len(chunks)):
             theirs = swap(base_of(far[1][j]), "batch", 1)
-            fars.append(swap((base_of(far[0][j]) + theirs).astype(bf16), "batch", 2))
+            sums.append((base_of(far[0][j]) + theirs).astype(bf16))
+        if CFG.get("ymerge"):
+            sums = [jnp.concatenate(sums, 0)]
+        if CFG.get("lowe"):
+            down = gate(down, sums[0])
+        fars = [swap(v, "batch", 2) for v in sums]
+        if CFG.get("lowl"):
+            order, value = down_bundles[-1]
+            down_bundles[-1] = (order, gate(value, fars[0]))
+        fars = [fars[0] if len(fars) == 1 else jnp.concatenate(fars, 0)]
     bases = [base_of(near[0]), swap(base_of(near[1]), "batch", 1)]
     tokens_here = near + [value for f in far for value in f]
 
@@ -397,7 +422,7 @@
             outs, out_specs = jax.ShapeDtypeStruct((pairs, tall, wide), f32), VMEM
         return call(
             functools.partial(
-                low_kernel, group, layers, rows, depth, rank, tuple(at), len(taken), by_request,
+                low_kernel, group, layers, rows, chunks, depth, rank, tuple(at), len(taken), by_request,
                 shift, before is not None, last,
             ),
             outs,

time: 92.9 us -> 88.5 us (0.953)
  waiting for transfers between devices: 51.8 us -> 46.2 us
    ppermute x20, waiting for transfers between devices: 51.8 us -> 46.2 us  [swap(): lax.ppermute(value, axis, [(i, i ^ bit) for i in range(lax.axis_size(axis...]
  transfers between devices with their start and end apart: 20 -> 20, of which waited for: 9 -> 10; matrix products, arithmetic and copies ran while one was open for 5% -> 5% of each run, Pallas kernels for 9% -> 10%
where the time goes in v8:
time: 88.5 us; the launch traced here: 88.4 us
  waiting for transfers between devices  46.2 us (52%)
  starting transfers between devices  21.3 us (24%)
  Pallas kernels  12.4 us (14%)
  matrix products  4.75 us (5%)
  local copies, waits for them, and re-layouts  3.36 us (4%)
    ppermute x20, waiting for transfers between devices, swap(): lax.ppermute(value, axis, [(i, i ^ bit) for i in range(lax.axis_size(axis...  46.2 us
    ppermute x20, starting transfers between devices, swap(): lax.ppermute(value, axis, [(i, i ^ bit) for i in range(lax.axis_size(axis...  21.3 us
    pallas_call x2, Pallas kernels, low_call(): call(functools.partial(low_kernel, group, layers, rows, chunks, depth, ra...  4.79 us
    dot_general x6, matrix products, base_of(): return jnp.dot(value, keys, preferred_element_type=f32)  4.75 us
    unnamed x14, local copies, waits for them, and re-layouts  3.35 us
    pallas_call x6, Pallas kernels, stack(): call(functools.partial(stack_kernel, tuple(moves), len(values), count), o...  2.81 us
    pallas_call x1, Pallas kernels, shards(): call(functools.partial(final_kernel, rows, rank, len(bases), len(fars), l...  2.11 us
  transfers between devices with their start and end apart: 20, of which 10 were waited for; matrix products, arithmetic and copies ran while one was open for 5% of the time, Pallas kernels for 10%

profile of v8, /device:TPU:0, one launch (start us, length us, event | category | flops | bytes accessed | tf_op | source)
XLA Modules:
  0.0 88.4 jit_solution(12859475660333634415)
XLA Ops:
  0.0 2.2 %copy-done = bf16[256,8192]{1,0:T(8,128)(2,1)S(1)} copy-done((bf16[256,8192]{1,0:T(8,128)(2,1)S(1)}, bf16[256,8192]{1,0:T(8,128)(2,1)}, u32[]{:S(2)}) %copy-start) | copy-done | bytes 4194328
  2.2 1.1 %copy-done.3 = bf16[512,768]{1,0:T(8,128)(2,1)S(1)} copy-done((bf16[512,768]{1,0:T(8,128)(2,1)S(1)}, bf16[512,768]{1,0:T(8,128)(2,1)}, u32[]{:S(2)}) %copy-start.3) | copy-done | bytes 786456
  3.3 1.7 %shard_map.73 = (bf16[256,768]{1,0:T(8,128)(2,1)S(1)}, bf16[256,768]{1,0:T(8,128)(2,1)S(1)}, bf16[256,2048]{1,0:T(8,128)(2,1)S(1)}, bf16[256,2048]{1,0:T(8,128)(...) custom-call(bf16[512,768]{1,0:T(8,128)(2,1)S(1)} %copy-done.3, ...), custom_call_target="tpu_custom_call" | custom-call | bytes 9961472 | tf_op jit(solution)/shard_map/pallas_call | solution.py:291
  5.0 4.1 %collective-permute-start.2 = (bf16[256,768]{1,0:T(8,128)(2,1)S(1)}, bf16[256,768]{1,0:T(8,128)(2,1)S(1)}, u32[]{:S(2)}, u32[]{:S(2)}) collective-permute-start(bf16[256,768]{1,0:T(8,128)(2,1)S(1)} %get-tuple-element.20.refs_0_), channel_id=1, source_target_pairs={{0,8},{1,9},{2,10},{3,11},{4,12},{5,13},{6,14},{7,15},{8,0},{9,1},... | collective-permute-start | bytes 1179656 | tf_op jit(solution)/shard_map/ppermute | solution.py:39
  9.1 1.5 %collective-permute-start = (bf16[176,2048]{1,0:T(8,128)(2,1)S(1)}, bf16[176,2048]{1,0:T(8,128)(2,1)S(1)}, u32[]{:S(2)}, u32[]{:S(2)}) collective-permute-start(bf16[176,2048]{1,0:T(8,128)(2,1)S(1)} %get-tuple-element.19), channel_id=1, source_target_pairs={{0,2},{1,3},{2,0},{3,1},{4,6},{5,7},{6,4},{7,5},{8,10},{9,11},{10,... | collective-permute-start | bytes 2162696 | tf_op jit(solution)/shard_map/ppermute | solution.py:39
  10.6 1.6 %collective-permute-start.1 = (bf16[256,768]{1,0:T(8,128)(2,1)S(1)}, bf16[256,768]{1,0:T(8,128)(2,1)S(1)}, u32[]{:S(2)}, u32[]{:S(2)}) collective-permute-start(bf16[256,768]{1,0:T(8,128)(2,1)S(1)} %get-tuple-element.20.refs_0_), channel_id=1, source_target_pairs={{0,4},{1,5},{2,6},{3,7},{4,0},{5,1},{6,2},{7,3},{8,12},{9,13},{10,... | collective-permute-start | bytes 1179656 | tf_op jit(solution)/shard_map/ppermute | solution.py:39
  12.2 14.5 %collective-permute-done.2.refs_0_.refs_4_.refs_1_ = bf16[256,768]{1,0:T(8,128)(2,1)S(1)} collective-permute-done((bf16[256,768]{1,0:T(8,128)(2,1)S(1)}, bf16[256,768]{1,0:T(8,128)(2,1)S(1)}, u32[]{:S(2)}, u32[]{:S(2)}) %collective-permute-start.2) | collective-permute-done | bytes 393248 | tf_op jit(solution)/shard_map/ppermute | solution.py:39
  28.5 1.3 %collective-permute-done.1.refs_1_.refs_2_ = bf16[256,768]{1,0:T(8,128)(2,1)S(1)} collective-permute-done((bf16[256,768]{1,0:T(8,128)(2,1)S(1)}, bf16[256,768]{1,0:T(8,128)(2,1)S(1)}, u32[]{:S(2)}, u32[]{:S(2)}) %collective-permute-start.1) | collective-permute-done | bytes 393248 | tf_op jit(solution)/shard_map/ppermute | solution.py:39
  30.1 2.2 %collective-permute-start.13 = (bf16[448,512]{1,0:T(8,128)(2,1)S(1)}, bf16[448,512]{1,0:T(8,128)(2,1)S(1)}, u32[]{:S(2)}, u32[]{:S(2)}) collective-permute-start(bf16[448,512]{1,0:T(8,128)(2,1)S(1)} %shard_map.78), channel_id=1, source_target_pairs={{0,8},{1,9},{2,10},{3,11},{4,12},{5,13},{6,14},{7,15},{8,0},{9,1},... | collective-permute-start | bytes 1376264 | tf_op jit(solution)/shard_map/ppermute | solution.py:39
  32.7 1.5 %collective-permute-start.3 = (bf16[512,768]{1,0:T(8,128)(2,1)S(1)}, bf16[512,768]{1,0:T(8,128)(2,1)S(1)}, u32[]{:S(2)}, u32[]{:S(2)}) collective-permute-start(bf16[512,768]{1,0:T(8,128)(2,1)S(1)} %shard_map.74), channel_id=1, source_target_pairs={{0,16},{16,0},{1,17},{17,1},{2,18},{18,2},{3,19},{19,3},{4,20},{20... | collective-permute-start | bytes 2359304 | tf_op jit(solution)/shard_map/ppermute | solution.py:39
  34.2 10.1 %collective-permute-done.4.refs_6_.refs_1_ = bf16[256,768]{1,0:T(8,128)(2,1)S(1)} collective-permute-done((bf16[256,768]{1,0:T(8,128)(2,1)S(1)}, bf16[256,768]{1,0:T(8,128)(2,1)S(1)}, u32[]{:S(2)}, u32[]{:S(2)}) %collective-permute-start.4) | collective-permute-done | bytes 393248 | tf_op jit(solution)/shard_map/ppermute | solution.py:39
  44.3 1.5 %collective-permute-start.5 = (bf16[256,768]{1,0:T(8,128)(2,1)S(1)}, bf16[256,768]{1,0:T(8,128)(2,1)S(1)}, u32[]{:S(2)}, u32[]{:S(2)}) collective-permute-start(bf16[256,768]{1,0:T(8,128)(2,1)S(1)} %collective-permute-done.4.refs_6_.refs_1_), channel_id=1, source_target_pairs={{0,16},{16,0},{1,17},{17,1},{2,18},{18,2},{3,19},{19,3},{4,20},{20... | collective-permute-start | bytes 1179656 | tf_op jit(solution)/shard_map/ppermute | solution.py:39
  46.1 1.3 %collective-permute-start.9 = (bf16[80,2048]{1,0:T(8,128)(2,1)S(1)}, bf16[80,2048]{1,0:T(8,128)(2,1)S(1)}, u32[]{:S(2)}, u32[]{:S(2)}) collective-permute-start(bf16[80,2048]{1,0:T(8,128)(2,1)S(1)} %get-tuple-element.25), channel_id=1, source_target_pairs={{0,2},{1,3},{2,0},{3,1},{4,6},{5,7},{6,4},{7,5},{8,10},{9,11},{10,... | collective-permute-start | bytes 983048 | tf_op jit(solution)/shard_map/ppermute | solution.py:39
  47.7 5.2 %collective-permute-done.13.refs_1_.refs_10_ = bf16[448,512]{1,0:T(8,128)(2,1)S(1)} collective-permute-done((bf16[448,512]{1,0:T(8,128)(2,1)S(1)}, bf16[448,512]{1,0:T(8,128)(2,1)S(1)}, u32[]{:S(2)}, u32[]{:S(2)}) %collective-permute-start.13) | collective-permute-done | bytes 458784 | tf_op jit(solution)/shard_map/ppermute | solution.py:39
  53.2 1.7 %collective-permute-start.17 = (bf16[448,512]{1,0:T(8,128)(2,1)S(1)}, bf16[448,512]{1,0:T(8,128)(2,1)S(1)}, u32[]{:S(2)}, u32[]{:S(2)}) collective-permute-start(bf16[448,512]{1,0:T(8,128)(2,1)S(1)} %collective-permute-done.13.refs_1_.refs_10_), channel_id=1, source_target_pairs={{0,4},{1,5},{2,6},{3,7},{4,0},{5,1},{6,2},{7,3},{8,12},{9,13},{10,... | collective-permute-start | bytes 1376264 | tf_op jit(solution)/shard_map/ppermute | solution.py:39
  55.0 5.1 %collective-permute-done.5.refs_7_ = bf16[256,768]{1,0:T(8,128)(2,1)S(1)} collective-permute-done((bf16[256,768]{1,0:T(8,128)(2,1)S(1)}, bf16[256,768]{1,0:T(8,128)(2,1)S(1)}, u32[]{:S(2)}, u32[]{:S(2)}) %collective-permute-start.5) | collective-permute-done | bytes 393248 | tf_op jit(solution)/shard_map/ppermute | solution.py:39
  60.0 1.6 %shard_map.75 = bf16[2048,768]{1,0:T(8,128)(2,1)S(1)} custom-call(bf16[256,768]{1,0:T(8,128)(2,1)S(1)} %get-tuple-element.20.refs_0_, bf16[256,768]{1,0:T(8,128)(2,1)S(1)} %get-tuple-element.21.refs_1_, bf16[256,768]{1,0:T(8,128)(2,1)S(1)} %collective-permute-done.1.refs_1_.refs_2_, bf16[512,768]{1,0:T(8,128)(2,1)S(1)} %collective-permute-done.3.refs_3_.refs_5_, ...), custom_call_target="tpu_custom_call" | custom-call | flops 5767499776 | tf_op jit(solution)/shard_map/pallas_call | solution.py:100
  61.6 4.8 %collective-permute-done.14.refs_2_.refs_11_ = bf16[448,512]{1,0:T(8,128)(2,1)S(1)} collective-permute-done((bf16[448,512]{1,0:T(8,128)(2,1)S(1)}, bf16[448,512]{1,0:T(8,128)(2,1)S(1)}, u32[]{:S(2)}, u32[]{:S(2)}) %collective-permute-start.14) | collective-permute-done | bytes 458784 | tf_op jit(solution)/shard_map/ppermute | solution.py:39
  70.8 1.6 %collective-permute-start.8 = (bf16[176,768]{1,0:T(8,128)(2,1)S(1)}, bf16[176,768]{1,0:T(8,128)(2,1)S(1)}, u32[]{:S(2)}, u32[]{:S(2)}) collective-permute-start(bf16[176,768]{1,0:T(8,128)(2,1)S(1)} %fusion), channel_id=1, source_target_pairs={{0,2},{1,3},{2,0},{3,1},{4,6},{5,7},{6,4},{7,5},{8,10},{9,11},{10,... | collective-permute-start | bytes 811016 | tf_op jit(solution)/shard_map/ppermute | solution.py:39
  73.5 3.2 %shard_map.81.refs_10_ = f32[2,512,256]{2,1,0:T(8,128)S(1)} custom-call(s32[8]{0:T(128)S(1)} %copy-done.5, s32[8]{0:T(128)S(1)} %copy-done.4, s32[8]{0:T(128)S(1)} %copy-done.6, bf16[256,2048]{1,0:T(8,128)(2,1)S(1)} %get-tuple-element.27.refs_3_, bf16[256,2048]{1,0:T(8,128)(2,1)S(1)} %collective-permute-done.15.refs_4_, ...), custom_call_target="tpu_custom_call" | custom-call | flops 5767499776 | tf_op jit(solution)/shard_map/pallas_call | solution.py:423
  76.7 1.6 %shard_map.82 = (f32[2,128,128]{2,1,0:T(8,128)S(1)}, f32[2,128,128]{2,1,0:T(8,128)S(1)}) custom-call(s32[8]{0:T(128)S(1)} %copy-done.5, s32[8]{0:T(128)S(1)} %copy-done.4, s32[8]{0:T(128)S(1)} %copy-done.6, bf16[256,2048]{1,0:T(8,128)(2,1)S(1)} %get-tuple-element.27.refs_3_, bf16[256,2048]{1,0:T(8,128)(2,1)S(1)} %collective-permute-done.15.refs_4_, ...), custom_call_target="tpu_custom_call" | custom-call | flops 17302499328 | tf_op jit(solution)/shard_map/pallas_call | solution.py:423
  80.1 1.6 %collective-permute-start.19 = (f32[1,128,128]{2,1,0:T(8,128)S(1)}, f32[1,128,128]{2,1,0:T(8,128)S(1)}, u32[]{:S(2)}, u32[]{:S(2)}) collective-permute-start(f32[1,128,128]{2,1,0:T(8,128)S(1)} %get-tuple-element.33), channel_id=1, source_target_pairs={{0,2},{1,3},{2,0},{3,1},{4,6},{5,7},{6,4},{7,5},{8,10},{9,11},{10,... | collective-permute-start | bytes 196616 | tf_op jit(solution)/shard_map/ppermute | solution.py:39
  81.7 3.8 %collective-permute-done.12 = bf16[80,768]{1,0:T(8,128)(2,1)S(1)} collective-permute-done((bf16[80,768]{1,0:T(8,128)(2,1)S(1)}, bf16[80,768]{1,0:T(8,128)(2,1)S(1)}, u32[]{:S(2)}, u32[]{:S(2)}) %collective-permute-start.12) | collective-permute-done | bytes 122912 | tf_op jit(solution)/shard_map/ppermute | solution.py:39
  86.3 2.1 %shard_map.83 = bf16[256,768]{1,0:T(8,128)(2,1)} custom-call(s32[8]{0:T(128)S(1)} %copy-done.5, s32[8]{0:T(128)S(1)} %copy-done.4, s32[8]{0:T(128)S(1)} %copy-done.6, bf16[256,768]{1,0:T(8,128)(2,1)S(1)} %pad_maximum_fusion.refs_3_, f32[256,768]{1,0:T(8,128)S(1)} %fusion.5.refs_4_, f32[256,768]{1,0:T(8,128)S(1)} %collective-permute-done.16.refs_5_, ...), custom_call_target="tpu_custom_call" | custom-call | flops 25165824 | bytes 1572864 | tf_op jit(solution)/shard_map/pallas_call | solution.py:443
  (50 shorter events, 11.1 us)
Async XLA Ops:
  3.3 24.1 %copy-start.2 = (bf16[512,16,64]{0,2,1:T(8,128)(2,1)S(1)}, bf16[512,16,64]{0,2,1:T(8,128)(2,1)}, u32[]{:S(2)}) copy-start(bf16[512,16,64]{0,2,1:T(8,128)(2,1)} %param.9) | copy-start | bytes 3145732
  3.3 24.1 %copy-start.4 = (s32[8]{0:T(128)S(1)}, s32[8]{0:T(128)}, u32[]{:S(2)}) copy-start(s32[8]{0:T(128)} %refs_1_.5) | copy-start | bytes 100
  5.0 21.8 %collective-permute-start.2 = (bf16[256,768]{1,0:T(8,128)(2,1)S(1)}, bf16[256,768]{1,0:T(8,128)(2,1)S(1)}, u32[]{:S(2)}, u32[]{:S(2)}) collective-permute-start(bf16[256,768]{1,0:T(8,128)(2,1)S(1)} %get-tuple-element.20.refs_0_), channel_id=1, source_target_pairs={{0,8},{1,9},{2,10},{3,11},{4,12},{5,13},{6,14},{7,15},{8,0},{9,1},... | collective-permute-start | bytes 1179656 | tf_op jit(solution)/shard_map/ppermute | solution.py:39
  9.1 36.7 %collective-permute-start = (bf16[176,2048]{1,0:T(8,128)(2,1)S(1)}, bf16[176,2048]{1,0:T(8,128)(2,1)S(1)}, u32[]{:S(2)}, u32[]{:S(2)}) collective-permute-start(bf16[176,2048]{1,0:T(8,128)(2,1)S(1)} %get-tuple-element.19), channel_id=1, source_target_pairs={{0,2},{1,3},{2,0},{3,1},{4,6},{5,7},{6,4},{7,5},{8,10},{9,11},{10,... | collective-permute-start | bytes 2162696 | tf_op jit(solution)/shard_map/ppermute | solution.py:39
  10.6 35.2 %collective-permute-start.6 = (bf16[176,2048]{1,0:T(8,128)(2,1)S(1)}, bf16[176,2048]{1,0:T(8,128)(2,1)S(1)}, u32[]{:S(2)}, u32[]{:S(2)}) collective-permute-start(bf16[176,2048]{1,0:T(8,128)(2,1)S(1)} %get-tuple-element.22), channel_id=1, source_target_pairs={{0,3},{1,2},{2,1},{3,0},{4,7},{5,6},{6,5},{7,4},{8,11},{9,10},{10,... | collective-permute-start | bytes 2162696 | tf_op jit(solution)/shard_map/ppermute | solution.py:39
  10.6 19.2 %collective-permute-start.1 = (bf16[256,768]{1,0:T(8,128)(2,1)S(1)}, bf16[256,768]{1,0:T(8,128)(2,1)S(1)}, u32[]{:S(2)}, u32[]{:S(2)}) collective-permute-start(bf16[256,768]{1,0:T(8,128)(2,1)S(1)} %get-tuple-element.20.refs_0_), channel_id=1, source_target_pairs={{0,4},{1,5},{2,6},{3,7},{4,0},{5,1},{6,2},{7,3},{8,12},{9,13},{10,... | collective-permute-start | bytes 1179656 | tf_op jit(solution)/shard_map/ppermute | solution.py:39
  26.8 17.6 %collective-permute-start.4 = (bf16[256,768]{1,0:T(8,128)(2,1)S(1)}, bf16[256,768]{1,0:T(8,128)(2,1)S(1)}, u32[]{:S(2)}, u32[]{:S(2)}) collective-permute-start(bf16[256,768]{1,0:T(8,128)(2,1)S(1)} %collective-permute-done.2.refs_0_.refs_4_.refs_1_), channel_id=1, source_target_pairs={{0,4},{1,5},{2,6},{3,7},{4,0},{5,1},{6,2},{7,3},{8,12},{9,13},{10,... | collective-permute-start | bytes 1179656 | tf_op jit(solution)/shard_map/ppermute | solution.py:39
  30.1 22.8 %collective-permute-start.13 = (bf16[448,512]{1,0:T(8,128)(2,1)S(1)}, bf16[448,512]{1,0:T(8,128)(2,1)S(1)}, u32[]{:S(2)}, u32[]{:S(2)}) collective-permute-start(bf16[448,512]{1,0:T(8,128)(2,1)S(1)} %shard_map.78), channel_id=1, source_target_pairs={{0,8},{1,9},{2,10},{3,11},{4,12},{5,13},{6,14},{7,15},{8,0},{9,1},... | collective-permute-start | bytes 1376264 | tf_op jit(solution)/shard_map/ppermute | solution.py:39
  32.7 20.5 %collective-permute-start.3 = (bf16[512,768]{1,0:T(8,128)(2,1)S(1)}, bf16[512,768]{1,0:T(8,128)(2,1)S(1)}, u32[]{:S(2)}, u32[]{:S(2)}) collective-permute-start(bf16[512,768]{1,0:T(8,128)(2,1)S(1)} %shard_map.74), channel_id=1, source_target_pairs={{0,16},{16,0},{1,17},{17,1},{2,18},{18,2},{3,19},{19,3},{4,20},{20... | collective-permute-start | bytes 2359304 | tf_op jit(solution)/shard_map/ppermute | solution.py:39
  44.3 15.7 %collective-permute-start.5 = (bf16[256,768]{1,0:T(8,128)(2,1)S(1)}, bf16[256,768]{1,0:T(8,128)(2,1)S(1)}, u32[]{:S(2)}, u32[]{:S(2)}) collective-permute-start(bf16[256,768]{1,0:T(8,128)(2,1)S(1)} %collective-permute-done.4.refs_6_.refs_1_), channel_id=1, source_target_pairs={{0,16},{16,0},{1,17},{17,1},{2,18},{18,2},{3,19},{19,3},{4,20},{20... | collective-permute-start | bytes 1179656 | tf_op jit(solution)/shard_map/ppermute | solution.py:39
  46.0 21.8 %collective-permute-start.10 = (bf16[80,2048]{1,0:T(8,128)(2,1)S(1)}, bf16[80,2048]{1,0:T(8,128)(2,1)S(1)}, u32[]{:S(2)}, u32[]{:S(2)}) collective-permute-start(bf16[80,2048]{1,0:T(8,128)(2,1)S(1)} %get-tuple-element.26), channel_id=1, source_target_pairs={{0,3},{1,2},{2,1},{3,0},{4,7},{5,6},{6,5},{7,4},{8,11},{9,10},{10,... | collective-permute-start | bytes 983048 | tf_op jit(solution)/shard_map/ppermute | solution.py:39
  46.1 27.4 %collective-permute-start.9 = (bf16[80,2048]{1,0:T(8,128)(2,1)S(1)}, bf16[80,2048]{1,0:T(8,128)(2,1)S(1)}, u32[]{:S(2)}, u32[]{:S(2)}) collective-permute-start(bf16[80,2048]{1,0:T(8,128)(2,1)S(1)} %get-tuple-element.25), channel_id=1, source_target_pairs={{0,2},{1,3},{2,0},{3,1},{4,6},{5,7},{6,4},{7,5},{8,10},{9,11},{10,... | collective-permute-start | bytes 983048 | tf_op jit(solution)/shard_map/ppermute | solution.py:39
  52.9 13.5 %collective-permute-start.14 = (bf16[448,512]{1,0:T(8,128)(2,1)S(1)}, bf16[448,512]{1,0:T(8,128)(2,1)S(1)}, u32[]{:S(2)}, u32[]{:S(2)}) collective-permute-start(bf16[448,512]{1,0:T(8,128)(2,1)S(1)} %shard_map.79), channel_id=1, source_target_pairs={{0,4},{1,5},{2,6},{3,7},{4,0},{5,1},{6,2},{7,3},{8,12},{9,13},{10,... | collective-permute-start | bytes 1376264 | tf_op jit(solution)/shard_map/ppermute | solution.py:39
  53.2 23.5 %collective-permute-start.17 = (bf16[448,512]{1,0:T(8,128)(2,1)S(1)}, bf16[448,512]{1,0:T(8,128)(2,1)S(1)}, u32[]{:S(2)}, u32[]{:S(2)}) collective-permute-start(bf16[448,512]{1,0:T(8,128)(2,1)S(1)} %collective-permute-done.13.refs_1_.refs_10_), channel_id=1, source_target_pairs={{0,4},{1,5},{2,6},{3,7},{4,0},{5,1},{6,2},{7,3},{8,12},{9,13},{10,... | collective-permute-start | bytes 1376264 | tf_op jit(solution)/shard_map/ppermute | solution.py:39
  66.5 5.9 %collective-permute-start.15 = (bf16[256,2048]{1,0:T(8,128)(2,1)S(1)}, bf16[256,2048]{1,0:T(8,128)(2,1)S(1)}, u32[]{:S(2)}, u32[]{:S(2)}) collective-permute-start(bf16[256,2048]{1,0:T(8,128)(2,1)S(1)} %shard_map.80), channel_id=1, source_target_pairs={{0,1},{1,0},{2,3},{3,2},{4,5},{5,4},{6,7},{7,6},{8,9},{9,8},{10,11... | collective-permute-start | bytes 3145736 | tf_op jit(solution)/shard_map/ppermute | solution.py:39
  67.3 2.7 %collective-permute-start.7 = (f32[176,768]{1,0:T(8,128)S(1)}, f32[176,768]{1,0:T(8,128)S(1)}, u32[]{:S(2)}, u32[]{:S(2)}) collective-permute-start(f32[176,768]{1,0:T(8,128)S(1)} %fusion.3), channel_id=1, source_target_pairs={{0,1},{1,0},{2,3},{3,2},{4,5},{5,4},{6,7},{7,6},{8,9},{9,8},{10,11... | collective-permute-start | bytes 1622024 | tf_op jit(solution)/shard_map/ppermute | solution.py:39
  68.5 10.4 %collective-permute-start.11 = (f32[80,768]{1,0:T(8,128)S(1)}, f32[80,768]{1,0:T(8,128)S(1)}, u32[]{:S(2)}, u32[]{:S(2)}) collective-permute-start(f32[80,768]{1,0:T(8,128)S(1)} %fusion.4), channel_id=1, source_target_pairs={{0,1},{1,0},{2,3},{3,2},{4,5},{5,4},{6,7},{7,6},{8,9},{9,8},{10,11... | collective-permute-start | bytes 737288 | tf_op jit(solution)/shard_map/ppermute | solution.py:39
  70.7 2.7 %copy-start.5 = (s32[8]{0:T(128)S(1)}, s32[8]{0:T(128)}, u32[]{:S(2)}) copy-start(s32[8]{0:T(128)} %refs_0_.5) | copy-start | bytes 100
  70.8 14.8 %collective-permute-start.8 = (bf16[176,768]{1,0:T(8,128)(2,1)S(1)}, bf16[176,768]{1,0:T(8,128)(2,1)S(1)}, u32[]{:S(2)}, u32[]{:S(2)}) collective-permute-start(bf16[176,768]{1,0:T(8,128)(2,1)S(1)} %fusion), channel_id=1, source_target_pairs={{0,2},{1,3},{2,0},{3,1},{4,6},{5,7},{6,4},{7,5},{8,10},{9,11},{10,... | collective-permute-start | bytes 811016 | tf_op jit(solution)/shard_map/ppermute | solution.py:39
  73.4 12.9 %collective-permute-start.16 = (f32[256,768]{1,0:T(8,128)S(1)}, f32[256,768]{1,0:T(8,128)S(1)}, u32[]{:S(2)}, u32[]{:S(2)}) collective-permute-start(f32[256,768]{1,0:T(8,128)S(1)} %fusion.6), channel_id=1, source_target_pairs={{0,1},{1,0},{2,3},{3,2},{4,5},{5,4},{6,7},{7,6},{8,9},{9,8},{10,11... | collective-permute-start | bytes 2359304 | tf_op jit(solution)/shard_map/ppermute | solution.py:39
  78.3 7.9 %copy-start.1 = (bf16[16,64,768]{2,1,0:T(8,128)(2,1)S(1)}, bf16[16,64,768]{2,1,0:T(8,128)(2,1)}, u32[]{:S(2)}) copy-start(bf16[16,64,768]{2,1,0:T(8,128)(2,1)} %refs_8_.1) | copy-start | bytes 4718596
  78.3 1.7 %collective-permute-start.18 = (f32[2,128,128]{2,1,0:T(8,128)S(1)}, f32[2,128,128]{2,1,0:T(8,128)S(1)}, u32[]{:S(2)}, u32[]{:S(2)}) collective-permute-start(f32[2,128,128]{2,1,0:T(8,128)S(1)} %get-tuple-element.32), channel_id=1, source_target_pairs={{0,1},{1,0},{2,3},{3,2},{4,5},{5,4},{6,7},{7,6},{8,9},{9,8},{10,11... | collective-permute-start | bytes 393224 | tf_op jit(solution)/shard_map/ppermute | solution.py:39
  79.5 6.0 %collective-permute-start.12 = (bf16[80,768]{1,0:T(8,128)(2,1)S(1)}, bf16[80,768]{1,0:T(8,128)(2,1)S(1)}, u32[]{:S(2)}, u32[]{:S(2)}) collective-permute-start(bf16[80,768]{1,0:T(8,128)(2,1)S(1)} %fusion.1), channel_id=1, source_target_pairs={{0,2},{1,3},{2,0},{3,1},{4,6},{5,7},{6,4},{7,5},{8,10},{9,11},{10,... | collective-permute-start | bytes 368648 | tf_op jit(solution)/shard_map/ppermute | solution.py:39
  80.1 6.2 %collective-permute-start.19 = (f32[1,128,128]{2,1,0:T(8,128)S(1)}, f32[1,128,128]{2,1,0:T(8,128)S(1)}, u32[]{:S(2)}, u32[]{:S(2)}) collective-permute-start(f32[1,128,128]{2,1,0:T(8,128)S(1)} %get-tuple-element.33), channel_id=1, source_target_pairs={{0,2},{1,3},{2,0},{3,1},{4,6},{5,7},{6,4},{7,5},{8,10},{9,11},{10,... | collective-permute-start | bytes 196616 | tf_op jit(solution)/shard_map/ppermute | solution.py:39
  (3 other events, 6.1 us)

commit v9 on v8

--- a/solution.py
+++ b/solution.py
@@ -13,7 +13,7 @@
 LAYER_CHIPS = 4
 VMEM_BYTES = 28 * 1024 * 1024
 CORE_FLOPS_PER_US = 1_153_500_000
-CFG = {'us': {}, 'z3': 2, 'c': 2, 'xcut': 2, 'ph': [11, 5]}
+CFG = {'us': {'all': 30, 'far': 2}, 'z3': 2, 'c': 'W', 'xcut': 2, 'ph': [11, 5]}
 WAITS = {"far": 12, "keys": 0, "all": 5, "across": 0, "near": 0, "low": (5, 15)}
 WAITS.update(CFG.get("us", {}))
 PHASES = tuple(CFG.get("ph", [8, 8]))
@@ -386,7 +386,8 @@
         down_bundles = over_layers(across_sent, down_sent)
 
     cm = CFG.get("c", 2)
-    near = [first[0], swap(gate(first[1], *[v for _, v in down_bundles[:cm]]) if cm else first[1], "batch", 1)]
+    c_ready = {"W": [keys], "Z3W": [keys, down_bundles[0][1]], "X": [swapped] if splits > 1 else []}.get(cm) if isinstance(cm, str) else [v for _, v in down_bundles[:cm]]
+    near = [first[0], swap(gate(first[1], *c_ready) if cm else first[1], "batch", 1)]
 
     def base_of(value):
         return jnp.dot(value, keys, preferred_element_type=f32)

time: 88.5 us -> 86.5 us (0.977)
  waiting for transfers between devices: 46.2 us -> 43.8 us
    ppermute x20, waiting for transfers between devices: 46.2 us -> 43.8 us  [swap(): lax.ppermute(value, axis, [(i, i ^ bit) for i in range(lax.axis_size(axis...]
  transfers between devices with their start and end apart: 20 -> 20, of which waited for: 10 -> 9; matrix products, arithmetic and copies ran while one was open for 5% -> 6% of each run, Pallas kernels for 10% -> 10%
where the time goes in v9:
time: 86.5 us; the launch traced here: 86.3 us
  waiting for transfers between devices  43.8 us (51%)
  starting transfers between devices  21.7 us (25%)
  Pallas kernels  12.4 us (14%)
  matrix products  4.75 us (5%)
  local copies, waits for them, and re-layouts  3.36 us (4%)
    ppermute x20, waiting for transfers between devices, swap(): lax.ppermute(value, axis, [(i, i ^ bit) for i in range(lax.axis_size(axis...  43.8 us
    ppermute x20, starting transfers between devices, swap(): lax.ppermute(value, axis, [(i, i ^ bit) for i in range(lax.axis_size(axis...  21.7 us
    pallas_call x2, Pallas kernels, low_call(): call(functools.partial(low_kernel, group, layers, rows, chunks, depth, ra...  4.78 us
    dot_general x6, matrix products, base_of(): return jnp.dot(value, keys, preferred_element_type=f32)  4.75 us
    unnamed x14, local copies, waits for them, and re-layouts  3.35 us
    pallas_call x6, Pallas kernels, stack(): call(functools.partial(stack_kernel, tuple(moves), len(values), count), o...  2.82 us
    pallas_call x1, Pallas kernels, shards(): call(functools.partial(final_kernel, rows, rank, len(bases), len(fars), l...  2.11 us
  transfers between devices with their start and end apart: 20, of which 9 were waited for; matrix products, arithmetic and copies ran while one was open for 6% of the time, Pallas kernels for 10%

profile of v9, /device:TPU:0, one launch (start us, length us, event | category | flops | bytes accessed | tf_op | source)
XLA Modules:
  0.0 86.3 jit_solution(15607350133787527718)
XLA Ops:
  0.0 2.2 %copy-done = bf16[256,8192]{1,0:T(8,128)(2,1)S(1)} copy-done((bf16[256,8192]{1,0:T(8,128)(2,1)S(1)}, bf16[256,8192]{1,0:T(8,128)(2,1)}, u32[]{:S(2)}) %copy-start) | copy-done | bytes 4194328
  2.2 1.1 %copy-done.3 = bf16[512,768]{1,0:T(8,128)(2,1)S(1)} copy-done((bf16[512,768]{1,0:T(8,128)(2,1)S(1)}, bf16[512,768]{1,0:T(8,128)(2,1)}, u32[]{:S(2)}) %copy-start.3) | copy-done | bytes 786456
  3.3 1.7 %shard_map.73 = (bf16[256,768]{1,0:T(8,128)(2,1)S(1)}, bf16[256,768]{1,0:T(8,128)(2,1)S(1)}, bf16[256,2048]{1,0:T(8,128)(2,1)S(1)}, bf16[256,2048]{1,0:T(8,128)(...) custom-call(bf16[512,768]{1,0:T(8,128)(2,1)S(1)} %copy-done.3, ...), custom_call_target="tpu_custom_call" | custom-call | bytes 9961472 | tf_op jit(solution)/shard_map/pallas_call | solution.py:291
  5.0 4.1 %collective-permute-start.2 = (bf16[256,768]{1,0:T(8,128)(2,1)S(1)}, bf16[256,768]{1,0:T(8,128)(2,1)S(1)}, u32[]{:S(2)}, u32[]{:S(2)}) collective-permute-start(bf16[256,768]{1,0:T(8,128)(2,1)S(1)} %get-tuple-element.20.refs_0_), channel_id=1, source_target_pairs={{0,8},{1,9},{2,10},{3,11},{4,12},{5,13},{6,14},{7,15},{8,0},{9,1},... | collective-permute-start | bytes 1179656 | tf_op jit(solution)/shard_map/ppermute | solution.py:39
  9.1 1.6 %collective-permute-start.1 = (bf16[256,768]{1,0:T(8,128)(2,1)S(1)}, bf16[256,768]{1,0:T(8,128)(2,1)S(1)}, u32[]{:S(2)}, u32[]{:S(2)}) collective-permute-start(bf16[256,768]{1,0:T(8,128)(2,1)S(1)} %get-tuple-element.20.refs_0_), channel_id=1, source_target_pairs={{0,4},{1,5},{2,6},{3,7},{4,0},{5,1},{6,2},{7,3},{8,12},{9,13},{10,... | collective-permute-start | bytes 1179656 | tf_op jit(solution)/shard_map/ppermute | solution.py:39
  10.7 1.5 %collective-permute-start = (bf16[176,2048]{1,0:T(8,128)(2,1)S(1)}, bf16[176,2048]{1,0:T(8,128)(2,1)S(1)}, u32[]{:S(2)}, u32[]{:S(2)}) collective-permute-start(bf16[176,2048]{1,0:T(8,128)(2,1)S(1)} %get-tuple-element.19), channel_id=1, source_target_pairs={{0,2},{1,3},{2,0},{3,1},{4,6},{5,7},{6,4},{7,5},{8,10},{9,11},{10,... | collective-permute-start | bytes 2162696 | tf_op jit(solution)/shard_map/ppermute | solution.py:39
  12.2 14.5 %collective-permute-done.2.refs_0_.refs_4_.refs_1_ = bf16[256,768]{1,0:T(8,128)(2,1)S(1)} collective-permute-done((bf16[256,768]{1,0:T(8,128)(2,1)S(1)}, bf16[256,768]{1,0:T(8,128)(2,1)S(1)}, u32[]{:S(2)}, u32[]{:S(2)}) %collective-permute-start.2) | collective-permute-done | bytes 393248 | tf_op jit(solution)/shard_map/ppermute | solution.py:39
  27.4 1.6 %collective-permute-start.3 = (bf16[512,768]{1,0:T(8,128)(2,1)S(1)}, bf16[512,768]{1,0:T(8,128)(2,1)S(1)}, u32[]{:S(2)}, u32[]{:S(2)}) collective-permute-start(bf16[512,768]{1,0:T(8,128)(2,1)S(1)} %shard_map.74), channel_id=1, source_target_pairs={{0,16},{16,0},{1,17},{17,1},{2,18},{18,2},{3,19},{19,3},{4,20},{20... | collective-permute-start | bytes 2359304 | tf_op jit(solution)/shard_map/ppermute | solution.py:39
  28.9 1.4 %collective-permute-start.4 = (bf16[256,768]{1,0:T(8,128)(2,1)S(1)}, bf16[256,768]{1,0:T(8,128)(2,1)S(1)}, u32[]{:S(2)}, u32[]{:S(2)}) collective-permute-start(bf16[256,768]{1,0:T(8,128)(2,1)S(1)} %collective-permute-done.2.refs_0_.refs_4_.refs_1_), channel_id=1, source_target_pairs={{0,4},{1,5},{2,6},{3,7},{4,0},{5,1},{6,2},{7,3},{8,12},{9,13},{10,... | collective-permute-start | bytes 1179656 | tf_op jit(solution)/shard_map/ppermute | solution.py:39
  30.4 1.1 %shard_map.78 = (bf16[448,512]{1,0:T(8,128)(2,1)S(1)}, bf16[448,512]{1,0:T(8,128)(2,1)S(1)}) custom-call(s32[8]{0:T(128)S(1)} %copy-done.4, bf16[16,64,512]{2,1,0:T(8,128)(2,1)S(1)} %bitcast.16), custom_call_target="tpu_custom_call" | custom-call | bytes 1835008 | tf_op jit(solution)/shard_map/pallas_call | solution.py:324
  31.7 2.4 %collective-permute-start.15 = (bf16[448,512]{1,0:T(8,128)(2,1)S(1)}, bf16[448,512]{1,0:T(8,128)(2,1)S(1)}, u32[]{:S(2)}, u32[]{:S(2)}) collective-permute-start(bf16[448,512]{1,0:T(8,128)(2,1)S(1)} %shard_map.79), channel_id=1, source_target_pairs={{0,8},{1,9},{2,10},{3,11},{4,12},{5,13},{6,14},{7,15},{8,0},{9,1},... | collective-permute-start | bytes 1376264 | tf_op jit(solution)/shard_map/ppermute | solution.py:39
  34.1 11.1 %collective-permute-done.4.refs_6_.refs_1_ = bf16[256,768]{1,0:T(8,128)(2,1)S(1)} collective-permute-done((bf16[256,768]{1,0:T(8,128)(2,1)S(1)}, bf16[256,768]{1,0:T(8,128)(2,1)S(1)}, u32[]{:S(2)}, u32[]{:S(2)}) %collective-permute-start.4) | collective-permute-done | bytes 393248 | tf_op jit(solution)/shard_map/ppermute | solution.py:39
  46.3 1.3 %collective-permute-start.9 = (bf16[80,2048]{1,0:T(8,128)(2,1)S(1)}, bf16[80,2048]{1,0:T(8,128)(2,1)S(1)}, u32[]{:S(2)}, u32[]{:S(2)}) collective-permute-start(bf16[80,2048]{1,0:T(8,128)(2,1)S(1)} %get-tuple-element.25), channel_id=1, source_target_pairs={{0,2},{1,3},{2,0},{3,1},{4,6},{5,7},{6,4},{7,5},{8,10},{9,11},{10,... | collective-permute-start | bytes 983048 | tf_op jit(solution)/shard_map/ppermute | solution.py:39
  47.9 6.2 %collective-permute-done.15.refs_10_ = bf16[448,512]{1,0:T(8,128)(2,1)S(1)} collective-permute-done((bf16[448,512]{1,0:T(8,128)(2,1)S(1)}, bf16[448,512]{1,0:T(8,128)(2,1)S(1)}, u32[]{:S(2)}, u32[]{:S(2)}) %collective-permute-start.15) | collective-permute-done | bytes 458784 | tf_op jit(solution)/shard_map/ppermute | solution.py:39
  54.1 2.0 %collective-permute-start.16 = (bf16[448,512]{1,0:T(8,128)(2,1)S(1)}, bf16[448,512]{1,0:T(8,128)(2,1)S(1)}, u32[]{:S(2)}, u32[]{:S(2)}) collective-permute-start(bf16[448,512]{1,0:T(8,128)(2,1)S(1)} %collective-permute-done.15.refs_10_), channel_id=1, source_target_pairs={{0,4},{1,5},{2,6},{3,7},{4,0},{5,1},{6,2},{7,3},{8,12},{9,13},{10,... | collective-permute-start | bytes 1376264 | tf_op jit(solution)/shard_map/ppermute | solution.py:39
  56.2 1.6 %shard_map.75.refs_1_ = bf16[2048,768]{1,0:T(8,128)(2,1)S(1)} custom-call(bf16[256,768]{1,0:T(8,128)(2,1)S(1)} %get-tuple-element.20.refs_0_, bf16[256,768]{1,0:T(8,128)(2,1)S(1)} %get-tuple-element.21.refs_1_, bf16[256,768]{1,0:T(8,128)(2,1)S(1)} %collective-permute-done.1.refs_1_.refs_2_, bf16[512,768]{1,0:T(8,128)(2,1)S(1)} %collective-permute-done.3.refs_3_.refs_5_, ...), custom_call_target="tpu_custom_call" | custom-call | flops 34604998656 | tf_op jit(solution)/shard_map/pallas_call | solution.py:100
  62.3 1.6 %collective-permute-start.8 = (bf16[176,768]{1,0:T(8,128)(2,1)S(1)}, bf16[176,768]{1,0:T(8,128)(2,1)S(1)}, u32[]{:S(2)}, u32[]{:S(2)}) collective-permute-start(bf16[176,768]{1,0:T(8,128)(2,1)S(1)} %fusion), channel_id=1, source_target_pairs={{0,2},{1,3},{2,0},{3,1},{4,6},{5,7},{6,4},{7,5},{8,10},{9,11},{10,... | collective-permute-start | bytes 811016 | tf_op jit(solution)/shard_map/ppermute | solution.py:39
  65.0 2.6 %collective-permute-done.17.refs_11_ = bf16[448,512]{1,0:T(8,128)(2,1)S(1)} collective-permute-done((bf16[448,512]{1,0:T(8,128)(2,1)S(1)}, bf16[448,512]{1,0:T(8,128)(2,1)S(1)}, u32[]{:S(2)}, u32[]{:S(2)}) %collective-permute-start.17) | collective-permute-done | bytes 458784 | tf_op jit(solution)/shard_map/ppermute | solution.py:39
  67.6 3.2 %shard_map.81.refs_10_ = f32[2,512,256]{2,1,0:T(8,128)S(1)} custom-call(s32[8]{0:T(128)S(1)} %copy-done.5, s32[8]{0:T(128)S(1)} %copy-done.4, s32[8]{0:T(128)S(1)} %copy-done.6, bf16[256,2048]{1,0:T(8,128)(2,1)S(1)} %get-tuple-element.27.refs_3_, bf16[256,2048]{1,0:T(8,128)(2,1)S(1)} %collective-permute-done.13.refs_4_, ...), custom_call_target="tpu_custom_call" | custom-call | flops 5767499776 | tf_op jit(solution)/shard_map/pallas_call | solution.py:424
  70.8 3.8 %collective-permute-done.16.refs_9_ = bf16[448,512]{1,0:T(8,128)(2,1)S(1)} collective-permute-done((bf16[448,512]{1,0:T(8,128)(2,1)S(1)}, bf16[448,512]{1,0:T(8,128)(2,1)S(1)}, u32[]{:S(2)}, u32[]{:S(2)}) %collective-permute-start.16) | collective-permute-done | bytes 458784 | tf_op jit(solution)/shard_map/ppermute | solution.py:39
  74.6 1.6 %shard_map.82 = (f32[2,128,128]{2,1,0:T(8,128)S(1)}, f32[2,128,128]{2,1,0:T(8,128)S(1)}) custom-call(s32[8]{0:T(128)S(1)} %copy-done.5, s32[8]{0:T(128)S(1)} %copy-done.4, s32[8]{0:T(128)S(1)} %copy-done.6, bf16[256,2048]{1,0:T(8,128)(2,1)S(1)} %get-tuple-element.27.refs_3_, bf16[256,2048]{1,0:T(8,128)(2,1)S(1)} %collective-permute-done.13.refs_4_, ...), custom_call_target="tpu_custom_call" | custom-call | flops 17302499328 | tf_op jit(solution)/shard_map/pallas_call | solution.py:424
  77.0 1.6 %collective-permute-start.12 = (bf16[80,768]{1,0:T(8,128)(2,1)S(1)}, bf16[80,768]{1,0:T(8,128)(2,1)S(1)}, u32[]{:S(2)}, u32[]{:S(2)}) collective-permute-start(bf16[80,768]{1,0:T(8,128)(2,1)S(1)} %fusion.1), channel_id=1, source_target_pairs={{0,2},{1,3},{2,0},{3,1},{4,6},{5,7},{6,4},{7,5},{8,10},{9,11},{10,... | collective-permute-start | bytes 368648 | tf_op jit(solution)/shard_map/ppermute | solution.py:39
  79.3 3.9 %collective-permute-done.12 = bf16[80,768]{1,0:T(8,128)(2,1)S(1)} collective-permute-done((bf16[80,768]{1,0:T(8,128)(2,1)S(1)}, bf16[80,768]{1,0:T(8,128)(2,1)S(1)}, u32[]{:S(2)}, u32[]{:S(2)}) %collective-permute-start.12) | collective-permute-done | bytes 122912 | tf_op jit(solution)/shard_map/ppermute | solution.py:39
  84.2 2.1 %shard_map.83 = bf16[256,768]{1,0:T(8,128)(2,1)} custom-call(s32[8]{0:T(128)S(1)} %copy-done.5, s32[8]{0:T(128)S(1)} %copy-done.4, s32[8]{0:T(128)S(1)} %copy-done.6, bf16[256,768]{1,0:T(8,128)(2,1)S(1)} %pad_maximum_fusion.refs_3_, f32[256,768]{1,0:T(8,128)S(1)} %fusion.5.refs_4_, f32[256,768]{1,0:T(8,128)S(1)} %collective-permute-done.14.refs_5_, ...), custom_call_target="tpu_custom_call" | custom-call | flops 25165824 | bytes 1572864 | tf_op jit(solution)/shard_map/pallas_call | solution.py:444
  (50 shorter events, 10.3 us)
Async XLA Ops:
  3.3 27.0 %copy-start.2 = (bf16[512,16,64]{0,2,1:T(8,128)(2,1)S(1)}, bf16[512,16,64]{0,2,1:T(8,128)(2,1)}, u32[]{:S(2)}) copy-start(bf16[512,16,64]{0,2,1:T(8,128)(2,1)} %param.9) | copy-start | bytes 3145732
  3.3 27.0 %copy-start.4 = (s32[8]{0:T(128)S(1)}, s32[8]{0:T(128)}, u32[]{:S(2)}) copy-start(s32[8]{0:T(128)} %refs_1_.5) | copy-start | bytes 100
  5.0 21.8 %collective-permute-start.2 = (bf16[256,768]{1,0:T(8,128)(2,1)S(1)}, bf16[256,768]{1,0:T(8,128)(2,1)S(1)}, u32[]{:S(2)}, u32[]{:S(2)}) collective-permute-start(bf16[256,768]{1,0:T(8,128)(2,1)S(1)} %get-tuple-element.20.refs_0_), channel_id=1, source_target_pairs={{0,8},{1,9},{2,10},{3,11},{4,12},{5,13},{6,14},{7,15},{8,0},{9,1},... | collective-permute-start | bytes 1179656 | tf_op jit(solution)/shard_map/ppermute | solution.py:39
  9.1 17.8 %collective-permute-start.1 = (bf16[256,768]{1,0:T(8,128)(2,1)S(1)}, bf16[256,768]{1,0:T(8,128)(2,1)S(1)}, u32[]{:S(2)}, u32[]{:S(2)}) collective-permute-start(bf16[256,768]{1,0:T(8,128)(2,1)S(1)} %get-tuple-element.20.refs_0_), channel_id=1, source_target_pairs={{0,4},{1,5},{2,6},{3,7},{4,0},{5,1},{6,2},{7,3},{8,12},{9,13},{10,... | collective-permute-start | bytes 1179656 | tf_op jit(solution)/shard_map/ppermute | solution.py:39
  10.7 35.3 %collective-permute-start = (bf16[176,2048]{1,0:T(8,128)(2,1)S(1)}, bf16[176,2048]{1,0:T(8,128)(2,1)S(1)}, u32[]{:S(2)}, u32[]{:S(2)}) collective-permute-start(bf16[176,2048]{1,0:T(8,128)(2,1)S(1)} %get-tuple-element.19), channel_id=1, source_target_pairs={{0,2},{1,3},{2,0},{3,1},{4,6},{5,7},{6,4},{7,5},{8,10},{9,11},{10,... | collective-permute-start | bytes 2162696 | tf_op jit(solution)/shard_map/ppermute | solution.py:39
  12.2 33.8 %collective-permute-start.6 = (bf16[176,2048]{1,0:T(8,128)(2,1)S(1)}, bf16[176,2048]{1,0:T(8,128)(2,1)S(1)}, u32[]{:S(2)}, u32[]{:S(2)}) collective-permute-start(bf16[176,2048]{1,0:T(8,128)(2,1)S(1)} %get-tuple-element.22), channel_id=1, source_target_pairs={{0,3},{1,2},{2,1},{3,0},{4,7},{5,6},{6,5},{7,4},{8,11},{9,10},{10,... | collective-permute-start | bytes 2162696 | tf_op jit(solution)/shard_map/ppermute | solution.py:39
  27.4 26.8 %collective-permute-start.3 = (bf16[512,768]{1,0:T(8,128)(2,1)S(1)}, bf16[512,768]{1,0:T(8,128)(2,1)S(1)}, u32[]{:S(2)}, u32[]{:S(2)}) collective-permute-start(bf16[512,768]{1,0:T(8,128)(2,1)S(1)} %shard_map.74), channel_id=1, source_target_pairs={{0,16},{16,0},{1,17},{17,1},{2,18},{18,2},{3,19},{19,3},{4,20},{20... | collective-permute-start | bytes 2359304 | tf_op jit(solution)/shard_map/ppermute | solution.py:39
  28.9 16.2 %collective-permute-start.4 = (bf16[256,768]{1,0:T(8,128)(2,1)S(1)}, bf16[256,768]{1,0:T(8,128)(2,1)S(1)}, u32[]{:S(2)}, u32[]{:S(2)}) collective-permute-start(bf16[256,768]{1,0:T(8,128)(2,1)S(1)} %collective-permute-done.2.refs_0_.refs_4_.refs_1_), channel_id=1, source_target_pairs={{0,4},{1,5},{2,6},{3,7},{4,0},{5,1},{6,2},{7,3},{8,12},{9,13},{10,... | collective-permute-start | bytes 1179656 | tf_op jit(solution)/shard_map/ppermute | solution.py:39
  31.7 22.4 %collective-permute-start.15 = (bf16[448,512]{1,0:T(8,128)(2,1)S(1)}, bf16[448,512]{1,0:T(8,128)(2,1)S(1)}, u32[]{:S(2)}, u32[]{:S(2)}) collective-permute-start(bf16[448,512]{1,0:T(8,128)(2,1)S(1)} %shard_map.79), channel_id=1, source_target_pairs={{0,8},{1,9},{2,10},{3,11},{4,12},{5,13},{6,14},{7,15},{8,0},{9,1},... | collective-permute-start | bytes 1376264 | tf_op jit(solution)/shard_map/ppermute | solution.py:39
  45.2 11.0 %collective-permute-start.5 = (bf16[256,768]{1,0:T(8,128)(2,1)S(1)}, bf16[256,768]{1,0:T(8,128)(2,1)S(1)}, u32[]{:S(2)}, u32[]{:S(2)}) collective-permute-start(bf16[256,768]{1,0:T(8,128)(2,1)S(1)} %collective-permute-done.4.refs_6_.refs_1_), channel_id=1, source_target_pairs={{0,16},{16,0},{1,17},{17,1},{2,18},{18,2},{3,19},{19,3},{4,20},{20... | collective-permute-start | bytes 1179656 | tf_op jit(solution)/shard_map/ppermute | solution.py:39
  46.2 12.4 %collective-permute-start.10 = (bf16[80,2048]{1,0:T(8,128)(2,1)S(1)}, bf16[80,2048]{1,0:T(8,128)(2,1)S(1)}, u32[]{:S(2)}, u32[]{:S(2)}) collective-permute-start(bf16[80,2048]{1,0:T(8,128)(2,1)S(1)} %get-tuple-element.26), channel_id=1, source_target_pairs={{0,3},{1,2},{2,1},{3,0},{4,7},{5,6},{6,5},{7,4},{8,11},{9,10},{10,... | collective-permute-start | bytes 983048 | tf_op jit(solution)/shard_map/ppermute | solution.py:39
  46.3 18.6 %collective-permute-start.9 = (bf16[80,2048]{1,0:T(8,128)(2,1)S(1)}, bf16[80,2048]{1,0:T(8,128)(2,1)S(1)}, u32[]{:S(2)}, u32[]{:S(2)}) collective-permute-start(bf16[80,2048]{1,0:T(8,128)(2,1)S(1)} %get-tuple-element.25), channel_id=1, source_target_pairs={{0,2},{1,3},{2,0},{3,1},{4,6},{5,7},{6,4},{7,5},{8,10},{9,11},{10,... | collective-permute-start | bytes 983048 | tf_op jit(solution)/shard_map/ppermute | solution.py:39
  54.1 13.5 %collective-permute-start.17 = (bf16[448,512]{1,0:T(8,128)(2,1)S(1)}, bf16[448,512]{1,0:T(8,128)(2,1)S(1)}, u32[]{:S(2)}, u32[]{:S(2)}) collective-permute-start(bf16[448,512]{1,0:T(8,128)(2,1)S(1)} %shard_map.80), channel_id=1, source_target_pairs={{0,4},{1,5},{2,6},{3,7},{4,0},{5,1},{6,2},{7,3},{8,12},{9,13},{10,... | collective-permute-start | bytes 1376264 | tf_op jit(solution)/shard_map/ppermute | solution.py:39
  54.1 20.5 %collective-permute-start.16 = (bf16[448,512]{1,0:T(8,128)(2,1)S(1)}, bf16[448,512]{1,0:T(8,128)(2,1)S(1)}, u32[]{:S(2)}, u32[]{:S(2)}) collective-permute-start(bf16[448,512]{1,0:T(8,128)(2,1)S(1)} %collective-permute-done.15.refs_10_), channel_id=1, source_target_pairs={{0,4},{1,5},{2,6},{3,7},{4,0},{5,1},{6,2},{7,3},{8,12},{9,13},{10,... | collective-permute-start | bytes 1376264 | tf_op jit(solution)/shard_map/ppermute | solution.py:39
  57.8 4.4 %collective-permute-start.13 = (bf16[256,2048]{1,0:T(8,128)(2,1)S(1)}, bf16[256,2048]{1,0:T(8,128)(2,1)S(1)}, u32[]{:S(2)}, u32[]{:S(2)}) collective-permute-start(bf16[256,2048]{1,0:T(8,128)(2,1)S(1)} %shard_map.77), channel_id=1, source_target_pairs={{0,1},{1,0},{2,3},{3,2},{4,5},{5,4},{6,7},{7,6},{8,9},{9,8},{10,11... | collective-permute-start | bytes 3145736 | tf_op jit(solution)/shard_map/ppermute | solution.py:39
  58.7 2.7 %collective-permute-start.7 = (f32[176,768]{1,0:T(8,128)S(1)}, f32[176,768]{1,0:T(8,128)S(1)}, u32[]{:S(2)}, u32[]{:S(2)}) collective-permute-start(f32[176,768]{1,0:T(8,128)S(1)} %fusion.3), channel_id=1, source_target_pairs={{0,1},{1,0},{2,3},{3,2},{4,5},{5,4},{6,7},{7,6},{8,9},{9,8},{10,11... | collective-permute-start | bytes 1622024 | tf_op jit(solution)/shard_map/ppermute | solution.py:39
  61.3 15.0 %collective-permute-start.11 = (f32[80,768]{1,0:T(8,128)S(1)}, f32[80,768]{1,0:T(8,128)S(1)}, u32[]{:S(2)}, u32[]{:S(2)}) collective-permute-start(f32[80,768]{1,0:T(8,128)S(1)} %fusion.4), channel_id=1, source_target_pairs={{0,1},{1,0},{2,3},{3,2},{4,5},{5,4},{6,7},{7,6},{8,9},{9,8},{10,11... | collective-permute-start | bytes 737288 | tf_op jit(solution)/shard_map/ppermute | solution.py:39
  62.2 5.4 %copy-start.5 = (s32[8]{0:T(128)S(1)}, s32[8]{0:T(128)}, u32[]{:S(2)}) copy-start(s32[8]{0:T(128)} %refs_0_.5) | copy-start | bytes 100
  62.3 20.9 %collective-permute-start.8 = (bf16[176,768]{1,0:T(8,128)(2,1)S(1)}, bf16[176,768]{1,0:T(8,128)(2,1)S(1)}, u32[]{:S(2)}, u32[]{:S(2)}) collective-permute-start(bf16[176,768]{1,0:T(8,128)(2,1)S(1)} %fusion), channel_id=1, source_target_pairs={{0,2},{1,3},{2,0},{3,1},{4,6},{5,7},{6,4},{7,5},{8,10},{9,11},{10,... | collective-permute-start | bytes 811016 | tf_op jit(solution)/shard_map/ppermute | solution.py:39
  64.9 19.3 %collective-permute-start.14 = (f32[256,768]{1,0:T(8,128)S(1)}, f32[256,768]{1,0:T(8,128)S(1)}, u32[]{:S(2)}, u32[]{:S(2)}) collective-permute-start(f32[256,768]{1,0:T(8,128)S(1)} %fusion.6), channel_id=1, source_target_pairs={{0,1},{1,0},{2,3},{3,2},{4,5},{5,4},{6,7},{7,6},{8,9},{9,8},{10,11... | collective-permute-start | bytes 2359304 | tf_op jit(solution)/shard_map/ppermute | solution.py:39
  76.2 7.9 %copy-start.1 = (bf16[16,64,768]{2,1,0:T(8,128)(2,1)S(1)}, bf16[16,64,768]{2,1,0:T(8,128)(2,1)}, u32[]{:S(2)}) copy-start(bf16[16,64,768]{2,1,0:T(8,128)(2,1)} %refs_8_.1) | copy-start | bytes 4718596
  76.2 2.3 %collective-permute-start.18 = (f32[2,128,128]{2,1,0:T(8,128)S(1)}, f32[2,128,128]{2,1,0:T(8,128)S(1)}, u32[]{:S(2)}, u32[]{:S(2)}) collective-permute-start(f32[2,128,128]{2,1,0:T(8,128)S(1)} %get-tuple-element.32), channel_id=1, source_target_pairs={{0,1},{1,0},{2,3},{3,2},{4,5},{5,4},{6,7},{7,6},{8,9},{9,8},{10,11... | collective-permute-start | bytes 393224 | tf_op jit(solution)/shard_map/ppermute | solution.py:39
  77.0 6.2 %collective-permute-start.12 = (bf16[80,768]{1,0:T(8,128)(2,1)S(1)}, bf16[80,768]{1,0:T(8,128)(2,1)S(1)}, u32[]{:S(2)}, u32[]{:S(2)}) collective-permute-start(bf16[80,768]{1,0:T(8,128)(2,1)S(1)} %fusion.1), channel_id=1, source_target_pairs={{0,2},{1,3},{2,0},{3,1},{4,6},{5,7},{6,4},{7,5},{8,10},{9,11},{10,... | collective-permute-start | bytes 368648 | tf_op jit(solution)/shard_map/ppermute | solution.py:39
  78.6 5.6 %collective-permute-start.19 = (f32[1,128,128]{2,1,0:T(8,128)S(1)}, f32[1,128,128]{2,1,0:T(8,128)S(1)}, u32[]{:S(2)}, u32[]{:S(2)}) collective-permute-start(f32[1,128,128]{2,1,0:T(8,128)S(1)} %get-tuple-element.33), channel_id=1, source_target_pairs={{0,2},{1,3},{2,0},{3,1},{4,6},{5,7},{6,4},{7,5},{8,10},{9,11},{10,... | collective-permute-start | bytes 196616 | tf_op jit(solution)/shard_map/ppermute | solution.py:39
  (3 other events, 8.7 us)

commit v10 on v9

--- a/solution.py
+++ b/solution.py
@@ -13,7 +13,7 @@
 LAYER_CHIPS = 4
 VMEM_BYTES = 28 * 1024 * 1024
 CORE_FLOPS_PER_US = 1_153_500_000
-CFG = {'us': {'all': 30, 'far': 2}, 'z3': 2, 'c': 'W', 'xcut': 2, 'ph': [11, 5]}
+CFG = {'us': {'all': 30, 'far': 12}, 'z3': 2, 'c': 'W', 'xcut': 2, 'ph': [13, 3]}
 WAITS = {"far": 12, "keys": 0, "all": 5, "across": 0, "near": 0, "low": (5, 15)}
 WAITS.update(CFG.get("us", {}))
 PHASES = tuple(CFG.get("ph", [8, 8]))

time: 86.5 us -> 82.4 us (0.953)
  waiting for transfers between devices: 43.8 us -> 38 us
  starting transfers between devices: 21.7 us -> 22.8 us
    ppermute x20, waiting for transfers between devices: 43.8 us -> 38 us  [swap(): lax.ppermute(value, axis, [(i, i ^ bit) for i in range(lax.axis_size(axis...]
    ppermute x20, starting transfers between devices: 21.7 us -> 22.8 us  [swap(): lax.ppermute(value, axis, [(i, i ^ bit) for i in range(lax.axis_size(axis...]
  transfers between devices with their start and end apart: 20 -> 20, of which waited for: 9 -> 7; matrix products, arithmetic and copies ran while one was open for 6% -> 6% of each run, Pallas kernels for 10% -> 11%
where the time goes in v10:
time: 82.4 us; the launch traced here: 82.2 us
  waiting for transfers between devices  38 us (46%)
  starting transfers between devices  22.8 us (28%)
  Pallas kernels  12.8 us (16%)
  matrix products  5 us (6%)
  local copies, waits for them, and re-layouts  3.36 us (4%)
    ppermute x20, waiting for transfers between devices, swap(): lax.ppermute(value, axis, [(i, i ^ bit) for i in range(lax.axis_size(axis...  38 us
    ppermute x20, starting transfers between devices, swap(): lax.ppermute(value, axis, [(i, i ^ bit) for i in range(lax.axis_size(axis...  22.8 us
    dot_general x6, matrix products, base_of(): return jnp.dot(value, keys, preferred_element_type=f32)  5 us
    pallas_call x2, Pallas kernels, low_call(): call(functools.partial(low_kernel, group, layers, rows, chunks, depth, ra...  4.81 us
    unnamed x14, local copies, waits for them, and re-layouts  3.35 us
    pallas_call x6, Pallas kernels, stack(): call(functools.partial(stack_kernel, tuple(moves), len(values), count), o...  3.1 us
    pallas_call x1, Pallas kernels, shards(): call(functools.partial(final_kernel, rows, rank, len(bases), len(fars), l...  2.11 us
    pallas_call x1, Pallas kernels, shards(): call(functools.partial(first_kernel, group, layers, splits, part, chunks)...  1.67 us
  transfers between devices with their start and end apart: 20, of which 7 were waited for; matrix products, arithmetic and copies ran while one was open for 6% of the time, Pallas kernels for 11%

profile of v10, /device:TPU:0, one launch (start us, length us, event | category | flops | bytes accessed | tf_op | source)
XLA Modules:
  0.0 82.2 jit_solution(15993364760396584060)
XLA Ops:
  0.0 2.2 %copy-done = bf16[256,8192]{1,0:T(8,128)(2,1)S(1)} copy-done((bf16[256,8192]{1,0:T(8,128)(2,1)S(1)}, bf16[256,8192]{1,0:T(8,128)(2,1)}, u32[]{:S(2)}) %copy-start) | copy-done | bytes 4194328
  2.2 1.1 %copy-done.3 = bf16[512,768]{1,0:T(8,128)(2,1)S(1)} copy-done((bf16[512,768]{1,0:T(8,128)(2,1)S(1)}, bf16[512,768]{1,0:T(8,128)(2,1)}, u32[]{:S(2)}) %copy-start.3) | copy-done | bytes 786456
  3.3 1.7 %shard_map.73 = (bf16[256,768]{1,0:T(8,128)(2,1)S(1)}, bf16[256,768]{1,0:T(8,128)(2,1)S(1)}, bf16[256,2048]{1,0:T(8,128)(2,1)S(1)}, bf16[256,2048]{1,0:T(8,128)(...) custom-call(bf16[512,768]{1,0:T(8,128)(2,1)S(1)} %copy-done.3, ...), custom_call_target="tpu_custom_call" | custom-call | bytes 9961472 | tf_op jit(solution)/shard_map/pallas_call | solution.py:291
  5.0 3.0 %collective-permute-start = (bf16[208,2048]{1,0:T(8,128)(2,1)S(1)}, bf16[208,2048]{1,0:T(8,128)(2,1)S(1)}, u32[]{:S(2)}, u32[]{:S(2)}) collective-permute-start(bf16[208,2048]{1,0:T(8,128)(2,1)S(1)} %get-tuple-element.19), channel_id=1, source_target_pairs={{0,2},{1,3},{2,0},{3,1},{4,6},{5,7},{6,4},{7,5},{8,10},{9,11},{10,... | collective-permute-start | bytes 2555912 | tf_op jit(solution)/shard_map/ppermute | solution.py:39
  8.0 2.6 %collective-permute-start.2 = (bf16[256,768]{1,0:T(8,128)(2,1)S(1)}, bf16[256,768]{1,0:T(8,128)(2,1)S(1)}, u32[]{:S(2)}, u32[]{:S(2)}) collective-permute-start(bf16[256,768]{1,0:T(8,128)(2,1)S(1)} %get-tuple-element.20.refs_0_), channel_id=1, source_target_pairs={{0,8},{1,9},{2,10},{3,11},{4,12},{5,13},{6,14},{7,15},{8,0},{9,1},... | collective-permute-start | bytes 1179656 | tf_op jit(solution)/shard_map/ppermute | solution.py:39
  10.6 1.6 %collective-permute-start.1 = (bf16[256,768]{1,0:T(8,128)(2,1)S(1)}, bf16[256,768]{1,0:T(8,128)(2,1)S(1)}, u32[]{:S(2)}, u32[]{:S(2)}) collective-permute-start(bf16[256,768]{1,0:T(8,128)(2,1)S(1)} %get-tuple-element.20.refs_0_), channel_id=1, source_target_pairs={{0,4},{1,5},{2,6},{3,7},{4,0},{5,1},{6,2},{7,3},{8,12},{9,13},{10,... | collective-permute-start | bytes 1179656 | tf_op jit(solution)/shard_map/ppermute | solution.py:39
  12.2 16.9 %collective-permute-done.2.refs_0_.refs_4_.refs_1_ = bf16[256,768]{1,0:T(8,128)(2,1)S(1)} collective-permute-done((bf16[256,768]{1,0:T(8,128)(2,1)S(1)}, bf16[256,768]{1,0:T(8,128)(2,1)S(1)}, u32[]{:S(2)}, u32[]{:S(2)}) %collective-permute-start.2) | collective-permute-done | bytes 393248 | tf_op jit(solution)/shard_map/ppermute | solution.py:39
  29.7 1.1 %shard_map.78 = (bf16[448,512]{1,0:T(8,128)(2,1)S(1)}, bf16[448,512]{1,0:T(8,128)(2,1)S(1)}) custom-call(s32[8]{0:T(128)S(1)} %copy-done.4, bf16[16,64,512]{2,1,0:T(8,128)(2,1)S(1)} %bitcast.16), custom_call_target="tpu_custom_call" | custom-call | bytes 1835008 | tf_op jit(solution)/shard_map/pallas_call | solution.py:324
  31.2 1.6 %collective-permute-start.3 = (bf16[512,768]{1,0:T(8,128)(2,1)S(1)}, bf16[512,768]{1,0:T(8,128)(2,1)S(1)}, u32[]{:S(2)}, u32[]{:S(2)}) collective-permute-start(bf16[512,768]{1,0:T(8,128)(2,1)S(1)} %shard_map.74), channel_id=1, source_target_pairs={{0,16},{16,0},{1,17},{17,1},{2,18},{18,2},{3,19},{19,3},{4,20},{20... | collective-permute-start | bytes 2359304 | tf_op jit(solution)/shard_map/ppermute | solution.py:39
  33.0 3.4 %collective-permute-start.15 = (bf16[448,512]{1,0:T(8,128)(2,1)S(1)}, bf16[448,512]{1,0:T(8,128)(2,1)S(1)}, u32[]{:S(2)}, u32[]{:S(2)}) collective-permute-start(bf16[448,512]{1,0:T(8,128)(2,1)S(1)} %shard_map.79), channel_id=1, source_target_pairs={{0,8},{1,9},{2,10},{3,11},{4,12},{5,13},{6,14},{7,15},{8,0},{9,1},... | collective-permute-start | bytes 1376264 | tf_op jit(solution)/shard_map/ppermute | solution.py:39
  36.4 8.5 %collective-permute-done.4.refs_6_.refs_1_ = bf16[256,768]{1,0:T(8,128)(2,1)S(1)} collective-permute-done((bf16[256,768]{1,0:T(8,128)(2,1)S(1)}, bf16[256,768]{1,0:T(8,128)(2,1)S(1)}, u32[]{:S(2)}, u32[]{:S(2)}) %collective-permute-start.4) | collective-permute-done | bytes 393248 | tf_op jit(solution)/shard_map/ppermute | solution.py:39
  45.3 2.6 %collective-permute-start.5 = (bf16[256,768]{1,0:T(8,128)(2,1)S(1)}, bf16[256,768]{1,0:T(8,128)(2,1)S(1)}, u32[]{:S(2)}, u32[]{:S(2)}) collective-permute-start(bf16[256,768]{1,0:T(8,128)(2,1)S(1)} %collective-permute-done.4.refs_6_.refs_1_), channel_id=1, source_target_pairs={{0,16},{16,0},{1,17},{17,1},{2,18},{18,2},{3,19},{19,3},{4,20},{20... | collective-permute-start | bytes 1179656 | tf_op jit(solution)/shard_map/ppermute | solution.py:39
  48.7 7.9 %collective-permute-done.15.refs_10_ = bf16[448,512]{1,0:T(8,128)(2,1)S(1)} collective-permute-done((bf16[448,512]{1,0:T(8,128)(2,1)S(1)}, bf16[448,512]{1,0:T(8,128)(2,1)S(1)}, u32[]{:S(2)}, u32[]{:S(2)}) %collective-permute-start.15) | collective-permute-done | bytes 458784 | tf_op jit(solution)/shard_map/ppermute | solution.py:39
  56.6 1.5 %collective-permute-start.9 = (bf16[48,2048]{1,0:T(8,128)(2,1)S(1)}, bf16[48,2048]{1,0:T(8,128)(2,1)S(1)}, u32[]{:S(2)}, u32[]{:S(2)}) collective-permute-start(bf16[48,2048]{1,0:T(8,128)(2,1)S(1)} %get-tuple-element.25), channel_id=1, source_target_pairs={{0,2},{1,3},{2,0},{3,1},{4,6},{5,7},{6,4},{7,5},{8,10},{9,11},{10,... | collective-permute-start | bytes 589832 | tf_op jit(solution)/shard_map/ppermute | solution.py:39
  58.9 1.6 %shard_map.75.refs_1_ = bf16[2048,768]{1,0:T(8,128)(2,1)S(1)} custom-call(bf16[256,768]{1,0:T(8,128)(2,1)S(1)} %get-tuple-element.20.refs_0_, bf16[256,768]{1,0:T(8,128)(2,1)S(1)} %get-tuple-element.21.refs_1_, bf16[256,768]{1,0:T(8,128)(2,1)S(1)} %collective-permute-done.1.refs_1_.refs_2_, bf16[512,768]{1,0:T(8,128)(2,1)S(1)} %collective-permute-done.3.refs_3_.refs_5_, ...), custom_call_target="tpu_custom_call" | custom-call | flops 34604998656 | tf_op jit(solution)/shard_map/pallas_call | solution.py:100
  62.7 1.0 %fusion.5.refs_4_ = f32[256,768]{1,0:T(8,128)S(1)} fusion(bf16[256,2048]{1,0:T(8,128)(2,1)S(1)} %get-tuple-element.27.refs_3_, bf16[2048,768]{1,0:T(8,128)(2,1)S(1)} %shard_map.75.refs_1_), kind=kOutput, calls=%fused_computation.9 | convolution fusion | flops 805306368 | bytes 4980736 | tf_op jit(solution)/shard_map/dot_general | solution.py:393
  65.2 1.6 %collective-permute-start.8 = (bf16[208,768]{1,0:T(8,128)(2,1)S(1)}, bf16[208,768]{1,0:T(8,128)(2,1)S(1)}, u32[]{:S(2)}, u32[]{:S(2)}) collective-permute-start(bf16[208,768]{1,0:T(8,128)(2,1)S(1)} %fusion), channel_id=1, source_target_pairs={{0,2},{1,3},{2,0},{3,1},{4,6},{5,7},{6,4},{7,5},{8,10},{9,11},{10,... | collective-permute-start | bytes 958472 | tf_op jit(solution)/shard_map/ppermute | solution.py:39
  66.9 1.0 %fusion.6 = f32[256,768]{1,0:T(8,128)S(1)} fusion(bf16[256,2048]{1,0:T(8,128)(2,1)S(1)} %collective-permute-done.13.refs_4_, bf16[2048,768]{1,0:T(8,128)(2,1)S(1)} %shard_map.75.refs_1_), kind=kOutput, calls=%fused_computation.10 | convolution fusion | flops 805306368 | bytes 4980736 | tf_op jit(solution)/shard_map/dot_general | solution.py:393
  68.1 3.2 %shard_map.81.refs_10_ = f32[2,512,256]{2,1,0:T(8,128)S(1)} custom-call(s32[8]{0:T(128)S(1)} %copy-done.5, s32[8]{0:T(128)S(1)} %copy-done.4, s32[8]{0:T(128)S(1)} %copy-done.6, bf16[256,2048]{1,0:T(8,128)(2,1)S(1)} %get-tuple-element.27.refs_3_, bf16[256,2048]{1,0:T(8,128)(2,1)S(1)} %collective-permute-done.13.refs_4_, ...), custom_call_target="tpu_custom_call" | custom-call | flops 5767499776 | tf_op jit(solution)/shard_map/pallas_call | solution.py:424
  71.3 1.6 %shard_map.82 = (f32[2,128,128]{2,1,0:T(8,128)S(1)}, f32[2,128,128]{2,1,0:T(8,128)S(1)}) custom-call(s32[8]{0:T(128)S(1)} %copy-done.5, s32[8]{0:T(128)S(1)} %copy-done.4, s32[8]{0:T(128)S(1)} %copy-done.6, bf16[256,2048]{1,0:T(8,128)(2,1)S(1)} %get-tuple-element.27.refs_3_, bf16[256,2048]{1,0:T(8,128)(2,1)S(1)} %collective-permute-done.13.refs_4_, ...), custom_call_target="tpu_custom_call" | custom-call | flops 17302499328 | tf_op jit(solution)/shard_map/pallas_call | solution.py:424
  74.1 1.6 %collective-permute-start.12 = (bf16[48,768]{1,0:T(8,128)(2,1)S(1)}, bf16[48,768]{1,0:T(8,128)(2,1)S(1)}, u32[]{:S(2)}, u32[]{:S(2)}) collective-permute-start(bf16[48,768]{1,0:T(8,128)(2,1)S(1)} %fusion.1), channel_id=1, source_target_pairs={{0,2},{1,3},{2,0},{3,1},{4,6},{5,7},{6,4},{7,5},{8,10},{9,11},{10,... | collective-permute-start | bytes 221192 | tf_op jit(solution)/shard_map/ppermute | solution.py:39
  76.4 2.2 %collective-permute-done.12 = bf16[48,768]{1,0:T(8,128)(2,1)S(1)} collective-permute-done((bf16[48,768]{1,0:T(8,128)(2,1)S(1)}, bf16[48,768]{1,0:T(8,128)(2,1)S(1)}, u32[]{:S(2)}, u32[]{:S(2)}) %collective-permute-start.12) | collective-permute-done | bytes 73760 | tf_op jit(solution)/shard_map/ppermute | solution.py:39
  78.7 1.4 %collective-permute-done.19 = f32[1,128,128]{2,1,0:T(8,128)S(1)} collective-permute-done((f32[1,128,128]{2,1,0:T(8,128)S(1)}, f32[1,128,128]{2,1,0:T(8,128)S(1)}, u32[]{:S(2)}, u32[]{:S(2)}) %collective-permute-start.19) | collective-permute-done | bytes 65568 | tf_op jit(solution)/shard_map/ppermute | solution.py:39
  80.1 2.1 %shard_map.83 = bf16[256,768]{1,0:T(8,128)(2,1)} custom-call(s32[8]{0:T(128)S(1)} %copy-done.5, s32[8]{0:T(128)S(1)} %copy-done.4, s32[8]{0:T(128)S(1)} %copy-done.6, bf16[256,768]{1,0:T(8,128)(2,1)S(1)} %pad_maximum_fusion.refs_3_, f32[256,768]{1,0:T(8,128)S(1)} %fusion.5.refs_4_, f32[256,768]{1,0:T(8,128)S(1)} %collective-permute-done.14.refs_5_, ...), custom_call_target="tpu_custom_call" | custom-call | flops 25165824 | bytes 1572864 | tf_op jit(solution)/shard_map/pallas_call | solution.py:444
  (50 shorter events, 9.0 us)
Async XLA Ops:
  3.3 26.4 %copy-start.2 = (bf16[512,16,64]{0,2,1:T(8,128)(2,1)S(1)}, bf16[512,16,64]{0,2,1:T(8,128)(2,1)}, u32[]{:S(2)}) copy-start(bf16[512,16,64]{0,2,1:T(8,128)(2,1)} %param.9) | copy-start | bytes 3145732
  3.3 26.4 %copy-start.4 = (s32[8]{0:T(128)S(1)}, s32[8]{0:T(128)}, u32[]{:S(2)}) copy-start(s32[8]{0:T(128)} %refs_1_.5) | copy-start | bytes 100
  5.0 40.3 %collective-permute-start = (bf16[208,2048]{1,0:T(8,128)(2,1)S(1)}, bf16[208,2048]{1,0:T(8,128)(2,1)S(1)}, u32[]{:S(2)}, u32[]{:S(2)}) collective-permute-start(bf16[208,2048]{1,0:T(8,128)(2,1)S(1)} %get-tuple-element.19), channel_id=1, source_target_pairs={{0,2},{1,3},{2,0},{3,1},{4,6},{5,7},{6,4},{7,5},{8,10},{9,11},{10,... | collective-permute-start | bytes 2555912 | tf_op jit(solution)/shard_map/ppermute | solution.py:39
  8.0 39.9 %collective-permute-start.6 = (bf16[208,2048]{1,0:T(8,128)(2,1)S(1)}, bf16[208,2048]{1,0:T(8,128)(2,1)S(1)}, u32[]{:S(2)}, u32[]{:S(2)}) collective-permute-start(bf16[208,2048]{1,0:T(8,128)(2,1)S(1)} %get-tuple-element.22), channel_id=1, source_target_pairs={{0,3},{1,2},{2,1},{3,0},{4,7},{5,6},{6,5},{7,4},{8,11},{9,10},{10,... | collective-permute-start | bytes 2555912 | tf_op jit(solution)/shard_map/ppermute | solution.py:39
  8.0 21.0 %collective-permute-start.2 = (bf16[256,768]{1,0:T(8,128)(2,1)S(1)}, bf16[256,768]{1,0:T(8,128)(2,1)S(1)}, u32[]{:S(2)}, u32[]{:S(2)}) collective-permute-start(bf16[256,768]{1,0:T(8,128)(2,1)S(1)} %get-tuple-element.20.refs_0_), channel_id=1, source_target_pairs={{0,8},{1,9},{2,10},{3,11},{4,12},{5,13},{6,14},{7,15},{8,0},{9,1},... | collective-permute-start | bytes 1179656 | tf_op jit(solution)/shard_map/ppermute | solution.py:39
  10.6 20.1 %collective-permute-start.1 = (bf16[256,768]{1,0:T(8,128)(2,1)S(1)}, bf16[256,768]{1,0:T(8,128)(2,1)S(1)}, u32[]{:S(2)}, u32[]{:S(2)}) collective-permute-start(bf16[256,768]{1,0:T(8,128)(2,1)S(1)} %get-tuple-element.20.refs_0_), channel_id=1, source_target_pairs={{0,4},{1,5},{2,6},{3,7},{4,0},{5,1},{6,2},{7,3},{8,12},{9,13},{10,... | collective-permute-start | bytes 1179656 | tf_op jit(solution)/shard_map/ppermute | solution.py:39
  29.1 15.8 %collective-permute-start.4 = (bf16[256,768]{1,0:T(8,128)(2,1)S(1)}, bf16[256,768]{1,0:T(8,128)(2,1)S(1)}, u32[]{:S(2)}, u32[]{:S(2)}) collective-permute-start(bf16[256,768]{1,0:T(8,128)(2,1)S(1)} %collective-permute-done.2.refs_0_.refs_4_.refs_1_), channel_id=1, source_target_pairs={{0,4},{1,5},{2,6},{3,7},{4,0},{5,1},{6,2},{7,3},{8,12},{9,13},{10,... | collective-permute-start | bytes 1179656 | tf_op jit(solution)/shard_map/ppermute | solution.py:39
  31.2 27.0 %collective-permute-start.3 = (bf16[512,768]{1,0:T(8,128)(2,1)S(1)}, bf16[512,768]{1,0:T(8,128)(2,1)S(1)}, u32[]{:S(2)}, u32[]{:S(2)}) collective-permute-start(bf16[512,768]{1,0:T(8,128)(2,1)S(1)} %shard_map.74), channel_id=1, source_target_pairs={{0,16},{16,0},{1,17},{17,1},{2,18},{18,2},{3,19},{19,3},{4,20},{20... | collective-permute-start | bytes 2359304 | tf_op jit(solution)/shard_map/ppermute | solution.py:39
  33.0 23.6 %collective-permute-start.15 = (bf16[448,512]{1,0:T(8,128)(2,1)S(1)}, bf16[448,512]{1,0:T(8,128)(2,1)S(1)}, u32[]{:S(2)}, u32[]{:S(2)}) collective-permute-start(bf16[448,512]{1,0:T(8,128)(2,1)S(1)} %shard_map.79), channel_id=1, source_target_pairs={{0,8},{1,9},{2,10},{3,11},{4,12},{5,13},{6,14},{7,15},{8,0},{9,1},... | collective-permute-start | bytes 1376264 | tf_op jit(solution)/shard_map/ppermute | solution.py:39
  45.2 22.9 %collective-permute-start.17 = (bf16[448,512]{1,0:T(8,128)(2,1)S(1)}, bf16[448,512]{1,0:T(8,128)(2,1)S(1)}, u32[]{:S(2)}, u32[]{:S(2)}) collective-permute-start(bf16[448,512]{1,0:T(8,128)(2,1)S(1)} %shard_map.80), channel_id=1, source_target_pairs={{0,4},{1,5},{2,6},{3,7},{4,0},{5,1},{6,2},{7,3},{8,12},{9,13},{10,... | collective-permute-start | bytes 1376264 | tf_op jit(solution)/shard_map/ppermute | solution.py:39
  45.3 13.6 %collective-permute-start.5 = (bf16[256,768]{1,0:T(8,128)(2,1)S(1)}, bf16[256,768]{1,0:T(8,128)(2,1)S(1)}, u32[]{:S(2)}, u32[]{:S(2)}) collective-permute-start(bf16[256,768]{1,0:T(8,128)(2,1)S(1)} %collective-permute-done.4.refs_6_.refs_1_), channel_id=1, source_target_pairs={{0,16},{16,0},{1,17},{17,1},{2,18},{18,2},{3,19},{19,3},{4,20},{20... | collective-permute-start | bytes 1179656 | tf_op jit(solution)/shard_map/ppermute | solution.py:39
  48.4 13.1 %collective-permute-start.10 = (bf16[48,2048]{1,0:T(8,128)(2,1)S(1)}, bf16[48,2048]{1,0:T(8,128)(2,1)S(1)}, u32[]{:S(2)}, u32[]{:S(2)}) collective-permute-start(bf16[48,2048]{1,0:T(8,128)(2,1)S(1)} %get-tuple-element.26), channel_id=1, source_target_pairs={{0,3},{1,2},{2,1},{3,0},{4,7},{5,6},{6,5},{7,4},{8,11},{9,10},{10,... | collective-permute-start | bytes 589832 | tf_op jit(solution)/shard_map/ppermute | solution.py:39
  56.6 11.3 %collective-permute-start.9 = (bf16[48,2048]{1,0:T(8,128)(2,1)S(1)}, bf16[48,2048]{1,0:T(8,128)(2,1)S(1)}, u32[]{:S(2)}, u32[]{:S(2)}) collective-permute-start(bf16[48,2048]{1,0:T(8,128)(2,1)S(1)} %get-tuple-element.25), channel_id=1, source_target_pairs={{0,2},{1,3},{2,0},{3,1},{4,6},{5,7},{6,4},{7,5},{8,10},{9,11},{10,... | collective-permute-start | bytes 589832 | tf_op jit(solution)/shard_map/ppermute | solution.py:39
  58.2 13.1 %collective-permute-start.16 = (bf16[448,512]{1,0:T(8,128)(2,1)S(1)}, bf16[448,512]{1,0:T(8,128)(2,1)S(1)}, u32[]{:S(2)}, u32[]{:S(2)}) collective-permute-start(bf16[448,512]{1,0:T(8,128)(2,1)S(1)} %collective-permute-done.15.refs_10_), channel_id=1, source_target_pairs={{0,4},{1,5},{2,6},{3,7},{4,0},{5,1},{6,2},{7,3},{8,12},{9,13},{10,... | collective-permute-start | bytes 1376264 | tf_op jit(solution)/shard_map/ppermute | solution.py:39
  60.6 4.7 %collective-permute-start.13 = (bf16[256,2048]{1,0:T(8,128)(2,1)S(1)}, bf16[256,2048]{1,0:T(8,128)(2,1)S(1)}, u32[]{:S(2)}, u32[]{:S(2)}) collective-permute-start(bf16[256,2048]{1,0:T(8,128)(2,1)S(1)} %shard_map.77), channel_id=1, source_target_pairs={{0,1},{1,0},{2,3},{3,2},{4,5},{5,4},{6,7},{7,6},{8,9},{9,8},{10,11... | collective-permute-start | bytes 3145736 | tf_op jit(solution)/shard_map/ppermute | solution.py:39
  61.5 2.7 %collective-permute-start.7 = (f32[208,768]{1,0:T(8,128)S(1)}, f32[208,768]{1,0:T(8,128)S(1)}, u32[]{:S(2)}, u32[]{:S(2)}) collective-permute-start(f32[208,768]{1,0:T(8,128)S(1)} %fusion.3), channel_id=1, source_target_pairs={{0,1},{1,0},{2,3},{3,2},{4,5},{5,4},{6,7},{7,6},{8,9},{9,8},{10,11... | collective-permute-start | bytes 1916936 | tf_op jit(solution)/shard_map/ppermute | solution.py:39
  64.2 9.2 %collective-permute-start.11 = (f32[48,768]{1,0:T(8,128)S(1)}, f32[48,768]{1,0:T(8,128)S(1)}, u32[]{:S(2)}, u32[]{:S(2)}) collective-permute-start(f32[48,768]{1,0:T(8,128)S(1)} %fusion.4), channel_id=1, source_target_pairs={{0,1},{1,0},{2,3},{3,2},{4,5},{5,4},{6,7},{7,6},{8,9},{9,8},{10,11... | collective-permute-start | bytes 442376 | tf_op jit(solution)/shard_map/ppermute | solution.py:39
  65.2 2.8 %copy-start.5 = (s32[8]{0:T(128)S(1)}, s32[8]{0:T(128)}, u32[]{:S(2)}) copy-start(s32[8]{0:T(128)} %refs_0_.5) | copy-start | bytes 100
  65.2 13.4 %collective-permute-start.8 = (bf16[208,768]{1,0:T(8,128)(2,1)S(1)}, bf16[208,768]{1,0:T(8,128)(2,1)S(1)}, u32[]{:S(2)}, u32[]{:S(2)}) collective-permute-start(bf16[208,768]{1,0:T(8,128)(2,1)S(1)} %fusion), channel_id=1, source_target_pairs={{0,2},{1,3},{2,0},{3,1},{4,6},{5,7},{6,4},{7,5},{8,10},{9,11},{10,... | collective-permute-start | bytes 958472 | tf_op jit(solution)/shard_map/ppermute | solution.py:39
  67.9 12.2 %collective-permute-start.14 = (f32[256,768]{1,0:T(8,128)S(1)}, f32[256,768]{1,0:T(8,128)S(1)}, u32[]{:S(2)}, u32[]{:S(2)}) collective-permute-start(f32[256,768]{1,0:T(8,128)S(1)} %fusion.6), channel_id=1, source_target_pairs={{0,1},{1,0},{2,3},{3,2},{4,5},{5,4},{6,7},{7,6},{8,9},{9,8},{10,11... | collective-permute-start | bytes 2359304 | tf_op jit(solution)/shard_map/ppermute | solution.py:39
  72.9 7.2 %copy-start.1 = (bf16[16,64,768]{2,1,0:T(8,128)(2,1)S(1)}, bf16[16,64,768]{2,1,0:T(8,128)(2,1)}, u32[]{:S(2)}) copy-start(bf16[16,64,768]{2,1,0:T(8,128)(2,1)} %refs_8_.1) | copy-start | bytes 4718596
  72.9 2.8 %collective-permute-start.18 = (f32[2,128,128]{2,1,0:T(8,128)S(1)}, f32[2,128,128]{2,1,0:T(8,128)S(1)}, u32[]{:S(2)}, u32[]{:S(2)}) collective-permute-start(f32[2,128,128]{2,1,0:T(8,128)S(1)} %get-tuple-element.32), channel_id=1, source_target_pairs={{0,1},{1,0},{2,3},{3,2},{4,5},{5,4},{6,7},{7,6},{8,9},{9,8},{10,11... | collective-permute-start | bytes 393224 | tf_op jit(solution)/shard_map/ppermute | solution.py:39
  74.1 4.6 %collective-permute-start.12 = (bf16[48,768]{1,0:T(8,128)(2,1)S(1)}, bf16[48,768]{1,0:T(8,128)(2,1)S(1)}, u32[]{:S(2)}, u32[]{:S(2)}) collective-permute-start(bf16[48,768]{1,0:T(8,128)(2,1)S(1)} %fusion.1), channel_id=1, source_target_pairs={{0,2},{1,3},{2,0},{3,1},{4,6},{5,7},{6,4},{7,5},{8,10},{9,11},{10,... | collective-permute-start | bytes 221192 | tf_op jit(solution)/shard_map/ppermute | solution.py:39
  75.7 4.3 %collective-permute-start.19 = (f32[1,128,128]{2,1,0:T(8,128)S(1)}, f32[1,128,128]{2,1,0:T(8,128)S(1)}, u32[]{:S(2)}, u32[]{:S(2)}) collective-permute-start(f32[1,128,128]{2,1,0:T(8,128)S(1)} %get-tuple-element.33), channel_id=1, source_target_pairs={{0,2},{1,3},{2,0},{3,1},{4,6},{5,7},{6,4},{7,5},{8,10},{9,11},{10,... | collective-permute-start | bytes 196616 | tf_op jit(solution)/shard_map/ppermute | solution.py:39
  (3 other events, 6.2 us)

commit v11 on v10

--- a/solution.py
+++ b/solution.py
@@ -165,52 +165,36 @@
         even, odd, refs = refs[0], refs[1], refs[2:]
     else:
         after, refs = refs[0], refs[1:]
-    held, refs = refs[0], refs[1:]
-    downs, refs = refs[:count], refs[count:]
-    tok_sems, sems = refs
     local_blocks = rows // BLOCK
     me = lax.axis_index("batch")
     layer, spot = me // group, me % group
-    first = {}
-    started = {}
-    for n, (t, a, _) in enumerate(entries):
-        if a not in started:
-            started[a] = pltpu.make_async_copy(arrays[a], downs[a], sems.at[a])
-            started[a].start()
-        first[t] = []
-        for i, (to, deep) in enumerate(places):
-            copy = pltpu.make_async_copy(
-                toks[i].at[:, pl.ds(t * depth, depth)],
-                held.at[pl.ds(to, deep), pl.ds(n * depth, depth)],
-                tok_sems.at[i, n],
-            )
-            copy.start()
-            first[t].append(copy)
     slots = []
     for s in range(group):
         for j in range(local_blocks):
             block = (layer * group + (spot ^ s)) * local_blocks + j
             owner, adapter, _ = table(lists, block)
             slots.append(owner - (layer * 2) // layers * shift if by_request else adapter)
-    ready = set()
     wide = 2 * local_blocks
     sums = [before[p] if has_sum else None for p in range(group // 2)]
     for n, (t, a, row) in enumerate(entries):
-        for copy in first[t]:
-            copy.wait()
-        if a not in ready:
-            started[a].wait()
-            ready.add(a)
         for p in range(group // 2):
             chosen = jnp.concatenate(
                 [
-                    downs[a][pl.ds(pl.multiple_of(row + slots[p * wide + i] * rank, rank), rank), :]
+                    arrays[a][pl.ds(pl.multiple_of(row + slots[p * wide + i] * rank, rank), rank), :]
                     for i in range(wide)
                 ],
                 0,
             )
+            held = jnp.concatenate(
+                [
+                    toks[i][:, t * depth : (t + 1) * depth]
+                    for i, (to, _) in enumerate(places)
+                    if to // (2 * rows) == p
+                ],
+                0,
+            )
             term = lax.dot_general(
-                held[2 * p * rows : 2 * (p + 1) * rows, n * depth : (n + 1) * depth],
+                held,
                 chosen,
                 (((1,), (1,)), ((), ())),
                 preferred_element_type=jnp.float32,
@@ -428,10 +412,8 @@
             ),
             outs,
             out_specs,
-            [SMEM] * 3 + [HBM] * (len(tokens_here) + len(taken)) + [VMEM] * (before is not None),
-            [pltpu.VMEM((group * rows, len(at) * depth), bf16)]
-            + [pltpu.VMEM(v.shape, bf16) for v in taken]
-            + [pltpu.SemaphoreType.DMA((len(tokens_here), len(at))), pltpu.SemaphoreType.DMA((len(taken),))],
+            [SMEM] * 3 + [VMEM] * (len(tokens_here) + len(taken) + (before is not None)),
+            [],
             WAITS["low"][last] * CORE_FLOPS_PER_US,
             0,
         )(*lists, *tokens_here, *taken, *([before] if before is not None else []))

time: 82.4 us -> 81.9 us (level)
  Pallas kernels: 12.8 us -> 10.6 us
  waiting for transfers between devices: 38 us -> 39.5 us
    pallas_call x2, Pallas kernels: 4.81 us -> 2.67 us  [low_call(): call(functools.partial(low_kernel, group, layers, rows, chunks, depth, ra...]
    ppermute x20, waiting for transfers between devices: 38 us -> 39.5 us  [swap(): lax.ppermute(value, axis, [(i, i ^ bit) for i in range(lax.axis_size(axis...]
  transfers between devices with their start and end apart: 20 -> 20, of which waited for: 7 -> 8; matrix products, arithmetic and copies ran while one was open for 6% -> 6% of each run, Pallas kernels for 11% -> 8%
where the time goes in v11:
time: 81.9 us; the launch traced here: 81.7 us
  waiting for transfers between devices  39.5 us (48%)
  starting transfers between devices  23 us (28%)
  Pallas kernels  10.6 us (13%)
  matrix products  5 us (6%)
  local copies, waits for them, and re-layouts  3.36 us (4%)
    ppermute x20, waiting for transfers between devices, swap(): lax.ppermute(value, axis, [(i, i ^ bit) for i in range(lax.axis_size(axis...  39.5 us
    ppermute x20, starting transfers between devices, swap(): lax.ppermute(value, axis, [(i, i ^ bit) for i in range(lax.axis_size(axis...  23 us
    dot_general x6, matrix products, base_of(): return jnp.dot(value, keys, preferred_element_type=f32)  5 us
    unnamed x14, local copies, waits for them, and re-layouts  3.35 us
    pallas_call x6, Pallas kernels, stack(): call(functools.partial(stack_kernel, tuple(moves), len(values), count), o...  3.1 us
    pallas_call x2, Pallas kernels, low_call(): call(functools.partial(low_kernel, group, layers, rows, chunks, depth, ra...  2.67 us
    pallas_call x1, Pallas kernels, shards(): call(functools.partial(final_kernel, rows, rank, len(bases), len(fars), l...  2.12 us
    pallas_call x1, Pallas kernels, shards(): call(functools.partial(first_kernel, group, layers, splits, part, chunks)...  1.67 us
  transfers between devices with their start and end apart: 20, of which 8 were waited for; matrix products, arithmetic and copies ran while one was open for 6% of the time, Pallas kernels for 8%

profile of v11, /device:TPU:0, one launch (start us, length us, event | category | flops | bytes accessed | tf_op | source)
XLA Modules:
  0.0 81.7 jit_solution(12086380403360812782)
XLA Ops:
  0.0 2.2 %copy-done = bf16[256,8192]{1,0:T(8,128)(2,1)S(1)} copy-done((bf16[256,8192]{1,0:T(8,128)(2,1)S(1)}, bf16[256,8192]{1,0:T(8,128)(2,1)}, u32[]{:S(2)}) %copy-start) | copy-done | bytes 4194328
  2.2 1.1 %copy-done.3 = bf16[512,768]{1,0:T(8,128)(2,1)S(1)} copy-done((bf16[512,768]{1,0:T(8,128)(2,1)S(1)}, bf16[512,768]{1,0:T(8,128)(2,1)}, u32[]{:S(2)}) %copy-start.3) | copy-done | bytes 786456
  3.3 1.7 %shard_map.73 = (bf16[256,768]{1,0:T(8,128)(2,1)S(1)}, bf16[256,768]{1,0:T(8,128)(2,1)S(1)}, bf16[256,2048]{1,0:T(8,128)(2,1)S(1)}, bf16[256,2048]{1,0:T(8,128)(...) custom-call(bf16[512,768]{1,0:T(8,128)(2,1)S(1)} %copy-done.3, ...), custom_call_target="tpu_custom_call" | custom-call | bytes 9961472 | tf_op jit(solution)/shard_map/pallas_call | solution.py:275
  5.0 3.0 %collective-permute-start = (bf16[208,2048]{1,0:T(8,128)(2,1)S(1)}, bf16[208,2048]{1,0:T(8,128)(2,1)S(1)}, u32[]{:S(2)}, u32[]{:S(2)}) collective-permute-start(bf16[208,2048]{1,0:T(8,128)(2,1)S(1)} %get-tuple-element.19), channel_id=1, source_target_pairs={{0,2},{1,3},{2,0},{3,1},{4,6},{5,7},{6,4},{7,5},{8,10},{9,11},{10,... | collective-permute-start | bytes 2555912 | tf_op jit(solution)/shard_map/ppermute | solution.py:39
  8.0 2.6 %collective-permute-start.2 = (bf16[256,768]{1,0:T(8,128)(2,1)S(1)}, bf16[256,768]{1,0:T(8,128)(2,1)S(1)}, u32[]{:S(2)}, u32[]{:S(2)}) collective-permute-start(bf16[256,768]{1,0:T(8,128)(2,1)S(1)} %get-tuple-element.20.refs_0_), channel_id=1, source_target_pairs={{0,8},{1,9},{2,10},{3,11},{4,12},{5,13},{6,14},{7,15},{8,0},{9,1},... | collective-permute-start | bytes 1179656 | tf_op jit(solution)/shard_map/ppermute | solution.py:39
  10.6 1.6 %collective-permute-start.1 = (bf16[256,768]{1,0:T(8,128)(2,1)S(1)}, bf16[256,768]{1,0:T(8,128)(2,1)S(1)}, u32[]{:S(2)}, u32[]{:S(2)}) collective-permute-start(bf16[256,768]{1,0:T(8,128)(2,1)S(1)} %get-tuple-element.20.refs_0_), channel_id=1, source_target_pairs={{0,4},{1,5},{2,6},{3,7},{4,0},{5,1},{6,2},{7,3},{8,12},{9,13},{10,... | collective-permute-start | bytes 1179656 | tf_op jit(solution)/shard_map/ppermute | solution.py:39
  12.2 16.9 %collective-permute-done.2.refs_0_.refs_4_.refs_1_ = bf16[256,768]{1,0:T(8,128)(2,1)S(1)} collective-permute-done((bf16[256,768]{1,0:T(8,128)(2,1)S(1)}, bf16[256,768]{1,0:T(8,128)(2,1)S(1)}, u32[]{:S(2)}, u32[]{:S(2)}) %collective-permute-start.2) | collective-permute-done | bytes 393248 | tf_op jit(solution)/shard_map/ppermute | solution.py:39
  29.7 1.1 %shard_map.78 = (bf16[448,512]{1,0:T(8,128)(2,1)S(1)}, bf16[448,512]{1,0:T(8,128)(2,1)S(1)}) custom-call(s32[8]{0:T(128)S(1)} %copy-done.4, bf16[16,64,512]{2,1,0:T(8,128)(2,1)S(1)} %bitcast.16), custom_call_target="tpu_custom_call" | custom-call | bytes 1835008 | tf_op jit(solution)/shard_map/pallas_call | solution.py:308
  31.2 1.6 %collective-permute-start.3 = (bf16[512,768]{1,0:T(8,128)(2,1)S(1)}, bf16[512,768]{1,0:T(8,128)(2,1)S(1)}, u32[]{:S(2)}, u32[]{:S(2)}) collective-permute-start(bf16[512,768]{1,0:T(8,128)(2,1)S(1)} %shard_map.74), channel_id=1, source_target_pairs={{0,16},{16,0},{1,17},{17,1},{2,18},{18,2},{3,19},{19,3},{4,20},{20... | collective-permute-start | bytes 2359304 | tf_op jit(solution)/shard_map/ppermute | solution.py:39
  33.0 3.4 %collective-permute-start.15 = (bf16[448,512]{1,0:T(8,128)(2,1)S(1)}, bf16[448,512]{1,0:T(8,128)(2,1)S(1)}, u32[]{:S(2)}, u32[]{:S(2)}) collective-permute-start(bf16[448,512]{1,0:T(8,128)(2,1)S(1)} %shard_map.79), channel_id=1, source_target_pairs={{0,8},{1,9},{2,10},{3,11},{4,12},{5,13},{6,14},{7,15},{8,0},{9,1},... | collective-permute-start | bytes 1376264 | tf_op jit(solution)/shard_map/ppermute | solution.py:39
  36.4 8.5 %collective-permute-done.4.refs_6_.refs_1_ = bf16[256,768]{1,0:T(8,128)(2,1)S(1)} collective-permute-done((bf16[256,768]{1,0:T(8,128)(2,1)S(1)}, bf16[256,768]{1,0:T(8,128)(2,1)S(1)}, u32[]{:S(2)}, u32[]{:S(2)}) %collective-permute-start.4) | collective-permute-done | bytes 393248 | tf_op jit(solution)/shard_map/ppermute | solution.py:39
  45.3 2.6 %collective-permute-start.5 = (bf16[256,768]{1,0:T(8,128)(2,1)S(1)}, bf16[256,768]{1,0:T(8,128)(2,1)S(1)}, u32[]{:S(2)}, u32[]{:S(2)}) collective-permute-start(bf16[256,768]{1,0:T(8,128)(2,1)S(1)} %collective-permute-done.4.refs_6_.refs_1_), channel_id=1, source_target_pairs={{0,16},{16,0},{1,17},{17,1},{2,18},{18,2},{3,19},{19,3},{4,20},{20... | collective-permute-start | bytes 1179656 | tf_op jit(solution)/shard_map/ppermute | solution.py:39
  48.7 7.9 %collective-permute-done.15.refs_10_ = bf16[448,512]{1,0:T(8,128)(2,1)S(1)} collective-permute-done((bf16[448,512]{1,0:T(8,128)(2,1)S(1)}, bf16[448,512]{1,0:T(8,128)(2,1)S(1)}, u32[]{:S(2)}, u32[]{:S(2)}) %collective-permute-start.15) | collective-permute-done | bytes 458784 | tf_op jit(solution)/shard_map/ppermute | solution.py:39
  56.6 1.5 %collective-permute-start.9 = (bf16[48,2048]{1,0:T(8,128)(2,1)S(1)}, bf16[48,2048]{1,0:T(8,128)(2,1)S(1)}, u32[]{:S(2)}, u32[]{:S(2)}) collective-permute-start(bf16[48,2048]{1,0:T(8,128)(2,1)S(1)} %get-tuple-element.25), channel_id=1, source_target_pairs={{0,2},{1,3},{2,0},{3,1},{4,6},{5,7},{6,4},{7,5},{8,10},{9,11},{10,... | collective-permute-start | bytes 589832 | tf_op jit(solution)/shard_map/ppermute | solution.py:39
  58.9 1.6 %shard_map.75.refs_1_ = bf16[2048,768]{1,0:T(8,128)(2,1)S(1)} custom-call(bf16[256,768]{1,0:T(8,128)(2,1)S(1)} %get-tuple-element.20.refs_0_, bf16[256,768]{1,0:T(8,128)(2,1)S(1)} %get-tuple-element.21.refs_1_, bf16[256,768]{1,0:T(8,128)(2,1)S(1)} %collective-permute-done.1.refs_1_.refs_2_, bf16[512,768]{1,0:T(8,128)(2,1)S(1)} %collective-permute-done.3.refs_3_.refs_5_, ...), custom_call_target="tpu_custom_call" | custom-call | flops 34604998656 | tf_op jit(solution)/shard_map/pallas_call | solution.py:100
  62.7 1.0 %fusion.5.refs_4_ = f32[256,768]{1,0:T(8,128)S(1)} fusion(bf16[256,2048]{1,0:T(8,128)(2,1)S(1)} %get-tuple-element.27.refs_3_, bf16[2048,768]{1,0:T(8,128)(2,1)S(1)} %shard_map.75.refs_1_), kind=kOutput, calls=%fused_computation.9 | convolution fusion | flops 805306368 | bytes 4980736 | tf_op jit(solution)/shard_map/dot_general | solution.py:377
  65.2 1.6 %collective-permute-start.8 = (bf16[208,768]{1,0:T(8,128)(2,1)S(1)}, bf16[208,768]{1,0:T(8,128)(2,1)S(1)}, u32[]{:S(2)}, u32[]{:S(2)}) collective-permute-start(bf16[208,768]{1,0:T(8,128)(2,1)S(1)} %fusion), channel_id=1, source_target_pairs={{0,2},{1,3},{2,0},{3,1},{4,6},{5,7},{6,4},{7,5},{8,10},{9,11},{10,... | collective-permute-start | bytes 958472 | tf_op jit(solution)/shard_map/ppermute | solution.py:39
  68.1 1.6 %shard_map.81.refs_10_ = f32[2,512,256]{2,1,0:T(8,128)S(1)} custom-call(s32[8]{0:T(128)S(1)} %copy-done.5, s32[8]{0:T(128)S(1)} %copy-done.4, s32[8]{0:T(128)S(1)} %copy-done.6, bf16[256,2048]{1,0:T(8,128)(2,1)S(1)} %get-tuple-element.27.refs_3_, bf16[256,2048]{1,0:T(8,128)(2,1)S(1)} %collective-permute-done.13.refs_4_, ...), custom_call_target="tpu_custom_call" | custom-call | flops 5767499776 | tf_op jit(solution)/shard_map/pallas_call | solution.py:408
  69.7 1.4 %collective-permute-done.16.refs_9_ = bf16[448,512]{1,0:T(8,128)(2,1)S(1)} collective-permute-done((bf16[448,512]{1,0:T(8,128)(2,1)S(1)}, bf16[448,512]{1,0:T(8,128)(2,1)S(1)}, u32[]{:S(2)}, u32[]{:S(2)}) %collective-permute-start.16) | collective-permute-done | bytes 458784 | tf_op jit(solution)/shard_map/ppermute | solution.py:39
  71.1 1.1 %shard_map.82 = (f32[2,128,128]{2,1,0:T(8,128)S(1)}, f32[2,128,128]{2,1,0:T(8,128)S(1)}) custom-call(s32[8]{0:T(128)S(1)} %copy-done.5, s32[8]{0:T(128)S(1)} %copy-done.4, s32[8]{0:T(128)S(1)} %copy-done.6, bf16[256,2048]{1,0:T(8,128)(2,1)S(1)} %get-tuple-element.27.refs_3_, bf16[256,2048]{1,0:T(8,128)(2,1)S(1)} %collective-permute-done.13.refs_4_, ...), custom_call_target="tpu_custom_call" | custom-call | flops 17302499328 | tf_op jit(solution)/shard_map/pallas_call | solution.py:408
  72.9 2.3 %collective-permute-start.12 = (bf16[48,768]{1,0:T(8,128)(2,1)S(1)}, bf16[48,768]{1,0:T(8,128)(2,1)S(1)}, u32[]{:S(2)}, u32[]{:S(2)}) collective-permute-start(bf16[48,768]{1,0:T(8,128)(2,1)S(1)} %fusion.1), channel_id=1, source_target_pairs={{0,2},{1,3},{2,0},{3,1},{4,6},{5,7},{6,4},{7,5},{8,10},{9,11},{10,... | collective-permute-start | bytes 221192 | tf_op jit(solution)/shard_map/ppermute | solution.py:39
  75.9 2.2 %collective-permute-done.12 = bf16[48,768]{1,0:T(8,128)(2,1)S(1)} collective-permute-done((bf16[48,768]{1,0:T(8,128)(2,1)S(1)}, bf16[48,768]{1,0:T(8,128)(2,1)S(1)}, u32[]{:S(2)}, u32[]{:S(2)}) %collective-permute-start.12) | collective-permute-done | bytes 73760 | tf_op jit(solution)/shard_map/ppermute | solution.py:39
  78.1 1.4 %collective-permute-done.19 = f32[1,128,128]{2,1,0:T(8,128)S(1)} collective-permute-done((f32[1,128,128]{2,1,0:T(8,128)S(1)}, f32[1,128,128]{2,1,0:T(8,128)S(1)}, u32[]{:S(2)}, u32[]{:S(2)}) %collective-permute-start.19) | collective-permute-done | bytes 65568 | tf_op jit(solution)/shard_map/ppermute | solution.py:39
  79.6 2.1 %shard_map.83 = bf16[256,768]{1,0:T(8,128)(2,1)} custom-call(s32[8]{0:T(128)S(1)} %copy-done.5, s32[8]{0:T(128)S(1)} %copy-done.4, s32[8]{0:T(128)S(1)} %copy-done.6, bf16[256,768]{1,0:T(8,128)(2,1)S(1)} %pad_maximum_fusion.refs_3_, f32[256,768]{1,0:T(8,128)S(1)} %fusion.5.refs_4_, f32[256,768]{1,0:T(8,128)S(1)} %collective-permute-done.14.refs_5_, ...), custom_call_target="tpu_custom_call" | custom-call | flops 25165824 | bytes 1572864 | tf_op jit(solution)/shard_map/pallas_call | solution.py:426
  (50 shorter events, 9.5 us)
Async XLA Ops:
  3.3 26.4 %copy-start.2 = (bf16[512,16,64]{0,2,1:T(8,128)(2,1)S(1)}, bf16[512,16,64]{0,2,1:T(8,128)(2,1)}, u32[]{:S(2)}) copy-start(bf16[512,16,64]{0,2,1:T(8,128)(2,1)} %param.9) | copy-start | bytes 3145732
  3.3 26.4 %copy-start.4 = (s32[8]{0:T(128)S(1)}, s32[8]{0:T(128)}, u32[]{:S(2)}) copy-start(s32[8]{0:T(128)} %refs_1_.5) | copy-start | bytes 100
  5.0 40.3 %collective-permute-start = (bf16[208,2048]{1,0:T(8,128)(2,1)S(1)}, bf16[208,2048]{1,0:T(8,128)(2,1)S(1)}, u32[]{:S(2)}, u32[]{:S(2)}) collective-permute-start(bf16[208,2048]{1,0:T(8,128)(2,1)S(1)} %get-tuple-element.19), channel_id=1, source_target_pairs={{0,2},{1,3},{2,0},{3,1},{4,6},{5,7},{6,4},{7,5},{8,10},{9,11},{10,... | collective-permute-start | bytes 2555912 | tf_op jit(solution)/shard_map/ppermute | solution.py:39
  8.0 39.9 %collective-permute-start.6 = (bf16[208,2048]{1,0:T(8,128)(2,1)S(1)}, bf16[208,2048]{1,0:T(8,128)(2,1)S(1)}, u32[]{:S(2)}, u32[]{:S(2)}) collective-permute-start(bf16[208,2048]{1,0:T(8,128)(2,1)S(1)} %get-tuple-element.22), channel_id=1, source_target_pairs={{0,3},{1,2},{2,1},{3,0},{4,7},{5,6},{6,5},{7,4},{8,11},{9,10},{10,... | collective-permute-start | bytes 2555912 | tf_op jit(solution)/shard_map/ppermute | solution.py:39
  8.0 21.0 %collective-permute-start.2 = (bf16[256,768]{1,0:T(8,128)(2,1)S(1)}, bf16[256,768]{1,0:T(8,128)(2,1)S(1)}, u32[]{:S(2)}, u32[]{:S(2)}) collective-permute-start(bf16[256,768]{1,0:T(8,128)(2,1)S(1)} %get-tuple-element.20.refs_0_), channel_id=1, source_target_pairs={{0,8},{1,9},{2,10},{3,11},{4,12},{5,13},{6,14},{7,15},{8,0},{9,1},... | collective-permute-start | bytes 1179656 | tf_op jit(solution)/shard_map/ppermute | solution.py:39
  10.6 20.1 %collective-permute-start.1 = (bf16[256,768]{1,0:T(8,128)(2,1)S(1)}, bf16[256,768]{1,0:T(8,128)(2,1)S(1)}, u32[]{:S(2)}, u32[]{:S(2)}) collective-permute-start(bf16[256,768]{1,0:T(8,128)(2,1)S(1)} %get-tuple-element.20.refs_0_), channel_id=1, source_target_pairs={{0,4},{1,5},{2,6},{3,7},{4,0},{5,1},{6,2},{7,3},{8,12},{9,13},{10,... | collective-permute-start | bytes 1179656 | tf_op jit(solution)/shard_map/ppermute | solution.py:39
  29.1 15.8 %collective-permute-start.4 = (bf16[256,768]{1,0:T(8,128)(2,1)S(1)}, bf16[256,768]{1,0:T(8,128)(2,1)S(1)}, u32[]{:S(2)}, u32[]{:S(2)}) collective-permute-start(bf16[256,768]{1,0:T(8,128)(2,1)S(1)} %collective-permute-done.2.refs_0_.refs_4_.refs_1_), channel_id=1, source_target_pairs={{0,4},{1,5},{2,6},{3,7},{4,0},{5,1},{6,2},{7,3},{8,12},{9,13},{10,... | collective-permute-start | bytes 1179656 | tf_op jit(solution)/shard_map/ppermute | solution.py:39
  31.2 27.0 %collective-permute-start.3 = (bf16[512,768]{1,0:T(8,128)(2,1)S(1)}, bf16[512,768]{1,0:T(8,128)(2,1)S(1)}, u32[]{:S(2)}, u32[]{:S(2)}) collective-permute-start(bf16[512,768]{1,0:T(8,128)(2,1)S(1)} %shard_map.74), channel_id=1, source_target_pairs={{0,16},{16,0},{1,17},{17,1},{2,18},{18,2},{3,19},{19,3},{4,20},{20... | collective-permute-start | bytes 2359304 | tf_op jit(solution)/shard_map/ppermute | solution.py:39
  33.0 23.6 %collective-permute-start.15 = (bf16[448,512]{1,0:T(8,128)(2,1)S(1)}, bf16[448,512]{1,0:T(8,128)(2,1)S(1)}, u32[]{:S(2)}, u32[]{:S(2)}) collective-permute-start(bf16[448,512]{1,0:T(8,128)(2,1)S(1)} %shard_map.79), channel_id=1, source_target_pairs={{0,8},{1,9},{2,10},{3,11},{4,12},{5,13},{6,14},{7,15},{8,0},{9,1},... | collective-permute-start | bytes 1376264 | tf_op jit(solution)/shard_map/ppermute | solution.py:39
  45.2 22.9 %collective-permute-start.17 = (bf16[448,512]{1,0:T(8,128)(2,1)S(1)}, bf16[448,512]{1,0:T(8,128)(2,1)S(1)}, u32[]{:S(2)}, u32[]{:S(2)}) collective-permute-start(bf16[448,512]{1,0:T(8,128)(2,1)S(1)} %shard_map.80), channel_id=1, source_target_pairs={{0,4},{1,5},{2,6},{3,7},{4,0},{5,1},{6,2},{7,3},{8,12},{9,13},{10,... | collective-permute-start | bytes 1376264 | tf_op jit(solution)/shard_map/ppermute | solution.py:39
  45.3 13.6 %collective-permute-start.5 = (bf16[256,768]{1,0:T(8,128)(2,1)S(1)}, bf16[256,768]{1,0:T(8,128)(2,1)S(1)}, u32[]{:S(2)}, u32[]{:S(2)}) collective-permute-start(bf16[256,768]{1,0:T(8,128)(2,1)S(1)} %collective-permute-done.4.refs_6_.refs_1_), channel_id=1, source_target_pairs={{0,16},{16,0},{1,17},{17,1},{2,18},{18,2},{3,19},{19,3},{4,20},{20... | collective-permute-start | bytes 1179656 | tf_op jit(solution)/shard_map/ppermute | solution.py:39
  48.4 13.1 %collective-permute-start.10 = (bf16[48,2048]{1,0:T(8,128)(2,1)S(1)}, bf16[48,2048]{1,0:T(8,128)(2,1)S(1)}, u32[]{:S(2)}, u32[]{:S(2)}) collective-permute-start(bf16[48,2048]{1,0:T(8,128)(2,1)S(1)} %get-tuple-element.26), channel_id=1, source_target_pairs={{0,3},{1,2},{2,1},{3,0},{4,7},{5,6},{6,5},{7,4},{8,11},{9,10},{10,... | collective-permute-start | bytes 589832 | tf_op jit(solution)/shard_map/ppermute | solution.py:39
  56.6 11.3 %collective-permute-start.9 = (bf16[48,2048]{1,0:T(8,128)(2,1)S(1)}, bf16[48,2048]{1,0:T(8,128)(2,1)S(1)}, u32[]{:S(2)}, u32[]{:S(2)}) collective-permute-start(bf16[48,2048]{1,0:T(8,128)(2,1)S(1)} %get-tuple-element.25), channel_id=1, source_target_pairs={{0,2},{1,3},{2,0},{3,1},{4,6},{5,7},{6,4},{7,5},{8,10},{9,11},{10,... | collective-permute-start | bytes 589832 | tf_op jit(solution)/shard_map/ppermute | solution.py:39
  58.2 12.9 %collective-permute-start.16 = (bf16[448,512]{1,0:T(8,128)(2,1)S(1)}, bf16[448,512]{1,0:T(8,128)(2,1)S(1)}, u32[]{:S(2)}, u32[]{:S(2)}) collective-permute-start(bf16[448,512]{1,0:T(8,128)(2,1)S(1)} %collective-permute-done.15.refs_10_), channel_id=1, source_target_pairs={{0,4},{1,5},{2,6},{3,7},{4,0},{5,1},{6,2},{7,3},{8,12},{9,13},{10,... | collective-permute-start | bytes 1376264 | tf_op jit(solution)/shard_map/ppermute | solution.py:39
  60.6 4.7 %collective-permute-start.13 = (bf16[256,2048]{1,0:T(8,128)(2,1)S(1)}, bf16[256,2048]{1,0:T(8,128)(2,1)S(1)}, u32[]{:S(2)}, u32[]{:S(2)}) collective-permute-start(bf16[256,2048]{1,0:T(8,128)(2,1)S(1)} %shard_map.77), channel_id=1, source_target_pairs={{0,1},{1,0},{2,3},{3,2},{4,5},{5,4},{6,7},{7,6},{8,9},{9,8},{10,11... | collective-permute-start | bytes 3145736 | tf_op jit(solution)/shard_map/ppermute | solution.py:39
  61.5 2.7 %collective-permute-start.7 = (f32[208,768]{1,0:T(8,128)S(1)}, f32[208,768]{1,0:T(8,128)S(1)}, u32[]{:S(2)}, u32[]{:S(2)}) collective-permute-start(f32[208,768]{1,0:T(8,128)S(1)} %fusion.3), channel_id=1, source_target_pairs={{0,1},{1,0},{2,3},{3,2},{4,5},{5,4},{6,7},{7,6},{8,9},{9,8},{10,11... | collective-permute-start | bytes 1916936 | tf_op jit(solution)/shard_map/ppermute | solution.py:39
  64.2 8.0 %collective-permute-start.11 = (f32[48,768]{1,0:T(8,128)S(1)}, f32[48,768]{1,0:T(8,128)S(1)}, u32[]{:S(2)}, u32[]{:S(2)}) collective-permute-start(f32[48,768]{1,0:T(8,128)S(1)} %fusion.4), channel_id=1, source_target_pairs={{0,1},{1,0},{2,3},{3,2},{4,5},{5,4},{6,7},{7,6},{8,9},{9,8},{10,11... | collective-permute-start | bytes 442376 | tf_op jit(solution)/shard_map/ppermute | solution.py:39
  65.2 2.8 %copy-start.5 = (s32[8]{0:T(128)S(1)}, s32[8]{0:T(128)}, u32[]{:S(2)}) copy-start(s32[8]{0:T(128)} %refs_0_.5) | copy-start | bytes 100
  65.2 12.9 %collective-permute-start.8 = (bf16[208,768]{1,0:T(8,128)(2,1)S(1)}, bf16[208,768]{1,0:T(8,128)(2,1)S(1)}, u32[]{:S(2)}, u32[]{:S(2)}) collective-permute-start(bf16[208,768]{1,0:T(8,128)(2,1)S(1)} %fusion), channel_id=1, source_target_pairs={{0,2},{1,3},{2,0},{3,1},{4,6},{5,7},{6,4},{7,5},{8,10},{9,11},{10,... | collective-permute-start | bytes 958472 | tf_op jit(solution)/shard_map/ppermute | solution.py:39
  67.9 11.6 %collective-permute-start.14 = (f32[256,768]{1,0:T(8,128)S(1)}, f32[256,768]{1,0:T(8,128)S(1)}, u32[]{:S(2)}, u32[]{:S(2)}) collective-permute-start(f32[256,768]{1,0:T(8,128)S(1)} %fusion.6), channel_id=1, source_target_pairs={{0,1},{1,0},{2,3},{3,2},{4,5},{5,4},{6,7},{7,6},{8,9},{9,8},{10,11... | collective-permute-start | bytes 2359304 | tf_op jit(solution)/shard_map/ppermute | solution.py:39
  72.2 7.4 %copy-start.1 = (bf16[16,64,768]{2,1,0:T(8,128)(2,1)S(1)}, bf16[16,64,768]{2,1,0:T(8,128)(2,1)}, u32[]{:S(2)}) copy-start(bf16[16,64,768]{2,1,0:T(8,128)(2,1)} %refs_8_.1) | copy-start | bytes 4718596
  72.2 3.0 %collective-permute-start.18 = (f32[2,128,128]{2,1,0:T(8,128)S(1)}, f32[2,128,128]{2,1,0:T(8,128)S(1)}, u32[]{:S(2)}, u32[]{:S(2)}) collective-permute-start(f32[2,128,128]{2,1,0:T(8,128)S(1)} %get-tuple-element.32), channel_id=1, source_target_pairs={{0,1},{1,0},{2,3},{3,2},{4,5},{5,4},{6,7},{7,6},{8,9},{9,8},{10,11... | collective-permute-start | bytes 393224 | tf_op jit(solution)/shard_map/ppermute | solution.py:39
  72.9 5.2 %collective-permute-start.12 = (bf16[48,768]{1,0:T(8,128)(2,1)S(1)}, bf16[48,768]{1,0:T(8,128)(2,1)S(1)}, u32[]{:S(2)}, u32[]{:S(2)}) collective-permute-start(bf16[48,768]{1,0:T(8,128)(2,1)S(1)} %fusion.1), channel_id=1, source_target_pairs={{0,2},{1,3},{2,0},{3,1},{4,6},{5,7},{6,4},{7,5},{8,10},{9,11},{10,... | collective-permute-start | bytes 221192 | tf_op jit(solution)/shard_map/ppermute | solution.py:39
  75.2 4.3 %collective-permute-start.19 = (f32[1,128,128]{2,1,0:T(8,128)S(1)}, f32[1,128,128]{2,1,0:T(8,128)S(1)}, u32[]{:S(2)}, u32[]{:S(2)}) collective-permute-start(f32[1,128,128]{2,1,0:T(8,128)S(1)} %get-tuple-element.33), channel_id=1, source_target_pairs={{0,2},{1,3},{2,0},{3,1},{4,6},{5,7},{6,4},{7,5},{8,10},{9,11},{10,... | collective-permute-start | bytes 196616 | tf_op jit(solution)/shard_map/ppermute | solution.py:39
  (3 other events, 6.2 us)
